TPU v7x, 32 devices: a whole 2x2x4 slice. The times are simulated.
32 devices in a mesh: sub: 4 (over z), crow: 4 (over x, core), ccol: 2 (over y).
Axes of the slice: x: 2, y: 2, z: 4, core: 2. Of those that a mesh axis runs over, the one named last changes fastest.
Arguments:
- rhs: float32 [24, 48, 3, 10, 256], P('sub', ('crow', 'ccol')), may hold values from -6 to 6
- start: float32 [24, 48, 3, 10, 256], P('sub', ('crow', 'ccol')), may hold values from -1.75 to 1.75
- stiffness: float32 [24, 48, 3, 10], P('sub', ('crow', 'ccol')), may hold values from 0.1 to 1
- sub_inverse: bfloat16 [32, 1920, 1920], P(('sub', 'crow', 'ccol')), may hold values from -0.0625 to 0.0625
- basis: bfloat16 [32, 1920, 128], P(('sub', 'crow', 'ccol')), may hold values from -0.0625 to 0.0625
- coarse_inverse: bfloat16 [4, 512, 2048], P(None, ('crow', 'ccol'), 'sub'), may hold values from -0.1875 to 0.1875
- offsets: int32 [4, 8], P('sub'), may hold values from 0 to 464, as said below
Outputs:
- solution: float32 [24, 48, 3, 10, 256], P('sub', ('crow', 'ccol'))
Inputs may be any that keep to these rules, and one draw needn't show every extreme that they name: In every row g, offsets[g, 0] = 0 and the offsets rise; each count (next offset minus this one, 512 after the last) lies between 48 and 128, and every group has a subdomain with exactly 128.
All inputs are finite; a program needn't handle non-finite values.
Results may differ from a plain program's by a relative error of at most 0.0037.
Values may be sent and summed in bfloat16 or wider, within the bound.
No kernel may reach another device: no remote copies, remote signals or barrier semaphores. Data moves between devices by JAX's collectives and lax.ppermute only.
A program may use at most 64 MiB of HBM per device.

v0:
```python
import jax
import jax.numpy as jnp
from jax import lax
from jax.sharding import PartitionSpec as P

ITERS = 2


def extended_2(block, sides, width):
    for axis, dim in sides:
        count = lax.axis_size(axis)
        forward = [(i, i + 1) for i in range(count - 1)]
        backward = [(target, source) for source, target in forward]
        low = lax.ppermute(
            lax.slice_in_dim(block, block.shape[dim] - width, None, axis=dim), axis, forward
        )
        high = lax.ppermute(lax.slice_in_dim(block, 0, width, axis=dim), axis, backward)
        block = jnp.concatenate([low, block, high], axis=dim)
    return block


def neighbours(widened):
    padded_z = jnp.pad(widened, ((0, 0), (0, 0), (0, 0), (1, 1), (0, 0)))
    beside = padded_z[2:, 1:-1, :, 1:-1] + padded_z[:-2, 1:-1, :, 1:-1]
    beside = beside + padded_z[1:-1, 2:, :, 1:-1] + padded_z[1:-1, :-2, :, 1:-1]
    beside = beside + padded_z[1:-1, 1:-1, :, 2:] + padded_z[1:-1, 1:-1, :, :-2]
    return beside


def shards(rhs, start, stiffness, sub_inverse, basis, coarse_inverse, offsets):
    cells_s, cells_q, comps, layers, columns = rhs.shape
    kgroup = coarse_inverse.shape[2]
    share_rows = coarse_inverse.shape[1]
    max_cols = basis.shape[2]
    group_offsets = offsets[0]
    groups = group_offsets.shape[0]
    counts = jnp.concatenate([group_offsets[1:], jnp.full((1,), kgroup, jnp.int32)]) - group_offsets
    member = lax.axis_index(("crow", "ccol"))
    sub_index = lax.axis_index("sub")
    member_ids = jnp.arange(groups, dtype=jnp.int32)
    picked = member_ids == member
    own_offset = jnp.sum(jnp.where(picked, group_offsets, 0))
    own_count = jnp.sum(jnp.where(picked, counts, 0))
    col_ids = jnp.arange(max_cols, dtype=jnp.int32)
    wanted = jnp.where(col_ids < own_count, own_offset + col_ids, -1)
    diagonal = (6.0 + stiffness)[..., None]
    flat_inverse = coarse_inverse.reshape(-1, kgroup)
    local_inverse = sub_inverse[0]
    local_basis = basis[0]
    solution = start
    for sweep in range(ITERS):
        widened = extended_2(solution, (("sub", 0), (("crow", "ccol"), 1)), 1)
        residual = rhs - (diagonal * solution - neighbours(widened))
        extended = extended_2(residual.astype(jnp.bfloat16), (("sub", 0), (("crow", "ccol"), 1)), 1)
        flat_res = extended.reshape(-1, columns)
        projected = lax.dot_general(
            local_basis, flat_res, (((0,), (0,)), ((), ())), preferred_element_type=jnp.float32
        )
        restricted = jnp.where(col_ids[:, None] < own_count, projected, 0.0).astype(jnp.bfloat16)
        place_piece = lax.all_gather(restricted, ("crow", "ccol"), axis=0, tiled=True)
        place_row_ids = jnp.arange(place_piece.shape[0], dtype=jnp.int32)
        owner_ids = place_row_ids // max_cols
        column = place_row_ids % max_cols
        matches = member_ids[:, None] == owner_ids[None, :]
        slot_base = jnp.sum(jnp.where(matches, group_offsets[:, None], 0), axis=0)
        slot_limit = jnp.sum(jnp.where(matches, counts[:, None], 0), axis=0)
        targets = jnp.where(column < slot_limit, slot_base + column, -1)
        place_selector = (jnp.arange(kgroup, dtype=jnp.int32)[:, None] == targets[None, :]).astype(
            jnp.bfloat16
        )
        placed_sum = jnp.dot(place_selector, place_piece, preferred_element_type=jnp.float32)
        coefficients = placed_sum.astype(jnp.bfloat16)
        partial_value = jnp.dot(flat_inverse, coefficients, preferred_element_type=jnp.float32)
        summed = lax.psum(partial_value, "sub")
        own_share = lax.dynamic_slice_in_dim(summed, sub_index * share_rows, share_rows, 0)
        amounts = own_share.astype(jnp.bfloat16)
        piece = lax.all_gather(amounts, ("crow", "ccol"), axis=0, tiled=True)
        row_ids = jnp.arange(piece.shape[0], dtype=jnp.int32)
        slot_ids = row_ids % share_rows * groups + row_ids // share_rows
        selector = (wanted[:, None] == slot_ids[None, :]).astype(jnp.bfloat16)
        chosen = jnp.dot(selector, piece, preferred_element_type=jnp.float32)
        chosen = chosen.astype(jnp.bfloat16)
        fine_part = jnp.dot(local_inverse, flat_res, preferred_element_type=jnp.float32)
        coarse_part = jnp.dot(local_basis, chosen, preferred_element_type=jnp.float32)
        correction = (fine_part + coarse_part).reshape(
            cells_s + 2, cells_q + 2, comps, layers, columns
        )
        solution = solution + correction[1:-1, 1:-1]
    return solution


def solution(mesh):
    return jax.shard_map(
        shards,
        mesh=mesh,
        in_specs=(
            P("sub", ("crow", "ccol"), None, None, None),
            P("sub", ("crow", "ccol"), None, None, None),
            P("sub", ("crow", "ccol"), None, None),
            P(("sub", "crow", "ccol"), None, None),
            P(("sub", "crow", "ccol"), None, None),
            P(None, ("crow", "ccol"), "sub"),
            P("sub", None),
        ),
        out_specs=P("sub", ("crow", "ccol"), None, None, None),
        check_vma=False,
    )
```

profile of v0, /device:TPU:0, one launch (start us, length us, event | category | flops | bytes accessed | tf_op | source)
XLA Modules:
  0.0 283.1 jit_solution(1412716013952685663)
XLA Ops:
  3.1 4.9 %collective-permute-start.1 = (f32[1,6,3,10,256]{4,3,2,1,0:T(8,128)S(1)}, f32[1,6,3,10,256]{4,3,2,1,0:T(8,128)S(1)}, u32[]{:S(2)}, u32[]{:S(2)}) collective-permute-start(f32[1,6,3,10,256]{4,3,2,1,0:T(8,128)S(1)} %get-tuple-element.16), channel_id=1, source_target_pairs={{0,8},{8,16},{16,24},{1,9},{9,17},{17,25},{2,10},{10,18},{18,26},{... | collective-permute-start | bytes 552968 | tf_op jit(solution)/shard_map/ppermute | solution.py:14
  10.3 4.0 %collective-permute-done.1 = f32[1,6,3,10,256]{4,3,2,1,0:T(8,128)S(1)} collective-permute-done((f32[1,6,3,10,256]{4,3,2,1,0:T(8,128)S(1)}, f32[1,6,3,10,256]{4,3,2,1,0:T(8,128)S(1)}, u32[]{:S(2)}, u32[]{:S(2)}) %collective-permute-start.1) | collective-permute-done | bytes 184352 | tf_op jit(solution)/shard_map/ppermute | solution.py:14
  14.7 3.8 %collective-permute-done = f32[1,6,3,10,256]{4,3,2,1,0:T(8,128)S(1)} collective-permute-done((f32[1,6,3,10,256]{4,3,2,1,0:T(8,128)S(1)}, f32[1,6,3,10,256]{4,3,2,1,0:T(8,128)S(1)}, u32[]{:S(2)}, u32[]{:S(2)}) %collective-permute-start) | collective-permute-done | bytes 184352 | tf_op jit(solution)/shard_map/ppermute | solution.py:17
  19.8 4.6 %collective-permute-start.3 = (f32[8,1,3,10,256]{4,3,2,1,0:T(8,128)S(1)}, f32[8,1,3,10,256]{4,3,2,1,0:T(8,128)S(1)}, u32[]{:S(2)}, u32[]{:S(2)}) collective-permute-start(f32[8,1,3,10,256]{4,3,2,1,0:T(8,128)S(1)} %get-tuple-element.11), channel_id=1, source_target_pairs={{0,1},{1,2},{2,3},{3,4},{4,5},{5,6},{6,7},{8,9},{9,10},{10,11},{11... | collective-permute-start | bytes 737288 | tf_op jit(solution)/shard_map/ppermute | solution.py:14
  24.5 5.6 %collective-permute-done.2 = f32[8,1,3,10,256]{4,3,2,1,0:T(8,128)S(1)} collective-permute-done((f32[8,1,3,10,256]{4,3,2,1,0:T(8,128)S(1)}, f32[8,1,3,10,256]{4,3,2,1,0:T(8,128)S(1)}, u32[]{:S(2)}, u32[]{:S(2)}) %collective-permute-start.2) | collective-permute-done | bytes 245792 | tf_op jit(solution)/shard_map/ppermute | solution.py:17
  30.1 5.1 %collective-permute-done.3 = f32[8,1,3,10,256]{4,3,2,1,0:T(8,128)S(1)} collective-permute-done((f32[8,1,3,10,256]{4,3,2,1,0:T(8,128)S(1)}, f32[8,1,3,10,256]{4,3,2,1,0:T(8,128)S(1)}, u32[]{:S(2)}, u32[]{:S(2)}) %collective-permute-start.3) | collective-permute-done | bytes 245792 | tf_op jit(solution)/shard_map/ppermute | solution.py:14
  37.4 3.5 %collective-permute-start.4 = (bf16[1,6,3,10,256]{4,3,2,1,0:T(8,128)(2,1)S(1)}, bf16[1,6,3,10,256]{4,3,2,1,0:T(8,128)(2,1)S(1)}, u32[]{:S(2)}, u32[]{:S(2)}) collective-permute-start(bf16[1,6,3,10,256]{4,3,2,1,0:T(8,128)(2,1)S(1)} %get-tuple-element.23), channel_id=1, source_target_pairs={{0,8},{8,16},{16,24},{1,9},{9,17},{17,25},{2,10},{10,18},{18,26},{... | collective-permute-start | bytes 276488 | tf_op jit(solution)/shard_map/ppermute | solution.py:14
  43.6 4.4 %collective-permute-done.5 = bf16[1,6,3,10,256]{4,3,2,1,0:T(8,128)(2,1)S(1)} collective-permute-done((bf16[1,6,3,10,256]{4,3,2,1,0:T(8,128)(2,1)S(1)}, bf16[1,6,3,10,256]{4,3,2,1,0:T(8,128)(2,1)S(1)}, u32[]{:S(2)}, u32[]{:S(2)}) %collective-permute-start.5) | collective-permute-done | bytes 92192 | tf_op jit(solution)/shard_map/ppermute | solution.py:17
  48.0 4.4 %collective-permute-start.6 = (bf16[8,1,3,10,256]{4,3,2,1,0:T(8,128)(2,1)S(1)}, bf16[8,1,3,10,256]{4,3,2,1,0:T(8,128)(2,1)S(1)}, u32[]{:S(2)}, u32[]{:S(2)}) collective-permute-start(bf16[8,1,3,10,256]{4,3,2,1,0:T(8,128)(2,1)S(1)} %get-tuple-element.19), channel_id=1, source_target_pairs={{0,1},{1,2},{2,3},{3,4},{4,5},{5,6},{6,7},{8,9},{9,10},{10,11},{11... | collective-permute-start | bytes 368648 | tf_op jit(solution)/shard_map/ppermute | solution.py:14
  56.1 5.0 %collective-permute-done.7 = bf16[8,1,3,10,256]{4,3,2,1,0:T(8,128)(2,1)} collective-permute-done((bf16[8,1,3,10,256]{4,3,2,1,0:T(8,128)(2,1)S(1)}, bf16[8,1,3,10,256]{4,3,2,1,0:T(8,128)(2,1)}, u32[]{:S(2)}, u32[]{:S(2)}) %collective-permute-start.7) | collective-permute-done | bytes 122912 | tf_op jit(solution)/shard_map/ppermute | solution.py:17
  65.2 19.0 %all_gather.12 = bf16[1024,256]{0,1:T(8,128)(2,1)S(1)} all-gather(bf16[128,256]{0,1:T(8,128)(2,1)S(1)} %fusion.38), channel_id=1, replica_groups=mesh['sub'=4,'crow'=4,'ccol'=2] {'crow','ccol'}, dimensions={0}, use_global_device_ids=true | all-gather | bytes 589824 | tf_op jit(solution)/shard_map/all_gather | solution.py:60
  85.0 23.4 %all-reduce.4 = bf16[256,256]{1,0:T(8,128)(2,1)S(1)} all-reduce(f32[256,256]{1,0:T(8,128)S(1)} %fusion.34), channel_id=1, replica_groups=mesh['sub'=4,'crow'=4,'ccol'=2] {'sub'}, use_global_device_ids=true, to_apply=%region_4.5 | all-reduce | flops 65536 | bytes 393216 | tf_op jit(solution)/shard_map/psum | solution.py:74
  108.4 18.6 %all_gather.13 = bf16[512,256]{1,0:T(8,128)(2,1)} all-gather(bf16[64,256]{1,0:T(8,128)(2,1)S(1)} %dynamic-slice_convert_fusion.1), channel_id=1, replica_groups=mesh['sub'=4,'crow'=4,'ccol'=2] {'crow','ccol'}, dimensions={0}, use_global_device_ids=true | all-gather | bytes 294912 | tf_op jit(solution)/shard_map/all_gather | solution.py:77
  128.7 6.8 %fusion.8 = f32[1920,256]{0,1:T(8,128)} fusion(f32[256,1920]{1,0:T(8,128)S(1)} %fusion.39, bf16[1920,256]{1,0:T(8,128)(2,1)S(1)} %copy-done.6, bf16[1,1920,1920]{2,1,0:T(8,128)(2,1)} %param.10), kind=kOutput, calls=%fused_computation.14 | convolution fusion | flops 1887928320 | bytes 12288000 | tf_op jit(solution)/shard_map/dot_general | solution.py:83
  139.1 2.4 slice_add_fusion.3
  142.9 4.6 %collective-permute-start.9 = (f32[1,6,3,10,256]{4,3,2,1,0:T(8,128)S(1)}, f32[1,6,3,10,256]{4,3,2,1,0:T(8,128)S(1)}, u32[]{:S(2)}, u32[]{:S(2)}) collective-permute-start(f32[1,6,3,10,256]{4,3,2,1,0:T(8,128)S(1)} %get-tuple-element.13), channel_id=1, source_target_pairs={{0,8},{8,16},{16,24},{1,9},{9,17},{17,25},{2,10},{10,18},{18,26},{... | collective-permute-start | bytes 552968 | tf_op jit(solution)/shard_map/ppermute | solution.py:14
  147.4 5.4 %collective-permute-done.8 = f32[1,6,3,10,256]{4,3,2,1,0:T(8,128)S(1)} collective-permute-done((f32[1,6,3,10,256]{4,3,2,1,0:T(8,128)S(1)}, f32[1,6,3,10,256]{4,3,2,1,0:T(8,128)S(1)}, u32[]{:S(2)}, u32[]{:S(2)}) %collective-permute-start.8) | collective-permute-done | bytes 184352 | tf_op jit(solution)/shard_map/ppermute | solution.py:17
  155.3 4.7 %collective-permute-start.11 = (f32[8,1,3,10,256]{4,3,2,1,0:T(8,128)S(1)}, f32[8,1,3,10,256]{4,3,2,1,0:T(8,128)S(1)}, u32[]{:S(2)}, u32[]{:S(2)}) collective-permute-start(f32[8,1,3,10,256]{4,3,2,1,0:T(8,128)S(1)} %get-tuple-element.9), channel_id=1, source_target_pairs={{0,1},{1,2},{2,3},{3,4},{4,5},{5,6},{6,7},{8,9},{9,10},{10,11},{11... | collective-permute-start | bytes 737288 | tf_op jit(solution)/shard_map/ppermute | solution.py:14
  160.1 6.2 %collective-permute-done.10 = f32[8,1,3,10,256]{4,3,2,1,0:T(8,128)S(1)} collective-permute-done((f32[8,1,3,10,256]{4,3,2,1,0:T(8,128)S(1)}, f32[8,1,3,10,256]{4,3,2,1,0:T(8,128)S(1)}, u32[]{:S(2)}, u32[]{:S(2)}) %collective-permute-start.10) | collective-permute-done | bytes 245792 | tf_op jit(solution)/shard_map/ppermute | solution.py:17
  166.3 5.0 %collective-permute-done.11 = f32[8,1,3,10,256]{4,3,2,1,0:T(8,128)S(1)} collective-permute-done((f32[8,1,3,10,256]{4,3,2,1,0:T(8,128)S(1)}, f32[8,1,3,10,256]{4,3,2,1,0:T(8,128)S(1)}, u32[]{:S(2)}, u32[]{:S(2)}) %collective-permute-start.11) | collective-permute-done | bytes 245792 | tf_op jit(solution)/shard_map/ppermute | solution.py:14
  173.4 4.1 %collective-permute-start.12 = (bf16[1,6,3,10,256]{4,3,2,1,0:T(8,128)(2,1)S(1)}, bf16[1,6,3,10,256]{4,3,2,1,0:T(8,128)(2,1)S(1)}, u32[]{:S(2)}, u32[]{:S(2)}) collective-permute-start(bf16[1,6,3,10,256]{4,3,2,1,0:T(8,128)(2,1)S(1)} %get-tuple-element.21), channel_id=1, source_target_pairs={{0,8},{8,16},{16,24},{1,9},{9,17},{17,25},{2,10},{10,18},{18,26},{... | collective-permute-start | bytes 276488 | tf_op jit(solution)/shard_map/ppermute | solution.py:14
  180.2 4.4 %collective-permute-done.13 = bf16[1,6,3,10,256]{4,3,2,1,0:T(8,128)(2,1)S(1)} collective-permute-done((bf16[1,6,3,10,256]{4,3,2,1,0:T(8,128)(2,1)S(1)}, bf16[1,6,3,10,256]{4,3,2,1,0:T(8,128)(2,1)S(1)}, u32[]{:S(2)}, u32[]{:S(2)}) %collective-permute-start.13) | collective-permute-done | bytes 92192 | tf_op jit(solution)/shard_map/ppermute | solution.py:17
  184.6 4.5 %collective-permute-start.14 = (bf16[8,1,3,10,256]{4,3,2,1,0:T(8,128)(2,1)S(1)}, bf16[8,1,3,10,256]{4,3,2,1,0:T(8,128)(2,1)S(1)}, u32[]{:S(2)}, u32[]{:S(2)}) collective-permute-start(bf16[8,1,3,10,256]{4,3,2,1,0:T(8,128)(2,1)S(1)} %get-tuple-element.17), channel_id=1, source_target_pairs={{0,1},{1,2},{2,3},{3,4},{4,5},{5,6},{6,7},{8,9},{9,10},{10,11},{11... | collective-permute-start | bytes 368648 | tf_op jit(solution)/shard_map/ppermute | solution.py:14
  190.6 3.5 %collective-permute-done.14 = bf16[8,1,3,10,256]{4,3,2,1,0:T(8,128)(2,1)S(1)} collective-permute-done((bf16[8,1,3,10,256]{4,3,2,1,0:T(8,128)(2,1)S(1)}, bf16[8,1,3,10,256]{4,3,2,1,0:T(8,128)(2,1)S(1)}, u32[]{:S(2)}, u32[]{:S(2)}) %collective-permute-start.14) | collective-permute-done | bytes 122912 | tf_op jit(solution)/shard_map/ppermute | solution.py:14
  194.1 4.6 %collective-permute-done.15 = bf16[8,1,3,10,256]{4,3,2,1,0:T(8,128)(2,1)S(1)} collective-permute-done((bf16[8,1,3,10,256]{4,3,2,1,0:T(8,128)(2,1)S(1)}, bf16[8,1,3,10,256]{4,3,2,1,0:T(8,128)(2,1)S(1)}, u32[]{:S(2)}, u32[]{:S(2)}) %collective-permute-start.15) | collective-permute-done | bytes 122912 | tf_op jit(solution)/shard_map/ppermute | solution.py:17
  200.2 2.3 reshape.101
  203.0 20.7 %all_gather.14 = bf16[1024,256]{0,1:T(8,128)(2,1)} all-gather(bf16[128,256]{0,1:T(8,128)(2,1)S(1)} %fusion.37), channel_id=1, replica_groups=mesh['sub'=4,'crow'=4,'ccol'=2] {'crow','ccol'}, dimensions={0}, use_global_device_ids=true | all-gather | bytes 589824 | tf_op jit(solution)/shard_map/all_gather | solution.py:60
  225.5 21.9 %all-reduce.5 = bf16[256,256]{1,0:T(8,128)(2,1)} all-reduce(f32[256,256]{1,0:T(8,128)S(1)} %fusion.32), channel_id=1, replica_groups=mesh['sub'=4,'crow'=4,'ccol'=2] {'sub'}, use_global_device_ids=true, to_apply=%region_5.6 | all-reduce | flops 65536 | bytes 393216 | tf_op jit(solution)/shard_map/psum | solution.py:74
  248.2 15.4 %all_gather.15 = bf16[512,256]{1,0:T(8,128)(2,1)S(1)} all-gather(bf16[64,256]{1,0:T(8,128)(2,1)S(1)} %dynamic-slice_convert_fusion), channel_id=1, replica_groups=mesh['sub'=4,'crow'=4,'ccol'=2] {'crow','ccol'}, dimensions={0}, use_global_device_ids=true | all-gather | bytes 294912 | tf_op jit(solution)/shard_map/all_gather | solution.py:77
  265.6 7.3 %fusion.14 = f32[1920,256]{0,1:T(8,128)} fusion(f32[256,1920]{1,0:T(8,128)} %fusion.40, bf16[1920,256]{1,0:T(8,128)(2,1)S(1)} %reshape.101, bf16[1,1920,1920]{2,1,0:T(8,128)(2,1)} %param.10), kind=kOutput, calls=%fused_computation.16 | convolution fusion | flops 1887928320 | bytes 12288000 | tf_op jit(solution)/shard_map/dot_general | solution.py:83
  272.9 2.8 %copy.63 = f32[1920,256]{1,0:T(8,128)} copy(f32[1920,256]{0,1:T(8,128)} %fusion.14) | data formatting | bytes 3932160 | tf_op jit(solution)/shard_map/add | solution.py:85
  275.8 3.4 %reshape.102 = f32[8,8,3,10,256]{4,3,2,1,0:T(8,128)} reshape(f32[1920,256]{1,0:T(8,128)} %copy.63) | data formatting | bytes 3932160 | tf_op jit(solution)/shard_map/reshape | solution.py:85
  (72 shorter events, 46.3 us)
Async XLA Ops:
  0.0 63.5 %copy-start = (bf16[1,1920,128]{2,1,0:T(8,128)(2,1)S(1)}, bf16[1,1920,128]{2,1,0:T(8,128)(2,1)}, u32[]{:S(2)}) copy-start(bf16[1,1920,128]{2,1,0:T(8,128)(2,1)} %param.11) | copy-start | bytes 1474564
  0.0 14.3 %copy-start.1 = (f32[6,6,3,10,256]{4,2,3,1,0:T(4,128)S(1)}, f32[6,6,3,10,256]{4,2,3,1,0:T(4,128)}, u32[]{:S(2)}) copy-start(f32[6,6,3,10,256]{4,2,3,1,0:T(4,128)} %param.8) | copy-start | bytes 3317764
  0.0 9.4 %copy-start.8 = (s32[1,8]{1,0:T(1,128)S(1)}, s32[1,8]{1,0:T(1,128)}, u32[]{:S(2)}) copy-start(s32[1,8]{1,0:T(1,128)} %param.13) | copy-start | bytes 100
  1.8 1.3 copy-start.2
  3.1 11.2 %collective-permute-start.1 = (f32[1,6,3,10,256]{4,3,2,1,0:T(8,128)S(1)}, f32[1,6,3,10,256]{4,3,2,1,0:T(8,128)S(1)}, u32[]{:S(2)}, u32[]{:S(2)}) collective-permute-start(f32[1,6,3,10,256]{4,3,2,1,0:T(8,128)S(1)} %get-tuple-element.16), channel_id=1, source_target_pairs={{0,8},{8,16},{16,24},{1,9},{9,17},{17,25},{2,10},{10,18},{18,26},{... | collective-permute-start | bytes 552968 | tf_op jit(solution)/shard_map/ppermute | solution.py:14
  8.1 10.4 %collective-permute-start = (f32[1,6,3,10,256]{4,3,2,1,0:T(8,128)S(1)}, f32[1,6,3,10,256]{4,3,2,1,0:T(8,128)S(1)}, u32[]{:S(2)}, u32[]{:S(2)}) collective-permute-start(f32[1,6,3,10,256]{4,3,2,1,0:T(8,128)S(1)} %get-tuple-element.15), channel_id=1, source_target_pairs={{8,0},{16,8},{24,16},{9,1},{17,9},{25,17},{10,2},{18,10},{26,18},{... | collective-permute-start | bytes 552968 | tf_op jit(solution)/shard_map/ppermute | solution.py:17
  14.6 9.8 %copy-start.7 = (f32[6,6,3,10]{3,2,1,0:T(4,128)S(1)}, f32[6,6,3,10]{3,2,1,0:T(4,128)}, u32[]{:S(2)}) copy-start(f32[6,6,3,10]{3,2,1,0:T(4,128)} %param.9) | copy-start | bytes 12964
  18.5 11.6 %collective-permute-start.2 = (f32[8,1,3,10,256]{4,3,2,1,0:T(8,128)S(1)}, f32[8,1,3,10,256]{4,3,2,1,0:T(8,128)S(1)}, u32[]{:S(2)}, u32[]{:S(2)}) collective-permute-start(f32[8,1,3,10,256]{4,3,2,1,0:T(8,128)S(1)} %get-tuple-element.12), channel_id=1, source_target_pairs={{1,0},{2,1},{3,2},{4,3},{5,4},{6,5},{7,6},{9,8},{10,9},{11,10},{12... | collective-permute-start | bytes 737288 | tf_op jit(solution)/shard_map/ppermute | solution.py:17
  19.8 15.3 %collective-permute-start.3 = (f32[8,1,3,10,256]{4,3,2,1,0:T(8,128)S(1)}, f32[8,1,3,10,256]{4,3,2,1,0:T(8,128)S(1)}, u32[]{:S(2)}, u32[]{:S(2)}) collective-permute-start(f32[8,1,3,10,256]{4,3,2,1,0:T(8,128)S(1)} %get-tuple-element.11), channel_id=1, source_target_pairs={{0,1},{1,2},{2,3},{3,4},{4,5},{5,6},{6,7},{8,9},{9,10},{10,11},{11... | collective-permute-start | bytes 737288 | tf_op jit(solution)/shard_map/ppermute | solution.py:14
  24.5 11.4 %copy-start.3 = (f32[6,6,3,10,256]{4,3,2,1,0:T(8,128)S(1)}, f32[6,6,3,10,256]{4,3,2,1,0:T(8,128)}, u32[]{:S(2)}) copy-start(f32[6,6,3,10,256]{4,3,2,1,0:T(8,128)} %copy-done.2) | copy-start | bytes 3317764
  24.5 11.4 %copy-start.4 = (f32[6,6,3,10,256]{4,2,3,1,0:T(4,128)S(1)}, f32[6,6,3,10,256]{4,2,3,1,0:T(4,128)}, u32[]{:S(2)}) copy-start(f32[6,6,3,10,256]{4,2,3,1,0:T(4,128)} %param.7) | copy-start | bytes 3317764
  37.4 6.1 %collective-permute-start.4 = (bf16[1,6,3,10,256]{4,3,2,1,0:T(8,128)(2,1)S(1)}, bf16[1,6,3,10,256]{4,3,2,1,0:T(8,128)(2,1)S(1)}, u32[]{:S(2)}, u32[]{:S(2)}) collective-permute-start(bf16[1,6,3,10,256]{4,3,2,1,0:T(8,128)(2,1)S(1)} %get-tuple-element.23), channel_id=1, source_target_pairs={{0,8},{8,16},{16,24},{1,9},{9,17},{17,25},{2,10},{10,18},{18,26},{... | collective-permute-start | bytes 276488 | tf_op jit(solution)/shard_map/ppermute | solution.py:14
  40.9 7.0 %collective-permute-start.5 = (bf16[1,6,3,10,256]{4,3,2,1,0:T(8,128)(2,1)S(1)}, bf16[1,6,3,10,256]{4,3,2,1,0:T(8,128)(2,1)S(1)}, u32[]{:S(2)}, u32[]{:S(2)}) collective-permute-start(bf16[1,6,3,10,256]{4,3,2,1,0:T(8,128)(2,1)S(1)} %get-tuple-element.24), channel_id=1, source_target_pairs={{8,0},{16,8},{24,16},{9,1},{17,9},{25,17},{10,2},{18,10},{26,18},{... | collective-permute-start | bytes 276488 | tf_op jit(solution)/shard_map/ppermute | solution.py:17
  48.0 8.1 %collective-permute-start.6 = (bf16[8,1,3,10,256]{4,3,2,1,0:T(8,128)(2,1)S(1)}, bf16[8,1,3,10,256]{4,3,2,1,0:T(8,128)(2,1)S(1)}, u32[]{:S(2)}, u32[]{:S(2)}) collective-permute-start(bf16[8,1,3,10,256]{4,3,2,1,0:T(8,128)(2,1)S(1)} %get-tuple-element.19), channel_id=1, source_target_pairs={{0,1},{1,2},{2,3},{3,4},{4,5},{5,6},{6,7},{8,9},{9,10},{10,11},{11... | collective-permute-start | bytes 368648 | tf_op jit(solution)/shard_map/ppermute | solution.py:14
  52.4 8.7 %collective-permute-start.7 = (bf16[8,1,3,10,256]{4,3,2,1,0:T(8,128)(2,1)S(1)}, bf16[8,1,3,10,256]{4,3,2,1,0:T(8,128)(2,1)}, u32[]{:S(2)}, u32[]{:S(2)}) collective-permute-start(bf16[8,1,3,10,256]{4,3,2,1,0:T(8,128)(2,1)S(1)} %get-tuple-element.20), channel_id=1, source_target_pairs={{1,0},{2,1},{3,2},{4,3},{5,4},{6,5},{7,6},{9,8},{10,9},{11,10},{12... | collective-permute-start | bytes 368648 | tf_op jit(solution)/shard_map/ppermute | solution.py:17
  62.3 21.9 %copy-start.9 = (bf16[4,64,512]{2,1,0:T(8,128)(2,1)S(1)}, bf16[4,64,512]{2,1,0:T(8,128)(2,1)}, u32[]{:S(2)}) copy-start(bf16[4,64,512]{2,1,0:T(8,128)(2,1)} %param.12) | copy-start | bytes 786436
  84.9 43.7 %copy-start.6 = (bf16[1920,256]{1,0:T(8,128)(2,1)S(1)}, bf16[1920,256]{1,0:T(8,128)(2,1)}, u32[]{:S(2)}) copy-start(bf16[1920,256]{1,0:T(8,128)(2,1)} %reshape.98) | copy-start | bytes 2949124
  141.6 11.2 %collective-permute-start.8 = (f32[1,6,3,10,256]{4,3,2,1,0:T(8,128)S(1)}, f32[1,6,3,10,256]{4,3,2,1,0:T(8,128)S(1)}, u32[]{:S(2)}, u32[]{:S(2)}) collective-permute-start(f32[1,6,3,10,256]{4,3,2,1,0:T(8,128)S(1)} %get-tuple-element.14), channel_id=1, source_target_pairs={{8,0},{16,8},{24,16},{9,1},{17,9},{25,17},{10,2},{18,10},{26,18},{... | collective-permute-start | bytes 552968 | tf_op jit(solution)/shard_map/ppermute | solution.py:17
  142.9 11.1 %collective-permute-start.9 = (f32[1,6,3,10,256]{4,3,2,1,0:T(8,128)S(1)}, f32[1,6,3,10,256]{4,3,2,1,0:T(8,128)S(1)}, u32[]{:S(2)}, u32[]{:S(2)}) collective-permute-start(f32[1,6,3,10,256]{4,3,2,1,0:T(8,128)S(1)} %get-tuple-element.13), channel_id=1, source_target_pairs={{0,8},{8,16},{16,24},{1,9},{9,17},{17,25},{2,10},{10,18},{18,26},{... | collective-permute-start | bytes 552968 | tf_op jit(solution)/shard_map/ppermute | solution.py:14
  154.0 12.2 %collective-permute-start.10 = (f32[8,1,3,10,256]{4,3,2,1,0:T(8,128)S(1)}, f32[8,1,3,10,256]{4,3,2,1,0:T(8,128)S(1)}, u32[]{:S(2)}, u32[]{:S(2)}) collective-permute-start(f32[8,1,3,10,256]{4,3,2,1,0:T(8,128)S(1)} %get-tuple-element.10), channel_id=1, source_target_pairs={{1,0},{2,1},{3,2},{4,3},{5,4},{6,5},{7,6},{9,8},{10,9},{11,10},{12... | collective-permute-start | bytes 737288 | tf_op jit(solution)/shard_map/ppermute | solution.py:17
  155.3 16.7 %copy-start.5 = (f32[6,6,3,10,256]{4,2,3,1,0:T(4,128)S(1)}, f32[6,6,3,10,256]{4,2,3,1,0:T(4,128)}, u32[]{:S(2)}) copy-start(f32[6,6,3,10,256]{4,2,3,1,0:T(4,128)} %param.7) | copy-start | bytes 3317764
  155.3 15.9 %collective-permute-start.11 = (f32[8,1,3,10,256]{4,3,2,1,0:T(8,128)S(1)}, f32[8,1,3,10,256]{4,3,2,1,0:T(8,128)S(1)}, u32[]{:S(2)}, u32[]{:S(2)}) collective-permute-start(f32[8,1,3,10,256]{4,3,2,1,0:T(8,128)S(1)} %get-tuple-element.9), channel_id=1, source_target_pairs={{0,1},{1,2},{2,3},{3,4},{4,5},{5,6},{6,7},{8,9},{9,10},{10,11},{11... | collective-permute-start | bytes 737288 | tf_op jit(solution)/shard_map/ppermute | solution.py:14
  173.4 6.8 %collective-permute-start.12 = (bf16[1,6,3,10,256]{4,3,2,1,0:T(8,128)(2,1)S(1)}, bf16[1,6,3,10,256]{4,3,2,1,0:T(8,128)(2,1)S(1)}, u32[]{:S(2)}, u32[]{:S(2)}) collective-permute-start(bf16[1,6,3,10,256]{4,3,2,1,0:T(8,128)(2,1)S(1)} %get-tuple-element.21), channel_id=1, source_target_pairs={{0,8},{8,16},{16,24},{1,9},{9,17},{17,25},{2,10},{10,18},{18,26},{... | collective-permute-start | bytes 276488 | tf_op jit(solution)/shard_map/ppermute | solution.py:14
  177.5 7.0 %collective-permute-start.13 = (bf16[1,6,3,10,256]{4,3,2,1,0:T(8,128)(2,1)S(1)}, bf16[1,6,3,10,256]{4,3,2,1,0:T(8,128)(2,1)S(1)}, u32[]{:S(2)}, u32[]{:S(2)}) collective-permute-start(bf16[1,6,3,10,256]{4,3,2,1,0:T(8,128)(2,1)S(1)} %get-tuple-element.22), channel_id=1, source_target_pairs={{8,0},{16,8},{24,16},{9,1},{17,9},{25,17},{10,2},{18,10},{26,18},{... | collective-permute-start | bytes 276488 | tf_op jit(solution)/shard_map/ppermute | solution.py:17
  184.6 9.5 %collective-permute-start.14 = (bf16[8,1,3,10,256]{4,3,2,1,0:T(8,128)(2,1)S(1)}, bf16[8,1,3,10,256]{4,3,2,1,0:T(8,128)(2,1)S(1)}, u32[]{:S(2)}, u32[]{:S(2)}) collective-permute-start(bf16[8,1,3,10,256]{4,3,2,1,0:T(8,128)(2,1)S(1)} %get-tuple-element.17), channel_id=1, source_target_pairs={{0,1},{1,2},{2,3},{3,4},{4,5},{5,6},{6,7},{8,9},{9,10},{10,11},{11... | collective-permute-start | bytes 368648 | tf_op jit(solution)/shard_map/ppermute | solution.py:14
  189.1 9.6 %collective-permute-start.15 = (bf16[8,1,3,10,256]{4,3,2,1,0:T(8,128)(2,1)S(1)}, bf16[8,1,3,10,256]{4,3,2,1,0:T(8,128)(2,1)S(1)}, u32[]{:S(2)}, u32[]{:S(2)}) collective-permute-start(bf16[8,1,3,10,256]{4,3,2,1,0:T(8,128)(2,1)S(1)} %get-tuple-element.18), channel_id=1, source_target_pairs={{1,0},{2,1},{3,2},{4,3},{5,4},{6,5},{7,6},{9,8},{10,9},{11,10},{12... | collective-permute-start | bytes 368648 | tf_op jit(solution)/shard_map/ppermute | solution.py:17
where the time goes:
time: 284 us; the launch traced here: 283 us
  blocking collectives  119 us (42%)
  waiting for transfers between devices  61.4 us (22%)
  starting transfers between devices  45.8 us (16%)
  matrix products  22.5 us (8%)
  local copies, waits for them, and re-layouts  19.8 us (7%)
  other arithmetic  14.1 us (5%)
    psum x2, blocking collectives, shards(): summed = lax.psum(partial_value, 'sub')  45.3 us
    all_gather x2, blocking collectives, shards(): lax.all_gather(restricted, ('crow', 'ccol'), axis=0, tiled=True)  39.7 us
    ppermute x8, waiting for transfers between devices, extended_2(): lax.ppermute(lax.slice_in_dim(block, 0, width, axis=dim), axis, backward)  39.4 us
    ppermute x8, starting transfers between devices, extended_2(): lax.ppermute(lax.slice_in_dim(block, block.shape[dim] - width, None, axis...  35.2 us
    all_gather x2, blocking collectives, shards(): piece = lax.all_gather(amounts, ('crow', 'ccol'), axis=0, tiled=True)  34 us
    ppermute x8, waiting for transfers between devices, extended_2(): lax.ppermute(lax.slice_in_dim(block, block.shape[dim] - width, None, axis...  22 us
    dot_general x2, matrix products, shards(): jnp.dot(local_inverse, flat_res, preferred_element_type=jnp.float32)  14.1 us
    ppermute x8, starting transfers between devices, extended_2(): lax.ppermute(lax.slice_in_dim(block, 0, width, axis=dim), axis, backward)  10.5 us
  transfers between devices with their start and end apart: 16, of which 16 were waited for; matrix products, arithmetic and copies ran while one was open for 1% of the time, Pallas kernels for 0%

commit v1 on v0

v1 whole, which is shorter than its diff:
```python
import jax
import jax.numpy as jnp
from jax import lax
from jax.sharding import PartitionSpec as P

ITERS = 2
GROUP_AXES = ("crow", "ccol")
ALL_AXES = ("sub", "crow", "ccol")


def swap(to_low, to_high, axis):
    count = lax.axis_size(axis)
    even = [(i, i + 1) for i in range(0, count - 1, 2)]
    odd = [(i, i + 1) for i in range(1, count - 1, 2)]
    is_even = lax.axis_index(axis) % 2 == 0
    first = lax.ppermute(
        jnp.where(is_even, to_high, to_low), axis, even + [(b, a) for a, b in even]
    )
    second = lax.ppermute(
        jnp.where(is_even, to_low, to_high), axis, odd + [(b, a) for a, b in odd]
    )
    return jnp.where(is_even, second, first), jnp.where(is_even, first, second)


def inside(solution, rhs, diagonal):
    padded = jnp.pad(solution, ((1, 1), (1, 1), (0, 0), (1, 1), (0, 0)))
    beside = padded[2:, 1:-1, :, 1:-1] + padded[:-2, 1:-1, :, 1:-1]
    beside = beside + padded[1:-1, 2:, :, 1:-1] + padded[1:-1, :-2, :, 1:-1]
    beside = beside + padded[1:-1, 1:-1, :, 2:] + padded[1:-1, 1:-1, :, :-2]
    return rhs - diagonal * solution + beside


def residual_window(solution, rhs, diagonal):
    bf16, f32 = jnp.bfloat16, jnp.float32
    row, rows = lax.axis_index("sub"), lax.axis_size("sub")
    col, cols = lax.axis_index(GROUP_AXES), lax.axis_size(GROUP_AXES)
    base = inside(solution, rhs, diagonal)
    own = solution.astype(bf16)
    low, high = swap(
        jnp.stack([base[:, 0].astype(bf16), own[:, 0]]),
        jnp.stack([base[:, -1].astype(bf16), own[:, -1]]),
        GROUP_AXES,
    )
    low, high = low.astype(f32), high.astype(f32)
    edge_low = jnp.where(col > 0, low[0] + solution[:, 0], 0.0)
    edge_high = jnp.where(col < cols - 1, high[0] + solution[:, -1], 0.0)
    wide = jnp.concatenate(
        [
            edge_low[:, None],
            base[:, :1] + low[1][:, None],
            base[:, 1:-1],
            base[:, -1:] + high[1][:, None],
            edge_high[:, None],
        ],
        axis=1,
    )
    wide_solution = jnp.concatenate([low[1][:, None], solution, high[1][:, None]], axis=1)
    above, below = swap(
        jnp.stack([wide[0], wide_solution[0]]).astype(bf16),
        jnp.stack([wide[-1], wide_solution[-1]]).astype(bf16),
        "sub",
    )
    above, below = above.astype(f32), below.astype(f32)
    first = jnp.where(row > 0, above[0] + wide_solution[0], 0.0)
    last = jnp.where(row < rows - 1, below[0] + wide_solution[-1], 0.0)
    window = jnp.concatenate(
        [
            first[None],
            wide[:1] + above[1][None],
            wide[1:-1],
            wide[-1:] + below[1][None],
            last[None],
        ],
        axis=0,
    )
    return window.astype(bf16).reshape(-1, solution.shape[-1])


def slots_of(offsets, kgroup, groups, depth):
    ends = jnp.concatenate(
        [offsets[..., 1:], jnp.full(offsets.shape[:-1] + (1,), kgroup, jnp.int32)], axis=-1
    )
    member = jnp.arange(groups, dtype=jnp.int32)[:, None]
    turn = jnp.arange(depth, dtype=jnp.int32)[None, :]
    first = offsets[..., None, None]
    slots = first + (member - first) % groups + turn * groups
    return slots, slots < ends[..., None, None]


def shards(rhs, start, stiffness, sub_inverse, basis, coarse_inverse, offsets):
    bf16, f32 = jnp.bfloat16, jnp.float32
    cells_s, cells_q, comps, layers, columns = rhs.shape
    n_sub, share_rows, kgroup = coarse_inverse.shape
    max_cols = basis.shape[2]
    groups = offsets.shape[1]
    depth = -(-max_cols // groups)
    padded_cols = groups * depth
    member = lax.axis_index(GROUP_AXES)
    sub_index = lax.axis_index("sub")

    every = lax.all_to_all(
        jnp.broadcast_to(offsets, (n_sub, groups)), "sub", 0, 0, tiled=True
    )
    slots, valid = slots_of(every, kgroup, groups, depth)
    own_slots = lax.dynamic_index_in_dim(slots, sub_index, 0, keepdims=False)
    own_valid = lax.dynamic_index_in_dim(valid, sub_index, 0, keepdims=False)
    member_slots = lax.dynamic_index_in_dim(own_slots, member, 0, keepdims=False).reshape(-1)
    member_valid = lax.dynamic_index_in_dim(own_valid, member, 0, keepdims=False).reshape(-1)
    member_start = lax.dynamic_index_in_dim(offsets[0], member, 0, keepdims=False)
    picked = jnp.where(member_valid, member_slots - member_start, -1)
    order = (jnp.arange(max_cols, dtype=jnp.int32)[:, None] == picked[None, :]).astype(bf16)
    local_basis = jnp.dot(basis[0], order, preferred_element_type=f32).astype(bf16)
    mine = lax.dynamic_index_in_dim(slots, member, 2, keepdims=False).reshape(n_sub, -1)
    mine_valid = lax.dynamic_index_in_dim(valid, member, 2, keepdims=False).reshape(n_sub, -1)
    rows = jnp.where(mine_valid, mine // groups, -1)
    row_pick = (rows[:, :, None] == jnp.arange(share_rows, dtype=jnp.int32)).astype(bf16)
    col_pick = (
        jnp.arange(kgroup, dtype=jnp.int32)[:, None]
        == jnp.where(own_valid, own_slots, -1).reshape(1, -1)
    ).astype(bf16)
    spread = jnp.einsum("gri,gik->grk", row_pick, coarse_inverse, preferred_element_type=f32)
    spread = jnp.dot(
        spread.astype(bf16).reshape(-1, kgroup), col_pick, preferred_element_type=f32
    ).astype(bf16)

    diagonal = (6.0 + stiffness)[..., None]
    local_inverse = sub_inverse[0]
    solution = start
    for sweep in range(ITERS):
        local_res = residual_window(solution, rhs, diagonal)
        restricted = lax.dot_general(
            local_basis, local_res, (((0,), (0,)), ((), ())), preferred_element_type=f32
        ).astype(bf16)
        gathered = lax.all_to_all(
            jnp.broadcast_to(restricted[None], (groups,) + restricted.shape),
            GROUP_AXES, 0, 0, tiled=True,
        )
        terms = jnp.dot(
            spread, gathered.reshape(-1, columns), preferred_element_type=f32
        ).astype(bf16)
        arrived = lax.all_to_all(
            terms.reshape(n_sub * groups, depth, columns), ALL_AXES, 0, 0, tiled=True
        )
        chosen = jnp.sum(
            arrived.reshape(n_sub, padded_cols, columns).astype(f32), axis=0
        ).astype(bf16)
        fine_part = jnp.dot(local_inverse, local_res, preferred_element_type=f32)
        coarse_part = jnp.dot(local_basis, chosen, preferred_element_type=f32)
        correction = (fine_part + coarse_part).reshape(
            cells_s + 2, cells_q + 2, comps, layers, columns
        )
        solution = solution + correction[1:-1, 1:-1]
    return solution


def solution(mesh):
    return jax.shard_map(
        shards,
        mesh=mesh,
        in_specs=(
            P("sub", ("crow", "ccol"), None, None, None),
            P("sub", ("crow", "ccol"), None, None, None),
            P("sub", ("crow", "ccol"), None, None),
            P(("sub", "crow", "ccol"), None, None),
            P(("sub", "crow", "ccol"), None, None),
            P(None, ("crow", "ccol"), "sub"),
            P("sub", None),
        ),
        out_specs=P("sub", ("crow", "ccol"), None, None, None),
        check_vma=False,
    )
```

time: 284 us -> 184 us (0.65)
  blocking collectives: 119 us -> 11.6 us
  local copies, waits for them, and re-layouts: 19.8 us -> 54 us
  waiting for transfers between devices: 61.4 us -> 34.8 us
  starting transfers between devices: 45.8 us -> 35.3 us
  other arithmetic: 14.1 us -> 18.9 us
  matrix products: 22.5 us -> 26.9 us
    all_gather x4 -> x0, blocking collectives: 73.7 us -> none  [the longest x2 39.7 us: shards(): lax.all_gather(restricted, ('crow', 'ccol'), axis=0, tiled=True)]
    psum x2 -> x0, blocking collectives: 45.3 us -> none  [shards(): summed = lax.psum(partial_value, 'sub')]
    ppermute x16 -> x8, waiting for transfers between devices: 61.4 us -> 20.4 us  [the longest x4 20.4 us: swap(): lax.ppermute(jnp.where(is_even, to_high, to_low), axis, even + [(b, a) fo...]
    ppermute x16 -> x8, starting transfers between devices: 45.8 us -> 11.5 us  [the longest x4 8.08 us: swap(): lax.ppermute(jnp.where(is_even, to_high, to_low), axis, even + [(b, a) fo...]
    all_to_all x0 -> x4, starting transfers between devices: none -> 23.7 us  [the longest x2 13.3 us: shards(): lax.all_to_all(terms.reshape(n_sub * groups, depth, columns), ALL_AXES, 0...]
    all_to_all x0 -> x4, waiting for transfers between devices: none -> 14.4 us  [the longest x2 7.64 us: shards(): lax.all_to_all(terms.reshape(n_sub * groups, depth, columns), ALL_AXES, 0...]
    all_to_all x0 -> x1, blocking collectives: none -> 11.6 us  [shards(): lax.all_to_all(jnp.broadcast_to(restricted[None], (groups,) + restricted....]
    concatenate x1 -> x3, local copies, waits for them, and re-layouts: 0.02 us -> 8.96 us  [the longest x2 8.95 us: residual_window(): jnp.concatenate([edge_low[:, None], base[:, :1] + low[1][:, None], base[:...]
  transfers between devices with their start and end apart: 16 -> 12, of which waited for: 16 -> 7; matrix products, arithmetic and copies ran while one was open for 1% -> 18% of each run, Pallas kernels for 0% -> 0%
where the time goes in v1:
time: 184 us; the launch traced here: 182 us
  local copies, waits for them, and re-layouts  54 us (29%)
  starting transfers between devices  35.3 us (19%)
  waiting for transfers between devices  34.8 us (19%)
  matrix products  26.9 us (15%)
  other arithmetic  18.9 us (10%)
  blocking collectives  11.6 us (6%)
    ppermute x4, waiting for transfers between devices, swap(): lax.ppermute(jnp.where(is_even, to_high, to_low), axis, even + [(b, a) fo...  20.4 us
    dot_general x2, matrix products, shards(): fine_part = jnp.dot(local_inverse, local_res, preferred_element_type=f32)  13.6 us
    all_to_all x2, starting transfers between devices, shards(): lax.all_to_all(terms.reshape(n_sub * groups, depth, columns), ALL_AXES, 0...  13.3 us
    all_to_all x1, blocking collectives, shards(): lax.all_to_all(jnp.broadcast_to(restricted[None], (groups,) + restricted....  11.6 us
    concatenate x2, local copies, waits for them, and re-layouts, residual_window(): jnp.concatenate([edge_low[:, None], base[:, :1] + low[1][:, None], base[:...  8.95 us
    ppermute x4, starting transfers between devices, swap(): lax.ppermute(jnp.where(is_even, to_high, to_low), axis, even + [(b, a) fo...  8.08 us
    convert_element_type x4, local copies, waits for them, and re-layouts, residual_window(): return window.astype(bf16).reshape(-1, solution.shape[-1])  7.64 us
    all_to_all x2, waiting for transfers between devices, shards(): lax.all_to_all(terms.reshape(n_sub * groups, depth, columns), ALL_AXES, 0...  7.64 us
  transfers between devices with their start and end apart: 12, of which 7 were waited for; matrix products, arithmetic and copies ran while one was open for 18% of the time, Pallas kernels for 0%

profile of v1, /device:TPU:0, one launch (start us, length us, event | category | flops | bytes accessed | tf_op | source)
XLA Modules:
  0.0 182.1 jit_solution(8451007077361788888)
XLA Ops:
  1.4 6.3 %all-to-all-start = ((s32[4,1,8]{2,1,0:T(1,128)}), s32[4,1,8]{2,1,0:T(1,128)S(1)}, u32[]{:S(2)}, u32[]{:S(2)}) async-start(s32[4,1,8]{2,1,0:T(1,128)} %broadcast_in_dim.32), calls=%async_computation | async-start | bytes 4096 | tf_op jit(solution)/shard_map/all_to_all | solution.py:101
  7.7 2.8 %copy.337 = bf16[6,6,3,10,256]{4,0,3,2,1:T(8,128)(2,1)} copy(f32[6,6,3,10,256]{4,2,3,1,0:T(4,128)} %param.8) | data formatting | bytes 1658880 | tf_op args[1]
  13.9 2.2 %fusion.17 = f32[6,6,3,10,256]{4,1,3,2,0:T(8,128)S(1)} fusion(f32[6,6,3,10,256]{4,1,3,2,0:T(8,128)S(1)} %copy.306, f32[6,6,3,10,256]{4,2,3,1,0:T(4,128)} %param.7, f32[6,6,3,10]{1,3,2,0:T(8,128)} %copy.288), kind=kLoop, calls=%fused_computation.29 | loop fusion | flops 2211840 | bytes 3322080 | tf_op jit(solution)/shard_map/add | solution.py:30
  19.8 2.2 %collective-permute-start.1 = (bf16[2,6,3,10,256]{4,0,3,2,1:T(2,128)(2,1)}, bf16[2,6,3,10,256]{4,0,3,2,1:T(2,128)(2,1)}, u32[]{:S(2)}, u32[]{:S(2)}) collective-permute-start(bf16[2,6,3,10,256]{4,0,3,2,1:T(2,128)(2,1)} %get-tuple-element.44), channel_id=1, source_target_pairs={{0,1},{2,3},{4,5},{6,7},{1,0},{3,2},{5,4},{7,6},{8,9},{10,11},{12,... | collective-permute-start | bytes 552968 | tf_op jit(solution)/shard_map/ppermute | solution.py:16
  22.5 2.4 %slice.243 = f32[6,4,3,10,256]{4,1,3,2,0:T(4,128)} slice(f32[6,6,3,10,256]{4,1,3,2,0:T(8,128)} %copy-done.6), slice={[0:6], [1:5], [0:3], [0:10], [0:256]} | slice | bytes 1474560 | tf_op jit(solution)/shard_map/slice | solution.py:51
  27.5 2.1 %collective-permute-done.1 = bf16[2,6,3,10,256]{4,0,3,2,1:T(2,128)(2,1)} collective-permute-done((bf16[2,6,3,10,256]{4,0,3,2,1:T(2,128)(2,1)}, bf16[2,6,3,10,256]{4,0,3,2,1:T(2,128)(2,1)}, u32[]{:S(2)}, u32[]{:S(2)}) %collective-permute-start.1) | collective-permute-done | bytes 184352 | tf_op jit(solution)/shard_map/ppermute | solution.py:16
  32.6 3.6 %slice_add_fusion.14 = (f32[6,1,3,10,256]{4,1,3,2,0:T(1,128)}, f32[6,1,3,10,256]{4,1,3,2,0:T(1,128)}, f32[6,1,3,10,256]{4,1,3,2,0:T(1,128)}, f32[6,1,3,10,256]{4,1,3,2,0:T(1,128)}) fusion(f32[6,6,3,10,256]{4,1,3,2,0:T(8,128)} %copy-done.6, f32[2,6,3,10,256]{4,0,3,2,1:T(2,128)S(1)} %get-tuple-element.58, f32[2,6,3,10,256]{4,0,3,2,1:T(2,128)S(1)} %get-tuple-element.57, ...), kind=kLoop, calls=%fused_computation.137 | loop fusion | flops 276480 | bytes 2211842 | tf_op jit(solution)/shard_map/add | solution.py:52
  36.3 5.0 %concatenate.21 = f32[6,8,3,10,256]{4,1,3,2,0:T(8,128)} concatenate(f32[6,1,3,10,256]{4,1,3,2,0:T(1,128)} %get-tuple-element.35, f32[6,1,3,10,256]{4,1,3,2,0:T(1,128)} %get-tuple-element.32, f32[6,4,3,10,256]{4,1,3,2,0:T(4,128)} %slice.243, f32[6,1,3,10,256]{4,1,3,2,0:T(1,128)} %get-tuple-element.31, f32[6,1,3,10,256]{4,1,3,2,0:T(1,128)} %get-tuple-element.36), dimensions={1} | concatenate | bytes 2949120 | tf_op jit(solution)/shard_map/concatenate | solution.py:47
  43.4 2.1 %collective-permute-start.3 = (bf16[2,8,3,10,256]{4,1,3,2,0:T(8,128)(2,1)S(1)}, bf16[2,8,3,10,256]{4,1,3,2,0:T(8,128)(2,1)S(1)}, u32[]{:S(2)}, u32[]{:S(2)}) collective-permute-start(bf16[2,8,3,10,256]{4,1,3,2,0:T(8,128)(2,1)S(1)} %get-tuple-element.53), channel_id=1, source_target_pairs={{0,8},{16,24},{8,0},{24,16},{1,9},{17,25},{9,1},{25,17},{2,10},{18... | collective-permute-start | bytes 737288 | tf_op jit(solution)/shard_map/ppermute | solution.py:16
  46.7 5.4 %collective-permute-done.3 = bf16[2,8,3,10,256]{4,1,3,2,0:T(8,128)(2,1)S(1)} collective-permute-done((bf16[2,8,3,10,256]{4,1,3,2,0:T(8,128)(2,1)S(1)}, bf16[2,8,3,10,256]{4,1,3,2,0:T(8,128)(2,1)S(1)}, u32[]{:S(2)}, u32[]{:S(2)}) %collective-permute-start.3) | collective-permute-done | bytes 245792 | tf_op jit(solution)/shard_map/ppermute | solution.py:16
  53.9 2.3 %convert_element_type.156 = bf16[1920,256]{1,0:T(8,128)(2,1)S(1)} reshape(bf16[8,8,3,10,256]{4,3,2,1,0:T(8,128)(2,1)} %copy.302) | data formatting | bytes 1966080 | tf_op jit(solution)/shard_map/convert_element_type | solution.py:76
  57.4 4.1 %all-to-all-start.1 = ((bf16[8,128,256]{2,1,0:T(8,128)(2,1)}), bf16[8,128,256]{2,1,0:T(8,128)(2,1)}, u32[]{:S(2)}, u32[]{:S(2)}) async-start(bf16[8,128,256]{2,1,0:T(8,128)(2,1)} %broadcast_in_dim.35), calls=%async_computation.1 | async-start | bytes 1048576 | tf_op jit(solution)/shard_map/all_to_all | solution.py:134
  63.6 6.7 %all-to-all-done.1 = bf16[8,128,256]{2,1,0:T(8,128)(2,1)} async-done(((bf16[8,128,256]{2,1,0:T(8,128)(2,1)}), bf16[8,128,256]{2,1,0:T(8,128)(2,1)}, u32[]{:S(2)}, u32[]{:S(2)}) %all-to-all-start.1) | async-done | bytes 524320 | tf_op jit(solution)/shard_map/all_to_all | solution.py:134
  70.3 2.5 %convolution_convert_fusion.3 = bf16[512,256]{1,0:T(8,128)(2,1)} fusion(bf16[512,1024]{1,0:T(8,128)(2,1)} %fusion.11, bf16[1024,256]{1,0:T(8,128)(2,1)} %bitcast.15), kind=kOutput, calls=%fused_computation.41 | convolution fusion | flops 268566528 | bytes 1835008 | tf_op jit(solution)/shard_map/dot_general | solution.py:138
  72.8 7.9 %all-to-all-start.2 = ((bf16[32,16,256]{2,1,0:T(8,128)(2,1)}), bf16[32,16,256]{2,1,0:T(8,128)(2,1)S(1)}, u32[]{:S(2)}, u32[]{:S(2)}) async-start(bf16[32,16,256]{2,1,0:T(8,128)(2,1)} %bitcast.111), calls=%async_computation.2 | async-start | bytes 524288 | tf_op jit(solution)/shard_map/all_to_all | solution.py:141
  80.8 6.8 %fusion.4 = f32[1920,256]{0,1:T(8,128)} fusion(bf16[1920,256]{1,0:T(8,128)(2,1)S(1)} %convert_element_type.156, bf16[1,1920,1920]{2,1,0:T(8,128)(2,1)} %param.10), kind=kOutput, calls=%fused_computation.18 | convolution fusion | flops 1887436800 | bytes 10321920 | tf_op jit(solution)/shard_map/dot_general | solution.py:147
  87.5 3.7 %all-to-all-done.2 = bf16[32,16,256]{2,1,0:T(8,128)(2,1)S(1)} async-done(((bf16[32,16,256]{2,1,0:T(8,128)(2,1)}), bf16[32,16,256]{2,1,0:T(8,128)(2,1)S(1)}, u32[]{:S(2)}, u32[]{:S(2)}) %all-to-all-start.2) | async-done | bytes 262176 | tf_op jit(solution)/shard_map/all_to_all | solution.py:141
  91.3 3.3 %convolution_add_fusion.1 = f32[1920,256]{0,1:T(8,128)} fusion(f32[1920,256]{0,1:T(8,128)} %fusion.4, bf16[128,1920]{1,0:T(8,128)(2,1)S(1)} %convolution_convert_fusion, bf16[128,256]{1,0:T(8,128)(2,1)S(1)} %bitcast_reduce_fusion.1), kind=kOutput, calls=%fused_computation.17 | convolution fusion | flops 126320640 | bytes 4489216 | tf_op jit(solution)/shard_map/dot_general | solution.py:148
  94.7 2.9 %copy.304 = f32[1920,256]{1,0:T(8,128)} copy(f32[1920,256]{0,1:T(8,128)} %convolution_add_fusion.1) | data formatting | bytes 3932160 | tf_op jit(solution)/shard_map/add | solution.py:149
  97.5 3.4 %reshape.222 = f32[8,8,3,10,256]{4,3,2,1,0:T(8,128)} reshape(f32[1920,256]{1,0:T(8,128)} %copy.304) | data formatting | bytes 3932160 | tf_op jit(solution)/shard_map/reshape | solution.py:149
  108.1 3.0 %collective-permute-start.5 = (bf16[2,6,3,10,256]{4,0,3,2,1:T(2,128)(2,1)S(1)}, bf16[2,6,3,10,256]{4,0,3,2,1:T(2,128)(2,1)S(1)}, u32[]{:S(2)}, u32[]{:S(2)}) collective-permute-start(bf16[2,6,3,10,256]{4,0,3,2,1:T(2,128)(2,1)S(1)} %get-tuple-element.40), channel_id=1, source_target_pairs={{0,1},{2,3},{4,5},{6,7},{1,0},{3,2},{5,4},{7,6},{8,9},{10,11},{12,... | collective-permute-start | bytes 552968 | tf_op jit(solution)/shard_map/ppermute | solution.py:16
  112.2 6.3 %collective-permute-done.5 = bf16[2,6,3,10,256]{4,0,3,2,1:T(2,128)(2,1)S(1)} collective-permute-done((bf16[2,6,3,10,256]{4,0,3,2,1:T(2,128)(2,1)S(1)}, bf16[2,6,3,10,256]{4,0,3,2,1:T(2,128)(2,1)S(1)}, u32[]{:S(2)}, u32[]{:S(2)}) %collective-permute-start.5) | collective-permute-done | bytes 184352 | tf_op jit(solution)/shard_map/ppermute | solution.py:16
  122.4 3.9 %concatenate.25 = f32[6,8,3,10,256]{4,1,3,2,0:T(8,128)S(1)} concatenate(f32[6,1,3,10,256]{4,1,3,2,0:T(1,128)} %get-tuple-element.37, f32[6,1,3,10,256]{4,1,3,2,0:T(1,128)} %get-tuple-element.24, f32[6,4,3,10,256]{4,1,3,2,0:T(4,128)} %slice.262, f32[6,1,3,10,256]{4,1,3,2,0:T(1,128)} %get-tuple-element.23, f32[6,1,3,10,256]{4,1,3,2,0:T(1,128)} %get-tuple-element.38), dimensions={1} | concatenate | bytes 2949120 | tf_op jit(solution)/shard_map/concatenate | solution.py:47
  128.1 6.6 %collective-permute-done.7 = bf16[2,8,3,10,256]{4,1,3,2,0:T(8,128)(2,1)S(1)} collective-permute-done((bf16[2,8,3,10,256]{4,1,3,2,0:T(8,128)(2,1)S(1)}, bf16[2,8,3,10,256]{4,1,3,2,0:T(8,128)(2,1)S(1)}, u32[]{:S(2)}, u32[]{:S(2)}) %collective-permute-start.7) | collective-permute-done | bytes 245792 | tf_op jit(solution)/shard_map/ppermute | solution.py:16
  136.5 2.3 %convert_element_type.172 = bf16[1920,256]{1,0:T(8,128)(2,1)S(1)} reshape(bf16[8,8,3,10,256]{4,3,2,1,0:T(8,128)(2,1)} %copy.316) | data formatting | bytes 1966080 | tf_op jit(solution)/shard_map/convert_element_type | solution.py:76
  139.2 11.6 %all_to_all.26 = bf16[8,128,256]{2,1,0:T(8,128)(2,1)S(1)} all-to-all(bf16[8,128,256]{2,1,0:T(8,128)(2,1)S(1)} %broadcast_in_dim.36), channel_id=1, replica_groups=mesh['sub'=4,'crow'=4,'ccol'=2] {'crow','ccol'}, dimensions={0} | all-to-all | bytes 1048576 | tf_op jit(solution)/shard_map/all_to_all | solution.py:134
  152.0 5.4 %all-to-all-start.4 = ((bf16[32,16,256]{2,1,0:T(8,128)(2,1)}), bf16[32,16,256]{2,1,0:T(8,128)(2,1)S(1)}, u32[]{:S(2)}, u32[]{:S(2)}) async-start(bf16[32,16,256]{2,1,0:T(8,128)(2,1)} %bitcast.110), calls=%async_computation.4 | async-start | bytes 524288 | tf_op jit(solution)/shard_map/all_to_all | solution.py:141
  157.4 6.8 %fusion.7 = f32[1920,256]{0,1:T(8,128)} fusion(bf16[1920,256]{1,0:T(8,128)(2,1)S(1)} %convert_element_type.172, bf16[1,1920,1920]{2,1,0:T(8,128)(2,1)} %param.10), kind=kOutput, calls=%fused_computation.19 | convolution fusion | flops 1887436800 | bytes 10321920 | tf_op jit(solution)/shard_map/dot_general | solution.py:147
  164.1 3.9 %all-to-all-done.4 = bf16[32,16,256]{2,1,0:T(8,128)(2,1)S(1)} async-done(((bf16[32,16,256]{2,1,0:T(8,128)(2,1)}), bf16[32,16,256]{2,1,0:T(8,128)(2,1)S(1)}, u32[]{:S(2)}, u32[]{:S(2)}) %all-to-all-start.4) | async-done | bytes 262176 | tf_op jit(solution)/shard_map/all_to_all | solution.py:141
  168.1 3.3 %convolution_add_fusion = f32[1920,256]{0,1:T(8,128)} fusion(f32[1920,256]{0,1:T(8,128)} %fusion.7, bf16[128,1920]{1,0:T(8,128)(2,1)S(1)} %copy-done.4, bf16[128,256]{1,0:T(8,128)(2,1)S(1)} %bitcast_reduce_fusion), kind=kOutput, calls=%fused_computation.16 | convolution fusion | flops 126320640 | bytes 4489216 | tf_op jit(solution)/shard_map/dot_general | solution.py:148
  171.4 2.9 %copy.318 = f32[1920,256]{1,0:T(8,128)} copy(f32[1920,256]{0,1:T(8,128)} %convolution_add_fusion) | data formatting | bytes 3932160 | tf_op jit(solution)/shard_map/add | solution.py:149
  174.3 3.4 %reshape.226 = f32[8,8,3,10,256]{4,3,2,1,0:T(8,128)} reshape(f32[1920,256]{1,0:T(8,128)} %copy.318) | data formatting | bytes 3932160 | tf_op jit(solution)/shard_map/reshape | solution.py:149
  (123 shorter events, 44.2 us)
Async XLA Ops:
  0.0 46.3 %copy-start = (bf16[1,1920,128]{2,1,0:T(8,128)(2,1)S(1)}, bf16[1,1920,128]{2,1,0:T(8,128)(2,1)}, u32[]{:S(2)}) copy-start(bf16[1,1920,128]{2,1,0:T(8,128)(2,1)} %param.11) | copy-start | bytes 1474564
  0.0 10.5 %copy-start.2 = (f32[6,6,3,10,256]{4,2,3,1,0:T(4,128)S(1)}, f32[6,6,3,10,256]{4,2,3,1,0:T(4,128)}, u32[]{:S(2)}) copy-start(f32[6,6,3,10,256]{4,2,3,1,0:T(4,128)} %param.8) | copy-start | bytes 3317764
  1.4 23.6 %all-to-all-start = ((s32[4,1,8]{2,1,0:T(1,128)}), s32[4,1,8]{2,1,0:T(1,128)S(1)}, u32[]{:S(2)}, u32[]{:S(2)}) async-start(s32[4,1,8]{2,1,0:T(1,128)} %broadcast_in_dim.32), calls=%async_computation | async-start | bytes 4096 | tf_op jit(solution)/shard_map/all_to_all | solution.py:101
  16.1 2.3 %copy-start.6 = (f32[6,6,3,10,256]{4,1,3,2,0:T(8,128)}, f32[6,6,3,10,256]{4,1,3,2,0:T(8,128)S(1)}, u32[]{:S(2)}) copy-start(f32[6,6,3,10,256]{4,1,3,2,0:T(8,128)S(1)} %fusion.17) | copy-start | bytes 3317764
  16.2 5.8 %copy-start.13 = (s32[1,8]{1,0:T(1,128)S(1)}, s32[1,8]{1,0:T(1,128)}, u32[]{:S(2)}) copy-start(s32[1,8]{1,0:T(1,128)} %param.13) | copy-start | bytes 100
  18.4 9.1 %collective-permute-start = (bf16[2,6,3,10,256]{4,0,3,2,1:T(2,128)(2,1)}, bf16[2,6,3,10,256]{4,0,3,2,1:T(2,128)(2,1)}, u32[]{:S(2)}, u32[]{:S(2)}) collective-permute-start(bf16[2,6,3,10,256]{4,0,3,2,1:T(2,128)(2,1)} %get-tuple-element.43), channel_id=1, source_target_pairs={{1,2},{3,4},{5,6},{2,1},{4,3},{6,5},{9,10},{11,12},{13,14},{10,9},... | collective-permute-start | bytes 552968 | tf_op jit(solution)/shard_map/ppermute | solution.py:19
  19.8 9.9 %collective-permute-start.1 = (bf16[2,6,3,10,256]{4,0,3,2,1:T(2,128)(2,1)}, bf16[2,6,3,10,256]{4,0,3,2,1:T(2,128)(2,1)}, u32[]{:S(2)}, u32[]{:S(2)}) collective-permute-start(bf16[2,6,3,10,256]{4,0,3,2,1:T(2,128)(2,1)} %get-tuple-element.44), channel_id=1, source_target_pairs={{0,1},{2,3},{4,5},{6,7},{1,0},{3,2},{5,4},{7,6},{8,9},{10,11},{12,... | collective-permute-start | bytes 552968 | tf_op jit(solution)/shard_map/ppermute | solution.py:16
  25.2 0.7 copy-start.12
  43.4 8.6 %collective-permute-start.3 = (bf16[2,8,3,10,256]{4,1,3,2,0:T(8,128)(2,1)S(1)}, bf16[2,8,3,10,256]{4,1,3,2,0:T(8,128)(2,1)S(1)}, u32[]{:S(2)}, u32[]{:S(2)}) collective-permute-start(bf16[2,8,3,10,256]{4,1,3,2,0:T(8,128)(2,1)S(1)} %get-tuple-element.53), channel_id=1, source_target_pairs={{0,8},{16,24},{8,0},{24,16},{1,9},{17,25},{9,1},{25,17},{2,10},{18... | collective-permute-start | bytes 737288 | tf_op jit(solution)/shard_map/ppermute | solution.py:16
  45.5 6.7 %copy-start.7 = (f32[6,8,3,10,256]{4,1,3,2,0:T(8,128)S(1)}, f32[6,8,3,10,256]{4,1,3,2,0:T(8,128)}, u32[]{:S(2)}) copy-start(f32[6,8,3,10,256]{4,1,3,2,0:T(8,128)} %concatenate.21) | copy-start | bytes 4423684
  45.5 6.5 %collective-permute-start.2 = (bf16[2,8,3,10,256]{4,1,3,2,0:T(8,128)(2,1)S(1)}, bf16[2,8,3,10,256]{4,1,3,2,0:T(8,128)(2,1)S(1)}, u32[]{:S(2)}, u32[]{:S(2)}) collective-permute-start(bf16[2,8,3,10,256]{4,1,3,2,0:T(8,128)(2,1)S(1)} %get-tuple-element.54), channel_id=1, source_target_pairs={{8,16},{16,8},{9,17},{17,9},{10,18},{18,10},{11,19},{19,11},{12,20... | collective-permute-start | bytes 737288 | tf_op jit(solution)/shard_map/ppermute | solution.py:19
  46.7 44.7 %copy-start.3 = (bf16[128,1920]{1,0:T(8,128)(2,1)}, bf16[128,1920]{1,0:T(8,128)(2,1)S(1)}, u32[]{:S(2)}) copy-start(bf16[128,1920]{1,0:T(8,128)(2,1)S(1)} %convolution_convert_fusion) | copy-start | bytes 1474564
  56.2 5.3 %copy-start.11 = (bf16[4,64,512]{2,1,0:T(8,128)(2,1)S(1)}, bf16[4,64,512]{2,1,0:T(8,128)(2,1)}, u32[]{:S(2)}) copy-start(bf16[4,64,512]{2,1,0:T(8,128)(2,1)} %param.12) | copy-start | bytes 786436
  57.4 13.0 %all-to-all-start.1 = ((bf16[8,128,256]{2,1,0:T(8,128)(2,1)}), bf16[8,128,256]{2,1,0:T(8,128)(2,1)}, u32[]{:S(2)}, u32[]{:S(2)}) async-start(bf16[8,128,256]{2,1,0:T(8,128)(2,1)} %broadcast_in_dim.35), calls=%async_computation.1 | async-start | bytes 1048576 | tf_op jit(solution)/shard_map/all_to_all | solution.py:134
  72.8 18.4 %all-to-all-start.2 = ((bf16[32,16,256]{2,1,0:T(8,128)(2,1)}), bf16[32,16,256]{2,1,0:T(8,128)(2,1)S(1)}, u32[]{:S(2)}, u32[]{:S(2)}) async-start(bf16[32,16,256]{2,1,0:T(8,128)(2,1)} %bitcast.111), calls=%async_computation.2 | async-start | bytes 524288 | tf_op jit(solution)/shard_map/all_to_all | solution.py:141
  103.6 1.4 copy-start.5
  103.6 1.4 copy-start.8
  107.4 4.8 %collective-permute-start.4 = (bf16[2,6,3,10,256]{4,0,3,2,1:T(2,128)(2,1)S(1)}, bf16[2,6,3,10,256]{4,0,3,2,1:T(2,128)(2,1)S(1)}, u32[]{:S(2)}, u32[]{:S(2)}) collective-permute-start(bf16[2,6,3,10,256]{4,0,3,2,1:T(2,128)(2,1)S(1)} %get-tuple-element.39), channel_id=1, source_target_pairs={{1,2},{3,4},{5,6},{2,1},{4,3},{6,5},{9,10},{11,12},{13,14},{10,9},... | collective-permute-start | bytes 552968 | tf_op jit(solution)/shard_map/ppermute | solution.py:19
  108.1 10.4 %collective-permute-start.5 = (bf16[2,6,3,10,256]{4,0,3,2,1:T(2,128)(2,1)S(1)}, bf16[2,6,3,10,256]{4,0,3,2,1:T(2,128)(2,1)S(1)}, u32[]{:S(2)}, u32[]{:S(2)}) collective-permute-start(bf16[2,6,3,10,256]{4,0,3,2,1:T(2,128)(2,1)S(1)} %get-tuple-element.40), channel_id=1, source_target_pairs={{0,1},{2,3},{4,5},{6,7},{1,0},{3,2},{5,4},{7,6},{8,9},{10,11},{12,... | collective-permute-start | bytes 552968 | tf_op jit(solution)/shard_map/ppermute | solution.py:16
  122.4 4.0 %copy-start.9 = (f32[6,1,3,10,256]{4,1,3,2,0:T(1,128)S(1)}, f32[6,1,3,10,256]{4,1,3,2,0:T(1,128)}, u32[]{:S(2)}) copy-start(f32[6,1,3,10,256]{4,1,3,2,0:T(1,128)} %slice_bitcast_fusion.2) | copy-start | bytes 552964
  122.4 4.0 %copy-start.10 = (f32[6,1,3,10,256]{4,1,3,2,0:T(1,128)S(1)}, f32[6,1,3,10,256]{4,1,3,2,0:T(1,128)}, u32[]{:S(2)}) copy-start(f32[6,1,3,10,256]{4,1,3,2,0:T(1,128)} %slice_bitcast_fusion.1) | copy-start | bytes 552964
  126.7 8.0 %collective-permute-start.7 = (bf16[2,8,3,10,256]{4,1,3,2,0:T(8,128)(2,1)S(1)}, bf16[2,8,3,10,256]{4,1,3,2,0:T(8,128)(2,1)S(1)}, u32[]{:S(2)}, u32[]{:S(2)}) collective-permute-start(bf16[2,8,3,10,256]{4,1,3,2,0:T(8,128)(2,1)S(1)} %get-tuple-element.49), channel_id=1, source_target_pairs={{0,8},{16,24},{8,0},{24,16},{1,9},{17,25},{9,1},{25,17},{2,10},{18... | collective-permute-start | bytes 737288 | tf_op jit(solution)/shard_map/ppermute | solution.py:16
  127.4 7.3 %collective-permute-start.6 = (bf16[2,8,3,10,256]{4,1,3,2,0:T(8,128)(2,1)S(1)}, bf16[2,8,3,10,256]{4,1,3,2,0:T(8,128)(2,1)S(1)}, u32[]{:S(2)}, u32[]{:S(2)}) collective-permute-start(bf16[2,8,3,10,256]{4,1,3,2,0:T(8,128)(2,1)S(1)} %get-tuple-element.50), channel_id=1, source_target_pairs={{8,16},{16,8},{9,17},{17,9},{10,18},{18,10},{11,19},{19,11},{12,20... | collective-permute-start | bytes 737288 | tf_op jit(solution)/shard_map/ppermute | solution.py:19
  136.5 2.4 %copy-start.4 = (bf16[128,1920]{1,0:T(8,128)(2,1)S(1)}, bf16[128,1920]{1,0:T(8,128)(2,1)}, u32[]{:S(2)}) copy-start(bf16[128,1920]{1,0:T(8,128)(2,1)} %copy-done.3) | copy-start | bytes 1474564
  138.8 12.0 %copy-start.14 = (bf16[512,1024]{1,0:T(8,128)(2,1)S(1)}, bf16[512,1024]{1,0:T(8,128)(2,1)}, u32[]{:S(2)}) copy-start(bf16[512,1024]{1,0:T(8,128)(2,1)} %fusion.11) | copy-start | bytes 3145732
  152.0 16.1 %all-to-all-start.4 = ((bf16[32,16,256]{2,1,0:T(8,128)(2,1)}), bf16[32,16,256]{2,1,0:T(8,128)(2,1)S(1)}, u32[]{:S(2)}, u32[]{:S(2)}) async-start(bf16[32,16,256]{2,1,0:T(8,128)(2,1)} %bitcast.110), calls=%async_computation.4 | async-start | bytes 524288 | tf_op jit(solution)/shard_map/all_to_all | solution.py:141
  179.3 2.9 %copy-start.1 = (bf16[1,1920,128]{2,1,0:T(8,128)(2,1)S(1)}, bf16[1,1920,128]{2,1,0:T(8,128)(2,1)}, u32[]{:S(2)}) copy-start(bf16[1,1920,128]{2,1,0:T(8,128)(2,1)} %param.11) | copy-start | bytes 1474564

commit v2 on v1

v2 whole, which is shorter than its diff:
```python
import functools

import jax
import jax.numpy as jnp
import numpy as np
from jax import lax
from jax.experimental import pallas as pl
from jax.experimental.pallas import tpu as pltpu
from jax.sharding import PartitionSpec as P

ITERS = 2
GROUP_AXES = ("crow", "ccol")
ALL_AXES = ("sub", "crow", "ccol")
bf16, f32 = jnp.bfloat16, jnp.float32
VMEM = pl.BlockSpec(memory_space=pltpu.VMEM)


def call(body, ins, outs, scratch=(), limit=24, flops=0):
    size = sum(x.size * x.dtype.itemsize for x in (*ins, *outs))
    return pl.pallas_call(
        body,
        out_shape=tuple(outs),
        in_specs=[VMEM] * len(ins),
        out_specs=tuple([VMEM] * len(outs)),
        scratch_shapes=list(scratch),
        compiler_params=pltpu.CompilerParams(vmem_limit_bytes=limit << 20),
        cost_estimate=pl.CostEstimate(flops=flops, bytes_accessed=size, transcendentals=0),
    )(*ins)


def swap(first, second, axis):
    count = lax.axis_size(axis)
    even = [(i, i + 1) for i in range(0, count - 1, 2)]
    odd = [(i, i + 1) for i in range(1, count - 1, 2)]
    return (
        lax.ppermute(first, axis, even + [(b, a) for a, b in even]),
        lax.ppermute(second, axis, odd + [(b, a) for a, b in odd]),
    )


def write_base(layers, rhs, diag, sol, base, shape):
    cells_s, cells_q, _, pad, columns = shape
    at = lax.broadcasted_iota(jnp.int32, (pad, columns), 0)
    comps = shape[2]
    used = comps * layers
    has_up, has_down = at < used, at < used
    for c in range(comps):
        has_up = has_up & (at != c * layers)
        has_down = has_down & (at != c * layers + layers - 1)
    for s in range(cells_s):
        for q in range(cells_q):
            i = s * cells_q + q
            x = sol[i]
            d = diag[i]
            d = jnp.concatenate([d] * (columns // d.shape[1]), axis=1)
            total = rhs[i] - d * x
            total = total + jnp.where(has_up, pltpu.roll(x, 1, 0), 0.0)
            total = total + jnp.where(has_down, pltpu.roll(x, pad - 1, 0), 0.0)
            if q > 0:
                total = total + sol[i - 1]
            if q < cells_q - 1:
                total = total + sol[i + 1]
            if s > 0:
                total = total + sol[i - cells_q]
            if s < cells_s - 1:
                total = total + sol[i + cells_q]
            base[i] = total


def write_column_messages(sol, base, first, second, shape):
    cells_s, cells_q = shape[:2]
    even = lax.axis_index(GROUP_AXES) % 2 == 0
    for out, q in (
        (first, jnp.where(even, cells_q - 1, 0)),
        (second, jnp.where(even, 0, cells_q - 1)),
    ):
        for s in range(cells_s):
            out[0, s] = base[s * cells_q + q].astype(bf16)
            out[1, s] = sol[s * cells_q + q].astype(bf16)


def open_kernel(shape, layers, start, rhs_in, diag, sol, rhs, base, first, second):
    cells_s, cells_q, comps, pad, columns = shape
    for source, target in ((start, sol), (rhs_in, rhs)):
        for s in range(cells_s):
            for q in range(cells_q):
                i = s * cells_q + q
                for c in range(comps):
                    target[i, c * layers : (c + 1) * layers, :] = source[s, q, c]
                target[i, comps * layers :, :] = jnp.zeros((pad - comps * layers, columns), f32)
    write_base(layers, rhs, diag, sol, base, shape)
    write_column_messages(sol, base, first, second, shape)


def column_sides(first, second):
    even = lax.axis_index(GROUP_AXES) % 2 == 0

    def low(kind, s):
        return jnp.where(even, second[kind, s].astype(f32), first[kind, s].astype(f32))

    def high(kind, s):
        return jnp.where(even, first[kind, s].astype(f32), second[kind, s].astype(f32))

    return low, high


def edge_cells(low, high, sol, s, cells_q):
    col, cols = lax.axis_index(GROUP_AXES), lax.axis_size(GROUP_AXES)
    left = jnp.where(col > 0, low(0, s) + sol[s * cells_q], 0.0)
    right = jnp.where(col < cols - 1, high(0, s) + sol[s * cells_q + cells_q - 1], 0.0)
    return left, right


def row_kernel(shape, sol, base, first_in, second_in, first, second):
    cells_s, cells_q = shape[:2]
    low, high = column_sides(first_in, second_in)
    even = lax.axis_index("sub") % 2 == 0
    for out, s in (
        (first, jnp.where(even, cells_s - 1, 0)),
        (second, jnp.where(even, 0, cells_s - 1)),
    ):
        left, right = edge_cells(low, high, sol, s, cells_q)
        out[0, 0] = left.astype(bf16)
        out[0, cells_q + 1] = right.astype(bf16)
        low_s, high_s = low(1, s), high(1, s)
        out[1, 0] = low_s.astype(bf16)
        out[1, cells_q + 1] = high_s.astype(bf16)
        for q in range(cells_q):
            value = base[s * cells_q + q]
            if q == 0:
                value = value + low_s
            if q == cells_q - 1:
                value = value + high_s
            out[0, q + 1] = value.astype(bf16)
            out[1, q + 1] = sol[s * cells_q + q].astype(bf16)


def window_kernel(
    shape, sol, base, first_q, second_q, first_s, second_s, basis_t, pack, message, packed, local
):
    cells_s, cells_q, _, pad, columns = shape
    wide = cells_q + 2
    low, high = column_sides(first_q, second_q)
    row, rows = lax.axis_index("sub"), lax.axis_size("sub")
    even = row % 2 == 0

    def above(kind, w):
        return jnp.where(even, second_s[kind, w].astype(f32), first_s[kind, w].astype(f32))

    def below(kind, w):
        return jnp.where(even, first_s[kind, w].astype(f32), second_s[kind, w].astype(f32))

    for s in range(cells_s):
        left, right = edge_cells(low, high, sol, s, cells_q)
        values = [left] + [base[s * cells_q + q] for q in range(cells_q)] + [right]
        values[1] = values[1] + low(1, s)
        values[cells_q] = values[cells_q] + high(1, s)
        for w in range(wide):
            value = values[w]
            if s == 0:
                value = value + above(1, w)
            if s == cells_s - 1:
                value = value + below(1, w)
            local[(s + 1) * wide + w] = value.astype(bf16)
    for s, side, place, there in (
        (0, above, 0, row > 0),
        (cells_s - 1, below, (cells_s + 1) * wide, row < rows - 1),
    ):
        near = [low(1, s)] + [sol[s * cells_q + q] for q in range(cells_q)] + [high(1, s)]
        for w in range(wide):
            local[place + w] = jnp.where(there, side(0, w) + near[w], 0.0).astype(bf16)
    flat = local[...].reshape(-1, columns)
    restricted = jnp.dot(basis_t[...], flat, preferred_element_type=f32).astype(bf16)
    for j in range(message.shape[0]):
        message[j] = restricted
    span, chunk = pack.shape
    for s in range(cells_s + 2):
        packed[s * span : (s + 1) * span, :] = jnp.dot(
            pack[...], flat[s * chunk : (s + 1) * chunk], preferred_element_type=f32
        ).astype(bf16)


def matmul_kernel(left, right, out):
    out[...] = jnp.dot(left[...], right[...], preferred_element_type=f32).astype(out.dtype)


def corrected(shape, arrived, fine, own_basis, sol, new):
    cells_s, cells_q, _, pad, columns = shape
    chosen = arrived[0].astype(f32)
    for h in range(1, arrived.shape[0]):
        chosen = chosen + arrived[h].astype(f32)
    chosen = chosen.astype(bf16)
    span = cells_q * pad
    for s in range(cells_s):
        part = slice(s * span, (s + 1) * span)
        change = fine[part, :] + jnp.dot(own_basis[part, :], chosen, preferred_element_type=f32)
        for q in range(cells_q):
            i = s * cells_q + q
            new[i] = sol[i] + change[q * pad : (q + 1) * pad]


def step_kernel(
    shape, layers, arrived, fine, own_basis, sol, rhs, diag, new, base, first, second
):
    corrected(shape, arrived, fine, own_basis, sol, new)
    write_base(layers, rhs, diag, new, base, shape)
    write_column_messages(new, base, first, second, shape)


def close_kernel(shape, layers, arrived, fine, own_basis, sol, out, new):
    cells_s, cells_q, comps, _, _ = shape
    corrected(shape, arrived, fine, own_basis, sol, new)
    for s in range(cells_s):
        for q in range(cells_q):
            for c in range(comps):
                out[s, q, c] = new[s * cells_q + q, c * layers : (c + 1) * layers, :]


def basis_kernel(basis, order, pack, pick, basis_t, own_basis):
    span, chunk = pack.shape
    rows = basis.shape[0] // span
    for s in range(rows):
        ordered = jnp.dot(
            basis[s * span : (s + 1) * span, :], order[...], preferred_element_type=f32
        ).astype(bf16)
        basis_t[:, s * chunk : (s + 1) * chunk] = lax.dot_general(
            ordered, pack[...], (((0,), (0,)), ((), ())), preferred_element_type=f32
        ).astype(bf16)
        if 0 < s < rows - 1:
            size = pick.shape[0]
            own_basis[(s - 1) * size : s * size, :] = jnp.dot(
                pick[...], ordered, preferred_element_type=f32
            ).astype(bf16)


def own_rows(sub_inverse, pick, rows):
    size, span = pick.shape
    width = sub_inverse.shape[2]
    return pl.pallas_call(
        lambda inverse, chosen, out: matmul_kernel(chosen, inverse.at[0], out),
        grid=(rows,),
        out_shape=jax.ShapeDtypeStruct((rows * size, width), bf16),
        in_specs=[
            pl.BlockSpec((1, span, width), lambda s: (0, s + 1, 0)),
            pl.BlockSpec((size, span), lambda s: (0, 0)),
        ],
        out_specs=pl.BlockSpec((size, width), lambda s: (s, 0)),
        compiler_params=pltpu.CompilerParams(vmem_limit_bytes=24 << 20),
        cost_estimate=pl.CostEstimate(
            flops=2 * rows * size * span * width,
            bytes_accessed=2 * rows * (size + span) * width,
            transcendentals=0,
        ),
    )(sub_inverse, pick)


def slots_of(offsets, kgroup, groups, depth):
    ends = jnp.concatenate(
        [offsets[..., 1:], jnp.full(offsets.shape[:-1] + (1,), kgroup, jnp.int32)], axis=-1
    )
    member = jnp.arange(groups, dtype=jnp.int32)[:, None]
    turn = jnp.arange(depth, dtype=jnp.int32)[None, :]
    first = offsets[..., None, None]
    slots = first + (member - first) % groups + turn * groups
    return slots, slots < ends[..., None, None]


def selections(basis, coarse_inverse, offsets):
    n_sub, share_rows, kgroup = coarse_inverse.shape
    max_cols = basis.shape[2]
    groups = offsets.shape[1]
    depth = -(-max_cols // groups)
    member = lax.axis_index(GROUP_AXES)
    sub_index = lax.axis_index("sub")
    every = lax.all_to_all(jnp.broadcast_to(offsets, (n_sub, groups)), "sub", 0, 0, tiled=True)
    slots, valid = slots_of(every, kgroup, groups, depth)
    own_slots, own_valid = slots_of(offsets[0], kgroup, groups, depth)
    member_slots = lax.dynamic_index_in_dim(own_slots, member, 0, keepdims=False).reshape(-1)
    member_valid = lax.dynamic_index_in_dim(own_valid, member, 0, keepdims=False).reshape(-1)
    member_start = lax.dynamic_index_in_dim(offsets[0], member, 0, keepdims=False)
    picked = jnp.where(member_valid, member_slots - member_start, -1)
    order = (jnp.arange(max_cols, dtype=jnp.int32)[:, None] == picked[None, :]).astype(bf16)
    mine = lax.dynamic_index_in_dim(slots, member, 2, keepdims=False).reshape(n_sub, -1)
    mine_valid = lax.dynamic_index_in_dim(valid, member, 2, keepdims=False).reshape(n_sub, -1)
    rows = jnp.where(mine_valid, mine // groups, -1)
    row_pick = (rows[:, :, None] == jnp.arange(share_rows, dtype=jnp.int32)).astype(bf16)
    col_pick = (
        jnp.arange(kgroup, dtype=jnp.int32)[:, None]
        == jnp.where(own_valid, own_slots, -1).reshape(1, -1)
    ).astype(bf16)
    spread = jnp.einsum("gri,gik->grk", row_pick, coarse_inverse, preferred_element_type=f32)
    spread = jnp.dot(
        spread.astype(bf16).reshape(-1, kgroup), col_pick, preferred_element_type=f32
    ).astype(bf16)
    return order, spread


def shards(rhs, start, stiffness, sub_inverse, basis, coarse_inverse, offsets):
    cells_s, cells_q, comps, layers, columns = rhs.shape
    n_sub = coarse_inverse.shape[0]
    groups = offsets.shape[1]
    depth = -(-basis.shape[2] // groups)
    coarse = groups * depth
    cells = cells_s * cells_q
    per_cell = comps * layers
    pad = -(-per_cell // 16) * 16
    wide = cells_q + 2
    shape = (cells_s, cells_q, comps, pad, columns)

    field = jax.ShapeDtypeStruct((cells, pad, columns), f32)
    column_message = jax.ShapeDtypeStruct((2, cells_s, pad, columns), bf16)
    row_message = jax.ShapeDtypeStruct((2, wide, pad, columns), bf16)

    pack_map = np.zeros((wide * per_cell, wide * pad), np.float32)
    for w in range(wide):
        for t in range(per_cell):
            pack_map[w * per_cell + t, w * pad + t] = 1.0
    pack = jnp.asarray(pack_map, bf16)
    pick = jnp.asarray(pack_map.T[pad : (wide - 1) * pad], bf16)

    diagonal = (6.0 + stiffness).reshape(cells, per_cell)
    diagonal = jnp.pad(diagonal, ((0, 0), (0, pad - per_cell)))
    diagonal = jnp.broadcast_to(diagonal[:, :, None], (cells, pad, 128))
    solution, rhs_cells, base, first, second = call(
        functools.partial(open_kernel, shape, layers),
        (start, rhs, diagonal),
        (field, field, field, column_message, column_message),
    )
    order, spread = selections(basis, coarse_inverse, offsets)
    basis_t, own_basis = call(
        basis_kernel,
        (basis[0], order, pack, pick),
        (
            jax.ShapeDtypeStruct((coarse, (cells_s + 2) * wide * pad), bf16),
            jax.ShapeDtypeStruct((cells * pad, coarse), bf16),
        ),
    )
    inverse_rows = own_rows(sub_inverse, pick, cells_s)

    for sweep in range(ITERS):
        first_q, second_q = swap(first, second, GROUP_AXES)
        first, second = call(
            functools.partial(row_kernel, shape),
            (solution, base, first_q, second_q),
            (row_message, row_message),
        )
        first_s, second_s = swap(first, second, "sub")
        message, packed = call(
            functools.partial(window_kernel, shape),
            (solution, base, first_q, second_q, first_s, second_s, basis_t, pack),
            (
                jax.ShapeDtypeStruct((groups, coarse, columns), bf16),
                jax.ShapeDtypeStruct((sub_inverse.shape[1], columns), bf16),
            ),
            scratch=(pltpu.VMEM(((cells_s + 2) * wide, pad, columns), bf16),),
        )
        gathered = lax.all_to_all(message, GROUP_AXES, 0, 0, tiled=True)
        (terms,) = call(
            matmul_kernel,
            (spread, gathered.reshape(-1, columns)),
            (jax.ShapeDtypeStruct((spread.shape[0], columns), bf16),),
            flops=2 * spread.size * columns,
        )
        arrived = lax.all_to_all(
            terms.reshape(n_sub * groups, depth, columns), ALL_AXES, 0, 0, tiled=True
        ).reshape(n_sub, coarse, columns)
        (fine,) = call(
            matmul_kernel,
            (inverse_rows, packed),
            (jax.ShapeDtypeStruct((cells * pad, columns), f32),),
            flops=2 * inverse_rows.size * columns,
        )
        if sweep < ITERS - 1:
            solution, base, first, second = call(
                functools.partial(step_kernel, shape, layers),
                (arrived, fine, own_basis, solution, rhs_cells, diagonal),
                (field, field, column_message, column_message),
            )
        else:
            (solution,) = call(
                functools.partial(close_kernel, shape, layers),
                (arrived, fine, own_basis, solution),
                (jax.ShapeDtypeStruct(rhs.shape, f32),),
                scratch=(pltpu.VMEM(field.shape, f32),),
            )
    return solution


def solution(mesh):
    return jax.shard_map(
        shards,
        mesh=mesh,
        in_specs=(
            P("sub", ("crow", "ccol"), None, None, None),
            P("sub", ("crow", "ccol"), None, None, None),
            P("sub", ("crow", "ccol"), None, None),
            P(("sub", "crow", "ccol"), None, None),
            P(("sub", "crow", "ccol"), None, None),
            P(None, ("crow", "ccol"), "sub"),
            P("sub", None),
        ),
        out_specs=P("sub", ("crow", "ccol"), None, None, None),
        check_vma=False,
    )
```

time: 184 us -> 134 us (0.73)
  matrix products: 26.9 us -> 1.11 us
  local copies, waits for them, and re-layouts: 54 us -> 29.7 us
  Pallas kernels: 0 us -> 18 us
  other arithmetic: 18.9 us -> 2.56 us
    dot_general x11 -> x2, matrix products: 26.9 us -> 1.11 us  [the longest x1 0.76 us: selections(): jnp.dot(spread.astype(bf16).reshape(-1, kgroup), col_pick, preferred_elem...]
    unnamed x34 -> x56, local copies, waits for them, and re-layouts: 4.49 us -> 24.3 us
    pallas_call x0 -> x13, Pallas kernels: none -> 18 us  [the longest x12 15.8 us: call(): pl.pallas_call(body, out_shape=tuple(outs), in_specs=[VMEM] * len(ins), o...]
    add x6 -> x1, other arithmetic: 10.5 us -> 0.9 us  [shards(): diagonal = (6.0 + stiffness).reshape(cells, per_cell)]
    concatenate x2 -> x0, local copies, waits for them, and re-layouts: 8.95 us -> none  [residual_window(): jnp.concatenate([edge_low[:, None], base[:, :1] + low[1][:, None], base[:...]
    slice x11 -> x0, local copies, waits for them, and re-layouts: 8.71 us -> none  [the longest x2 3.5 us: residual_window(): base[:, 1:-1]]
    add x4 -> x1, local copies, waits for them, and re-layouts: 8.45 us -> 0.08 us  [slots_of(): slots = first + (member - first) % groups + turn * groups]
    convert_element_type x11 -> x0, local copies, waits for them, and re-layouts: 8.31 us -> none  [the longest x4 7.64 us: residual_window(): return window.astype(bf16).reshape(-1, solution.shape[-1])]
  transfers between devices with their start and end apart: 12 -> 12, of which waited for: 7 -> 6; matrix products, arithmetic and copies ran while one was open for 18% -> 6% of each run, Pallas kernels for 0% -> 6%
where the time goes in v2:
time: 134 us; the launch traced here: 133 us
  starting transfers between devices  35.8 us (27%)
  waiting for transfers between devices  33 us (25%)
  local copies, waits for them, and re-layouts  29.7 us (22%)
  Pallas kernels  18 us (13%)
  blocking collectives  12.3 us (9%)
  other arithmetic  2.56 us (2%)
    unnamed x56, local copies, waits for them, and re-layouts  24.3 us
    ppermute x4, waiting for transfers between devices, swap(): lax.ppermute(first, axis, even + [(b, a) for a, b in even])  18.3 us
    pallas_call x12, Pallas kernels, call(): pl.pallas_call(body, out_shape=tuple(outs), in_specs=[VMEM] * len(ins), o...  15.8 us
    all_to_all x2, starting transfers between devices, shards(): lax.all_to_all(terms.reshape(n_sub * groups, depth, columns), ALL_AXES, 0...  15.1 us
    all_to_all x1, blocking collectives, shards(): gathered = lax.all_to_all(message, GROUP_AXES, 0, 0, tiled=True)  12.3 us
    all_to_all x1, waiting for transfers between devices, shards(): gathered = lax.all_to_all(message, GROUP_AXES, 0, 0, tiled=True)  7.96 us
    all_to_all x2, waiting for transfers between devices, shards(): lax.all_to_all(terms.reshape(n_sub * groups, depth, columns), ALL_AXES, 0...  6.65 us
    all_to_all x1, starting transfers between devices, selections(): lax.all_to_all(jnp.broadcast_to(offsets, (n_sub, groups)), 'sub', 0, 0, t...  6.32 us
  transfers between devices with their start and end apart: 12, of which 6 were waited for; matrix products, arithmetic and copies ran while one was open for 6% of the time, Pallas kernels for 6%

profile of v2, /device:TPU:0, one launch (start us, length us, event | category | flops | bytes accessed | tf_op | source)
XLA Modules:
  0.0 132.8 jit_solution(2757632299575775861)
XLA Ops:
  0.0 1.2 broadcast_in_dim.11
  1.2 6.3 %all-to-all-start = ((s32[4,1,8]{2,1,0:T(1,128)}), s32[4,1,8]{2,1,0:T(1,128)S(1)}, u32[]{:S(2)}, u32[]{:S(2)}) async-start(s32[4,1,8]{2,1,0:T(1,128)} %broadcast_in_dim.11), calls=%async_computation | async-start | bytes 4096 | tf_op jit(solution)/shard_map/all_to_all | solution.py:275
  8.6 1.8 %copy.17.rhs_in = f32[6,6,3,10,256]{4,3,2,1,0:T(8,128)S(1)} copy(f32[6,6,3,10,256]{4,2,3,1,0:T(4,128)} %param.9) | data formatting | bytes 2211840 | tf_op args[0]
  10.9 1.6 %shard_map.94 = (f32[36,32,256]{2,1,0:T(8,128)S(1)}, f32[36,32,256]{2,1,0:T(8,128)S(1)}, f32[36,32,256]{2,1,0:T(8,128)S(1)}, bf16[2,6,32,256]{3,2,1,0:T(8,128)(2,1)}, bf16[2,6,32,256]{3,2,1,0:T(8,128)(2,1)}) custom-call(f32[6,6,3,10,256]{4,3,2,1,0:T(8,128)S(1)} %copy.16.start, f32[6,6,3,10,256]{4,3,2,1,0:T(8,128)S(1)} %copy.17.rhs_in, ...), custom_call_target="tpu_custom_call" | custom-call | bytes 6733824 | tf_op jit(solution)/shard_map/pallas_call | solution.py:20
  13.6 1.5 %collective-permute-start = (bf16[2,6,32,256]{3,2,1,0:T(8,128)(2,1)}, bf16[2,6,32,256]{3,2,1,0:T(8,128)(2,1)}, u32[]{:S(2)}, u32[]{:S(2)}) collective-permute-start(bf16[2,6,32,256]{3,2,1,0:T(8,128)(2,1)} %get-tuple-element.26), channel_id=1, source_target_pairs={{0,1},{2,3},{4,5},{6,7},{1,0},{3,2},{5,4},{7,6},{8,9},{10,11},{12,... | collective-permute-start | bytes 589832 | tf_op jit(solution)/shard_map/ppermute | solution.py:36
  15.1 1.4 %collective-permute-start.1 = (bf16[2,6,32,256]{3,2,1,0:T(8,128)(2,1)}, bf16[2,6,32,256]{3,2,1,0:T(8,128)(2,1)}, u32[]{:S(2)}, u32[]{:S(2)}) collective-permute-start(bf16[2,6,32,256]{3,2,1,0:T(8,128)(2,1)} %get-tuple-element.27), channel_id=1, source_target_pairs={{1,2},{3,4},{5,6},{2,1},{4,3},{6,5},{9,10},{11,12},{13,14},{10,9},... | collective-permute-start | bytes 589832 | tf_op jit(solution)/shard_map/ppermute | solution.py:37
  22.3 2.0 %shard_map.96 = (bf16[128,2048]{1,0:T(8,128)(2,1)S(1)}, bf16[1152,128]{1,0:T(8,128)(2,1)S(1)}) custom-call(bf16[1920,128]{1,0:T(8,128)(2,1)S(1)} %bitcast.26, bf16[128,128]{1,0:T(8,128)(2,1)S(1)} %fusion.4.order, bf16[240,256]{1,0:T(8,128)(2,1)S(1)} %copy-done.13, bf16[192,240]{1,0:T(8,128)(2,1)S(1)} %copy-done.23), custom_call_target="tpu_custom_call" | custom-call | bytes 1558528 | tf_op jit(solution)/shard_map/pallas_call | solution.py:20
  25.3 1.9 %shard_map.95 = (bf16[2,8,32,256]{3,2,1,0:T(8,128)(2,1)}, bf16[2,8,32,256]{3,2,1,0:T(8,128)(2,1)}) custom-call(f32[36,32,256]{2,1,0:T(8,128)S(1)} %get-tuple-element.24.sol, f32[36,32,256]{2,1,0:T(8,128)S(1)} %get-tuple-element.25.base, bf16[2,6,32,256]{3,2,1,0:T(8,128)(2,1)} %collective-permute-done.first_in.first_q, ...), custom_call_target="tpu_custom_call" | custom-call | bytes 3276800 | tf_op jit(solution)/shard_map/pallas_call | solution.py:20
  27.2 2.0 %collective-permute-start.2 = (bf16[2,8,32,256]{3,2,1,0:T(8,128)(2,1)}, bf16[2,8,32,256]{3,2,1,0:T(8,128)(2,1)}, u32[]{:S(2)}, u32[]{:S(2)}) collective-permute-start(bf16[2,8,32,256]{3,2,1,0:T(8,128)(2,1)} %get-tuple-element.28), channel_id=1, source_target_pairs={{0,8},{16,24},{8,0},{24,16},{1,9},{17,25},{9,1},{25,17},{2,10},{18... | collective-permute-start | bytes 786440 | tf_op jit(solution)/shard_map/ppermute | solution.py:36
  29.2 1.4 %collective-permute-start.3 = (bf16[2,8,32,256]{3,2,1,0:T(8,128)(2,1)}, bf16[2,8,32,256]{3,2,1,0:T(8,128)(2,1)}, u32[]{:S(2)}, u32[]{:S(2)}) collective-permute-start(bf16[2,8,32,256]{3,2,1,0:T(8,128)(2,1)} %get-tuple-element.29), channel_id=1, source_target_pairs={{8,16},{16,8},{9,17},{17,9},{10,18},{18,10},{11,19},{19,11},{12,20... | collective-permute-start | bytes 786440 | tf_op jit(solution)/shard_map/ppermute | solution.py:37
  30.8 5.4 %collective-permute-done.2.first_s = bf16[2,8,32,256]{3,2,1,0:T(8,128)(2,1)} collective-permute-done((bf16[2,8,32,256]{3,2,1,0:T(8,128)(2,1)}, bf16[2,8,32,256]{3,2,1,0:T(8,128)(2,1)}, u32[]{:S(2)}, u32[]{:S(2)}) %collective-permute-start.2) | collective-permute-done | bytes 262176 | tf_op jit(solution)/shard_map/ppermute | solution.py:36
  38.2 1.9 %shard_map.97 = (bf16[8,128,256]{2,1,0:T(8,128)(2,1)S(1)}, bf16[1920,256]{1,0:T(8,128)(2,1)S(1)}) custom-call(f32[36,32,256]{2,1,0:T(8,128)S(1)} %get-tuple-element.24.sol, f32[36,32,256]{2,1,0:T(8,128)S(1)} %get-tuple-element.25.base, bf16[2,6,32,256]{3,2,1,0:T(8,128)(2,1)} %collective-permute-done.first_in.first_q, ...), custom_call_target="tpu_custom_call" | custom-call | bytes 5431296 | tf_op jit(solution)/shard_map/pallas_call | solution.py:20
  41.8 4.2 %all-to-all-start.1 = ((bf16[8,128,256]{2,1,0:T(8,128)(2,1)}), bf16[8,128,256]{2,1,0:T(8,128)(2,1)}, u32[]{:S(2)}, u32[]{:S(2)}) async-start(bf16[8,128,256]{2,1,0:T(8,128)(2,1)} %copy-done.21), calls=%async_computation.1 | async-start | bytes 1048576 | tf_op jit(solution)/shard_map/all_to_all | solution.py:357
  47.2 8.0 %all-to-all-done.1 = bf16[8,128,256]{2,1,0:T(8,128)(2,1)} async-done(((bf16[8,128,256]{2,1,0:T(8,128)(2,1)}), bf16[8,128,256]{2,1,0:T(8,128)(2,1)}, u32[]{:S(2)}, u32[]{:S(2)}) %all-to-all-start.1) | async-done | bytes 524320 | tf_op jit(solution)/shard_map/all_to_all | solution.py:357
  55.1 1.5 %shard_map.98 = bf16[512,256]{1,0:T(8,128)(2,1)S(1)} custom-call(bf16[512,1024]{1,0:T(8,128)(2,1)S(1)} %fusion.1.left, bf16[1024,256]{1,0:T(8,128)(2,1)} %bitcast.6.right), custom_call_target="tpu_custom_call" | custom-call | flops 268435456 | bytes 1835008 | tf_op jit(solution)/shard_map/pallas_call | solution.py:20
  57.4 7.8 %all-to-all-start.2 = ((bf16[32,16,256]{2,1,0:T(8,128)(2,1)}), bf16[32,16,256]{2,1,0:T(8,128)(2,1)}, u32[]{:S(2)}, u32[]{:S(2)}) async-start(bf16[32,16,256]{2,1,0:T(8,128)(2,1)} %bitcast.25), calls=%async_computation.2 | async-start | bytes 524288 | tf_op jit(solution)/shard_map/all_to_all | solution.py:364
  65.2 3.1 %copy-done.3 = bf16[1,1920,1920]{2,1,0:T(8,128)(2,1)S(1)} copy-done((bf16[1,1920,1920]{2,1,0:T(8,128)(2,1)S(1)}, bf16[1,1920,1920]{2,1,0:T(8,128)(2,1)}, u32[]{:S(2)}) %copy-start.3) | copy-done | bytes 7372824
  68.3 2.3 %shard_map.99.left = bf16[1152,1920]{1,0:T(8,128)(2,1)S(1)} custom-call(bf16[1,1920,1920]{2,1,0:T(8,128)(2,1)S(1)} %copy-done.3, bf16[192,240]{1,0:T(8,128)(2,1)S(1)} %copy-done.24), custom_call_target="tpu_custom_call" | custom-call | flops 1061683200 | bytes 9953280 | tf_op jit(solution)/shard_map/pallas_call | solution.py:239
  70.5 1.4 %shard_map.100.fine = f32[1152,256]{1,0:T(8,128)S(1)} custom-call(bf16[1152,1920]{1,0:T(8,128)(2,1)S(1)} %shard_map.99.left, bf16[1920,256]{1,0:T(8,128)(2,1)S(1)} %copy-done.18), custom_call_target="tpu_custom_call" | custom-call | flops 1132462080 | bytes 6586368 | tf_op jit(solution)/shard_map/pallas_call | solution.py:20
  71.9 2.1 %copy-done.1 = bf16[1152,1920]{1,0:T(8,128)(2,1)} copy-done((bf16[1152,1920]{1,0:T(8,128)(2,1)}, bf16[1152,1920]{1,0:T(8,128)(2,1)S(1)}, u32[]{:S(2)}) %copy-start.1) | copy-done | bytes 4423704
  75.8 1.3 copy-done.5
  77.1 1.3 copy-done.12
  78.4 1.9 %shard_map.101 = (f32[36,32,256]{2,1,0:T(8,128)S(1)}, f32[36,32,256]{2,1,0:T(8,128)S(1)}, bf16[2,6,32,256]{3,2,1,0:T(8,128)(2,1)S(1)}, bf16[2,6,32,256]{3,2,1,0:T(8,128)(2,1)S(1)}) custom-call(bf16[4,128,256]{2,1,0:T(8,128)(2,1)} %bitcast.8.arrived, f32[1152,256]{1,0:T(8,128)S(1)} %copy-done.5, bf16[1152,128]{1,0:T(8,128)(2,1)S(1)} %get-tuple-element.33.own_basis, ...), custom_call_target="tpu_custom_call" | custom-call | bytes 7438336 | tf_op jit(solution)/shard_map/pallas_call | solution.py:20
  81.9 6.6 %collective-permute-done.4.first_in.first_q = bf16[2,6,32,256]{3,2,1,0:T(8,128)(2,1)S(1)} collective-permute-done((bf16[2,6,32,256]{3,2,1,0:T(8,128)(2,1)S(1)}, bf16[2,6,32,256]{3,2,1,0:T(8,128)(2,1)S(1)}, u32[]{:S(2)}, u32[]{:S(2)}) %collective-permute-start.4) | collective-permute-done | bytes 196640 | tf_op jit(solution)/shard_map/ppermute | solution.py:36
  88.5 1.7 %collective-permute-start.6 = (bf16[2,8,32,256]{3,2,1,0:T(8,128)(2,1)S(1)}, bf16[2,8,32,256]{3,2,1,0:T(8,128)(2,1)S(1)}, u32[]{:S(2)}, u32[]{:S(2)}) collective-permute-start(bf16[2,8,32,256]{3,2,1,0:T(8,128)(2,1)S(1)} %get-tuple-element.39), channel_id=1, source_target_pairs={{0,8},{16,24},{8,0},{24,16},{1,9},{17,25},{9,1},{25,17},{2,10},{18... | collective-permute-start | bytes 786440 | tf_op jit(solution)/shard_map/ppermute | solution.py:36
  90.9 6.4 %collective-permute-done.6.first_s = bf16[2,8,32,256]{3,2,1,0:T(8,128)(2,1)S(1)} collective-permute-done((bf16[2,8,32,256]{3,2,1,0:T(8,128)(2,1)S(1)}, bf16[2,8,32,256]{3,2,1,0:T(8,128)(2,1)S(1)}, u32[]{:S(2)}, u32[]{:S(2)}) %collective-permute-start.6) | collective-permute-done | bytes 262176 | tf_op jit(solution)/shard_map/ppermute | solution.py:36
  98.9 12.3 %all_to_all.26 = bf16[8,128,256]{2,1,0:T(8,128)(2,1)S(1)} all-to-all(bf16[8,128,256]{2,1,0:T(8,128)(2,1)S(1)} %get-tuple-element.41), channel_id=1, replica_groups=mesh['sub'=4,'crow'=4,'ccol'=2] {'crow','ccol'}, dimensions={0} | all-to-all | bytes 1048576 | tf_op jit(solution)/shard_map/all_to_all | solution.py:357
  112.3 7.3 %all-to-all-start.4 = ((bf16[32,16,256]{2,1,0:T(8,128)(2,1)}), bf16[32,16,256]{2,1,0:T(8,128)(2,1)S(1)}, u32[]{:S(2)}, u32[]{:S(2)}) async-start(bf16[32,16,256]{2,1,0:T(8,128)(2,1)} %bitcast.10), calls=%async_computation.4 | async-start | bytes 524288 | tf_op jit(solution)/shard_map/all_to_all | solution.py:364
  119.7 2.2 %copy-done.2 = bf16[1152,1920]{1,0:T(8,128)(2,1)S(1)} copy-done((bf16[1152,1920]{1,0:T(8,128)(2,1)S(1)}, bf16[1152,1920]{1,0:T(8,128)(2,1)}, u32[]{:S(2)}) %copy-start.2) | copy-done | bytes 4423704
  123.1 1.4 %shard_map.105.fine = f32[1152,256]{1,0:T(8,128)S(1)} custom-call(bf16[1152,1920]{1,0:T(8,128)(2,1)S(1)} %copy-done.2, bf16[1920,256]{1,0:T(8,128)(2,1)S(1)} %copy-done.20), custom_call_target="tpu_custom_call" | custom-call | flops 1132462080 | bytes 6586368 | tf_op jit(solution)/shard_map/pallas_call | solution.py:20
  124.5 5.8 %all-to-all-done.4 = bf16[32,16,256]{2,1,0:T(8,128)(2,1)S(1)} async-done(((bf16[32,16,256]{2,1,0:T(8,128)(2,1)}), bf16[32,16,256]{2,1,0:T(8,128)(2,1)S(1)}, u32[]{:S(2)}, u32[]{:S(2)}) %all-to-all-start.4) | async-done | bytes 262176 | tf_op jit(solution)/shard_map/all_to_all | solution.py:364
  130.8 2.0 %copy.18 = f32[6,6,3,10,256]{4,2,3,1,0:T(4,128)} copy(f32[6,6,3,10,256]{4,3,2,1,0:T(8,128)S(1)} %shard_map.106) | data formatting | bytes 2211840 | tf_op jit(solution)/shard_map/pallas_call | solution.py:20
  (92 shorter events, 23.9 us)
Async XLA Ops:
  0.0 46.0 %copy-start = (bf16[4,64,512]{2,1,0:T(8,128)(2,1)S(1)}, bf16[4,64,512]{2,1,0:T(8,128)(2,1)}, u32[]{:S(2)}) copy-start(bf16[4,64,512]{2,1,0:T(8,128)(2,1)} %param.14) | copy-start | bytes 786436
  1.2 23.9 %all-to-all-start = ((s32[4,1,8]{2,1,0:T(1,128)}), s32[4,1,8]{2,1,0:T(1,128)S(1)}, u32[]{:S(2)}, u32[]{:S(2)}) async-start(s32[4,1,8]{2,1,0:T(1,128)} %broadcast_in_dim.11), calls=%async_computation | async-start | bytes 4096 | tf_op jit(solution)/shard_map/all_to_all | solution.py:275
  8.6 1.8 %copy-start.25 = (f32[6,6,3,10,256]{4,2,3,1,0:T(4,128)S(1)}, f32[6,6,3,10,256]{4,2,3,1,0:T(4,128)}, u32[]{:S(2)}) copy-start(f32[6,6,3,10,256]{4,2,3,1,0:T(4,128)} %param.10) | copy-start | bytes 3317764
  10.9 5.5 %copy-start.26 = (s32[1,8]{1,0:T(1,128)S(1)}, s32[1,8]{1,0:T(1,128)}, u32[]{:S(2)}) copy-start(s32[1,8]{1,0:T(1,128)} %param.15) | copy-start | bytes 100
  12.5 1.0 copy-start.11
  13.6 11.8 %collective-permute-start = (bf16[2,6,32,256]{3,2,1,0:T(8,128)(2,1)}, bf16[2,6,32,256]{3,2,1,0:T(8,128)(2,1)}, u32[]{:S(2)}, u32[]{:S(2)}) collective-permute-start(bf16[2,6,32,256]{3,2,1,0:T(8,128)(2,1)} %get-tuple-element.26), channel_id=1, source_target_pairs={{0,1},{2,3},{4,5},{6,7},{1,0},{3,2},{5,4},{7,6},{8,9},{10,11},{12,... | collective-permute-start | bytes 589832 | tf_op jit(solution)/shard_map/ppermute | solution.py:36
  15.1 10.2 %collective-permute-start.1 = (bf16[2,6,32,256]{3,2,1,0:T(8,128)(2,1)}, bf16[2,6,32,256]{3,2,1,0:T(8,128)(2,1)}, u32[]{:S(2)}, u32[]{:S(2)}) collective-permute-start(bf16[2,6,32,256]{3,2,1,0:T(8,128)(2,1)} %get-tuple-element.27), channel_id=1, source_target_pairs={{1,2},{3,4},{5,6},{2,1},{4,3},{6,5},{9,10},{11,12},{13,14},{10,9},... | collective-permute-start | bytes 589832 | tf_op jit(solution)/shard_map/ppermute | solution.py:37
  20.4 1.0 copy-start.22
  27.2 9.1 %collective-permute-start.2 = (bf16[2,8,32,256]{3,2,1,0:T(8,128)(2,1)}, bf16[2,8,32,256]{3,2,1,0:T(8,128)(2,1)}, u32[]{:S(2)}, u32[]{:S(2)}) collective-permute-start(bf16[2,8,32,256]{3,2,1,0:T(8,128)(2,1)} %get-tuple-element.28), channel_id=1, source_target_pairs={{0,8},{16,24},{8,0},{24,16},{1,9},{17,25},{9,1},{25,17},{2,10},{18... | collective-permute-start | bytes 786440 | tf_op jit(solution)/shard_map/ppermute | solution.py:36
  29.2 7.0 %collective-permute-start.3 = (bf16[2,8,32,256]{3,2,1,0:T(8,128)(2,1)}, bf16[2,8,32,256]{3,2,1,0:T(8,128)(2,1)}, u32[]{:S(2)}, u32[]{:S(2)}) collective-permute-start(bf16[2,8,32,256]{3,2,1,0:T(8,128)(2,1)} %get-tuple-element.29), channel_id=1, source_target_pairs={{8,16},{16,8},{9,17},{17,9},{10,18},{18,10},{11,19},{19,11},{12,20... | collective-permute-start | bytes 786440 | tf_op jit(solution)/shard_map/ppermute | solution.py:37
  36.3 1.0 copy-start.9
  40.1 0.9 copy-start.17
  41.8 13.3 %all-to-all-start.1 = ((bf16[8,128,256]{2,1,0:T(8,128)(2,1)}), bf16[8,128,256]{2,1,0:T(8,128)(2,1)}, u32[]{:S(2)}, u32[]{:S(2)}) async-start(bf16[8,128,256]{2,1,0:T(8,128)(2,1)} %copy-done.21), calls=%async_computation.1 | async-start | bytes 1048576 | tf_op jit(solution)/shard_map/all_to_all | solution.py:357
  47.1 23.4 %copy-start.6 = (bf16[512,1024]{1,0:T(8,128)(2,1)}, bf16[512,1024]{1,0:T(8,128)(2,1)S(1)}, u32[]{:S(2)}) copy-start(bf16[512,1024]{1,0:T(8,128)(2,1)S(1)} %fusion.1.left) | copy-start | bytes 3145732
  47.1 18.0 %copy-start.24 = (bf16[192,240]{1,0:T(8,128)(2,1)S(1)}, bf16[192,240]{1,0:T(8,128)(2,1)}, u32[]{:S(2)}) copy-start(bf16[192,240]{1,0:T(8,128)(2,1)} %constant.83.clone.pick.chosen) | copy-start | bytes 276484
  57.4 18.4 %all-to-all-start.2 = ((bf16[32,16,256]{2,1,0:T(8,128)(2,1)}), bf16[32,16,256]{2,1,0:T(8,128)(2,1)}, u32[]{:S(2)}, u32[]{:S(2)}) async-start(bf16[32,16,256]{2,1,0:T(8,128)(2,1)} %bitcast.25), calls=%async_computation.2 | async-start | bytes 524288 | tf_op jit(solution)/shard_map/all_to_all | solution.py:364
  65.2 3.1 %copy-start.3 = (bf16[1,1920,1920]{2,1,0:T(8,128)(2,1)S(1)}, bf16[1,1920,1920]{2,1,0:T(8,128)(2,1)}, u32[]{:S(2)}) copy-start(bf16[1,1920,1920]{2,1,0:T(8,128)(2,1)} %inverse.1) | copy-start | bytes 22118404
  68.3 2.3 %copy-start.18 = (bf16[1920,256]{1,0:T(8,128)(2,1)S(1)}, bf16[1920,256]{1,0:T(8,128)(2,1)}, u32[]{:S(2)}) copy-start(bf16[1920,256]{1,0:T(8,128)(2,1)} %copy-done.17) | copy-start | bytes 2949124
  71.9 2.1 %copy-start.1 = (bf16[1152,1920]{1,0:T(8,128)(2,1)}, bf16[1152,1920]{1,0:T(8,128)(2,1)S(1)}, u32[]{:S(2)}) copy-start(bf16[1152,1920]{1,0:T(8,128)(2,1)S(1)} %shard_map.99.left) | copy-start | bytes 13271044
  74.0 1.0 copy-start.4
  75.8 1.3 copy-start.5
  77.1 1.3 copy-start.12
  80.2 17.0 %copy-start.10 = (bf16[128,2048]{1,0:T(8,128)(2,1)S(1)}, bf16[128,2048]{1,0:T(8,128)(2,1)}, u32[]{:S(2)}) copy-start(bf16[128,2048]{1,0:T(8,128)(2,1)} %copy-done.8) | copy-start | bytes 1572868
  80.2 17.0 %copy-start.15 = (bf16[240,256]{1,0:T(8,128)(2,1)S(1)}, bf16[240,256]{1,0:T(8,128)(2,1)}, u32[]{:S(2)}) copy-start(bf16[240,256]{1,0:T(8,128)(2,1)} %constant.82.clone.pack) | copy-start | bytes 368644
  80.3 8.2 %collective-permute-start.4 = (bf16[2,6,32,256]{3,2,1,0:T(8,128)(2,1)S(1)}, bf16[2,6,32,256]{3,2,1,0:T(8,128)(2,1)S(1)}, u32[]{:S(2)}, u32[]{:S(2)}) collective-permute-start(bf16[2,6,32,256]{3,2,1,0:T(8,128)(2,1)S(1)} %get-tuple-element.37), channel_id=1, source_target_pairs={{0,1},{2,3},{4,5},{6,7},{1,0},{3,2},{5,4},{7,6},{8,9},{10,11},{12,... | collective-permute-start | bytes 589832 | tf_op jit(solution)/shard_map/ppermute | solution.py:36
  81.2 7.2 %collective-permute-start.5 = (bf16[2,6,32,256]{3,2,1,0:T(8,128)(2,1)S(1)}, bf16[2,6,32,256]{3,2,1,0:T(8,128)(2,1)S(1)}, u32[]{:S(2)}, u32[]{:S(2)}) collective-permute-start(bf16[2,6,32,256]{3,2,1,0:T(8,128)(2,1)S(1)} %get-tuple-element.38), channel_id=1, source_target_pairs={{1,2},{3,4},{5,6},{2,1},{4,3},{6,5},{9,10},{11,12},{13,14},{10,9},... | collective-permute-start | bytes 589832 | tf_op jit(solution)/shard_map/ppermute | solution.py:37
  88.5 8.7 %collective-permute-start.6 = (bf16[2,8,32,256]{3,2,1,0:T(8,128)(2,1)S(1)}, bf16[2,8,32,256]{3,2,1,0:T(8,128)(2,1)S(1)}, u32[]{:S(2)}, u32[]{:S(2)}) collective-permute-start(bf16[2,8,32,256]{3,2,1,0:T(8,128)(2,1)S(1)} %get-tuple-element.39), channel_id=1, source_target_pairs={{0,8},{16,24},{8,0},{24,16},{1,9},{17,25},{9,1},{25,17},{2,10},{18... | collective-permute-start | bytes 786440 | tf_op jit(solution)/shard_map/ppermute | solution.py:36
  90.2 7.0 %collective-permute-start.7 = (bf16[2,8,32,256]{3,2,1,0:T(8,128)(2,1)S(1)}, bf16[2,8,32,256]{3,2,1,0:T(8,128)(2,1)S(1)}, u32[]{:S(2)}, u32[]{:S(2)}) collective-permute-start(bf16[2,8,32,256]{3,2,1,0:T(8,128)(2,1)S(1)} %get-tuple-element.40), channel_id=1, source_target_pairs={{8,16},{16,8},{9,17},{17,9},{10,18},{18,10},{11,19},{19,11},{12,20... | collective-permute-start | bytes 786440 | tf_op jit(solution)/shard_map/ppermute | solution.py:37
  98.9 12.3 %copy-start.7 = (bf16[512,1024]{1,0:T(8,128)(2,1)S(1)}, bf16[512,1024]{1,0:T(8,128)(2,1)}, u32[]{:S(2)}) copy-start(bf16[512,1024]{1,0:T(8,128)(2,1)} %copy-done.6) | copy-start | bytes 3145732
  112.3 18.0 %all-to-all-start.4 = ((bf16[32,16,256]{2,1,0:T(8,128)(2,1)}), bf16[32,16,256]{2,1,0:T(8,128)(2,1)S(1)}, u32[]{:S(2)}, u32[]{:S(2)}) async-start(bf16[32,16,256]{2,1,0:T(8,128)(2,1)} %bitcast.10), calls=%async_computation.4 | async-start | bytes 524288 | tf_op jit(solution)/shard_map/all_to_all | solution.py:364
  119.7 2.3 %copy-start.2 = (bf16[1152,1920]{1,0:T(8,128)(2,1)S(1)}, bf16[1152,1920]{1,0:T(8,128)(2,1)}, u32[]{:S(2)}) copy-start(bf16[1152,1920]{1,0:T(8,128)(2,1)} %copy-done.1) | copy-start | bytes 13271044
  121.9 1.2 copy-start.20
  (7 other events, 6.0 us)

commit v3 on v2

v3 whole, which is shorter than its diff:
```python
import functools
import math

import jax
import jax.numpy as jnp
from jax import lax
from jax.experimental import pallas as pl
from jax.experimental.pallas import tpu as pltpu
from jax.sharding import PartitionSpec as P

ITERS = 2
GROUP_AXES = ("crow", "ccol")
ALL_AXES = ("sub", "crow", "ccol")
bf16, f32 = jnp.bfloat16, jnp.float32
VMEM = pl.BlockSpec(memory_space=pltpu.VMEM)
HBM = pl.BlockSpec(memory_space=pltpu.HBM)


def sized(x):
    return math.prod(x.shape) * jnp.dtype(x.dtype).itemsize


def call(body, ins, outs, scratch=(), flops=0, held=()):
    size = sum(sized(x) for x in (*ins, *outs))
    room = size + sum(sized(x) for x in scratch if getattr(x, "dtype", None) in (bf16, f32))
    return pl.pallas_call(
        body,
        out_shape=tuple(outs),
        in_specs=[HBM if i in held else VMEM for i in range(len(ins))],
        out_specs=tuple(
            HBM if getattr(x, "memory_space", None) == pltpu.HBM else VMEM for x in outs
        ),
        scratch_shapes=list(scratch),
        compiler_params=pltpu.CompilerParams(vmem_limit_bytes=room + (4 << 20)),
        cost_estimate=pl.CostEstimate(flops=flops, bytes_accessed=size, transcendentals=0),
    )(
        *[
            pltpu.with_memory_space_constraint(x, pltpu.HBM) if i in held else x
            for i, x in enumerate(ins)
        ]
    )


def begun(source, target, sem):
    copy = pltpu.make_async_copy(source, target, sem)
    copy.start()
    return copy


def packing(cells, per_cell, pad):
    row = lax.broadcasted_iota(jnp.int32, (cells * per_cell, cells * pad), 0)
    column = lax.broadcasted_iota(jnp.int32, (cells * per_cell, cells * pad), 1)
    for w in range(1, cells):
        column = column - jnp.where(row >= w * per_cell, pad - per_cell, 0)
    return jnp.where(row == column, 1.0, 0.0).astype(bf16)


def swap(first, second, axis):
    count = lax.axis_size(axis)
    even = [(i, i + 1) for i in range(0, count - 1, 2)]
    odd = [(i, i + 1) for i in range(1, count - 1, 2)]
    return (
        lax.ppermute(first, axis, even + [(b, a) for a, b in even]),
        lax.ppermute(second, axis, odd + [(b, a) for a, b in odd]),
    )


def diagonal_of(stiffness, s, q, comps, layers, pad, columns):
    at = lax.broadcasted_iota(jnp.int32, (pad, layers), 0)
    layer = lax.broadcasted_iota(jnp.int32, (pad, layers), 1)
    column = jnp.zeros((pad, layers), f32)
    for c in range(comps):
        column = jnp.where(at == layer + c * layers, stiffness[s, q, c : c + 1, :], column)
    column = 6.0 + jnp.sum(column, axis=1, keepdims=True)
    return jnp.broadcast_to(column, (pad, columns))


def write_base(layers, begin, stiffness, field, base, shape):
    cells_s, cells_q, comps, pad, columns = shape
    at = lax.broadcasted_iota(jnp.int32, (pad, columns), 0)
    has_up, has_down = at < comps * layers, at < comps * layers
    for c in range(comps):
        has_up = has_up & (at != c * layers)
        has_down = has_down & (at != c * layers + layers - 1)
    for s in range(cells_s):
        for q in range(cells_q):
            i = s * cells_q + q
            x = field[i]
            diagonal = diagonal_of(stiffness, s, q, comps, layers, pad, columns)
            total = begin[i] - diagonal * x
            total = total + jnp.where(has_up, pltpu.roll(x, 1, 0), 0.0)
            total = total + jnp.where(has_down, pltpu.roll(x, pad - 1, 0), 0.0)
            if q > 0:
                total = total + field[i - 1]
            if q < cells_q - 1:
                total = total + field[i + 1]
            if s > 0:
                total = total + field[i - cells_q]
            if s < cells_s - 1:
                total = total + field[i + cells_q]
            base[i] = total


def write_column_messages(sol, base, first, second, shape):
    cells_s, cells_q = shape[:2]
    even = lax.axis_index(GROUP_AXES) % 2 == 0
    for out, q in (
        (first, jnp.where(even, cells_q - 1, 0)),
        (second, jnp.where(even, 0, cells_q - 1)),
    ):
        for s in range(cells_s):
            out[0, s] = base[s * cells_q + q].astype(bf16)
            out[1, s] = sol[s * cells_q + q].astype(bf16)


def open_kernel(
    shape, layers, start, rhs, stiffness, offsets, sol, base, first, second, sent, begin
):
    cells_s, cells_q, comps, pad, columns = shape
    sent[...] = jnp.broadcast_to(offsets[...], sent.shape)
    for s in range(cells_s):
        for q in range(cells_q):
            i = s * cells_q + q
            for source, target in ((start, sol), (rhs, begin)):
                for c in range(comps):
                    target[i, c * layers : (c + 1) * layers, :] = source[s, q, c]
                target[i, comps * layers :, :] = jnp.zeros((pad - comps * layers, columns), f32)
    write_base(layers, begin, stiffness, sol, base, shape)
    write_column_messages(sol, base, first, second, shape)


def column_sides(first, second):
    even = lax.axis_index(GROUP_AXES) % 2 == 0

    def low(kind, s):
        return jnp.where(even, second[kind, s].astype(f32), first[kind, s].astype(f32))

    def high(kind, s):
        return jnp.where(even, first[kind, s].astype(f32), second[kind, s].astype(f32))

    return low, high


def edge_cells(low, high, sol, s, cells_q):
    col, cols = lax.axis_index(GROUP_AXES), lax.axis_size(GROUP_AXES)
    left = jnp.where(col > 0, low(0, s) + sol[s * cells_q], 0.0)
    right = jnp.where(col < cols - 1, high(0, s) + sol[s * cells_q + cells_q - 1], 0.0)
    return left, right


def row_kernel(shape, sol, base, first_in, second_in, first, second):
    cells_s, cells_q = shape[:2]
    low, high = column_sides(first_in, second_in)
    even = lax.axis_index("sub") % 2 == 0
    for out, s in (
        (first, jnp.where(even, cells_s - 1, 0)),
        (second, jnp.where(even, 0, cells_s - 1)),
    ):
        left, right = edge_cells(low, high, sol, s, cells_q)
        out[0, 0] = left.astype(bf16)
        out[0, cells_q + 1] = right.astype(bf16)
        low_s, high_s = low(1, s), high(1, s)
        out[1, 0] = low_s.astype(bf16)
        out[1, cells_q + 1] = high_s.astype(bf16)
        for q in range(cells_q):
            value = base[s * cells_q + q]
            if q == 0:
                value = value + low_s
            if q == cells_q - 1:
                value = value + high_s
            out[0, q + 1] = value.astype(bf16)
            out[1, q + 1] = sol[s * cells_q + q].astype(bf16)


def window_kernel(
    shape,
    sol,
    base,
    first_q,
    second_q,
    first_s,
    second_s,
    basis_t,
    message,
    local_kept,
    local,
    restricted,
    sems,
):
    cells_s, cells_q, _, pad, columns = shape
    wide = cells_q + 2
    low, high = column_sides(first_q, second_q)
    row, rows = lax.axis_index("sub"), lax.axis_size("sub")
    even = row % 2 == 0

    def above(kind, w):
        return jnp.where(even, second_s[kind, w].astype(f32), first_s[kind, w].astype(f32))

    def below(kind, w):
        return jnp.where(even, first_s[kind, w].astype(f32), second_s[kind, w].astype(f32))

    for s in range(cells_s):
        left, right = edge_cells(low, high, sol, s, cells_q)
        values = [left] + [base[s * cells_q + q] for q in range(cells_q)] + [right]
        values[1] = values[1] + low(1, s)
        values[cells_q] = values[cells_q] + high(1, s)
        for w in range(wide):
            value = values[w]
            if s == 0:
                value = value + above(1, w)
            if s == cells_s - 1:
                value = value + below(1, w)
            local[(s + 1) * wide + w] = value.astype(bf16)
    for s, side, place, there in (
        (0, above, 0, row > 0),
        (cells_s - 1, below, (cells_s + 1) * wide, row < rows - 1),
    ):
        near = [low(1, s)] + [sol[s * cells_q + q] for q in range(cells_q)] + [high(1, s)]
        for w in range(wide):
            local[place + w] = jnp.where(there, side(0, w) + near[w], 0.0).astype(bf16)
    copies = [begun(local, local_kept, sems.at[0])]
    restricted[...] = jnp.dot(
        basis_t[...], local[...].reshape(-1, columns), preferred_element_type=f32
    ).astype(bf16)
    for j in range(message.shape[0]):
        copies.append(begun(restricted, message.at[j], sems.at[j + 1]))
    for copy in copies:
        copy.wait()


def terms_kernel(spread, gathered, out, kept, sem):
    kept[...] = jnp.dot(spread[...], gathered[...], preferred_element_type=f32).astype(bf16)
    begun(kept, out, sem).wait()


def fine_kernel(shape, layers, steps, last, local_kept, inverse_kept, sol_kept, *refs):
    cells_s, cells_q, comps, pad, columns = shape
    if last:
        out, local, inverse, packed, sol, fine, sems = refs
        fields = ((sol_kept, sol),)
    else:
        base_kept, stiffness, out, base_out, local, inverse, packed, sol, fine, base, sems = refs
        fields = ((sol_kept, sol), (base_kept, base))
    per_cell = comps * layers
    wide = cells_q + 2
    span, chunk = wide * per_cell, wide * pad
    size = cells_s // steps
    loaded = begun(local_kept, local, sems.at[0])
    arriving = [
        begun(
            inverse_kept.at[0, pl.ds((k * size + 1) * span, size * span)],
            inverse.at[pl.ds(k * size * span, size * span)],
            sems.at[k + 1],
        )
        for k in range(steps)
    ]
    others = [begun(a, b, sems.at[steps + 1 + k]) for k, (a, b) in enumerate(fields)]
    pack = packing(wide, per_cell, pad)
    loaded.wait()
    for s in range(packed.shape[0] // span):
        part = local[s * wide : (s + 1) * wide].reshape(chunk, columns)
        packed[s * span : (s + 1) * span, :] = jnp.dot(
            pack, part, preferred_element_type=f32
        ).astype(bf16)
    for k in range(steps):
        arriving[k].wait()
        rows = jnp.dot(
            inverse[k * size * span : (k + 1) * size * span, :],
            packed[...],
            preferred_element_type=f32,
        )
        for s in range(size):
            for q in range(cells_q):
                i = (k * size + s) * cells_q + q
                first = s * span + (q + 1) * per_cell
                fine[i, :per_cell, :] = rows[first : first + per_cell]
                fine[i, per_cell:, :] = jnp.zeros((pad - per_cell, columns), f32)
    for copy in others:
        copy.wait()
    for i in range(fine.shape[0]):
        sol[i] = sol[i] + fine[i]
    copies = [begun(sol, out, sems.at[steps + 3])]
    if not last:
        write_base(layers, base, stiffness, fine, base, shape)
        copies.append(begun(base, base_out, sems.at[steps + 4]))
    for copy in copies:
        copy.wait()


def fine_product(shape, layers, local, sub_inverse, sol, base, stiffness, last):
    cells_s, cells_q, comps, pad, columns = shape
    width = sub_inverse.shape[2]
    rows = cells_s * (cells_q + 2) * comps * layers
    steps = 3 if cells_s % 3 == 0 else 1
    kept = pltpu.HBM((cells_s * cells_q, pad, columns), f32)
    field = pltpu.VMEM(kept.shape, f32)
    return call(
        functools.partial(fine_kernel, shape, layers, steps, last),
        (local, sub_inverse, sol) if last else (local, sub_inverse, sol, base, stiffness),
        (kept,) if last else (kept, kept),
        scratch=(
            pltpu.VMEM(local.shape, bf16),
            pltpu.VMEM((rows, width), bf16),
            pltpu.VMEM((width, columns), bf16),
        )
        + ((field, field) if last else (field, field, field))
        + (pltpu.SemaphoreType.DMA((steps + 5,)),),
        flops=2 * rows * width * columns,
        held=(0, 1, 2) if last else (0, 1, 2, 3),
    )


def coarse_part(shape, arrived, basis_p, coarse):
    cells_s, cells_q, _, pad, _ = shape
    chosen = arrived[0].astype(f32)
    for h in range(1, arrived.shape[0]):
        chosen = chosen + arrived[h].astype(f32)
    chosen = chosen.astype(bf16)
    chunk = (cells_q + 2) * pad
    for s in range(cells_s):
        first = (s + 1) * chunk + pad
        rows = jnp.dot(
            basis_p[first : first + cells_q * pad, :], chosen, preferred_element_type=f32
        )
        coarse[s * cells_q : (s + 1) * cells_q] = rows.reshape(cells_q, pad, -1)


def step_kernel(
    shape,
    layers,
    arrived,
    basis_kept,
    sol_kept,
    base_kept,
    stiffness,
    new,
    base,
    first,
    second,
    basis_p,
    coarse,
    begin,
    sems,
):
    sources, targets = (basis_kept, sol_kept, base_kept), (basis_p, new, begin)
    copies = [begun(a, b, sems.at[k]) for k, (a, b) in enumerate(zip(sources, targets))]
    copies[0].wait()
    coarse_part(shape, arrived, basis_p, coarse)
    copies[1].wait()
    for i in range(new.shape[0]):
        new[i] = new[i] + coarse[i]
    copies[2].wait()
    write_base(layers, begin, stiffness, coarse, base, shape)
    write_column_messages(new, base, first, second, shape)


def close_kernel(shape, layers, arrived, basis_kept, sol_kept, out, basis_p, coarse, sol, sems):
    cells_s, cells_q, comps, _, _ = shape
    sources, targets = (basis_kept, sol_kept), (basis_p, sol)
    copies = [begun(a, b, sems.at[k]) for k, (a, b) in enumerate(zip(sources, targets))]
    copies[0].wait()
    coarse_part(shape, arrived, basis_p, coarse)
    copies[1].wait()
    for s in range(cells_s):
        for q in range(cells_q):
            i = s * cells_q + q
            for c in range(comps):
                part = slice(c * layers, (c + 1) * layers)
                out[s, q, c] = sol[i, part, :] + coarse[i, part, :]


def places(offsets, g, j, groups, depth, kgroup, shape):
    first = offsets[g, j]
    end = kgroup if j == groups - 1 else offsets[g, j + 1]
    at = lax.broadcasted_iota(jnp.int32, shape, 1)
    turn = at
    member = jnp.zeros(shape, jnp.int32)
    for m in range(1, groups):
        member = member + jnp.where(at >= m * depth, 1, 0)
        turn = turn - jnp.where(at >= m * depth, depth, 0)
    shifted = member - lax.rem(first, groups)
    shifted = jnp.where(shifted < 0, shifted + groups, shifted)
    place = shifted + turn * groups
    return first, place, place < end - first


def basis_kernel(dims, offsets, basis, basis_t, basis_p):
    wide, per_cell, pad, groups, depth, kgroup = dims
    span, chunk = wide * per_cell, wide * pad
    pack = packing(wide, per_cell, pad)
    member = lax.axis_index(GROUP_AXES)
    shape = (basis.shape[2], groups * depth)
    row = lax.broadcasted_iota(jnp.int32, shape, 0)
    order = jnp.zeros(shape, f32)
    for j in range(groups):
        _, place, valid = places(offsets, 0, j, groups, depth, kgroup, shape)
        order = order + jnp.where((row == place) & valid & (member == j), 1.0, 0.0)
    order = order.astype(bf16)
    for s in range(basis.shape[1] // span):
        ordered = jnp.dot(
            basis[0, s * span : (s + 1) * span, :], order, preferred_element_type=f32
        ).astype(bf16)
        part = slice(s * chunk, (s + 1) * chunk)
        basis_t[:, part] = lax.dot_general(
            ordered, pack, (((0,), (0,)), ((), ())), preferred_element_type=f32
        ).astype(bf16)
        basis_p[part, :] = lax.dot_general(
            pack, ordered, (((0,), (0,)), ((), ())), preferred_element_type=f32
        ).astype(bf16)


def spread_kernel(dims, every, inverse, out, columns):
    groups, depth, kgroup = dims
    g = pl.program_id(0)
    member = lax.axis_index(GROUP_AXES)

    @pl.when(g == 0)
    def _():
        own = lax.axis_index("sub")
        shape = (kgroup, groups * depth)
        slot = lax.broadcasted_iota(jnp.int32, shape, 0)
        for j in range(groups):
            first, place, valid = places(every, own, j, groups, depth, kgroup, shape)
            columns[:, j * groups * depth : (j + 1) * groups * depth] = jnp.where(
                (slot == place + first) & valid, 1.0, 0.0
            ).astype(bf16)

    rows = inverse.shape[1]
    turn = lax.broadcasted_iota(jnp.int32, (depth, rows), 0)
    index = lax.broadcasted_iota(jnp.int32, (depth, rows), 1)
    picks = []
    for j in range(groups):
        first = every[g, j]
        end = kgroup if j == groups - 1 else every[g, j + 1]
        begin = lax.div(first - member + groups - 1, groups)
        wanted = (index == turn + begin) & (index * groups + member < end)
        picks.append(jnp.where(wanted, 1.0, 0.0).astype(bf16))
    picked = jnp.dot(
        jnp.concatenate(picks, axis=0), inverse[0], preferred_element_type=f32
    ).astype(bf16)
    out[...] = jnp.dot(picked, columns[...], preferred_element_type=f32).astype(bf16)


def spread_inverse(every, coarse_inverse, depth):
    n_sub, share_rows, kgroup = coarse_inverse.shape
    groups = every.shape[1]
    coarse = groups * depth
    return pl.pallas_call(
        functools.partial(spread_kernel, (groups, depth, kgroup)),
        grid=(n_sub,),
        out_shape=pltpu.HBM((n_sub * coarse, groups * coarse), bf16),
        in_specs=[
            pl.BlockSpec(memory_space=pltpu.SMEM),
            pl.BlockSpec((1, share_rows, kgroup), lambda g: (g, 0, 0)),
        ],
        out_specs=pl.BlockSpec((coarse, groups * coarse), lambda g: (g, 0)),
        scratch_shapes=[pltpu.VMEM((kgroup, groups * coarse), bf16)],
        compiler_params=pltpu.CompilerParams(vmem_limit_bytes=10 << 20),
        cost_estimate=pl.CostEstimate(
            flops=2 * n_sub * coarse * groups * coarse * kgroup,
            bytes_accessed=4 * n_sub * coarse * groups * coarse,
            transcendentals=0,
        ),
    )(every, coarse_inverse)


def shards(rhs, start, stiffness, sub_inverse, basis, coarse_inverse, offsets):
    cells_s, cells_q, comps, layers, columns = rhs.shape
    n_sub, _, kgroup = coarse_inverse.shape
    groups = offsets.shape[1]
    depth = -(-basis.shape[2] // groups)
    coarse = groups * depth
    cells = cells_s * cells_q
    per_cell = comps * layers
    pad = -(-per_cell // 16) * 16
    wide = cells_q + 2
    shape = (cells_s, cells_q, comps, pad, columns)

    field = jax.ShapeDtypeStruct((cells, pad, columns), f32)
    column_message = jax.ShapeDtypeStruct((2, cells_s, pad, columns), bf16)
    row_message = jax.ShapeDtypeStruct((2, wide, pad, columns), bf16)

    rows = (cells_s + 2) * wide * pad

    solution, base, first, second, sent = call(
        functools.partial(open_kernel, shape, layers),
        (start, rhs, stiffness, offsets),
        (
            field,
            field,
            column_message,
            column_message,
            jax.ShapeDtypeStruct((n_sub, groups), jnp.int32),
        ),
        scratch=(pltpu.VMEM(field.shape, f32),),
    )
    basis_t, basis_p = pl.pallas_call(
        functools.partial(basis_kernel, (wide, per_cell, pad, groups, depth, kgroup)),
        out_shape=(pltpu.HBM((coarse, rows), bf16), pltpu.HBM((rows, coarse), bf16)),
        in_specs=[pl.BlockSpec(memory_space=pltpu.SMEM), VMEM],
        out_specs=(
            pl.BlockSpec((coarse, rows), lambda: (0, 0)),
            pl.BlockSpec((rows, coarse), lambda: (0, 0)),
        ),
        compiler_params=pltpu.CompilerParams(vmem_limit_bytes=12 << 20),
        cost_estimate=pl.CostEstimate(
            flops=6 * rows * coarse * wide * pad, bytes_accessed=6 * basis.size, transcendentals=0
        ),
    )(offsets, basis)
    sent, _ = lax.optimization_barrier((sent, basis_t))
    every = lax.all_to_all(sent, "sub", 0, 0, tiled=True)
    spread = spread_inverse(every, coarse_inverse, depth)

    for sweep in range(ITERS):
        first_q, second_q = swap(first, second, GROUP_AXES)
        if sweep == 0:
            first_q, second_q, basis_t = lax.optimization_barrier((first_q, second_q, basis_t))
        first, second = call(
            functools.partial(row_kernel, shape),
            (solution, base, first_q, second_q),
            (row_message, row_message),
        )
        first_s, second_s = swap(first, second, "sub")
        message, local = call(
            functools.partial(window_kernel, shape),
            (solution, base, first_q, second_q, first_s, second_s, basis_t),
            (
                pltpu.HBM((groups, coarse, columns), bf16),
                pltpu.HBM(((cells_s + 2) * wide, pad, columns), bf16),
            ),
            scratch=(
                pltpu.VMEM(((cells_s + 2) * wide, pad, columns), bf16),
                pltpu.VMEM((coarse, columns), bf16),
                pltpu.SemaphoreType.DMA((groups + 1,)),
            ),
            flops=2 * rows * coarse * columns,
        )
        gathered = lax.all_to_all(message, GROUP_AXES, 0, 0, tiled=True)
        (terms,) = call(
            terms_kernel,
            (spread, gathered.reshape(-1, columns)),
            (pltpu.HBM((spread.shape[0], columns), bf16),),
            scratch=(pltpu.VMEM((spread.shape[0], columns), bf16), pltpu.SemaphoreType.DMA),
            flops=2 * spread.size * columns,
        )
        arrived = lax.all_to_all(
            terms.reshape(n_sub * groups, depth, columns), ALL_AXES, 0, 0, tiled=True
        ).reshape(n_sub, coarse, columns)
        last = sweep == ITERS - 1
        kept = fine_product(
            shape, layers, local, sub_inverse, solution, base, stiffness, last
        )
        if last:
            (solution,) = call(
                functools.partial(close_kernel, shape, layers),
                (arrived, basis_p, *kept),
                (jax.ShapeDtypeStruct(rhs.shape, f32),),
                scratch=(
                    pltpu.VMEM((rows, coarse), bf16),
                    pltpu.VMEM(field.shape, f32),
                    pltpu.VMEM(field.shape, f32),
                    pltpu.SemaphoreType.DMA((2,)),
                ),
                held=(1, 2),
            )
        else:
            solution, base, first, second = call(
                functools.partial(step_kernel, shape, layers),
                (arrived, basis_p, *kept, stiffness),
                (field, field, column_message, column_message),
                scratch=(
                    pltpu.VMEM((rows, coarse), bf16),
                    pltpu.VMEM(field.shape, f32),
                    pltpu.VMEM(field.shape, f32),
                    pltpu.SemaphoreType.DMA((3,)),
                ),
                held=(1, 2, 3),
            )
    return solution


def solution(mesh):
    return jax.shard_map(
        shards,
        mesh=mesh,
        in_specs=(
            P("sub", ("crow", "ccol"), None, None, None),
            P("sub", ("crow", "ccol"), None, None, None),
            P("sub", ("crow", "ccol"), None, None),
            P(("sub", "crow", "ccol"), None, None),
            P(("sub", "crow", "ccol"), None, None),
            P(None, ("crow", "ccol"), "sub"),
            P("sub", None),
        ),
        out_specs=P("sub", ("crow", "ccol"), None, None, None),
        check_vma=False,
    )
```

time: 134 us -> 115 us (0.86)
  local copies, waits for them, and re-layouts: 29.7 us -> 6.92 us
  Pallas kernels: 18 us -> 33.8 us
  starting transfers between devices: 35.8 us -> 29.8 us
  waiting for transfers between devices: 33 us -> 29.5 us
  other arithmetic: 2.56 us -> 0 us
  blocking collectives: 12.3 us -> 14 us
    unnamed x56 -> x24, local copies, waits for them, and re-layouts: 24.3 us -> 4.88 us
    pallas_call x13, Pallas kernels: 18 us -> 33.8 us  [the longest x11 26.5 us: call(): pl.pallas_call(body, out_shape=tuple(outs), in_specs=[HBM if i in held el...]
    all_to_all x2, starting transfers between devices: 15.1 us -> 9.67 us  [shards(): lax.all_to_all(terms.reshape(n_sub * groups, depth, columns), ALL_AXES, 0...]
    all_to_all x1, waiting for transfers between devices: 7.96 us -> 4.3 us  [shards(): gathered = lax.all_to_all(message, GROUP_AXES, 0, 0, tiled=True)]
    ppermute x4, waiting for transfers between devices: 18.3 us -> 15.7 us  [swap(): lax.ppermute(first, axis, even + [(b, a) for a, b in even])]
    all_to_all x1, blocking collectives: 12.3 us -> 14 us  [shards(): gathered = lax.all_to_all(message, GROUP_AXES, 0, 0, tiled=True)]
    broadcast_in_dim x2 -> x0, local copies, waits for them, and re-layouts: 1.45 us -> none  [the longest x1 1.24 us: selections(): jnp.broadcast_to(offsets, (n_sub, groups))]
    all_to_all x2, waiting for transfers between devices: 6.65 us -> 8.07 us  [shards(): lax.all_to_all(terms.reshape(n_sub * groups, depth, columns), ALL_AXES, 0...]
  transfers between devices with their start and end apart: 12 -> 12, of which waited for: 6 -> 8; matrix products, arithmetic and copies ran while one was open for 6% -> 0% of each run, Pallas kernels for 6% -> 20%
where the time goes in v3:
time: 115 us; the launch traced here: 114 us
  Pallas kernels  33.8 us (29%)
  starting transfers between devices  29.8 us (26%)
  waiting for transfers between devices  29.5 us (26%)
  blocking collectives  14 us (12%)
  local copies, waits for them, and re-layouts  6.92 us (6%)
    pallas_call x11, Pallas kernels, call(): pl.pallas_call(body, out_shape=tuple(outs), in_specs=[HBM if i in held el...  26.5 us
    ppermute x4, waiting for transfers between devices, swap(): lax.ppermute(first, axis, even + [(b, a) for a, b in even])  15.7 us
    all_to_all x1, blocking collectives, shards(): gathered = lax.all_to_all(message, GROUP_AXES, 0, 0, tiled=True)  14 us
    all_to_all x2, starting transfers between devices, shards(): lax.all_to_all(terms.reshape(n_sub * groups, depth, columns), ALL_AXES, 0...  9.67 us
    all_to_all x2, waiting for transfers between devices, shards(): lax.all_to_all(terms.reshape(n_sub * groups, depth, columns), ALL_AXES, 0...  8.07 us
    ppermute x4, starting transfers between devices, swap(): lax.ppermute(first, axis, even + [(b, a) for a, b in even])  7.06 us
    all_to_all x1, starting transfers between devices, shards(): every = lax.all_to_all(sent, 'sub', 0, 0, tiled=True)  4.97 us
    unnamed x24, local copies, waits for them, and re-layouts  4.88 us
  transfers between devices with their start and end apart: 12, of which 8 were waited for; matrix products, arithmetic and copies ran while one was open for 0% of the time, Pallas kernels for 20%

profile of v3, /device:TPU:0, one launch (start us, length us, event | category | flops | bytes accessed | tf_op | source)
XLA Modules:
  0.0 114.2 jit_solution(13198122255841203769)
XLA Ops:
  0.0 1.8 %copy.12.rhs = f32[6,6,3,10,256]{4,3,2,1,0:T(8,128)S(1)} copy(f32[6,6,3,10,256]{4,2,3,1,0:T(4,128)} %param.7) | data formatting | bytes 2211840 | tf_op args[0]
  2.7 1.7 %shard_map.73 = (f32[36,32,256]{2,1,0:T(8,128)S(1)}, f32[36,32,256]{2,1,0:T(8,128)S(1)}, bf16[2,6,32,256]{3,2,1,0:T(8,128)(2,1)S(1)}, bf16[2,6,32,256]{3,2,1,0:T(8,128)(2,1)S(1)}, s32[4,8]{1,0:T(4,128)}) custom-call(f32[6,6,3,10,256]{4,3,2,1,0:T(8,128)S(1)} %copy.11.start, f32[6,6,3,10,256]{4,3,2,1,0:T(8,128)S(1)} %copy.12.rhs, ...), custom_call_target="tpu_custom_call" | custom-call | bytes 4968832 | tf_op jit(solution)/shard_map/pallas_call | solution.py:26
  4.4 3.0 %collective-permute-start = (bf16[2,6,32,256]{3,2,1,0:T(8,128)(2,1)S(1)}, bf16[2,6,32,256]{3,2,1,0:T(8,128)(2,1)S(1)}, u32[]{:S(2)}, u32[]{:S(2)}) collective-permute-start(bf16[2,6,32,256]{3,2,1,0:T(8,128)(2,1)S(1)} %get-tuple-element.35), channel_id=1, source_target_pairs={{0,1},{2,3},{4,5},{6,7},{1,0},{3,2},{5,4},{7,6},{8,9},{10,11},{12,... | collective-permute-start | bytes 589832 | tf_op jit(solution)/shard_map/ppermute | solution.py:63
  8.0 3.7 %shard_map.74 = (bf16[128,2048]{1,0:T(8,128)(2,1)}, bf16[2048,128]{1,0:T(8,128)(2,1)}) custom-call(s32[1,8]{1,0:T(1,128)S(1)} %copy-done.7, bf16[1,1920,128]{2,1,0:T(8,128)(2,1)S(1)} %copy-done.8), custom_call_target="tpu_custom_call" | custom-call | flops 402653184 | bytes 1474560 | tf_op jit(solution)/shard_map/pallas_call | solution.py:497
  11.7 3.0 %collective-permute-done.first_in.first_q = bf16[2,6,32,256]{3,2,1,0:T(8,128)(2,1)S(1)} collective-permute-done((bf16[2,6,32,256]{3,2,1,0:T(8,128)(2,1)S(1)}, bf16[2,6,32,256]{3,2,1,0:T(8,128)(2,1)S(1)}, u32[]{:S(2)}, u32[]{:S(2)}) %collective-permute-start) | collective-permute-done | bytes 196640 | tf_op jit(solution)/shard_map/ppermute | solution.py:63
  15.6 1.6 %collective-permute-start.2 = (bf16[2,8,32,256]{3,2,1,0:T(8,128)(2,1)}, bf16[2,8,32,256]{3,2,1,0:T(8,128)(2,1)}, u32[]{:S(2)}, u32[]{:S(2)}) collective-permute-start(bf16[2,8,32,256]{3,2,1,0:T(8,128)(2,1)} %get-tuple-element.39), channel_id=1, source_target_pairs={{0,8},{16,24},{8,0},{24,16},{1,9},{17,25},{9,1},{25,17},{2,10},{18... | collective-permute-start | bytes 786440 | tf_op jit(solution)/shard_map/ppermute | solution.py:63
  17.2 1.4 %collective-permute-start.3 = (bf16[2,8,32,256]{3,2,1,0:T(8,128)(2,1)}, bf16[2,8,32,256]{3,2,1,0:T(8,128)(2,1)}, u32[]{:S(2)}, u32[]{:S(2)}) collective-permute-start(bf16[2,8,32,256]{3,2,1,0:T(8,128)(2,1)} %get-tuple-element.40), channel_id=1, source_target_pairs={{8,16},{16,8},{9,17},{17,9},{10,18},{18,10},{11,19},{19,11},{12,20... | collective-permute-start | bytes 786440 | tf_op jit(solution)/shard_map/ppermute | solution.py:64
  18.6 5.0 %all-to-all-start = ((s32[4,1,8]{2,1,0:T(1,128)}), s32[4,1,8]{2,1,0:T(1,128)S(1)}, u32[]{:S(2)}, u32[]{:S(2)}) async-start(s32[4,1,8]{2,1,0:T(1,128)} %bitcast.1), calls=%async_computation | async-start | bytes 4096 | tf_op jit(solution)/shard_map/all_to_all | solution.py:511
  23.5 1.5 %collective-permute-done.2.first_s = bf16[2,8,32,256]{3,2,1,0:T(8,128)(2,1)} collective-permute-done((bf16[2,8,32,256]{3,2,1,0:T(8,128)(2,1)}, bf16[2,8,32,256]{3,2,1,0:T(8,128)(2,1)}, u32[]{:S(2)}, u32[]{:S(2)}) %collective-permute-start.2) | collective-permute-done | bytes 262176 | tf_op jit(solution)/shard_map/ppermute | solution.py:63
  25.0 2.7 %shard_map.77 = (bf16[8,128,256]{2,1,0:T(8,128)(2,1)}, bf16[64,32,256]{2,1,0:T(8,128)(2,1)}) custom-call(f32[36,32,256]{2,1,0:T(8,128)S(1)} %get-tuple-element.33.sol.sol_kept, f32[36,32,256]{2,1,0:T(8,128)S(1)} %get-tuple-element.34.base.refs_0_, bf16[2,6,32,256]{3,2,1,0:T(8,128)(2,1)S(1)} %collective-permute-done.first_in.first_q, ...), custom_call_target="tpu_custom_call" | custom-call | flops 134217728 | bytes 5373952 | tf_op jit(solution)/shard_map/pallas_call | solution.py:26
  27.7 1.3 %all-to-all-done = s32[4,1,8]{2,1,0:T(1,128)S(1)} async-done(((s32[4,1,8]{2,1,0:T(1,128)}), s32[4,1,8]{2,1,0:T(1,128)S(1)}, u32[]{:S(2)}, u32[]{:S(2)}) %all-to-all-start) | async-done | bytes 160 | tf_op jit(solution)/shard_map/all_to_all | solution.py:511
  29.1 4.7 %all-to-all-start.1 = ((bf16[8,128,256]{2,1,0:T(8,128)(2,1)}), bf16[8,128,256]{2,1,0:T(8,128)(2,1)S(1)}, u32[]{:S(2)}, u32[]{:S(2)}) async-start(bf16[8,128,256]{2,1,0:T(8,128)(2,1)} %get-tuple-element.42), calls=%async_computation.1 | async-start | bytes 1048576 | tf_op jit(solution)/shard_map/all_to_all | solution.py:538
  33.8 0.9 copy-done.9
  34.7 3.6 %shard_map.75.spread = bf16[512,1024]{1,0:T(8,128)(2,1)} custom-call(s32[4,8]{1,0:T(4,128)S(1)} %bitcast.14, bf16[4,64,512]{2,1,0:T(8,128)(2,1)S(1)} %copy-done.9), custom_call_target="tpu_custom_call" | custom-call | flops 536870912 | bytes 2097152 | tf_op jit(solution)/shard_map/pallas_call | solution.py:448
  38.3 4.3 %all-to-all-done.1 = bf16[8,128,256]{2,1,0:T(8,128)(2,1)S(1)} async-done(((bf16[8,128,256]{2,1,0:T(8,128)(2,1)}), bf16[8,128,256]{2,1,0:T(8,128)(2,1)S(1)}, u32[]{:S(2)}, u32[]{:S(2)}) %all-to-all-start.1) | async-done | bytes 524320 | tf_op jit(solution)/shard_map/all_to_all | solution.py:538
  42.6 1.2 %copy-done.3 = bf16[512,1024]{1,0:T(8,128)(2,1)S(1)} copy-done((bf16[512,1024]{1,0:T(8,128)(2,1)S(1)}, bf16[512,1024]{1,0:T(8,128)(2,1)}, u32[]{:S(2)}) %copy-start.3) | copy-done | bytes 1048600
  43.9 1.2 %shard_map.78 = bf16[512,256]{1,0:T(8,128)(2,1)} custom-call(bf16[512,1024]{1,0:T(8,128)(2,1)S(1)} %copy-done.3, bf16[1024,256]{1,0:T(8,128)(2,1)S(1)} %bitcast.10), custom_call_target="tpu_custom_call" | custom-call | flops 268435456 | bytes 1835008 | tf_op jit(solution)/shard_map/pallas_call | solution.py:26
  45.0 4.7 %all-to-all-start.2 = ((bf16[32,16,256]{2,1,0:T(8,128)(2,1)}), bf16[32,16,256]{2,1,0:T(8,128)(2,1)S(1)}, u32[]{:S(2)}, u32[]{:S(2)}) async-start(bf16[32,16,256]{2,1,0:T(8,128)(2,1)} %bitcast.15), calls=%async_computation.2 | async-start | bytes 524288 | tf_op jit(solution)/shard_map/all_to_all | solution.py:546
  49.7 7.0 %shard_map.79 = (f32[36,32,256]{2,1,0:T(8,128)}, f32[36,32,256]{2,1,0:T(8,128)}) custom-call(bf16[64,32,256]{2,1,0:T(8,128)(2,1)} %get-tuple-element.44.local_kept, bf16[1,1920,1920]{2,1,0:T(8,128)(2,1)} %inverse_kept.3, f32[36,32,256]{2,1,0:T(8,128)} %copy-done, f32[36,32,256]{2,1,0:T(8,128)} %copy-done.1, f32[6,6,3,10]{3,2,1,0:T(4,128)S(1)} %copy-done.6), custom_call_target="tpu_custom_call" | custom-call | flops 1415577600 | bytes 13144288 | tf_op jit(solution)/shard_map/pallas_call | solution.py:26
  56.8 3.6 %all-to-all-done.2 = bf16[32,16,256]{2,1,0:T(8,128)(2,1)S(1)} async-done(((bf16[32,16,256]{2,1,0:T(8,128)(2,1)}), bf16[32,16,256]{2,1,0:T(8,128)(2,1)S(1)}, u32[]{:S(2)}, u32[]{:S(2)}) %all-to-all-start.2) | async-done | bytes 262176 | tf_op jit(solution)/shard_map/all_to_all | solution.py:546
  60.4 2.5 %shard_map.80 = (f32[36,32,256]{2,1,0:T(8,128)S(1)}, f32[36,32,256]{2,1,0:T(8,128)S(1)}, bf16[2,6,32,256]{3,2,1,0:T(8,128)(2,1)S(1)}, bf16[2,6,32,256]{3,2,1,0:T(8,128)(2,1)S(1)}) custom-call(bf16[4,128,256]{2,1,0:T(8,128)(2,1)S(1)} %bitcast.13, bf16[2048,128]{1,0:T(8,128)(2,1)} %get-tuple-element.43.basis_kept, f32[36,32,256]{2,1,0:T(8,128)} %get-tuple-element.45.sol_kept, ...), custom_call_target="tpu_custom_call" | custom-call | bytes 5902560 | tf_op jit(solution)/shard_map/pallas_call | solution.py:26
  64.5 5.5 %collective-permute-done.4.first_in.first_q = bf16[2,6,32,256]{3,2,1,0:T(8,128)(2,1)S(1)} collective-permute-done((bf16[2,6,32,256]{3,2,1,0:T(8,128)(2,1)S(1)}, bf16[2,6,32,256]{3,2,1,0:T(8,128)(2,1)S(1)}, u32[]{:S(2)}, u32[]{:S(2)}) %collective-permute-start.4) | collective-permute-done | bytes 196640 | tf_op jit(solution)/shard_map/ppermute | solution.py:63
  70.0 1.7 %collective-permute-start.6 = (bf16[2,8,32,256]{3,2,1,0:T(8,128)(2,1)S(1)}, bf16[2,8,32,256]{3,2,1,0:T(8,128)(2,1)S(1)}, u32[]{:S(2)}, u32[]{:S(2)}) collective-permute-start(bf16[2,8,32,256]{3,2,1,0:T(8,128)(2,1)S(1)} %get-tuple-element.51), channel_id=1, source_target_pairs={{0,8},{16,24},{8,0},{24,16},{1,9},{17,25},{9,1},{25,17},{2,10},{18... | collective-permute-start | bytes 786440 | tf_op jit(solution)/shard_map/ppermute | solution.py:63
  72.3 5.8 %collective-permute-done.6.first_s = bf16[2,8,32,256]{3,2,1,0:T(8,128)(2,1)S(1)} collective-permute-done((bf16[2,8,32,256]{3,2,1,0:T(8,128)(2,1)S(1)}, bf16[2,8,32,256]{3,2,1,0:T(8,128)(2,1)S(1)}, u32[]{:S(2)}, u32[]{:S(2)}) %collective-permute-start.6) | collective-permute-done | bytes 262176 | tf_op jit(solution)/shard_map/ppermute | solution.py:63
  78.1 1.6 %shard_map.82 = (bf16[8,128,256]{2,1,0:T(8,128)(2,1)}, bf16[64,32,256]{2,1,0:T(8,128)(2,1)}) custom-call(f32[36,32,256]{2,1,0:T(8,128)S(1)} %get-tuple-element.47.sol.sol_kept, f32[36,32,256]{2,1,0:T(8,128)S(1)} %get-tuple-element.48.base, bf16[2,6,32,256]{3,2,1,0:T(8,128)(2,1)S(1)} %collective-permute-done.4.first_in.first_q, ...), custom_call_target="tpu_custom_call" | custom-call | flops 134217728 | bytes 5373952 | tf_op jit(solution)/shard_map/pallas_call | solution.py:26
  79.8 14.0 %all_to_all.31 = bf16[8,128,256]{2,1,0:T(8,128)(2,1)S(1)} all-to-all(bf16[8,128,256]{2,1,0:T(8,128)(2,1)} %get-tuple-element.53), channel_id=1, replica_groups=mesh['sub'=4,'crow'=4,'ccol'=2] {'crow','ccol'}, dimensions={0} | all-to-all | bytes 1048576 | tf_op jit(solution)/shard_map/all_to_all | solution.py:538
  93.8 1.2 %shard_map.83 = bf16[512,256]{1,0:T(8,128)(2,1)} custom-call(bf16[512,1024]{1,0:T(8,128)(2,1)S(1)} %copy-done.4, bf16[1024,256]{1,0:T(8,128)(2,1)S(1)} %bitcast.11), custom_call_target="tpu_custom_call" | custom-call | flops 268435456 | bytes 1835008 | tf_op jit(solution)/shard_map/pallas_call | solution.py:26
  94.9 5.0 %all-to-all-start.4 = ((bf16[32,16,256]{2,1,0:T(8,128)(2,1)}), bf16[32,16,256]{2,1,0:T(8,128)(2,1)S(1)}, u32[]{:S(2)}, u32[]{:S(2)}) async-start(bf16[32,16,256]{2,1,0:T(8,128)(2,1)} %bitcast.16), calls=%async_computation.4 | async-start | bytes 524288 | tf_op jit(solution)/shard_map/all_to_all | solution.py:546
  99.9 6.1 %shard_map.84.sol_kept = f32[36,32,256]{2,1,0:T(8,128)} custom-call(bf16[64,32,256]{2,1,0:T(8,128)(2,1)} %get-tuple-element.54.local_kept, bf16[1,1920,1920]{2,1,0:T(8,128)(2,1)} %inverse_kept.3, f32[36,32,256]{2,1,0:T(8,128)} %copy-done.2), custom_call_target="tpu_custom_call" | custom-call | flops 1415577600 | bytes 10780672 | tf_op jit(solution)/shard_map/pallas_call | solution.py:26
  106.0 4.4 %all-to-all-done.4 = bf16[32,16,256]{2,1,0:T(8,128)(2,1)S(1)} async-done(((bf16[32,16,256]{2,1,0:T(8,128)(2,1)}), bf16[32,16,256]{2,1,0:T(8,128)(2,1)S(1)}, u32[]{:S(2)}, u32[]{:S(2)}) %all-to-all-start.4) | async-done | bytes 262176 | tf_op jit(solution)/shard_map/all_to_all | solution.py:546
  110.4 1.7 %shard_map.85 = f32[6,6,3,10,256]{4,3,2,1,0:T(8,128)S(1)} custom-call(bf16[4,128,256]{2,1,0:T(8,128)(2,1)S(1)} %bitcast.12, bf16[2048,128]{1,0:T(8,128)(2,1)} %get-tuple-element.43.basis_kept, f32[36,32,256]{2,1,0:T(8,128)} %shard_map.84.sol_kept), custom_call_target="tpu_custom_call" | custom-call | bytes 3072000 | tf_op jit(solution)/shard_map/pallas_call | solution.py:26
  112.1 2.0 %copy.14 = f32[6,6,3,10,256]{4,2,3,1,0:T(4,128)} copy(f32[6,6,3,10,256]{4,3,2,1,0:T(8,128)S(1)} %shard_map.85) | data formatting | bytes 2211840 | tf_op jit(solution)/shard_map/pallas_call | solution.py:26
  (31 shorter events, 4.7 us)
Async XLA Ops:
  0.0 1.8 %copy-start.10 = (f32[6,6,3,10,256]{4,2,3,1,0:T(4,128)S(1)}, f32[6,6,3,10,256]{4,2,3,1,0:T(4,128)}, u32[]{:S(2)}) copy-start(f32[6,6,3,10,256]{4,2,3,1,0:T(4,128)} %param.8) | copy-start | bytes 3317764
  1.8 0.9 copy-start.6
  1.8 0.9 copy-start.7
  2.7 5.3 %copy-start.8 = (bf16[1,1920,128]{2,1,0:T(8,128)(2,1)S(1)}, bf16[1,1920,128]{2,1,0:T(8,128)(2,1)}, u32[]{:S(2)}) copy-start(bf16[1,1920,128]{2,1,0:T(8,128)(2,1)} %basis.1) | copy-start | bytes 1474564
  4.4 20.6 %copy-start = (f32[36,32,256]{2,1,0:T(8,128)}, f32[36,32,256]{2,1,0:T(8,128)S(1)}, u32[]{:S(2)}) copy-start(f32[36,32,256]{2,1,0:T(8,128)S(1)} %get-tuple-element.33.sol.sol_kept) | copy-start | bytes 3538948
  4.4 20.6 %copy-start.1 = (f32[36,32,256]{2,1,0:T(8,128)}, f32[36,32,256]{2,1,0:T(8,128)S(1)}, u32[]{:S(2)}) copy-start(f32[36,32,256]{2,1,0:T(8,128)S(1)} %get-tuple-element.34.base.refs_0_) | copy-start | bytes 3538948
  4.4 10.4 %collective-permute-start = (bf16[2,6,32,256]{3,2,1,0:T(8,128)(2,1)S(1)}, bf16[2,6,32,256]{3,2,1,0:T(8,128)(2,1)S(1)}, u32[]{:S(2)}, u32[]{:S(2)}) collective-permute-start(bf16[2,6,32,256]{3,2,1,0:T(8,128)(2,1)S(1)} %get-tuple-element.35), channel_id=1, source_target_pairs={{0,1},{2,3},{4,5},{6,7},{1,0},{3,2},{5,4},{7,6},{8,9},{10,11},{12,... | collective-permute-start | bytes 589832 | tf_op jit(solution)/shard_map/ppermute | solution.py:63
  7.4 7.4 %collective-permute-start.1 = (bf16[2,6,32,256]{3,2,1,0:T(8,128)(2,1)S(1)}, bf16[2,6,32,256]{3,2,1,0:T(8,128)(2,1)S(1)}, u32[]{:S(2)}, u32[]{:S(2)}) collective-permute-start(bf16[2,6,32,256]{3,2,1,0:T(8,128)(2,1)S(1)} %get-tuple-element.36), channel_id=1, source_target_pairs={{1,2},{3,4},{5,6},{2,1},{4,3},{6,5},{9,10},{11,12},{13,14},{10,9},... | collective-permute-start | bytes 589832 | tf_op jit(solution)/shard_map/ppermute | solution.py:64
  11.7 13.3 %copy-start.5 = (bf16[128,2048]{1,0:T(8,128)(2,1)S(1)}, bf16[128,2048]{1,0:T(8,128)(2,1)}, u32[]{:S(2)}) copy-start(bf16[128,2048]{1,0:T(8,128)(2,1)} %get-tuple-element.41.basis_t) | copy-start | bytes 1572868
  15.6 9.4 %collective-permute-start.2 = (bf16[2,8,32,256]{3,2,1,0:T(8,128)(2,1)}, bf16[2,8,32,256]{3,2,1,0:T(8,128)(2,1)}, u32[]{:S(2)}, u32[]{:S(2)}) collective-permute-start(bf16[2,8,32,256]{3,2,1,0:T(8,128)(2,1)} %get-tuple-element.39), channel_id=1, source_target_pairs={{0,8},{16,24},{8,0},{24,16},{1,9},{17,25},{9,1},{25,17},{2,10},{18... | collective-permute-start | bytes 786440 | tf_op jit(solution)/shard_map/ppermute | solution.py:63
  17.2 7.8 %collective-permute-start.3 = (bf16[2,8,32,256]{3,2,1,0:T(8,128)(2,1)}, bf16[2,8,32,256]{3,2,1,0:T(8,128)(2,1)}, u32[]{:S(2)}, u32[]{:S(2)}) collective-permute-start(bf16[2,8,32,256]{3,2,1,0:T(8,128)(2,1)} %get-tuple-element.40), channel_id=1, source_target_pairs={{8,16},{16,8},{9,17},{17,9},{10,18},{18,10},{11,19},{19,11},{12,20... | collective-permute-start | bytes 786440 | tf_op jit(solution)/shard_map/ppermute | solution.py:64
  18.6 10.5 %all-to-all-start = ((s32[4,1,8]{2,1,0:T(1,128)}), s32[4,1,8]{2,1,0:T(1,128)S(1)}, u32[]{:S(2)}, u32[]{:S(2)}) async-start(s32[4,1,8]{2,1,0:T(1,128)} %bitcast.1), calls=%async_computation | async-start | bytes 4096 | tf_op jit(solution)/shard_map/all_to_all | solution.py:511
  29.1 13.6 %all-to-all-start.1 = ((bf16[8,128,256]{2,1,0:T(8,128)(2,1)}), bf16[8,128,256]{2,1,0:T(8,128)(2,1)S(1)}, u32[]{:S(2)}, u32[]{:S(2)}) async-start(bf16[8,128,256]{2,1,0:T(8,128)(2,1)} %get-tuple-element.42), calls=%async_computation.1 | async-start | bytes 1048576 | tf_op jit(solution)/shard_map/all_to_all | solution.py:538
  33.8 0.9 copy-start.9
  42.6 1.2 %copy-start.3 = (bf16[512,1024]{1,0:T(8,128)(2,1)S(1)}, bf16[512,1024]{1,0:T(8,128)(2,1)}, u32[]{:S(2)}) copy-start(bf16[512,1024]{1,0:T(8,128)(2,1)} %shard_map.75.spread) | copy-start | bytes 3145732
  45.0 15.4 %all-to-all-start.2 = ((bf16[32,16,256]{2,1,0:T(8,128)(2,1)}), bf16[32,16,256]{2,1,0:T(8,128)(2,1)S(1)}, u32[]{:S(2)}, u32[]{:S(2)}) async-start(bf16[32,16,256]{2,1,0:T(8,128)(2,1)} %bitcast.15), calls=%async_computation.2 | async-start | bytes 524288 | tf_op jit(solution)/shard_map/all_to_all | solution.py:546
  62.9 16.8 %copy-start.2 = (f32[36,32,256]{2,1,0:T(8,128)}, f32[36,32,256]{2,1,0:T(8,128)S(1)}, u32[]{:S(2)}) copy-start(f32[36,32,256]{2,1,0:T(8,128)S(1)} %get-tuple-element.47.sol.sol_kept) | copy-start | bytes 3538948
  62.9 7.0 %collective-permute-start.4 = (bf16[2,6,32,256]{3,2,1,0:T(8,128)(2,1)S(1)}, bf16[2,6,32,256]{3,2,1,0:T(8,128)(2,1)S(1)}, u32[]{:S(2)}, u32[]{:S(2)}) collective-permute-start(bf16[2,6,32,256]{3,2,1,0:T(8,128)(2,1)S(1)} %get-tuple-element.49), channel_id=1, source_target_pairs={{0,1},{2,3},{4,5},{6,7},{1,0},{3,2},{5,4},{7,6},{8,9},{10,11},{12,... | collective-permute-start | bytes 589832 | tf_op jit(solution)/shard_map/ppermute | solution.py:63
  63.8 6.1 %collective-permute-start.5 = (bf16[2,6,32,256]{3,2,1,0:T(8,128)(2,1)S(1)}, bf16[2,6,32,256]{3,2,1,0:T(8,128)(2,1)S(1)}, u32[]{:S(2)}, u32[]{:S(2)}) collective-permute-start(bf16[2,6,32,256]{3,2,1,0:T(8,128)(2,1)S(1)} %get-tuple-element.50), channel_id=1, source_target_pairs={{1,2},{3,4},{5,6},{2,1},{4,3},{6,5},{9,10},{11,12},{13,14},{10,9},... | collective-permute-start | bytes 589832 | tf_op jit(solution)/shard_map/ppermute | solution.py:64
  70.0 8.1 %collective-permute-start.6 = (bf16[2,8,32,256]{3,2,1,0:T(8,128)(2,1)S(1)}, bf16[2,8,32,256]{3,2,1,0:T(8,128)(2,1)S(1)}, u32[]{:S(2)}, u32[]{:S(2)}) collective-permute-start(bf16[2,8,32,256]{3,2,1,0:T(8,128)(2,1)S(1)} %get-tuple-element.51), channel_id=1, source_target_pairs={{0,8},{16,24},{8,0},{24,16},{1,9},{17,25},{9,1},{25,17},{2,10},{18... | collective-permute-start | bytes 786440 | tf_op jit(solution)/shard_map/ppermute | solution.py:63
  71.7 6.4 %collective-permute-start.7 = (bf16[2,8,32,256]{3,2,1,0:T(8,128)(2,1)S(1)}, bf16[2,8,32,256]{3,2,1,0:T(8,128)(2,1)S(1)}, u32[]{:S(2)}, u32[]{:S(2)}) collective-permute-start(bf16[2,8,32,256]{3,2,1,0:T(8,128)(2,1)S(1)} %get-tuple-element.52), channel_id=1, source_target_pairs={{8,16},{16,8},{9,17},{17,9},{10,18},{18,10},{11,19},{19,11},{12,20... | collective-permute-start | bytes 786440 | tf_op jit(solution)/shard_map/ppermute | solution.py:64
  79.8 14.0 %copy-start.4 = (bf16[512,1024]{1,0:T(8,128)(2,1)S(1)}, bf16[512,1024]{1,0:T(8,128)(2,1)}, u32[]{:S(2)}) copy-start(bf16[512,1024]{1,0:T(8,128)(2,1)} %shard_map.75.spread) | copy-start | bytes 3145732
  94.9 15.5 %all-to-all-start.4 = ((bf16[32,16,256]{2,1,0:T(8,128)(2,1)}), bf16[32,16,256]{2,1,0:T(8,128)(2,1)S(1)}, u32[]{:S(2)}, u32[]{:S(2)}) async-start(bf16[32,16,256]{2,1,0:T(8,128)(2,1)} %bitcast.16), calls=%async_computation.4 | async-start | bytes 524288 | tf_op jit(solution)/shard_map/all_to_all | solution.py:546

commit v4 on v3

--- a/solution.py
+++ b/solution.py
@@ -47,9 +47,11 @@
     return copy
 
 
-def packing(cells, per_cell, pad):
-    row = lax.broadcasted_iota(jnp.int32, (cells * per_cell, cells * pad), 0)
-    column = lax.broadcasted_iota(jnp.int32, (cells * per_cell, cells * pad), 1)
+def packing(cells, per_cell, pad, turned=False):
+    shape = (cells * per_cell, cells * pad)
+    shape = shape[::-1] if turned else shape
+    row = lax.broadcasted_iota(jnp.int32, shape, 1 if turned else 0)
+    column = lax.broadcasted_iota(jnp.int32, shape, 0 if turned else 1)
     for w in range(1, cells):
         column = column - jnp.where(row >= w * per_cell, pad - per_cell, 0)
     return jnp.where(row == column, 1.0, 0.0).astype(bf16)
@@ -65,6 +67,11 @@
     )
 
 
+def doubled(held, step):
+    count = lax.axis_size("sub")
+    return held + lax.ppermute(held, "sub", [(i, i ^ step) for i in range(count)])
+
+
 def diagonal_of(stiffness, s, q, comps, layers, pad, columns):
     at = lax.broadcasted_iota(jnp.int32, (pad, layers), 0)
     layer = lax.broadcasted_iota(jnp.int32, (pad, layers), 1)
@@ -75,7 +82,7 @@
     return jnp.broadcast_to(column, (pad, columns))
 
 
-def write_base(layers, begin, stiffness, field, base, shape):
+def write_base(layers, begin, stiffness, field, base, shape, only=None):
     cells_s, cells_q, comps, pad, columns = shape
     at = lax.broadcasted_iota(jnp.int32, (pad, columns), 0)
     has_up, has_down = at < comps * layers, at < comps * layers
@@ -83,7 +90,7 @@
         has_up = has_up & (at != c * layers)
         has_down = has_down & (at != c * layers + layers - 1)
     for s in range(cells_s):
-        for q in range(cells_q):
+        for q in only or range(cells_q):
             i = s * cells_q + q
             x = field[i]
             diagonal = diagonal_of(stiffness, s, q, comps, layers, pad, columns)
@@ -113,20 +120,52 @@
             out[1, s] = sol[s * cells_q + q].astype(bf16)
 
 
+def unpack_cell(source, target, i, shape, layers):
+    _, _, comps, pad, columns = shape
+    for c in range(comps):
+        target[i, c * layers : (c + 1) * layers, :] = source[:, c, :]
+    target[i, comps * layers :, :] = jnp.zeros((pad - comps * layers, columns), f32)
+
+
+def open_sides_kernel(
+    shape, layers, start, rhs, stiffness, first, second, raw, raw_rhs, stiff, sol, begin, base, sems
+):
+    cells_s, cells_q = shape[:2]
+    sides = (0, cells_q - 1)
+    near = (0, 1, cells_q - 2, cells_q - 1)
+    copies = [
+        begun(stiffness, stiff, sems.at[0]),
+        begun(start.at[:, pl.ds(0, 2)], raw.at[:, pl.ds(0, 2)], sems.at[1]),
+        begun(start.at[:, pl.ds(cells_q - 2, 2)], raw.at[:, pl.ds(2, 2)], sems.at[2]),
+        begun(rhs.at[:, pl.ds(0, 1)], raw_rhs.at[:, pl.ds(0, 1)], sems.at[3]),
+        begun(rhs.at[:, pl.ds(cells_q - 1, 1)], raw_rhs.at[:, pl.ds(1, 1)], sems.at[4]),
+    ]
+    for copy in copies:
+        copy.wait()
+    for s in range(cells_s):
+        for k, q in enumerate(near):
+            unpack_cell(raw.at[s, k], sol, s * cells_q + q, shape, layers)
+        for k, q in enumerate(sides):
+            unpack_cell(raw_rhs.at[s, k], begin, s * cells_q + q, shape, layers)
+    write_base(layers, begin, stiff, sol, base, shape, sides)
+    write_column_messages(sol, base, first, second, shape)
+
+
 def open_kernel(
-    shape, layers, start, rhs, stiffness, offsets, sol, base, first, second, sent, begin
+    shape, layers, start, rhs, stiffness, offsets, sol, base, sent, raw, raw_rhs, stiff, own, begin, sems
 ):
-    cells_s, cells_q, comps, pad, columns = shape
-    sent[...] = jnp.broadcast_to(offsets[...], sent.shape)
+    cells_s, cells_q = shape[:2]
+    sources, targets = (stiffness, offsets, start, rhs), (stiff, own, raw, raw_rhs)
+    copies = [begun(a, b, sems.at[k]) for k, (a, b) in enumerate(zip(sources, targets))]
+    for copy in copies:
+        copy.wait()
+    group = lax.broadcasted_iota(jnp.int32, sent.shape, 0)
+    sent[...] = jnp.where(group == lax.axis_index("sub"), own[...], 0)
     for s in range(cells_s):
         for q in range(cells_q):
-            i = s * cells_q + q
-            for source, target in ((start, sol), (rhs, begin)):
-                for c in range(comps):
-                    target[i, c * layers : (c + 1) * layers, :] = source[s, q, c]
-                target[i, comps * layers :, :] = jnp.zeros((pad - comps * layers, columns), f32)
-    write_base(layers, begin, stiffness, sol, base, shape)
-    write_column_messages(sol, base, first, second, shape)
+            unpack_cell(raw.at[s, q], sol, s * cells_q + q, shape, layers)
+            unpack_cell(raw_rhs.at[s, q], begin, s * cells_q + q, shape, layers)
+    write_base(layers, begin, stiff, sol, base, shape)
 
 
 def column_sides(first, second):
@@ -310,22 +349,14 @@
     )
 
 
-def coarse_part(shape, arrived, basis_p, coarse):
-    cells_s, cells_q, _, pad, _ = shape
+def coarse_values(arrived):
     chosen = arrived[0].astype(f32)
     for h in range(1, arrived.shape[0]):
         chosen = chosen + arrived[h].astype(f32)
-    chosen = chosen.astype(bf16)
-    chunk = (cells_q + 2) * pad
-    for s in range(cells_s):
-        first = (s + 1) * chunk + pad
-        rows = jnp.dot(
-            basis_p[first : first + cells_q * pad, :], chosen, preferred_element_type=f32
-        )
-        coarse[s * cells_q : (s + 1) * cells_q] = rows.reshape(cells_q, pad, -1)
-
-
-def step_kernel(
+    return chosen.astype(bf16)
+
+
+def step_sides_kernel(
     shape,
     layers,
     arrived,
@@ -333,45 +364,82 @@
     sol_kept,
     base_kept,
     stiffness,
-    new,
-    base,
     first,
     second,
+    coarse,
     basis_p,
-    coarse,
+    stiff,
+    sol,
     begin,
+    base,
     sems,
 ):
-    sources, targets = (basis_kept, sol_kept, base_kept), (basis_p, new, begin)
+    cells_s, cells_q, _, pad, columns = shape
+    sides = (0, cells_q - 1)
+    copies = [begun(basis_kept, basis_p, sems.at[0]), begun(stiffness, stiff, sems.at[1])]
+    for s in range(cells_s):
+        for q in sides:
+            i = s * cells_q + q
+            copies.append(begun(sol_kept.at[i], sol.at[i], sems.at[len(copies)]))
+            copies.append(begun(base_kept.at[i], begin.at[i], sems.at[len(copies)]))
+    chosen = coarse_values(arrived)
+    copies[0].wait()
+    span = cells_q * pad
+    for s in range(cells_s):
+        rows = jnp.dot(
+            basis_p[s * span : (s + 1) * span, :], chosen, preferred_element_type=f32
+        )
+        coarse[s * cells_q : (s + 1) * cells_q] = rows.reshape(cells_q, pad, columns)
+    for copy in copies[1:]:
+        copy.wait()
+    for s in range(cells_s):
+        for q in sides:
+            i = s * cells_q + q
+            sol[i] = sol[i] + coarse[i]
+    write_base(layers, begin, stiff, coarse, base, shape, sides)
+    write_column_messages(sol, base, first, second, shape)
+
+
+def step_kernel(shape, layers, coarse, sol_kept, base_kept, stiffness, new, base, stiff, begin, sems):
+    sources, targets = (stiffness, sol_kept, base_kept), (stiff, new, begin)
     copies = [begun(a, b, sems.at[k]) for k, (a, b) in enumerate(zip(sources, targets))]
-    copies[0].wait()
-    coarse_part(shape, arrived, basis_p, coarse)
-    copies[1].wait()
+    for copy in copies:
+        copy.wait()
     for i in range(new.shape[0]):
         new[i] = new[i] + coarse[i]
-    copies[2].wait()
-    write_base(layers, begin, stiffness, coarse, base, shape)
-    write_column_messages(new, base, first, second, shape)
-
-
-def close_kernel(shape, layers, arrived, basis_kept, sol_kept, out, basis_p, coarse, sol, sems):
-    cells_s, cells_q, comps, _, _ = shape
-    sources, targets = (basis_kept, sol_kept), (basis_p, sol)
-    copies = [begun(a, b, sems.at[k]) for k, (a, b) in enumerate(zip(sources, targets))]
+    write_base(layers, begin, stiff, coarse, base, shape)
+
+
+def close_kernel(
+    shape, layers, arrived, basis_kept, sol_kept, out_kept, basis_p, sol, out, sems
+):
+    cells_s, cells_q, comps, pad, columns = shape
+    span = cells_q * pad
+    copies = [begun(basis_kept, basis_p, sems.at[0])]
+    for s in range(cells_s):
+        part = pl.ds(s * cells_q, cells_q)
+        copies.append(begun(sol_kept.at[part], sol.at[part], sems.at[s + 1]))
+    chosen = coarse_values(arrived)
     copies[0].wait()
-    coarse_part(shape, arrived, basis_p, coarse)
-    copies[1].wait()
-    for s in range(cells_s):
+    results = []
+    for s in range(cells_s):
+        rows = jnp.dot(
+            basis_p[s * span : (s + 1) * span, :], chosen, preferred_element_type=f32
+        )
+        copies[s + 1].wait()
         for q in range(cells_q):
-            i = s * cells_q + q
+            total = sol[s * cells_q + q] + rows[q * pad : (q + 1) * pad]
             for c in range(comps):
-                part = slice(c * layers, (c + 1) * layers)
-                out[s, q, c] = sol[i, part, :] + coarse[i, part, :]
-
-
-def places(offsets, g, j, groups, depth, kgroup, shape):
+                out[s, q, :, c, :] = total[c * layers : (c + 1) * layers]
+        results.append(begun(out.at[s], out_kept.at[s], sems.at[cells_s + 1 + s]))
+    for copy in results:
+        copy.wait()
+
+
+def places(offsets, g, j, groups, depth, kgroup):
     first = offsets[g, j]
     end = kgroup if j == groups - 1 else offsets[g, j + 1]
+    shape = (1, groups * depth)
     at = lax.broadcasted_iota(jnp.int32, shape, 1)
     turn = at
     member = jnp.zeros(shape, jnp.int32)
@@ -384,29 +452,67 @@
     return first, place, place < end - first
 
 
-def basis_kernel(dims, offsets, basis, basis_t, basis_p):
-    wide, per_cell, pad, groups, depth, kgroup = dims
+def ordering(dims, offsets):
+    groups, depth, kgroup, count = dims
+    member = lax.axis_index(GROUP_AXES)
+    wanted = jnp.full((1, groups * depth), -1, jnp.int32)
+    for j in range(groups):
+        _, place, valid = places(offsets, 0, j, groups, depth, kgroup)
+        wanted = jnp.where(valid & (member == j), place, wanted)
+    row = lax.broadcasted_iota(jnp.int32, (count, groups * depth), 0)
+    return jnp.where(row == wanted, 1.0, 0.0).astype(bf16)
+
+
+def basis_turned_kernel(cell, dims, offsets, basis_kept, basis_t, kept, basis, sems):
+    wide, per_cell, pad = cell
     span, chunk = wide * per_cell, wide * pad
+    copy = begun(basis_kept.at[0], basis, sems.at[0])
     pack = packing(wide, per_cell, pad)
-    member = lax.axis_index(GROUP_AXES)
-    shape = (basis.shape[2], groups * depth)
-    row = lax.broadcasted_iota(jnp.int32, shape, 0)
-    order = jnp.zeros(shape, f32)
-    for j in range(groups):
-        _, place, valid = places(offsets, 0, j, groups, depth, kgroup, shape)
-        order = order + jnp.where((row == place) & valid & (member == j), 1.0, 0.0)
-    order = order.astype(bf16)
-    for s in range(basis.shape[1] // span):
+    order = ordering(dims, offsets)
+    copy.wait()
+    for s in range(basis.shape[0] // span):
         ordered = jnp.dot(
-            basis[0, s * span : (s + 1) * span, :], order, preferred_element_type=f32
+            basis[s * span : (s + 1) * span, :], order, preferred_element_type=f32
         ).astype(bf16)
-        part = slice(s * chunk, (s + 1) * chunk)
-        basis_t[:, part] = lax.dot_general(
+        basis_t[:, s * chunk : (s + 1) * chunk] = lax.dot_general(
             ordered, pack, (((0,), (0,)), ((), ())), preferred_element_type=f32
         ).astype(bf16)
-        basis_p[part, :] = lax.dot_general(
-            pack, ordered, (((0,), (0,)), ((), ())), preferred_element_type=f32
+    begun(basis_t, kept, sems.at[1]).wait()
+
+
+def basis_own_kernel(cell, dims, offsets, basis_kept, own_kept, basis, basis_p, sems):
+    wide, per_cell, pad = cell
+    span = wide * per_cell
+    size = (wide - 2) * pad
+    copy = begun(basis_kept.at[0], basis, sems.at[0])
+    pack = packing(wide, per_cell, pad, True)[pad : pad + size]
+    order = ordering(dims, offsets)
+    copy.wait()
+    for s in range(basis_p.shape[0] // size):
+        ordered = jnp.dot(
+            basis[(s + 1) * span : (s + 2) * span, :], order, preferred_element_type=f32
         ).astype(bf16)
+        basis_p[s * size : (s + 1) * size, :] = jnp.dot(
+            pack, ordered, preferred_element_type=f32
+        ).astype(bf16)
+    begun(basis_p, own_kept, sems.at[1]).wait()
+
+
+def ordered_basis(body, cell, dims, offsets, basis, shape, both):
+    held = [] if both else [pltpu.VMEM(shape, bf16)]
+    return pl.pallas_call(
+        functools.partial(body, cell, dims),
+        out_shape=([jax.ShapeDtypeStruct(shape, bf16)] if both else []) + [pltpu.HBM(shape, bf16)],
+        in_specs=[pl.BlockSpec(memory_space=pltpu.SMEM), HBM],
+        out_specs=([VMEM] if both else []) + [HBM],
+        scratch_shapes=[pltpu.VMEM(basis.shape[1:], bf16), *held, pltpu.SemaphoreType.DMA((2,))],
+        compiler_params=pltpu.CompilerParams(vmem_limit_bytes=12 << 20),
+        cost_estimate=pl.CostEstimate(
+            flops=4 * shape[0] * shape[1] * cell[0] * cell[2],
+            bytes_accessed=4 * basis.size,
+            transcendentals=0,
+        ),
+    )(offsets, pltpu.with_memory_space_constraint(basis, pltpu.HBM))
 
 
 def spread_kernel(dims, every, inverse, out, columns):
@@ -417,12 +523,12 @@
     @pl.when(g == 0)
     def _():
         own = lax.axis_index("sub")
-        shape = (kgroup, groups * depth)
-        slot = lax.broadcasted_iota(jnp.int32, shape, 0)
+        slot = lax.broadcasted_iota(jnp.int32, (kgroup, groups * depth), 0)
         for j in range(groups):
-            first, place, valid = places(every, own, j, groups, depth, kgroup, shape)
+            first, place, valid = places(every, own, j, groups, depth, kgroup)
+            wanted = jnp.where(valid, place + first, -1)
             columns[:, j * groups * depth : (j + 1) * groups * depth] = jnp.where(
-                (slot == place + first) & valid, 1.0, 0.0
+                slot == wanted, 1.0, 0.0
             ).astype(bf16)
 
     rows = inverse.shape[1]
@@ -482,48 +588,66 @@
 
     rows = (cells_s + 2) * wide * pad
 
-    solution, base, first, second, sent = call(
+    start_cells, rhs_cells = (x.transpose(0, 1, 3, 2, 4) for x in (start, rhs))
+    tail = (layers, comps, columns)
+    first, second = call(
+        functools.partial(open_sides_kernel, shape, layers),
+        (start_cells, rhs_cells, stiffness),
+        (column_message, column_message),
+        scratch=(
+            pltpu.VMEM((cells_s, 4) + tail, f32),
+            pltpu.VMEM((cells_s, 2) + tail, f32),
+            pltpu.VMEM(stiffness.shape, f32),
+            pltpu.VMEM(field.shape, f32),
+            pltpu.VMEM(field.shape, f32),
+            pltpu.VMEM(field.shape, f32),
+            pltpu.SemaphoreType.DMA((5,)),
+        ),
+        held=(0, 1, 2),
+    )
+    solution, base, sent = call(
         functools.partial(open_kernel, shape, layers),
-        (start, rhs, stiffness, offsets),
-        (
-            field,
-            field,
-            column_message,
-            column_message,
-            jax.ShapeDtypeStruct((n_sub, groups), jnp.int32),
+        (start_cells, rhs_cells, stiffness, offsets),
+        (field, field, jax.ShapeDtypeStruct((n_sub, groups), jnp.int32)),
+        scratch=(
+            pltpu.VMEM((cells_s, cells_q) + tail, f32),
+            pltpu.VMEM((cells_s, cells_q) + tail, f32),
+            pltpu.VMEM(stiffness.shape, f32),
+            pltpu.VMEM(offsets.shape, jnp.int32),
+            pltpu.VMEM(field.shape, f32),
+            pltpu.SemaphoreType.DMA((4,)),
         ),
-        scratch=(pltpu.VMEM(field.shape, f32),),
+        held=(0, 1, 2, 3),
     )
-    basis_t, basis_p = pl.pallas_call(
-        functools.partial(basis_kernel, (wide, per_cell, pad, groups, depth, kgroup)),
-        out_shape=(pltpu.HBM((coarse, rows), bf16), pltpu.HBM((rows, coarse), bf16)),
-        in_specs=[pl.BlockSpec(memory_space=pltpu.SMEM), VMEM],
-        out_specs=(
-            pl.BlockSpec((coarse, rows), lambda: (0, 0)),
-            pl.BlockSpec((rows, coarse), lambda: (0, 0)),
-        ),
-        compiler_params=pltpu.CompilerParams(vmem_limit_bytes=12 << 20),
-        cost_estimate=pl.CostEstimate(
-            flops=6 * rows * coarse * wide * pad, bytes_accessed=6 * basis.size, transcendentals=0
-        ),
-    )(offsets, basis)
-    sent, _ = lax.optimization_barrier((sent, basis_t))
-    every = lax.all_to_all(sent, "sub", 0, 0, tiled=True)
-    spread = spread_inverse(every, coarse_inverse, depth)
+    cell = (wide, per_cell, pad)
+    dims = (groups, depth, kgroup, basis.shape[2])
+    basis_t = basis_kept = basis_p = every = spread = None
 
     for sweep in range(ITERS):
+        last = sweep == ITERS - 1
         first_q, second_q = swap(first, second, GROUP_AXES)
         if sweep == 0:
-            first_q, second_q, basis_t = lax.optimization_barrier((first_q, second_q, basis_t))
+            every = sent
+            rounds = (n_sub - 1).bit_length()
+            for power in range(rounds - 1):
+                every = doubled(every, 1 << power)
+            first_q, second_q, every = lax.optimization_barrier((first_q, second_q, every))
         first, second = call(
             functools.partial(row_kernel, shape),
             (solution, base, first_q, second_q),
             (row_message, row_message),
         )
         first_s, second_s = swap(first, second, "sub")
+        if sweep == 0:
+            later, _ = lax.optimization_barrier((basis, first))
+            basis_t, basis_kept = ordered_basis(
+                basis_turned_kernel, cell, dims, offsets, later, (coarse, rows), True
+            )
+            every = doubled(every, 1 << (rounds - 1))
+            first_s, second_s, every = lax.optimization_barrier((first_s, second_s, every))
         message, local = call(
             functools.partial(window_kernel, shape),
-            (solution, base, first_q, second_q, first_s, second_s, basis_t),
+            (solution, base, first_q, second_q, first_s, second_s, basis_t if sweep == 0 else basis_kept),
             (
                 pltpu.HBM((groups, coarse, columns), bf16),
                 pltpu.HBM(((cells_s + 2) * wide, pad, columns), bf16),
@@ -535,48 +659,68 @@
             ),
             flops=2 * rows * coarse * columns,
         )
+        if sweep == 0:
+            later, _ = lax.optimization_barrier((basis, message))
+            (basis_p,) = ordered_basis(
+                basis_own_kernel, cell, dims, offsets, later, (cells * pad, coarse), False
+            )
+            waited, basis_p = lax.optimization_barrier((every, basis_p))
+            spread = spread_inverse(waited, coarse_inverse, depth)
         gathered = lax.all_to_all(message, GROUP_AXES, 0, 0, tiled=True)
+        held = pltpu.VMEM((spread.shape[0], columns), bf16)
         (terms,) = call(
             terms_kernel,
             (spread, gathered.reshape(-1, columns)),
-            (pltpu.HBM((spread.shape[0], columns), bf16),),
-            scratch=(pltpu.VMEM((spread.shape[0], columns), bf16), pltpu.SemaphoreType.DMA),
+            (pltpu.HBM(held.shape, bf16),),
+            scratch=(held, pltpu.SemaphoreType.DMA),
             flops=2 * spread.size * columns,
         )
         arrived = lax.all_to_all(
             terms.reshape(n_sub * groups, depth, columns), ALL_AXES, 0, 0, tiled=True
         ).reshape(n_sub, coarse, columns)
-        last = sweep == ITERS - 1
         kept = fine_product(
             shape, layers, local, sub_inverse, solution, base, stiffness, last
         )
         if last:
-            (solution,) = call(
+            (out,) = call(
                 functools.partial(close_kernel, shape, layers),
                 (arrived, basis_p, *kept),
-                (jax.ShapeDtypeStruct(rhs.shape, f32),),
+                (pltpu.HBM((cells_s, cells_q) + tail, f32),),
                 scratch=(
-                    pltpu.VMEM((rows, coarse), bf16),
+                    pltpu.VMEM(basis_p.shape, bf16),
                     pltpu.VMEM(field.shape, f32),
-                    pltpu.VMEM(field.shape, f32),
-                    pltpu.SemaphoreType.DMA((2,)),
+                    pltpu.VMEM((cells_s, cells_q) + tail, f32),
+                    pltpu.SemaphoreType.DMA((2 * cells_s + 1,)),
                 ),
                 held=(1, 2),
             )
         else:
-            solution, base, first, second = call(
+            first, second, change = call(
+                functools.partial(step_sides_kernel, shape, layers),
+                (arrived, basis_p, *kept, stiffness),
+                (column_message, column_message, field),
+                scratch=(
+                    pltpu.VMEM(basis_p.shape, bf16),
+                    pltpu.VMEM(stiffness.shape, f32),
+                    pltpu.VMEM(field.shape, f32),
+                    pltpu.VMEM(field.shape, f32),
+                    pltpu.VMEM(field.shape, f32),
+                    pltpu.SemaphoreType.DMA((4 * cells_s + 2,)),
+                ),
+                held=(1, 2, 3, 4),
+            )
+            solution, base = call(
                 functools.partial(step_kernel, shape, layers),
-                (arrived, basis_p, *kept, stiffness),
-                (field, field, column_message, column_message),
+                (change, *kept, stiffness),
+                (field, field),
                 scratch=(
-                    pltpu.VMEM((rows, coarse), bf16),
-                    pltpu.VMEM(field.shape, f32),
+                    pltpu.VMEM(stiffness.shape, f32),
                     pltpu.VMEM(field.shape, f32),
                     pltpu.SemaphoreType.DMA((3,)),
                 ),
                 held=(1, 2, 3),
             )
-    return solution
+    return out.transpose(0, 1, 3, 2, 4)
 
 
 def solution(mesh):

time: 115 us -> 110 us (0.957)
  Pallas kernels: 33.8 us -> 43.4 us
  waiting for transfers between devices: 29.5 us -> 22.9 us
  local copies, waits for them, and re-layouts: 6.92 us -> 1.27 us
  starting transfers between devices: 29.8 us -> 26.8 us
    ppermute x4, waiting for transfers between devices: 15.7 us -> 8.81 us  [swap(): lax.ppermute(first, axis, even + [(b, a) for a, b in even])]
    pallas_call x11 -> x13, Pallas kernels: 26.5 us -> 31.6 us  [call(): pl.pallas_call(body, out_shape=tuple(outs), in_specs=[HBM if i in held el...]
    all_to_all x1 -> x0, starting transfers between devices: 4.97 us -> none  [shards(): every = lax.all_to_all(sent, 'sub', 0, 0, tiled=True)]
    pallas_call x1 -> x2, Pallas kernels: 3.69 us -> 8.16 us  [ordered_basis(): pl.pallas_call(functools.partial(body, cell, dims), out_shape=([jax.Shape...]
    ppermute x0 -> x2, waiting for transfers between devices: none -> 4.3 us  [doubled(): lax.ppermute(held, 'sub', [(i, i ^ step) for i in range(count)])]
    unnamed x24 -> x18, local copies, waits for them, and re-layouts: 4.88 us -> 1.27 us
    ppermute x4, starting transfers between devices: 7.06 us -> 9.99 us  [swap(): lax.ppermute(first, axis, even + [(b, a) for a, b in even])]
    all_to_all x1, waiting for transfers between devices: 4.3 us -> 1.58 us  [shards(): gathered = lax.all_to_all(message, GROUP_AXES, 0, 0, tiled=True)]
  transfers between devices with their start and end apart: 12 -> 13, of which waited for: 8 -> 8; matrix products, arithmetic and copies ran while one was open for 0% -> 0% of each run, Pallas kernels for 20% -> 28%
where the time goes in v4:
time: 110 us; the launch traced here: 109 us
  Pallas kernels  43.4 us (39%)
  starting transfers between devices  26.8 us (24%)
  waiting for transfers between devices  22.9 us (21%)
  blocking collectives  14.2 us (13%)
  local copies, waits for them, and re-layouts  1.27 us (1%)
    pallas_call x13, Pallas kernels, call(): pl.pallas_call(body, out_shape=tuple(outs), in_specs=[HBM if i in held el...  31.6 us
    all_to_all x1, blocking collectives, shards(): gathered = lax.all_to_all(message, GROUP_AXES, 0, 0, tiled=True)  14.2 us
    ppermute x4, starting transfers between devices, swap(): lax.ppermute(first, axis, even + [(b, a) for a, b in even])  9.99 us
    ppermute x4, waiting for transfers between devices, swap(): lax.ppermute(first, axis, even + [(b, a) for a, b in even])  8.81 us
    all_to_all x2, starting transfers between devices, shards(): lax.all_to_all(terms.reshape(n_sub * groups, depth, columns), ALL_AXES, 0...  8.64 us
    all_to_all x2, waiting for transfers between devices, shards(): lax.all_to_all(terms.reshape(n_sub * groups, depth, columns), ALL_AXES, 0...  8.25 us
    pallas_call x2, Pallas kernels, ordered_basis(): pl.pallas_call(functools.partial(body, cell, dims), out_shape=([jax.Shape...  8.16 us
    ppermute x2, waiting for transfers between devices, doubled(): lax.ppermute(held, 'sub', [(i, i ^ step) for i in range(count)])  4.3 us
  transfers between devices with their start and end apart: 13, of which 8 were waited for; matrix products, arithmetic and copies ran while one was open for 0% of the time, Pallas kernels for 28%

profile of v4, /device:TPU:0, one launch (start us, length us, event | category | flops | bytes accessed | tf_op | source)
XLA Modules:
  0.0 109.0 jit_solution(4117040390701024404)
XLA Ops:
  0.0 2.0 %shard_map.74 = (bf16[2,6,32,256]{3,2,1,0:T(8,128)(2,1)S(1)}, bf16[2,6,32,256]{3,2,1,0:T(8,128)(2,1)S(1)}) custom-call(f32[6,6,10,3,256]{4,3,2,1,0:T(4,128)} %bitcast.13, f32[6,6,10,3,256]{4,3,2,1,0:T(4,128)} %bitcast.15, f32[6,6,3,10]{3,2,1,0:T(4,128)} %stiffness.7), custom_call_target="tpu_custom_call" | custom-call | bytes 2609376 | tf_op jit(solution)/shard_map/pallas_call | solution.py:26
  2.0 3.0 %collective-permute-start = (bf16[2,6,32,256]{3,2,1,0:T(8,128)(2,1)S(1)}, bf16[2,6,32,256]{3,2,1,0:T(8,128)(2,1)S(1)}, u32[]{:S(2)}, u32[]{:S(2)}) collective-permute-start(bf16[2,6,32,256]{3,2,1,0:T(8,128)(2,1)S(1)} %get-tuple-element.39), channel_id=1, source_target_pairs={{0,1},{2,3},{4,5},{6,7},{1,0},{3,2},{5,4},{7,6},{8,9},{10,11},{12,... | collective-permute-start | bytes 589832 | tf_op jit(solution)/shard_map/ppermute | solution.py:65
  5.7 3.5 %shard_map.73 = (f32[36,32,256]{2,1,0:T(8,128)S(1)}, f32[36,32,256]{2,1,0:T(8,128)S(1)}, s32[4,8]{1,0:T(4,128)S(1)}) custom-call(f32[6,6,10,3,256]{4,3,2,1,0:T(4,128)} %bitcast.14, f32[6,6,10,3,256]{4,3,2,1,0:T(4,128)} %bitcast.16, f32[6,6,3,10]{3,2,1,0:T(4,128)} %stiffness.7, s32[1,8]{1,0:T(1,128)} %offsets.5), custom_call_target="tpu_custom_call" | custom-call | bytes 4575616 | tf_op jit(solution)/shard_map/pallas_call | solution.py:26
  9.2 1.6 %collective-permute-start.2 = (s32[4,8]{1,0:T(4,128)S(1)}, s32[4,8]{1,0:T(4,128)S(1)}, u32[]{:S(2)}, u32[]{:S(2)}) collective-permute-start(s32[4,8]{1,0:T(4,128)S(1)} %get-tuple-element.41), channel_id=1, source_target_pairs={{0,8},{8,0},{16,24},{24,16},{1,9},{9,1},{17,25},{25,17},{2,10},{10... | collective-permute-start | bytes 392 | tf_op jit(solution)/shard_map/ppermute | solution.py:72
  10.9 2.0 %collective-permute-done.2 = s32[4,8]{1,0:T(4,128)S(1)} collective-permute-done((s32[4,8]{1,0:T(4,128)S(1)}, s32[4,8]{1,0:T(4,128)S(1)}, u32[]{:S(2)}, u32[]{:S(2)}) %collective-permute-start.2) | collective-permute-done | bytes 160 | tf_op jit(solution)/shard_map/ppermute | solution.py:72
  13.0 0.7 collective-permute-start.4
  13.7 4.4 %collective-permute-start.3 = (bf16[2,8,32,256]{3,2,1,0:T(8,128)(2,1)S(1)}, bf16[2,8,32,256]{3,2,1,0:T(8,128)(2,1)S(1)}, u32[]{:S(2)}, u32[]{:S(2)}) collective-permute-start(bf16[2,8,32,256]{3,2,1,0:T(8,128)(2,1)S(1)} %get-tuple-element.44), channel_id=1, source_target_pairs={{0,8},{16,24},{8,0},{24,16},{1,9},{17,25},{9,1},{25,17},{2,10},{18... | collective-permute-start | bytes 786440 | tf_op jit(solution)/shard_map/ppermute | solution.py:65
  18.1 4.5 %shard_map.76 = (bf16[128,2048]{1,0:T(8,128)(2,1)S(1)}, bf16[128,2048]{1,0:T(8,128)(2,1)}) custom-call(s32[1,8]{1,0:T(1,128)S(1)} %copy-done.7, bf16[1,1920,128]{2,1,0:T(8,128)(2,1)} %basis_kept.1), custom_call_target="tpu_custom_call" | custom-call | flops 268435456 | bytes 983040 | tf_op jit(solution)/shard_map/pallas_call | solution.py:503
  22.7 2.3 %collective-permute-done.5 = s32[4,8]{1,0:T(4,128)S(1)} collective-permute-done((s32[4,8]{1,0:T(4,128)S(1)}, s32[4,8]{1,0:T(4,128)S(1)}, u32[]{:S(2)}, u32[]{:S(2)}) %collective-permute-start.5) | collective-permute-done | bytes 160 | tf_op jit(solution)/shard_map/ppermute | solution.py:72
  25.1 1.6 %shard_map.77 = (bf16[8,128,256]{2,1,0:T(8,128)(2,1)}, bf16[64,32,256]{2,1,0:T(8,128)(2,1)}) custom-call(f32[36,32,256]{2,1,0:T(8,128)S(1)} %get-tuple-element.37.sol.sol_kept, f32[36,32,256]{2,1,0:T(8,128)S(1)} %get-tuple-element.38.base.refs_0_, bf16[2,6,32,256]{3,2,1,0:T(8,128)(2,1)S(1)} %collective-permute-done.first_in.first_q, ...), custom_call_target="tpu_custom_call" | custom-call | flops 134217728 | bytes 5373952 | tf_op jit(solution)/shard_map/pallas_call | solution.py:26
  26.7 3.9 %all-to-all-start = ((bf16[8,128,256]{2,1,0:T(8,128)(2,1)}), bf16[8,128,256]{2,1,0:T(8,128)(2,1)S(1)}, u32[]{:S(2)}, u32[]{:S(2)}) async-start(bf16[8,128,256]{2,1,0:T(8,128)(2,1)} %get-tuple-element.52), calls=%async_computation | async-start | bytes 1048576 | tf_op jit(solution)/shard_map/all_to_all | solution.py:669
  30.6 3.6 %shard_map.78.basis_kept = bf16[1152,128]{1,0:T(8,128)(2,1)} custom-call(s32[1,8]{1,0:T(1,128)S(1)} %copy-done.7, bf16[1,1920,128]{2,1,0:T(8,128)(2,1)} %basis_kept.1), custom_call_target="tpu_custom_call" | custom-call | flops 150994944 | bytes 983040 | tf_op jit(solution)/shard_map/pallas_call | solution.py:503
  34.2 3.6 %shard_map.79.spread = bf16[512,1024]{1,0:T(8,128)(2,1)} custom-call(s32[4,8]{1,0:T(4,128)S(1)} %add.7.every, bf16[4,64,512]{2,1,0:T(8,128)(2,1)S(1)} %copy-done.8), custom_call_target="tpu_custom_call" | custom-call | flops 536870912 | bytes 2097152 | tf_op jit(solution)/shard_map/pallas_call | solution.py:554
  37.9 1.6 %all-to-all-done = bf16[8,128,256]{2,1,0:T(8,128)(2,1)S(1)} async-done(((bf16[8,128,256]{2,1,0:T(8,128)(2,1)}), bf16[8,128,256]{2,1,0:T(8,128)(2,1)S(1)}, u32[]{:S(2)}, u32[]{:S(2)}) %all-to-all-start) | async-done | bytes 524320 | tf_op jit(solution)/shard_map/all_to_all | solution.py:669
  39.5 1.2 %copy-done.3 = bf16[512,1024]{1,0:T(8,128)(2,1)S(1)} copy-done((bf16[512,1024]{1,0:T(8,128)(2,1)S(1)}, bf16[512,1024]{1,0:T(8,128)(2,1)}, u32[]{:S(2)}) %copy-start.3) | copy-done | bytes 1048600
  40.7 1.2 %shard_map.80 = bf16[512,256]{1,0:T(8,128)(2,1)} custom-call(bf16[512,1024]{1,0:T(8,128)(2,1)S(1)} %copy-done.3, bf16[1024,256]{1,0:T(8,128)(2,1)S(1)} %bitcast.9), custom_call_target="tpu_custom_call" | custom-call | flops 268435456 | bytes 1835008 | tf_op jit(solution)/shard_map/pallas_call | solution.py:26
  41.8 3.9 %all-to-all-start.1 = ((bf16[32,16,256]{2,1,0:T(8,128)(2,1)}), bf16[32,16,256]{2,1,0:T(8,128)(2,1)S(1)}, u32[]{:S(2)}, u32[]{:S(2)}) async-start(bf16[32,16,256]{2,1,0:T(8,128)(2,1)} %bitcast.17), calls=%async_computation.1 | async-start | bytes 524288 | tf_op jit(solution)/shard_map/all_to_all | solution.py:678
  45.8 7.0 %shard_map.81 = (f32[36,32,256]{2,1,0:T(8,128)}, f32[36,32,256]{2,1,0:T(8,128)}) custom-call(bf16[64,32,256]{2,1,0:T(8,128)(2,1)} %get-tuple-element.56.local_kept, bf16[1,1920,1920]{2,1,0:T(8,128)(2,1)} %inverse_kept.3, f32[36,32,256]{2,1,0:T(8,128)} %copy-done, f32[36,32,256]{2,1,0:T(8,128)} %copy-done.1, f32[6,6,3,10]{3,2,1,0:T(4,128)S(1)} %copy-done.5), custom_call_target="tpu_custom_call" | custom-call | flops 1415577600 | bytes 13144288 | tf_op jit(solution)/shard_map/pallas_call | solution.py:26
  52.9 3.6 %all-to-all-done.1 = bf16[32,16,256]{2,1,0:T(8,128)(2,1)S(1)} async-done(((bf16[32,16,256]{2,1,0:T(8,128)(2,1)}), bf16[32,16,256]{2,1,0:T(8,128)(2,1)S(1)}, u32[]{:S(2)}, u32[]{:S(2)}) %all-to-all-start.1) | async-done | bytes 262176 | tf_op jit(solution)/shard_map/all_to_all | solution.py:678
  56.5 1.9 %shard_map.82 = (bf16[2,6,32,256]{3,2,1,0:T(8,128)(2,1)S(1)}, bf16[2,6,32,256]{3,2,1,0:T(8,128)(2,1)S(1)}, f32[36,32,256]{2,1,0:T(8,128)S(1)}) custom-call(bf16[4,128,256]{2,1,0:T(8,128)(2,1)S(1)} %bitcast.11, bf16[1152,128]{1,0:T(8,128)(2,1)} %shard_map.78.basis_kept, f32[36,32,256]{2,1,0:T(8,128)} %get-tuple-element.57.sol_kept, ...), custom_call_target="tpu_custom_call" | custom-call | bytes 4493536 | tf_op jit(solution)/shard_map/pallas_call | solution.py:26
  58.4 0.9 collective-permute-start.6
  59.9 2.5 %shard_map.83 = (f32[36,32,256]{2,1,0:T(8,128)S(1)}, f32[36,32,256]{2,1,0:T(8,128)S(1)}) custom-call(f32[36,32,256]{2,1,0:T(8,128)S(1)} %get-tuple-element.59.coarse, f32[36,32,256]{2,1,0:T(8,128)} %get-tuple-element.57.sol_kept, f32[36,32,256]{2,1,0:T(8,128)} %get-tuple-element.58.base_kept, f32[6,6,3,10]{3,2,1,0:T(4,128)} %stiffness.7), custom_call_target="tpu_custom_call" | custom-call | bytes 5902560 | tf_op jit(solution)/shard_map/pallas_call | solution.py:26
  62.4 3.0 %collective-permute-done.6.first_in.first_q = bf16[2,6,32,256]{3,2,1,0:T(8,128)(2,1)S(1)} collective-permute-done((bf16[2,6,32,256]{3,2,1,0:T(8,128)(2,1)S(1)}, bf16[2,6,32,256]{3,2,1,0:T(8,128)(2,1)S(1)}, u32[]{:S(2)}, u32[]{:S(2)}) %collective-permute-start.6) | collective-permute-done | bytes 196640 | tf_op jit(solution)/shard_map/ppermute | solution.py:65
  65.4 1.7 %collective-permute-start.8 = (bf16[2,8,32,256]{3,2,1,0:T(8,128)(2,1)S(1)}, bf16[2,8,32,256]{3,2,1,0:T(8,128)(2,1)S(1)}, u32[]{:S(2)}, u32[]{:S(2)}) collective-permute-start(bf16[2,8,32,256]{3,2,1,0:T(8,128)(2,1)S(1)} %get-tuple-element.64), channel_id=1, source_target_pairs={{0,8},{16,24},{8,0},{24,16},{1,9},{17,25},{9,1},{25,17},{2,10},{18... | collective-permute-start | bytes 786440 | tf_op jit(solution)/shard_map/ppermute | solution.py:65
  67.8 5.8 %collective-permute-done.8.first_s = bf16[2,8,32,256]{3,2,1,0:T(8,128)(2,1)S(1)} collective-permute-done((bf16[2,8,32,256]{3,2,1,0:T(8,128)(2,1)S(1)}, bf16[2,8,32,256]{3,2,1,0:T(8,128)(2,1)S(1)}, u32[]{:S(2)}, u32[]{:S(2)}) %collective-permute-start.8) | collective-permute-done | bytes 262176 | tf_op jit(solution)/shard_map/ppermute | solution.py:65
  73.5 1.7 %shard_map.85 = (bf16[8,128,256]{2,1,0:T(8,128)(2,1)}, bf16[64,32,256]{2,1,0:T(8,128)(2,1)}) custom-call(f32[36,32,256]{2,1,0:T(8,128)S(1)} %get-tuple-element.60.sol.sol_kept, f32[36,32,256]{2,1,0:T(8,128)S(1)} %get-tuple-element.61.base, bf16[2,6,32,256]{3,2,1,0:T(8,128)(2,1)S(1)} %collective-permute-done.6.first_in.first_q, ...), custom_call_target="tpu_custom_call" | custom-call | flops 134217728 | bytes 5373952 | tf_op jit(solution)/shard_map/pallas_call | solution.py:26
  75.2 14.2 %all_to_all.20 = bf16[8,128,256]{2,1,0:T(8,128)(2,1)S(1)} all-to-all(bf16[8,128,256]{2,1,0:T(8,128)(2,1)} %get-tuple-element.67), channel_id=1, replica_groups=mesh['sub'=4,'crow'=4,'ccol'=2] {'crow','ccol'}, dimensions={0} | all-to-all | bytes 1048576 | tf_op jit(solution)/shard_map/all_to_all | solution.py:669
  89.4 1.1 %shard_map.86 = bf16[512,256]{1,0:T(8,128)(2,1)} custom-call(bf16[512,1024]{1,0:T(8,128)(2,1)S(1)} %copy-done.4, bf16[1024,256]{1,0:T(8,128)(2,1)S(1)} %bitcast.10), custom_call_target="tpu_custom_call" | custom-call | flops 268435456 | bytes 1835008 | tf_op jit(solution)/shard_map/pallas_call | solution.py:26
  90.5 4.7 %all-to-all-start.3 = ((bf16[32,16,256]{2,1,0:T(8,128)(2,1)}), bf16[32,16,256]{2,1,0:T(8,128)(2,1)S(1)}, u32[]{:S(2)}, u32[]{:S(2)}) async-start(bf16[32,16,256]{2,1,0:T(8,128)(2,1)} %bitcast.18), calls=%async_computation.3 | async-start | bytes 524288 | tf_op jit(solution)/shard_map/all_to_all | solution.py:678
  95.2 6.1 %shard_map.87.sol_kept = f32[36,32,256]{2,1,0:T(8,128)} custom-call(bf16[64,32,256]{2,1,0:T(8,128)(2,1)} %get-tuple-element.68.local_kept, bf16[1,1920,1920]{2,1,0:T(8,128)(2,1)} %inverse_kept.3, f32[36,32,256]{2,1,0:T(8,128)} %copy-done.2), custom_call_target="tpu_custom_call" | custom-call | flops 1415577600 | bytes 10780672 | tf_op jit(solution)/shard_map/pallas_call | solution.py:26
  101.3 4.6 %all-to-all-done.3 = bf16[32,16,256]{2,1,0:T(8,128)(2,1)S(1)} async-done(((bf16[32,16,256]{2,1,0:T(8,128)(2,1)}), bf16[32,16,256]{2,1,0:T(8,128)(2,1)S(1)}, u32[]{:S(2)}, u32[]{:S(2)}) %all-to-all-start.3) | async-done | bytes 262176 | tf_op jit(solution)/shard_map/all_to_all | solution.py:678
  105.9 2.9 %shard_map.88 = f32[6,6,10,3,256]{4,3,2,1,0:T(4,128)} custom-call(bf16[4,128,256]{2,1,0:T(8,128)(2,1)S(1)} %bitcast.12, bf16[1152,128]{1,0:T(8,128)(2,1)} %shard_map.78.basis_kept, f32[36,32,256]{2,1,0:T(8,128)} %shard_map.87.sol_kept), custom_call_target="tpu_custom_call" | custom-call | bytes 2842624 | tf_op jit(solution)/shard_map/pallas_call | solution.py:26
  (31 shorter events, 2.3 us)
Async XLA Ops:
  2.0 10.8 %collective-permute-start = (bf16[2,6,32,256]{3,2,1,0:T(8,128)(2,1)S(1)}, bf16[2,6,32,256]{3,2,1,0:T(8,128)(2,1)S(1)}, u32[]{:S(2)}, u32[]{:S(2)}) collective-permute-start(bf16[2,6,32,256]{3,2,1,0:T(8,128)(2,1)S(1)} %get-tuple-element.39), channel_id=1, source_target_pairs={{0,1},{2,3},{4,5},{6,7},{1,0},{3,2},{5,4},{7,6},{8,9},{10,11},{12,... | collective-permute-start | bytes 589832 | tf_op jit(solution)/shard_map/ppermute | solution.py:65
  5.1 7.8 %collective-permute-start.1 = (bf16[2,6,32,256]{3,2,1,0:T(8,128)(2,1)S(1)}, bf16[2,6,32,256]{3,2,1,0:T(8,128)(2,1)S(1)}, u32[]{:S(2)}, u32[]{:S(2)}) collective-permute-start(bf16[2,6,32,256]{3,2,1,0:T(8,128)(2,1)S(1)} %get-tuple-element.40), channel_id=1, source_target_pairs={{1,2},{3,4},{5,6},{2,1},{4,3},{6,5},{9,10},{11,12},{13,14},{10,9},... | collective-permute-start | bytes 589832 | tf_op jit(solution)/shard_map/ppermute | solution.py:66
  9.2 15.9 %copy-start = (f32[36,32,256]{2,1,0:T(8,128)}, f32[36,32,256]{2,1,0:T(8,128)S(1)}, u32[]{:S(2)}) copy-start(f32[36,32,256]{2,1,0:T(8,128)S(1)} %get-tuple-element.37.sol.sol_kept) | copy-start | bytes 3538948
  9.2 15.9 %copy-start.1 = (f32[36,32,256]{2,1,0:T(8,128)}, f32[36,32,256]{2,1,0:T(8,128)S(1)}, u32[]{:S(2)}) copy-start(f32[36,32,256]{2,1,0:T(8,128)S(1)} %get-tuple-element.38.base.refs_0_) | copy-start | bytes 3538948
  9.2 3.7 %collective-permute-start.2 = (s32[4,8]{1,0:T(4,128)S(1)}, s32[4,8]{1,0:T(4,128)S(1)}, u32[]{:S(2)}, u32[]{:S(2)}) collective-permute-start(s32[4,8]{1,0:T(4,128)S(1)} %get-tuple-element.41), channel_id=1, source_target_pairs={{0,8},{8,0},{16,24},{24,16},{1,9},{9,1},{17,25},{25,17},{2,10},{10... | collective-permute-start | bytes 392 | tf_op jit(solution)/shard_map/ppermute | solution.py:72
  12.9 5.2 %copy-start.7 = (s32[1,8]{1,0:T(1,128)S(1)}, s32[1,8]{1,0:T(1,128)}, u32[]{:S(2)}) copy-start(s32[1,8]{1,0:T(1,128)} %offsets.5) | copy-start | bytes 100
  13.0 12.0 %collective-permute-start.4 = (bf16[2,8,32,256]{3,2,1,0:T(8,128)(2,1)S(1)}, bf16[2,8,32,256]{3,2,1,0:T(8,128)(2,1)S(1)}, u32[]{:S(2)}, u32[]{:S(2)}) collective-permute-start(bf16[2,8,32,256]{3,2,1,0:T(8,128)(2,1)S(1)} %get-tuple-element.45), channel_id=1, source_target_pairs={{8,16},{16,8},{9,17},{17,9},{10,18},{18,10},{11,19},{19,11},{12,20... | collective-permute-start | bytes 786440 | tf_op jit(solution)/shard_map/ppermute | solution.py:66
  13.7 11.4 %collective-permute-start.3 = (bf16[2,8,32,256]{3,2,1,0:T(8,128)(2,1)S(1)}, bf16[2,8,32,256]{3,2,1,0:T(8,128)(2,1)S(1)}, u32[]{:S(2)}, u32[]{:S(2)}) collective-permute-start(bf16[2,8,32,256]{3,2,1,0:T(8,128)(2,1)S(1)} %get-tuple-element.44), channel_id=1, source_target_pairs={{0,8},{16,24},{8,0},{24,16},{1,9},{17,25},{9,1},{25,17},{2,10},{18... | collective-permute-start | bytes 786440 | tf_op jit(solution)/shard_map/ppermute | solution.py:65
  18.1 6.8 %collective-permute-start.5 = (s32[4,8]{1,0:T(4,128)S(1)}, s32[4,8]{1,0:T(4,128)S(1)}, u32[]{:S(2)}, u32[]{:S(2)}) collective-permute-start(s32[4,8]{1,0:T(4,128)S(1)} %add.6), channel_id=1, source_target_pairs={{0,16},{8,24},{16,0},{24,8},{1,17},{9,25},{17,1},{25,9},{2,18},{10... | collective-permute-start | bytes 392 | tf_op jit(solution)/shard_map/ppermute | solution.py:72
  26.7 7.5 %copy-start.8 = (bf16[4,64,512]{2,1,0:T(8,128)(2,1)S(1)}, bf16[4,64,512]{2,1,0:T(8,128)(2,1)}, u32[]{:S(2)}) copy-start(bf16[4,64,512]{2,1,0:T(8,128)(2,1)} %inverse.1) | copy-start | bytes 786436
  26.7 12.7 %all-to-all-start = ((bf16[8,128,256]{2,1,0:T(8,128)(2,1)}), bf16[8,128,256]{2,1,0:T(8,128)(2,1)S(1)}, u32[]{:S(2)}, u32[]{:S(2)}) async-start(bf16[8,128,256]{2,1,0:T(8,128)(2,1)} %get-tuple-element.52), calls=%async_computation | async-start | bytes 1048576 | tf_op jit(solution)/shard_map/all_to_all | solution.py:669
  39.4 1.2 %copy-start.3 = (bf16[512,1024]{1,0:T(8,128)(2,1)S(1)}, bf16[512,1024]{1,0:T(8,128)(2,1)}, u32[]{:S(2)}) copy-start(bf16[512,1024]{1,0:T(8,128)(2,1)} %shard_map.79.spread) | copy-start | bytes 3145732
  40.7 5.1 %copy-start.5 = (f32[6,6,3,10]{3,2,1,0:T(4,128)S(1)}, f32[6,6,3,10]{3,2,1,0:T(4,128)}, u32[]{:S(2)}) copy-start(f32[6,6,3,10]{3,2,1,0:T(4,128)} %stiffness.7) | copy-start | bytes 12964
  41.8 14.6 %all-to-all-start.1 = ((bf16[32,16,256]{2,1,0:T(8,128)(2,1)}), bf16[32,16,256]{2,1,0:T(8,128)(2,1)S(1)}, u32[]{:S(2)}, u32[]{:S(2)}) async-start(bf16[32,16,256]{2,1,0:T(8,128)(2,1)} %bitcast.17), calls=%async_computation.1 | async-start | bytes 524288 | tf_op jit(solution)/shard_map/all_to_all | solution.py:678
  58.4 7.0 %collective-permute-start.6 = (bf16[2,6,32,256]{3,2,1,0:T(8,128)(2,1)S(1)}, bf16[2,6,32,256]{3,2,1,0:T(8,128)(2,1)S(1)}, u32[]{:S(2)}, u32[]{:S(2)}) collective-permute-start(bf16[2,6,32,256]{3,2,1,0:T(8,128)(2,1)S(1)} %get-tuple-element.62), channel_id=1, source_target_pairs={{0,1},{2,3},{4,5},{6,7},{1,0},{3,2},{5,4},{7,6},{8,9},{10,11},{12,... | collective-permute-start | bytes 589832 | tf_op jit(solution)/shard_map/ppermute | solution.py:65
  59.2 6.1 %collective-permute-start.7 = (bf16[2,6,32,256]{3,2,1,0:T(8,128)(2,1)S(1)}, bf16[2,6,32,256]{3,2,1,0:T(8,128)(2,1)S(1)}, u32[]{:S(2)}, u32[]{:S(2)}) collective-permute-start(bf16[2,6,32,256]{3,2,1,0:T(8,128)(2,1)S(1)} %get-tuple-element.63), channel_id=1, source_target_pairs={{1,2},{3,4},{5,6},{2,1},{4,3},{6,5},{9,10},{11,12},{13,14},{10,9},... | collective-permute-start | bytes 589832 | tf_op jit(solution)/shard_map/ppermute | solution.py:66
  62.4 11.1 %copy-start.2 = (f32[36,32,256]{2,1,0:T(8,128)}, f32[36,32,256]{2,1,0:T(8,128)S(1)}, u32[]{:S(2)}) copy-start(f32[36,32,256]{2,1,0:T(8,128)S(1)} %get-tuple-element.60.sol.sol_kept) | copy-start | bytes 3538948
  65.4 8.2 %copy-start.6 = (bf16[128,2048]{1,0:T(8,128)(2,1)S(1)}, bf16[128,2048]{1,0:T(8,128)(2,1)}, u32[]{:S(2)}) copy-start(bf16[128,2048]{1,0:T(8,128)(2,1)} %get-tuple-element.66.basis_t) | copy-start | bytes 1572868
  65.4 8.1 %collective-permute-start.8 = (bf16[2,8,32,256]{3,2,1,0:T(8,128)(2,1)S(1)}, bf16[2,8,32,256]{3,2,1,0:T(8,128)(2,1)S(1)}, u32[]{:S(2)}, u32[]{:S(2)}) collective-permute-start(bf16[2,8,32,256]{3,2,1,0:T(8,128)(2,1)S(1)} %get-tuple-element.64), channel_id=1, source_target_pairs={{0,8},{16,24},{8,0},{24,16},{1,9},{17,25},{9,1},{25,17},{2,10},{18... | collective-permute-start | bytes 786440 | tf_op jit(solution)/shard_map/ppermute | solution.py:65
  67.1 6.4 %collective-permute-start.9 = (bf16[2,8,32,256]{3,2,1,0:T(8,128)(2,1)S(1)}, bf16[2,8,32,256]{3,2,1,0:T(8,128)(2,1)S(1)}, u32[]{:S(2)}, u32[]{:S(2)}) collective-permute-start(bf16[2,8,32,256]{3,2,1,0:T(8,128)(2,1)S(1)} %get-tuple-element.65), channel_id=1, source_target_pairs={{8,16},{16,8},{9,17},{17,9},{10,18},{18,10},{11,19},{19,11},{12,20... | collective-permute-start | bytes 786440 | tf_op jit(solution)/shard_map/ppermute | solution.py:66
  75.2 14.2 %copy-start.4 = (bf16[512,1024]{1,0:T(8,128)(2,1)S(1)}, bf16[512,1024]{1,0:T(8,128)(2,1)}, u32[]{:S(2)}) copy-start(bf16[512,1024]{1,0:T(8,128)(2,1)} %shard_map.79.spread) | copy-start | bytes 3145732
  90.5 15.4 %all-to-all-start.3 = ((bf16[32,16,256]{2,1,0:T(8,128)(2,1)}), bf16[32,16,256]{2,1,0:T(8,128)(2,1)S(1)}, u32[]{:S(2)}, u32[]{:S(2)}) async-start(bf16[32,16,256]{2,1,0:T(8,128)(2,1)} %bitcast.18), calls=%async_computation.3 | async-start | bytes 524288 | tf_op jit(solution)/shard_map/all_to_all | solution.py:678

commit v5 on v4

--- a/solution.py
+++ b/solution.py
@@ -9,6 +9,7 @@
 from jax.sharding import PartitionSpec as P
 
 ITERS = 2
+PARTNER = 2
 GROUP_AXES = ("crow", "ccol")
 ALL_AXES = ("sub", "crow", "ccol")
 bf16, f32 = jnp.bfloat16, jnp.float32
@@ -211,6 +212,10 @@
             out[1, q + 1] = sol[s * cells_q + q].astype(bf16)
 
 
+def side_of(member):
+    return (member // PARTNER) % 2
+
+
 def window_kernel(
     shape,
     sol,
@@ -258,11 +263,14 @@
         for w in range(wide):
             local[place + w] = jnp.where(there, side(0, w) + near[w], 0.0).astype(bf16)
     copies = [begun(local, local_kept, sems.at[0])]
-    restricted[...] = jnp.dot(
+    product = jnp.dot(
         basis_t[...], local[...].reshape(-1, columns), preferred_element_type=f32
     ).astype(bf16)
+    half = columns // 2
+    for k in range(2):
+        restricted[k] = product[:, k * half : (k + 1) * half]
     for j in range(message.shape[0]):
-        copies.append(begun(restricted, message.at[j], sems.at[j + 1]))
+        copies.append(begun(restricted.at[side_of(j)], message.at[j], sems.at[j + 1]))
     for copy in copies:
         copy.wait()
 
@@ -349,11 +357,19 @@
     )
 
 
-def coarse_values(arrived):
-    chosen = arrived[0].astype(f32)
-    for h in range(1, arrived.shape[0]):
-        chosen = chosen + arrived[h].astype(f32)
-    return chosen.astype(bf16)
+def coarse_values(arrived, depth):
+    sums = []
+    for c in range(arrived.shape[1]):
+        total = arrived[0, c].astype(f32)
+        for h in range(1, arrived.shape[0]):
+            total = total + arrived[h, c].astype(f32)
+        sums.append(total)
+    rows = []
+    for m in range(arrived.shape[1]):
+        part = slice(side_of(m) * depth, (side_of(m) + 1) * depth)
+        low = m - side_of(m) * PARTNER
+        rows.append(jnp.concatenate([sums[low][part], sums[low + PARTNER][part]], axis=1))
+    return jnp.concatenate(rows, axis=0).astype(bf16)
 
 
 def step_sides_kernel(
@@ -382,7 +398,7 @@
             i = s * cells_q + q
             copies.append(begun(sol_kept.at[i], sol.at[i], sems.at[len(copies)]))
             copies.append(begun(base_kept.at[i], begin.at[i], sems.at[len(copies)]))
-    chosen = coarse_values(arrived)
+    chosen = coarse_values(arrived, arrived.shape[2] // 2)
     copies[0].wait()
     span = cells_q * pad
     for s in range(cells_s):
@@ -419,7 +435,7 @@
     for s in range(cells_s):
         part = pl.ds(s * cells_q, cells_q)
         copies.append(begun(sol_kept.at[part], sol.at[part], sems.at[s + 1]))
-    chosen = coarse_values(arrived)
+    chosen = coarse_values(arrived, arrived.shape[2] // 2)
     copies[0].wait()
     results = []
     for s in range(cells_s):
@@ -463,111 +479,138 @@
     return jnp.where(row == wanted, 1.0, 0.0).astype(bf16)
 
 
-def basis_turned_kernel(cell, dims, offsets, basis_kept, basis_t, kept, basis, sems):
+def basis_kernel(cell, dims, offsets, basis_kept, basis_t, turned_kept, own_kept, basis, own, sems):
     wide, per_cell, pad = cell
     span, chunk = wide * per_cell, wide * pad
+    size = chunk - 2 * pad
     copy = begun(basis_kept.at[0], basis, sems.at[0])
     pack = packing(wide, per_cell, pad)
+    pack_own = packing(wide, per_cell, pad, True)[pad : pad + size]
     order = ordering(dims, offsets)
+    rows = basis.shape[0] // span
     copy.wait()
-    for s in range(basis.shape[0] // span):
+    for s in range(rows):
         ordered = jnp.dot(
             basis[s * span : (s + 1) * span, :], order, preferred_element_type=f32
         ).astype(bf16)
         basis_t[:, s * chunk : (s + 1) * chunk] = lax.dot_general(
             ordered, pack, (((0,), (0,)), ((), ())), preferred_element_type=f32
         ).astype(bf16)
-    begun(basis_t, kept, sems.at[1]).wait()
-
-
-def basis_own_kernel(cell, dims, offsets, basis_kept, own_kept, basis, basis_p, sems):
-    wide, per_cell, pad = cell
-    span = wide * per_cell
-    size = (wide - 2) * pad
-    copy = begun(basis_kept.at[0], basis, sems.at[0])
-    pack = packing(wide, per_cell, pad, True)[pad : pad + size]
-    order = ordering(dims, offsets)
-    copy.wait()
-    for s in range(basis_p.shape[0] // size):
-        ordered = jnp.dot(
-            basis[(s + 1) * span : (s + 2) * span, :], order, preferred_element_type=f32
-        ).astype(bf16)
-        basis_p[s * size : (s + 1) * size, :] = jnp.dot(
-            pack, ordered, preferred_element_type=f32
-        ).astype(bf16)
-    begun(basis_p, own_kept, sems.at[1]).wait()
-
-
-def ordered_basis(body, cell, dims, offsets, basis, shape, both):
-    held = [] if both else [pltpu.VMEM(shape, bf16)]
+        if 0 < s < rows - 1:
+            own[(s - 1) * size : s * size, :] = jnp.dot(
+                pack_own, ordered, preferred_element_type=f32
+            ).astype(bf16)
+    copies = [begun(basis_t, turned_kept, sems.at[1]), begun(own, own_kept, sems.at[2])]
+    for copy in copies:
+        copy.wait()
+
+
+def ordered_basis(cell, dims, offsets, basis, turned, own):
     return pl.pallas_call(
-        functools.partial(body, cell, dims),
-        out_shape=([jax.ShapeDtypeStruct(shape, bf16)] if both else []) + [pltpu.HBM(shape, bf16)],
+        functools.partial(basis_kernel, cell, dims),
+        out_shape=(jax.ShapeDtypeStruct(turned, bf16), pltpu.HBM(turned, bf16), pltpu.HBM(own, bf16)),
         in_specs=[pl.BlockSpec(memory_space=pltpu.SMEM), HBM],
-        out_specs=([VMEM] if both else []) + [HBM],
-        scratch_shapes=[pltpu.VMEM(basis.shape[1:], bf16), *held, pltpu.SemaphoreType.DMA((2,))],
+        out_specs=(VMEM, HBM, HBM),
+        scratch_shapes=[
+            pltpu.VMEM(basis.shape[1:], bf16),
+            pltpu.VMEM(own, bf16),
+            pltpu.SemaphoreType.DMA((3,)),
+        ],
         compiler_params=pltpu.CompilerParams(vmem_limit_bytes=12 << 20),
         cost_estimate=pl.CostEstimate(
-            flops=4 * shape[0] * shape[1] * cell[0] * cell[2],
-            bytes_accessed=4 * basis.size,
+            flops=6 * turned[0] * turned[1] * cell[0] * cell[2],
+            bytes_accessed=6 * basis.size,
             transcendentals=0,
         ),
     )(offsets, pltpu.with_memory_space_constraint(basis, pltpu.HBM))
 
 
-def spread_kernel(dims, every, inverse, out, columns):
+def first_index(first, member, groups):
+    if groups & (groups - 1) == 0:
+        return lax.shift_right_logical(first - member + groups - 1, groups.bit_length() - 1)
+    return lax.div(first - member + groups - 1, groups)
+
+
+def spread_kernel(dims, every, inverse_kept, partner_kept, out_kept, inverse, columns, picked, out, sems):
     groups, depth, kgroup = dims
-    g = pl.program_id(0)
+    coarse = groups * depth
     member = lax.axis_index(GROUP_AXES)
-
-    @pl.when(g == 0)
-    def _():
-        own = lax.axis_index("sub")
-        slot = lax.broadcasted_iota(jnp.int32, (kgroup, groups * depth), 0)
-        for j in range(groups):
-            first, place, valid = places(every, own, j, groups, depth, kgroup)
-            wanted = jnp.where(valid, place + first, -1)
-            columns[:, j * groups * depth : (j + 1) * groups * depth] = jnp.where(
-                slot == wanted, 1.0, 0.0
-            ).astype(bf16)
-
-    rows = inverse.shape[1]
+    own = lax.axis_index("sub")
+    side = side_of(member)
+    copies = [
+        begun(inverse_kept, inverse.at[side], sems.at[0]),
+        begun(partner_kept, inverse.at[1 - side], sems.at[1]),
+    ]
+    slot = lax.broadcasted_iota(jnp.int32, (kgroup, coarse), 0)
+    for j in range(groups):
+        first, place, valid = places(every, own, j, groups, depth, kgroup)
+        wanted = jnp.where(valid, place + first, -1)
+        columns[:, j * coarse : (j + 1) * coarse] = jnp.where(slot == wanted, 1.0, 0.0).astype(bf16)
+    _, n_sub, rows, _ = inverse.shape
     turn = lax.broadcasted_iota(jnp.int32, (depth, rows), 0)
     index = lax.broadcasted_iota(jnp.int32, (depth, rows), 1)
-    picks = []
-    for j in range(groups):
-        first = every[g, j]
-        end = kgroup if j == groups - 1 else every[g, j + 1]
-        begin = lax.div(first - member + groups - 1, groups)
-        wanted = (index == turn + begin) & (index * groups + member < end)
-        picks.append(jnp.where(wanted, 1.0, 0.0).astype(bf16))
-    picked = jnp.dot(
-        jnp.concatenate(picks, axis=0), inverse[0], preferred_element_type=f32
-    ).astype(bf16)
-    out[...] = jnp.dot(picked, columns[...], preferred_element_type=f32).astype(bf16)
-
-
-def spread_inverse(every, coarse_inverse, depth):
+    for copy in copies:
+        copy.wait()
+    span = 2 * coarse
+    steps = max(n_sub // 4, 1)
+    size = n_sub // steps
+
+    def some(k, _):
+        for t in range(size):
+            g = k * size + t
+            for b in range(2):
+                m = member + (b - side) * PARTNER
+                picks = []
+                for j in range(groups):
+                    first = every[g, j]
+                    end = kgroup if j == groups - 1 else every[g, j + 1]
+                    begin = first_index(first, m, groups)
+                    wanted = (index == turn + begin) & (index * groups + m < end)
+                    picks.append(jnp.where(wanted, 1.0, 0.0).astype(bf16))
+                part = jnp.dot(
+                    jnp.concatenate(picks, axis=0), inverse[b, g], preferred_element_type=f32
+                ).astype(bf16)
+                for j in range(groups):
+                    at = t * span + (2 * j + b) * depth
+                    picked[at : at + depth, :] = part[j * depth : (j + 1) * depth]
+        out[...] = jnp.dot(picked[...], columns[...], preferred_element_type=f32).astype(bf16)
+        begun(out, out_kept.at[pl.ds(k * size * span, size * span)], sems.at[2]).wait()
+        return 0
+
+    lax.fori_loop(0, steps, some, 0)
+
+
+def spread_inverse(every, coarse_inverse, partner, depth):
     n_sub, share_rows, kgroup = coarse_inverse.shape
     groups = every.shape[1]
     coarse = groups * depth
+    rows = n_sub * 2 * coarse
+    part = rows // max(n_sub // 4, 1)
     return pl.pallas_call(
         functools.partial(spread_kernel, (groups, depth, kgroup)),
-        grid=(n_sub,),
-        out_shape=pltpu.HBM((n_sub * coarse, groups * coarse), bf16),
-        in_specs=[
-            pl.BlockSpec(memory_space=pltpu.SMEM),
-            pl.BlockSpec((1, share_rows, kgroup), lambda g: (g, 0, 0)),
+        out_shape=pltpu.HBM((rows, groups * coarse), bf16),
+        in_specs=[pl.BlockSpec(memory_space=pltpu.SMEM), HBM, HBM],
+        out_specs=HBM,
+        scratch_shapes=[
+            pltpu.VMEM((2,) + coarse_inverse.shape, bf16),
+            pltpu.VMEM((kgroup, groups * coarse), bf16),
+            pltpu.VMEM((part, kgroup), bf16),
+            pltpu.VMEM((part, groups * coarse), bf16),
+            pltpu.SemaphoreType.DMA((3,)),
         ],
-        out_specs=pl.BlockSpec((coarse, groups * coarse), lambda g: (g, 0)),
-        scratch_shapes=[pltpu.VMEM((kgroup, groups * coarse), bf16)],
-        compiler_params=pltpu.CompilerParams(vmem_limit_bytes=10 << 20),
+        compiler_params=pltpu.CompilerParams(
+            vmem_limit_bytes=(16 << 20) + 4 * coarse_inverse.size + 8 * part * groups * coarse
+        ),
         cost_estimate=pl.CostEstimate(
-            flops=2 * n_sub * coarse * groups * coarse * kgroup,
-            bytes_accessed=4 * n_sub * coarse * groups * coarse,
+            flops=2 * rows * groups * coarse * kgroup,
+            bytes_accessed=2 * rows * groups * coarse,
             transcendentals=0,
         ),
-    )(every, coarse_inverse)
+    )(
+        every,
+        pltpu.with_memory_space_constraint(coarse_inverse, pltpu.HBM),
+        pltpu.with_memory_space_constraint(partner, pltpu.HBM),
+    )
 
 
 def shards(rhs, start, stiffness, sub_inverse, basis, coarse_inverse, offsets):
@@ -640,44 +683,45 @@
         first_s, second_s = swap(first, second, "sub")
         if sweep == 0:
             later, _ = lax.optimization_barrier((basis, first))
-            basis_t, basis_kept = ordered_basis(
-                basis_turned_kernel, cell, dims, offsets, later, (coarse, rows), True
+            basis_t, basis_kept, basis_p = ordered_basis(
+                cell, dims, offsets, later, (coarse, rows), (cells * pad, coarse)
             )
+            shared, _ = lax.optimization_barrier((coarse_inverse, basis_t))
+            pairs = [(i, i ^ PARTNER) for i in range(groups)]
+            partner = lax.ppermute(shared, GROUP_AXES, pairs)
             every = doubled(every, 1 << (rounds - 1))
-            first_s, second_s, every = lax.optimization_barrier((first_s, second_s, every))
+            first_s, second_s, every, partner = lax.optimization_barrier(
+                (first_s, second_s, every, partner)
+            )
         message, local = call(
             functools.partial(window_kernel, shape),
             (solution, base, first_q, second_q, first_s, second_s, basis_t if sweep == 0 else basis_kept),
             (
-                pltpu.HBM((groups, coarse, columns), bf16),
+                pltpu.HBM((groups, coarse, columns // 2), bf16),
                 pltpu.HBM(((cells_s + 2) * wide, pad, columns), bf16),
             ),
             scratch=(
                 pltpu.VMEM(((cells_s + 2) * wide, pad, columns), bf16),
-                pltpu.VMEM((coarse, columns), bf16),
+                pltpu.VMEM((2, coarse, columns // 2), bf16),
                 pltpu.SemaphoreType.DMA((groups + 1,)),
             ),
             flops=2 * rows * coarse * columns,
         )
         if sweep == 0:
-            later, _ = lax.optimization_barrier((basis, message))
-            (basis_p,) = ordered_basis(
-                basis_own_kernel, cell, dims, offsets, later, (cells * pad, coarse), False
-            )
-            waited, basis_p = lax.optimization_barrier((every, basis_p))
-            spread = spread_inverse(waited, coarse_inverse, depth)
+            waited, _ = lax.optimization_barrier((every, message))
+            spread = spread_inverse(waited, coarse_inverse, partner, depth)
         gathered = lax.all_to_all(message, GROUP_AXES, 0, 0, tiled=True)
-        held = pltpu.VMEM((spread.shape[0], columns), bf16)
+        held = pltpu.VMEM((spread.shape[0], columns // 2), bf16)
         (terms,) = call(
             terms_kernel,
-            (spread, gathered.reshape(-1, columns)),
+            (spread, gathered.reshape(-1, columns // 2)),
             (pltpu.HBM(held.shape, bf16),),
             scratch=(held, pltpu.SemaphoreType.DMA),
-            flops=2 * spread.size * columns,
+            flops=2 * spread.size * columns // 2,
         )
         arrived = lax.all_to_all(
-            terms.reshape(n_sub * groups, depth, columns), ALL_AXES, 0, 0, tiled=True
-        ).reshape(n_sub, coarse, columns)
+            terms.reshape(n_sub * groups, 2 * depth, columns // 2), ALL_AXES, 0, 0, tiled=True
+        ).reshape(n_sub, groups, 2 * depth, columns // 2)
         kept = fine_product(
             shape, layers, local, sub_inverse, solution, base, stiffness, last
         )

time: 110 us -> 107 us (0.973)
  blocking collectives: 14.2 us -> 11 us
  starting transfers between devices: 26.8 us -> 29.6 us
  Pallas kernels: 43.4 us -> 41 us
    ppermute x2, starting transfers between devices: 1.64 us -> 5.47 us  [doubled(): lax.ppermute(held, 'sub', [(i, i ^ step) for i in range(count)])]
    pallas_call x2 -> x1, Pallas kernels: 8.16 us -> 4.49 us  [ordered_basis(): pl.pallas_call(functools.partial(basis_kernel, cell, dims), out_shape=(ja...]
    all_to_all x1, blocking collectives: 14.2 us -> 11 us  [shards(): gathered = lax.all_to_all(message, GROUP_AXES, 0, 0, tiled=True)]
    ppermute x4, starting transfers between devices: 9.99 us -> 7.19 us  [swap(): lax.ppermute(first, axis, even + [(b, a) for a, b in even])]
  transfers between devices with their start and end apart: 13 -> 14, of which waited for: 8 -> 7; matrix products, arithmetic and copies ran while one was open for 0% -> 0% of each run, Pallas kernels for 28% -> 27%
where the time goes in v5:
time: 107 us; the launch traced here: 106 us
  Pallas kernels  41 us (38%)
  starting transfers between devices  29.6 us (28%)
  waiting for transfers between devices  22.2 us (21%)
  blocking collectives  11 us (10%)
  local copies, waits for them, and re-layouts  1.64 us (2%)
    pallas_call x13, Pallas kernels, call(): pl.pallas_call(body, out_shape=tuple(outs), in_specs=[HBM if i in held el...  32 us
    all_to_all x1, blocking collectives, shards(): gathered = lax.all_to_all(message, GROUP_AXES, 0, 0, tiled=True)  11 us
    all_to_all x2, starting transfers between devices, shards(): lax.all_to_all(terms.reshape(n_sub * groups, 2 * depth, columns // 2), AL...  9.64 us
    ppermute x4, waiting for transfers between devices, swap(): lax.ppermute(first, axis, even + [(b, a) for a, b in even])  8.53 us
    all_to_all x2, waiting for transfers between devices, shards(): lax.all_to_all(terms.reshape(n_sub * groups, 2 * depth, columns // 2), AL...  8.22 us
    ppermute x4, starting transfers between devices, swap(): lax.ppermute(first, axis, even + [(b, a) for a, b in even])  7.19 us
    ppermute x2, starting transfers between devices, doubled(): lax.ppermute(held, 'sub', [(i, i ^ step) for i in range(count)])  5.47 us
    pallas_call x1, Pallas kernels, spread_inverse(): pl.pallas_call(functools.partial(spread_kernel, (groups, depth, kgroup)),...  4.49 us
  transfers between devices with their start and end apart: 14, of which 7 were waited for; matrix products, arithmetic and copies ran while one was open for 0% of the time, Pallas kernels for 27%

profile of v5, /device:TPU:0, one launch (start us, length us, event | category | flops | bytes accessed | tf_op | source)
XLA Modules:
  0.0 105.8 jit_solution(3918141436826544098)
XLA Ops:
  0.0 2.0 %shard_map.74 = (bf16[2,6,32,256]{3,2,1,0:T(8,128)(2,1)S(1)}, bf16[2,6,32,256]{3,2,1,0:T(8,128)(2,1)S(1)}) custom-call(f32[6,6,10,3,256]{4,3,2,1,0:T(4,128)} %bitcast.13, f32[6,6,10,3,256]{4,3,2,1,0:T(4,128)} %bitcast.15, f32[6,6,3,10]{3,2,1,0:T(4,128)} %stiffness.7), custom_call_target="tpu_custom_call" | custom-call | bytes 2609376 | tf_op jit(solution)/shard_map/pallas_call | solution.py:27
  2.0 3.0 %collective-permute-start = (bf16[2,6,32,256]{3,2,1,0:T(8,128)(2,1)S(1)}, bf16[2,6,32,256]{3,2,1,0:T(8,128)(2,1)S(1)}, u32[]{:S(2)}, u32[]{:S(2)}) collective-permute-start(bf16[2,6,32,256]{3,2,1,0:T(8,128)(2,1)S(1)} %get-tuple-element.40), channel_id=1, source_target_pairs={{0,1},{2,3},{4,5},{6,7},{1,0},{3,2},{5,4},{7,6},{8,9},{10,11},{12,... | collective-permute-start | bytes 589832 | tf_op jit(solution)/shard_map/ppermute | solution.py:66
  5.7 3.5 %shard_map.73 = (f32[36,32,256]{2,1,0:T(8,128)S(1)}, f32[36,32,256]{2,1,0:T(8,128)S(1)}, s32[4,8]{1,0:T(4,128)S(1)}) custom-call(f32[6,6,10,3,256]{4,3,2,1,0:T(4,128)} %bitcast.14, f32[6,6,10,3,256]{4,3,2,1,0:T(4,128)} %bitcast.16, f32[6,6,3,10]{3,2,1,0:T(4,128)} %stiffness.7, s32[1,8]{1,0:T(1,128)} %offsets.3), custom_call_target="tpu_custom_call" | custom-call | bytes 4575616 | tf_op jit(solution)/shard_map/pallas_call | solution.py:27
  9.2 1.6 %collective-permute-start.2 = (s32[4,8]{1,0:T(4,128)S(1)}, s32[4,8]{1,0:T(4,128)S(1)}, u32[]{:S(2)}, u32[]{:S(2)}) collective-permute-start(s32[4,8]{1,0:T(4,128)S(1)} %get-tuple-element.42), channel_id=1, source_target_pairs={{0,8},{8,0},{16,24},{24,16},{1,9},{9,1},{17,25},{25,17},{2,10},{10... | collective-permute-start | bytes 392 | tf_op jit(solution)/shard_map/ppermute | solution.py:73
  10.9 2.0 %collective-permute-done.2 = s32[4,8]{1,0:T(4,128)S(1)} collective-permute-done((s32[4,8]{1,0:T(4,128)S(1)}, s32[4,8]{1,0:T(4,128)S(1)}, u32[]{:S(2)}, u32[]{:S(2)}) %collective-permute-start.2) | collective-permute-done | bytes 160 | tf_op jit(solution)/shard_map/ppermute | solution.py:73
  13.0 1.6 %collective-permute-start.3 = (bf16[2,8,32,256]{3,2,1,0:T(8,128)(2,1)S(1)}, bf16[2,8,32,256]{3,2,1,0:T(8,128)(2,1)S(1)}, u32[]{:S(2)}, u32[]{:S(2)}) collective-permute-start(bf16[2,8,32,256]{3,2,1,0:T(8,128)(2,1)S(1)} %get-tuple-element.45), channel_id=1, source_target_pairs={{0,8},{16,24},{8,0},{24,16},{1,9},{17,25},{9,1},{25,17},{2,10},{18... | collective-permute-start | bytes 786440 | tf_op jit(solution)/shard_map/ppermute | solution.py:66
  15.3 4.5 %shard_map.76 = (bf16[128,2048]{1,0:T(8,128)(2,1)S(1)}, bf16[128,2048]{1,0:T(8,128)(2,1)}, bf16[1152,128]{1,0:T(8,128)(2,1)}) custom-call(s32[1,8]{1,0:T(1,128)S(1)} %copy-done.7, bf16[1,1920,128]{2,1,0:T(8,128)(2,1)} %basis_kept), custom_call_target="tpu_custom_call" | custom-call | flops 402653184 | bytes 1474560 | tf_op jit(solution)/shard_map/pallas_call | solution.py:509
  20.3 3.8 %collective-permute-start.5 = (s32[4,8]{1,0:T(4,128)S(1)}, s32[4,8]{1,0:T(4,128)S(1)}, u32[]{:S(2)}, u32[]{:S(2)}) collective-permute-start(s32[4,8]{1,0:T(4,128)S(1)} %add.6), channel_id=1, source_target_pairs={{0,16},{8,24},{16,0},{24,8},{1,17},{9,25},{17,1},{25,9},{2,18},{10... | collective-permute-start | bytes 392 | tf_op jit(solution)/shard_map/ppermute | solution.py:73
  24.2 1.9 %collective-permute-done.5 = s32[4,8]{1,0:T(4,128)S(1)} collective-permute-done((s32[4,8]{1,0:T(4,128)S(1)}, s32[4,8]{1,0:T(4,128)S(1)}, u32[]{:S(2)}, u32[]{:S(2)}) %collective-permute-start.5) | collective-permute-done | bytes 160 | tf_op jit(solution)/shard_map/ppermute | solution.py:73
  26.1 1.5 %shard_map.77 = (bf16[8,128,128]{2,1,0:T(8,128)(2,1)}, bf16[64,32,256]{2,1,0:T(8,128)(2,1)}) custom-call(f32[36,32,256]{2,1,0:T(8,128)S(1)} %get-tuple-element.38.sol.sol_kept, f32[36,32,256]{2,1,0:T(8,128)S(1)} %get-tuple-element.39.base.refs_0_, bf16[2,6,32,256]{3,2,1,0:T(8,128)(2,1)S(1)} %collective-permute-done.first_in.first_q, ...), custom_call_target="tpu_custom_call" | custom-call | flops 134217728 | bytes 5111808 | tf_op jit(solution)/shard_map/pallas_call | solution.py:27
  27.7 3.9 %all-to-all-start = ((bf16[8,128,128]{2,1,0:T(8,128)(2,1)}), bf16[8,128,128]{2,1,0:T(8,128)(2,1)S(1)}, u32[]{:S(2)}, u32[]{:S(2)}) async-start(bf16[8,128,128]{2,1,0:T(8,128)(2,1)} %get-tuple-element.54), calls=%async_computation | async-start | bytes 524288 | tf_op jit(solution)/shard_map/all_to_all | solution.py:713
  31.6 4.5 %shard_map.78.spread = bf16[1024,1024]{1,0:T(8,128)(2,1)} custom-call(s32[4,8]{1,0:T(4,128)S(1)} %add.7.every, bf16[4,64,512]{2,1,0:T(8,128)(2,1)} %inverse_kept.3, bf16[4,64,512]{2,1,0:T(8,128)(2,1)} %copy-done.9), custom_call_target="tpu_custom_call" | custom-call | flops 1073741824 | bytes 2097152 | tf_op jit(solution)/shard_map/pallas_call | solution.py:589
  36.1 1.5 %all-to-all-done = bf16[8,128,128]{2,1,0:T(8,128)(2,1)S(1)} async-done(((bf16[8,128,128]{2,1,0:T(8,128)(2,1)}), bf16[8,128,128]{2,1,0:T(8,128)(2,1)S(1)}, u32[]{:S(2)}, u32[]{:S(2)}) %all-to-all-start) | async-done | bytes 262176 | tf_op jit(solution)/shard_map/all_to_all | solution.py:713
  37.7 1.6 %copy-done.3 = bf16[1024,1024]{1,0:T(8,128)(2,1)S(1)} copy-done((bf16[1024,1024]{1,0:T(8,128)(2,1)S(1)}, bf16[1024,1024]{1,0:T(8,128)(2,1)}, u32[]{:S(2)}) %copy-start.3) | copy-done | bytes 2097176
  39.3 1.4 %shard_map.79 = bf16[1024,128]{1,0:T(8,128)(2,1)} custom-call(bf16[1024,1024]{1,0:T(8,128)(2,1)S(1)} %copy-done.3, bf16[1024,128]{1,0:T(8,128)(2,1)S(1)} %bitcast.11), custom_call_target="tpu_custom_call" | custom-call | flops 268435456 | bytes 2621440 | tf_op jit(solution)/shard_map/pallas_call | solution.py:27
  40.7 4.7 %all-to-all-start.1 = ((bf16[32,32,128]{2,1,0:T(8,128)(2,1)}), bf16[32,32,128]{2,1,0:T(8,128)(2,1)S(1)}, u32[]{:S(2)}, u32[]{:S(2)}) async-start(bf16[32,32,128]{2,1,0:T(8,128)(2,1)} %bitcast.17), calls=%async_computation.1 | async-start | bytes 524288 | tf_op jit(solution)/shard_map/all_to_all | solution.py:722
  45.5 7.1 %shard_map.80 = (f32[36,32,256]{2,1,0:T(8,128)}, f32[36,32,256]{2,1,0:T(8,128)}) custom-call(bf16[64,32,256]{2,1,0:T(8,128)(2,1)} %get-tuple-element.58.local_kept, bf16[1,1920,1920]{2,1,0:T(8,128)(2,1)} %inverse_kept.5, f32[36,32,256]{2,1,0:T(8,128)} %copy-done, f32[36,32,256]{2,1,0:T(8,128)} %copy-done.1, f32[6,6,3,10]{3,2,1,0:T(4,128)S(1)} %copy-done.5), custom_call_target="tpu_custom_call" | custom-call | flops 1415577600 | bytes 13144288 | tf_op jit(solution)/shard_map/pallas_call | solution.py:27
  52.5 3.6 %all-to-all-done.1 = bf16[32,32,128]{2,1,0:T(8,128)(2,1)S(1)} async-done(((bf16[32,32,128]{2,1,0:T(8,128)(2,1)}), bf16[32,32,128]{2,1,0:T(8,128)(2,1)S(1)}, u32[]{:S(2)}, u32[]{:S(2)}) %all-to-all-start.1) | async-done | bytes 262176 | tf_op jit(solution)/shard_map/all_to_all | solution.py:722
  56.1 1.9 %shard_map.81 = (bf16[2,6,32,256]{3,2,1,0:T(8,128)(2,1)S(1)}, bf16[2,6,32,256]{3,2,1,0:T(8,128)(2,1)S(1)}, f32[36,32,256]{2,1,0:T(8,128)S(1)}) custom-call(bf16[4,8,32,128]{3,2,1,0:T(8,128)(2,1)S(1)} %bitcast.9, bf16[1152,128]{1,0:T(8,128)(2,1)} %get-tuple-element.57.basis_kept, f32[36,32,256]{2,1,0:T(8,128)} %get-tuple-element.59.sol_kept, ...), custom_call_target="tpu_custom_call" | custom-call | bytes 4493536 | tf_op jit(solution)/shard_map/pallas_call | solution.py:27
  58.0 0.8 collective-permute-start.7
  59.5 2.5 %shard_map.82 = (f32[36,32,256]{2,1,0:T(8,128)S(1)}, f32[36,32,256]{2,1,0:T(8,128)S(1)}) custom-call(f32[36,32,256]{2,1,0:T(8,128)S(1)} %get-tuple-element.61.coarse, f32[36,32,256]{2,1,0:T(8,128)} %get-tuple-element.59.sol_kept, f32[36,32,256]{2,1,0:T(8,128)} %get-tuple-element.60.base_kept, f32[6,6,3,10]{3,2,1,0:T(4,128)} %stiffness.7), custom_call_target="tpu_custom_call" | custom-call | bytes 5902560 | tf_op jit(solution)/shard_map/pallas_call | solution.py:27
  62.0 2.9 %collective-permute-done.7.first_in.first_q = bf16[2,6,32,256]{3,2,1,0:T(8,128)(2,1)S(1)} collective-permute-done((bf16[2,6,32,256]{3,2,1,0:T(8,128)(2,1)S(1)}, bf16[2,6,32,256]{3,2,1,0:T(8,128)(2,1)S(1)}, u32[]{:S(2)}, u32[]{:S(2)}) %collective-permute-start.7) | collective-permute-done | bytes 196640 | tf_op jit(solution)/shard_map/ppermute | solution.py:66
  65.1 1.7 %collective-permute-start.9 = (bf16[2,8,32,256]{3,2,1,0:T(8,128)(2,1)S(1)}, bf16[2,8,32,256]{3,2,1,0:T(8,128)(2,1)S(1)}, u32[]{:S(2)}, u32[]{:S(2)}) collective-permute-start(bf16[2,8,32,256]{3,2,1,0:T(8,128)(2,1)S(1)} %get-tuple-element.66), channel_id=1, source_target_pairs={{0,8},{16,24},{8,0},{24,16},{1,9},{17,25},{9,1},{25,17},{2,10},{18... | collective-permute-start | bytes 786440 | tf_op jit(solution)/shard_map/ppermute | solution.py:66
  66.7 0.8 collective-permute-start.10
  67.6 5.6 %collective-permute-done.9.first_s = bf16[2,8,32,256]{3,2,1,0:T(8,128)(2,1)S(1)} collective-permute-done((bf16[2,8,32,256]{3,2,1,0:T(8,128)(2,1)S(1)}, bf16[2,8,32,256]{3,2,1,0:T(8,128)(2,1)S(1)}, u32[]{:S(2)}, u32[]{:S(2)}) %collective-permute-start.9) | collective-permute-done | bytes 262176 | tf_op jit(solution)/shard_map/ppermute | solution.py:66
  73.2 1.6 %shard_map.84 = (bf16[8,128,128]{2,1,0:T(8,128)(2,1)}, bf16[64,32,256]{2,1,0:T(8,128)(2,1)}) custom-call(f32[36,32,256]{2,1,0:T(8,128)S(1)} %get-tuple-element.62.sol.sol_kept, f32[36,32,256]{2,1,0:T(8,128)S(1)} %get-tuple-element.63.base, bf16[2,6,32,256]{3,2,1,0:T(8,128)(2,1)S(1)} %collective-permute-done.7.first_in.first_q, ...), custom_call_target="tpu_custom_call" | custom-call | flops 134217728 | bytes 5111808 | tf_op jit(solution)/shard_map/pallas_call | solution.py:27
  74.7 11.0 %all_to_all.20 = bf16[8,128,128]{2,1,0:T(8,128)(2,1)S(1)} all-to-all(bf16[8,128,128]{2,1,0:T(8,128)(2,1)} %get-tuple-element.69), channel_id=1, replica_groups=mesh['sub'=4,'crow'=4,'ccol'=2] {'crow','ccol'}, dimensions={0} | all-to-all | bytes 524288 | tf_op jit(solution)/shard_map/all_to_all | solution.py:713
  85.7 1.4 %shard_map.85 = bf16[1024,128]{1,0:T(8,128)(2,1)} custom-call(bf16[1024,1024]{1,0:T(8,128)(2,1)S(1)} %copy-done.4, bf16[1024,128]{1,0:T(8,128)(2,1)S(1)} %bitcast.12), custom_call_target="tpu_custom_call" | custom-call | flops 268435456 | bytes 2621440 | tf_op jit(solution)/shard_map/pallas_call | solution.py:27
  87.1 4.9 %all-to-all-start.3 = ((bf16[32,32,128]{2,1,0:T(8,128)(2,1)}), bf16[32,32,128]{2,1,0:T(8,128)(2,1)S(1)}, u32[]{:S(2)}, u32[]{:S(2)}) async-start(bf16[32,32,128]{2,1,0:T(8,128)(2,1)} %bitcast.18), calls=%async_computation.3 | async-start | bytes 524288 | tf_op jit(solution)/shard_map/all_to_all | solution.py:722
  92.1 6.1 %shard_map.86.sol_kept = f32[36,32,256]{2,1,0:T(8,128)} custom-call(bf16[64,32,256]{2,1,0:T(8,128)(2,1)} %get-tuple-element.70.local_kept, bf16[1,1920,1920]{2,1,0:T(8,128)(2,1)} %inverse_kept.5, f32[36,32,256]{2,1,0:T(8,128)} %copy-done.2), custom_call_target="tpu_custom_call" | custom-call | flops 1415577600 | bytes 10780672 | tf_op jit(solution)/shard_map/pallas_call | solution.py:27
  98.1 4.6 %all-to-all-done.3 = bf16[32,32,128]{2,1,0:T(8,128)(2,1)S(1)} async-done(((bf16[32,32,128]{2,1,0:T(8,128)(2,1)}), bf16[32,32,128]{2,1,0:T(8,128)(2,1)S(1)}, u32[]{:S(2)}, u32[]{:S(2)}) %all-to-all-start.3) | async-done | bytes 262176 | tf_op jit(solution)/shard_map/all_to_all | solution.py:722
  102.7 2.9 %shard_map.87 = f32[6,6,10,3,256]{4,3,2,1,0:T(4,128)} custom-call(bf16[4,8,32,128]{3,2,1,0:T(8,128)(2,1)S(1)} %bitcast.10, bf16[1152,128]{1,0:T(8,128)(2,1)} %get-tuple-element.57.basis_kept, f32[36,32,256]{2,1,0:T(8,128)} %shard_map.86.sol_kept), custom_call_target="tpu_custom_call" | custom-call | bytes 2842624 | tf_op jit(solution)/shard_map/pallas_call | solution.py:27
  (34 shorter events, 2.7 us)
Async XLA Ops:
  2.0 10.8 %collective-permute-start = (bf16[2,6,32,256]{3,2,1,0:T(8,128)(2,1)S(1)}, bf16[2,6,32,256]{3,2,1,0:T(8,128)(2,1)S(1)}, u32[]{:S(2)}, u32[]{:S(2)}) collective-permute-start(bf16[2,6,32,256]{3,2,1,0:T(8,128)(2,1)S(1)} %get-tuple-element.40), channel_id=1, source_target_pairs={{0,1},{2,3},{4,5},{6,7},{1,0},{3,2},{5,4},{7,6},{8,9},{10,11},{12,... | collective-permute-start | bytes 589832 | tf_op jit(solution)/shard_map/ppermute | solution.py:66
  5.1 7.8 %collective-permute-start.1 = (bf16[2,6,32,256]{3,2,1,0:T(8,128)(2,1)S(1)}, bf16[2,6,32,256]{3,2,1,0:T(8,128)(2,1)S(1)}, u32[]{:S(2)}, u32[]{:S(2)}) collective-permute-start(bf16[2,6,32,256]{3,2,1,0:T(8,128)(2,1)S(1)} %get-tuple-element.41), channel_id=1, source_target_pairs={{1,2},{3,4},{5,6},{2,1},{4,3},{6,5},{9,10},{11,12},{13,14},{10,9},... | collective-permute-start | bytes 589832 | tf_op jit(solution)/shard_map/ppermute | solution.py:67
  9.2 16.9 %copy-start = (f32[36,32,256]{2,1,0:T(8,128)}, f32[36,32,256]{2,1,0:T(8,128)S(1)}, u32[]{:S(2)}) copy-start(f32[36,32,256]{2,1,0:T(8,128)S(1)} %get-tuple-element.38.sol.sol_kept) | copy-start | bytes 3538948
  9.2 16.9 %copy-start.1 = (f32[36,32,256]{2,1,0:T(8,128)}, f32[36,32,256]{2,1,0:T(8,128)S(1)}, u32[]{:S(2)}) copy-start(f32[36,32,256]{2,1,0:T(8,128)S(1)} %get-tuple-element.39.base.refs_0_) | copy-start | bytes 3538948
  9.2 3.7 %collective-permute-start.2 = (s32[4,8]{1,0:T(4,128)S(1)}, s32[4,8]{1,0:T(4,128)S(1)}, u32[]{:S(2)}, u32[]{:S(2)}) collective-permute-start(s32[4,8]{1,0:T(4,128)S(1)} %get-tuple-element.42), channel_id=1, source_target_pairs={{0,8},{8,0},{16,24},{24,16},{1,9},{9,1},{17,25},{25,17},{2,10},{10... | collective-permute-start | bytes 392 | tf_op jit(solution)/shard_map/ppermute | solution.py:73
  12.9 2.4 %copy-start.7 = (s32[1,8]{1,0:T(1,128)S(1)}, s32[1,8]{1,0:T(1,128)}, u32[]{:S(2)}) copy-start(s32[1,8]{1,0:T(1,128)} %offsets.3) | copy-start | bytes 100
  13.0 6.8 %copy-start.8 = (bf16[4,64,512]{2,1,0:T(8,128)(2,1)S(1)}, bf16[4,64,512]{2,1,0:T(8,128)(2,1)}, u32[]{:S(2)}) copy-start(bf16[4,64,512]{2,1,0:T(8,128)(2,1)} %inverse_kept.3) | copy-start | bytes 786436
  13.0 13.1 %collective-permute-start.3 = (bf16[2,8,32,256]{3,2,1,0:T(8,128)(2,1)S(1)}, bf16[2,8,32,256]{3,2,1,0:T(8,128)(2,1)S(1)}, u32[]{:S(2)}, u32[]{:S(2)}) collective-permute-start(bf16[2,8,32,256]{3,2,1,0:T(8,128)(2,1)S(1)} %get-tuple-element.45), channel_id=1, source_target_pairs={{0,8},{16,24},{8,0},{24,16},{1,9},{17,25},{9,1},{25,17},{2,10},{18... | collective-permute-start | bytes 786440 | tf_op jit(solution)/shard_map/ppermute | solution.py:66
  14.6 11.4 %collective-permute-start.4 = (bf16[2,8,32,256]{3,2,1,0:T(8,128)(2,1)S(1)}, bf16[2,8,32,256]{3,2,1,0:T(8,128)(2,1)S(1)}, u32[]{:S(2)}, u32[]{:S(2)}) collective-permute-start(bf16[2,8,32,256]{3,2,1,0:T(8,128)(2,1)S(1)} %get-tuple-element.46), channel_id=1, source_target_pairs={{8,16},{16,8},{9,17},{17,9},{10,18},{18,10},{11,19},{19,11},{12,20... | collective-permute-start | bytes 786440 | tf_op jit(solution)/shard_map/ppermute | solution.py:67
  19.8 6.2 %collective-permute-start.6 = (bf16[4,64,512]{2,1,0:T(8,128)(2,1)S(1)}, bf16[4,64,512]{2,1,0:T(8,128)(2,1)S(1)}, u32[]{:S(2)}, u32[]{:S(2)}) collective-permute-start(bf16[4,64,512]{2,1,0:T(8,128)(2,1)S(1)} %copy-done.8), channel_id=1, source_target_pairs={{0,2},{1,3},{2,0},{3,1},{4,6},{5,7},{6,4},{7,5},{8,10},{9,11},{10,... | collective-permute-start | bytes 786440 | tf_op jit(solution)/shard_map/ppermute | solution.py:691
  20.3 5.7 %collective-permute-start.5 = (s32[4,8]{1,0:T(4,128)S(1)}, s32[4,8]{1,0:T(4,128)S(1)}, u32[]{:S(2)}, u32[]{:S(2)}) collective-permute-start(s32[4,8]{1,0:T(4,128)S(1)} %add.6), channel_id=1, source_target_pairs={{0,16},{8,24},{16,0},{24,8},{1,17},{9,25},{17,1},{25,9},{2,18},{10... | collective-permute-start | bytes 392 | tf_op jit(solution)/shard_map/ppermute | solution.py:73
  26.1 1.6 %copy-start.9 = (bf16[4,64,512]{2,1,0:T(8,128)(2,1)}, bf16[4,64,512]{2,1,0:T(8,128)(2,1)S(1)}, u32[]{:S(2)}) copy-start(bf16[4,64,512]{2,1,0:T(8,128)(2,1)S(1)} %collective-permute-done.6.partner_kept) | copy-start | bytes 786436
  27.7 10.0 %all-to-all-start = ((bf16[8,128,128]{2,1,0:T(8,128)(2,1)}), bf16[8,128,128]{2,1,0:T(8,128)(2,1)S(1)}, u32[]{:S(2)}, u32[]{:S(2)}) async-start(bf16[8,128,128]{2,1,0:T(8,128)(2,1)} %get-tuple-element.54), calls=%async_computation | async-start | bytes 524288 | tf_op jit(solution)/shard_map/all_to_all | solution.py:713
  37.7 1.6 %copy-start.3 = (bf16[1024,1024]{1,0:T(8,128)(2,1)S(1)}, bf16[1024,1024]{1,0:T(8,128)(2,1)}, u32[]{:S(2)}) copy-start(bf16[1024,1024]{1,0:T(8,128)(2,1)} %shard_map.78.spread) | copy-start | bytes 6291460
  39.3 6.2 %copy-start.5 = (f32[6,6,3,10]{3,2,1,0:T(4,128)S(1)}, f32[6,6,3,10]{3,2,1,0:T(4,128)}, u32[]{:S(2)}) copy-start(f32[6,6,3,10]{3,2,1,0:T(4,128)} %stiffness.7) | copy-start | bytes 12964
  40.7 15.4 %all-to-all-start.1 = ((bf16[32,32,128]{2,1,0:T(8,128)(2,1)}), bf16[32,32,128]{2,1,0:T(8,128)(2,1)S(1)}, u32[]{:S(2)}, u32[]{:S(2)}) async-start(bf16[32,32,128]{2,1,0:T(8,128)(2,1)} %bitcast.17), calls=%async_computation.1 | async-start | bytes 524288 | tf_op jit(solution)/shard_map/all_to_all | solution.py:722
  58.0 7.0 %collective-permute-start.7 = (bf16[2,6,32,256]{3,2,1,0:T(8,128)(2,1)S(1)}, bf16[2,6,32,256]{3,2,1,0:T(8,128)(2,1)S(1)}, u32[]{:S(2)}, u32[]{:S(2)}) collective-permute-start(bf16[2,6,32,256]{3,2,1,0:T(8,128)(2,1)S(1)} %get-tuple-element.64), channel_id=1, source_target_pairs={{0,1},{2,3},{4,5},{6,7},{1,0},{3,2},{5,4},{7,6},{8,9},{10,11},{12,... | collective-permute-start | bytes 589832 | tf_op jit(solution)/shard_map/ppermute | solution.py:66
  58.9 6.1 %collective-permute-start.8 = (bf16[2,6,32,256]{3,2,1,0:T(8,128)(2,1)S(1)}, bf16[2,6,32,256]{3,2,1,0:T(8,128)(2,1)S(1)}, u32[]{:S(2)}, u32[]{:S(2)}) collective-permute-start(bf16[2,6,32,256]{3,2,1,0:T(8,128)(2,1)S(1)} %get-tuple-element.65), channel_id=1, source_target_pairs={{1,2},{3,4},{5,6},{2,1},{4,3},{6,5},{9,10},{11,12},{13,14},{10,9},... | collective-permute-start | bytes 589832 | tf_op jit(solution)/shard_map/ppermute | solution.py:67
  62.0 11.1 %copy-start.2 = (f32[36,32,256]{2,1,0:T(8,128)}, f32[36,32,256]{2,1,0:T(8,128)S(1)}, u32[]{:S(2)}) copy-start(f32[36,32,256]{2,1,0:T(8,128)S(1)} %get-tuple-element.62.sol.sol_kept) | copy-start | bytes 3538948
  65.0 8.2 %copy-start.6 = (bf16[128,2048]{1,0:T(8,128)(2,1)S(1)}, bf16[128,2048]{1,0:T(8,128)(2,1)}, u32[]{:S(2)}) copy-start(bf16[128,2048]{1,0:T(8,128)(2,1)} %get-tuple-element.68.basis_t) | copy-start | bytes 1572868
  65.1 8.1 %collective-permute-start.9 = (bf16[2,8,32,256]{3,2,1,0:T(8,128)(2,1)S(1)}, bf16[2,8,32,256]{3,2,1,0:T(8,128)(2,1)S(1)}, u32[]{:S(2)}, u32[]{:S(2)}) collective-permute-start(bf16[2,8,32,256]{3,2,1,0:T(8,128)(2,1)S(1)} %get-tuple-element.66), channel_id=1, source_target_pairs={{0,8},{16,24},{8,0},{24,16},{1,9},{17,25},{9,1},{25,17},{2,10},{18... | collective-permute-start | bytes 786440 | tf_op jit(solution)/shard_map/ppermute | solution.py:66
  66.7 6.4 %collective-permute-start.10 = (bf16[2,8,32,256]{3,2,1,0:T(8,128)(2,1)S(1)}, bf16[2,8,32,256]{3,2,1,0:T(8,128)(2,1)S(1)}, u32[]{:S(2)}, u32[]{:S(2)}) collective-permute-start(bf16[2,8,32,256]{3,2,1,0:T(8,128)(2,1)S(1)} %get-tuple-element.67), channel_id=1, source_target_pairs={{8,16},{16,8},{9,17},{17,9},{10,18},{18,10},{11,19},{19,11},{12,20... | collective-permute-start | bytes 786440 | tf_op jit(solution)/shard_map/ppermute | solution.py:67
  73.2 12.5 %copy-start.4 = (bf16[1024,1024]{1,0:T(8,128)(2,1)S(1)}, bf16[1024,1024]{1,0:T(8,128)(2,1)}, u32[]{:S(2)}) copy-start(bf16[1024,1024]{1,0:T(8,128)(2,1)} %shard_map.78.spread) | copy-start | bytes 6291460
  87.1 15.6 %all-to-all-start.3 = ((bf16[32,32,128]{2,1,0:T(8,128)(2,1)}), bf16[32,32,128]{2,1,0:T(8,128)(2,1)S(1)}, u32[]{:S(2)}, u32[]{:S(2)}) async-start(bf16[32,32,128]{2,1,0:T(8,128)(2,1)} %bitcast.18), calls=%async_computation.3 | async-start | bytes 524288 | tf_op jit(solution)/shard_map/all_to_all | solution.py:722

commit v6 on v5

--- a/solution.py
+++ b/solution.py
@@ -243,6 +243,7 @@
     def below(kind, w):
         return jnp.where(even, first_s[kind, w].astype(f32), second_s[kind, w].astype(f32))
 
+    copies = []
     for s in range(cells_s):
         left, right = edge_cells(low, high, sol, s, cells_q)
         values = [left] + [base[s * cells_q + q] for q in range(cells_q)] + [right]
@@ -255,6 +256,8 @@
             if s == cells_s - 1:
                 value = value + below(1, w)
             local[(s + 1) * wide + w] = value.astype(bf16)
+        part = pl.ds((s + 1) * wide, wide)
+        copies.append(begun(local.at[part], local_kept.at[part], sems.at[len(copies)]))
     for s, side, place, there in (
         (0, above, 0, row > 0),
         (cells_s - 1, below, (cells_s + 1) * wide, row < rows - 1),
@@ -262,7 +265,8 @@
         near = [low(1, s)] + [sol[s * cells_q + q] for q in range(cells_q)] + [high(1, s)]
         for w in range(wide):
             local[place + w] = jnp.where(there, side(0, w) + near[w], 0.0).astype(bf16)
-    copies = [begun(local, local_kept, sems.at[0])]
+        part = pl.ds(place, wide)
+        copies.append(begun(local.at[part], local_kept.at[part], sems.at[len(copies)]))
     product = jnp.dot(
         basis_t[...], local[...].reshape(-1, columns), preferred_element_type=f32
     ).astype(bf16)
@@ -270,7 +274,7 @@
     for k in range(2):
         restricted[k] = product[:, k * half : (k + 1) * half]
     for j in range(message.shape[0]):
-        copies.append(begun(restricted.at[side_of(j)], message.at[j], sems.at[j + 1]))
+        copies.append(begun(restricted.at[side_of(j)], message.at[j], sems.at[len(copies)]))
     for copy in copies:
         copy.wait()
 
@@ -393,11 +397,10 @@
     cells_s, cells_q, _, pad, columns = shape
     sides = (0, cells_q - 1)
     copies = [begun(basis_kept, basis_p, sems.at[0]), begun(stiffness, stiff, sems.at[1])]
-    for s in range(cells_s):
-        for q in sides:
-            i = s * cells_q + q
-            copies.append(begun(sol_kept.at[i], sol.at[i], sems.at[len(copies)]))
-            copies.append(begun(base_kept.at[i], begin.at[i], sems.at[len(copies)]))
+    for q in sides:
+        copies.append(begun(sol_kept.at[:, q], sol.at[:, q], sems.at[len(copies)]))
+        copies.append(begun(base_kept.at[:, q], begin.at[:, q], sems.at[len(copies)]))
+    sol, begin = (x.reshape(cells_s * cells_q, pad, columns) for x in (sol, begin))
     chosen = coarse_values(arrived, arrived.shape[2] // 2)
     copies[0].wait()
     span = cells_q * pad
@@ -686,13 +689,11 @@
             basis_t, basis_kept, basis_p = ordered_basis(
                 cell, dims, offsets, later, (coarse, rows), (cells * pad, coarse)
             )
-            shared, _ = lax.optimization_barrier((coarse_inverse, basis_t))
+            shared, _ = lax.optimization_barrier((coarse_inverse, first))
             pairs = [(i, i ^ PARTNER) for i in range(groups)]
             partner = lax.ppermute(shared, GROUP_AXES, pairs)
             every = doubled(every, 1 << (rounds - 1))
-            first_s, second_s, every, partner = lax.optimization_barrier(
-                (first_s, second_s, every, partner)
-            )
+            first_s, second_s, every = lax.optimization_barrier((first_s, second_s, every))
         message, local = call(
             functools.partial(window_kernel, shape),
             (solution, base, first_q, second_q, first_s, second_s, basis_t if sweep == 0 else basis_kept),
@@ -703,7 +704,7 @@
             scratch=(
                 pltpu.VMEM(((cells_s + 2) * wide, pad, columns), bf16),
                 pltpu.VMEM((2, coarse, columns // 2), bf16),
-                pltpu.SemaphoreType.DMA((groups + 1,)),
+                pltpu.SemaphoreType.DMA((groups + cells_s + 2,)),
             ),
             flops=2 * rows * coarse * columns,
         )
@@ -741,15 +742,20 @@
         else:
             first, second, change = call(
                 functools.partial(step_sides_kernel, shape, layers),
-                (arrived, basis_p, *kept, stiffness),
+                (
+                    arrived,
+                    basis_p,
+                    *(x.reshape(cells_s, cells_q, pad, columns) for x in kept),
+                    stiffness,
+                ),
                 (column_message, column_message, field),
                 scratch=(
                     pltpu.VMEM(basis_p.shape, bf16),
                     pltpu.VMEM(stiffness.shape, f32),
+                    pltpu.VMEM((cells_s, cells_q, pad, columns), f32),
+                    pltpu.VMEM((cells_s, cells_q, pad, columns), f32),
                     pltpu.VMEM(field.shape, f32),
-                    pltpu.VMEM(field.shape, f32),
-                    pltpu.VMEM(field.shape, f32),
-                    pltpu.SemaphoreType.DMA((4 * cells_s + 2,)),
+                    pltpu.SemaphoreType.DMA((6,)),
                 ),
                 held=(1, 2, 3, 4),
             )

time: 107 us -> 105 us (0.981)
  starting transfers between devices: 29.6 us -> 28.1 us
    ppermute x2, starting transfers between devices: 5.47 us -> 1.88 us  [doubled(): lax.ppermute(held, 'sub', [(i, i ^ step) for i in range(count)])]
    ppermute x4, starting transfers between devices: 7.19 us -> 10 us  [swap(): lax.ppermute(first, axis, even + [(b, a) for a, b in even])]
  transfers between devices with their start and end apart: 14 -> 14, of which waited for: 7 -> 8; matrix products, arithmetic and copies ran while one was open for 0% -> 0% of each run, Pallas kernels for 27% -> 28%
where the time goes in v6:
time: 105 us; the launch traced here: 104 us
  Pallas kernels  40.5 us (39%)
  starting transfers between devices  28.1 us (27%)
  waiting for transfers between devices  21.6 us (21%)
  blocking collectives  11 us (10%)
  local copies, waits for them, and re-layouts  2.31 us (2%)
    pallas_call x13, Pallas kernels, call(): pl.pallas_call(body, out_shape=tuple(outs), in_specs=[HBM if i in held el...  31.5 us
    all_to_all x1, blocking collectives, shards(): gathered = lax.all_to_all(message, GROUP_AXES, 0, 0, tiled=True)  11 us
    ppermute x4, starting transfers between devices, swap(): lax.ppermute(first, axis, even + [(b, a) for a, b in even])  10 us
    all_to_all x2, starting transfers between devices, shards(): lax.all_to_all(terms.reshape(n_sub * groups, 2 * depth, columns // 2), AL...  9.46 us
    ppermute x4, waiting for transfers between devices, swap(): lax.ppermute(first, axis, even + [(b, a) for a, b in even])  8.62 us
    all_to_all x2, waiting for transfers between devices, shards(): lax.all_to_all(terms.reshape(n_sub * groups, 2 * depth, columns // 2), AL...  8.22 us
    pallas_call x1, Pallas kernels, spread_inverse(): pl.pallas_call(functools.partial(spread_kernel, (groups, depth, kgroup)),...  4.5 us
    pallas_call x1, Pallas kernels, ordered_basis(): pl.pallas_call(functools.partial(basis_kernel, cell, dims), out_shape=(ja...  4.48 us
  transfers between devices with their start and end apart: 14, of which 8 were waited for; matrix products, arithmetic and copies ran while one was open for 0% of the time, Pallas kernels for 28%

profile of v6, /device:TPU:0, one launch (start us, length us, event | category | flops | bytes accessed | tf_op | source)
XLA Modules:
  0.0 103.9 jit_solution(9283467772990043078)
XLA Ops:
  0.0 2.0 %shard_map.74 = (bf16[2,6,32,256]{3,2,1,0:T(8,128)(2,1)S(1)}, bf16[2,6,32,256]{3,2,1,0:T(8,128)(2,1)S(1)}) custom-call(f32[6,6,10,3,256]{4,3,2,1,0:T(4,128)} %bitcast.15, f32[6,6,10,3,256]{4,3,2,1,0:T(4,128)} %bitcast.17, f32[6,6,3,10]{3,2,1,0:T(4,128)} %stiffness.7), custom_call_target="tpu_custom_call" | custom-call | bytes 2609376 | tf_op jit(solution)/shard_map/pallas_call | solution.py:27
  2.0 3.0 %collective-permute-start = (bf16[2,6,32,256]{3,2,1,0:T(8,128)(2,1)S(1)}, bf16[2,6,32,256]{3,2,1,0:T(8,128)(2,1)S(1)}, u32[]{:S(2)}, u32[]{:S(2)}) collective-permute-start(bf16[2,6,32,256]{3,2,1,0:T(8,128)(2,1)S(1)} %get-tuple-element.39), channel_id=1, source_target_pairs={{0,1},{2,3},{4,5},{6,7},{1,0},{3,2},{5,4},{7,6},{8,9},{10,11},{12,... | collective-permute-start | bytes 589832 | tf_op jit(solution)/shard_map/ppermute | solution.py:66
  5.7 3.5 %shard_map.73 = (f32[36,32,256]{2,1,0:T(8,128)S(1)}, f32[36,32,256]{2,1,0:T(8,128)S(1)}, s32[4,8]{1,0:T(4,128)S(1)}) custom-call(f32[6,6,10,3,256]{4,3,2,1,0:T(4,128)} %bitcast.16, f32[6,6,10,3,256]{4,3,2,1,0:T(4,128)} %bitcast.18, f32[6,6,3,10]{3,2,1,0:T(4,128)} %stiffness.7, s32[1,8]{1,0:T(1,128)} %offsets.3), custom_call_target="tpu_custom_call" | custom-call | bytes 4575616 | tf_op jit(solution)/shard_map/pallas_call | solution.py:27
  9.2 1.6 %collective-permute-start.2 = (s32[4,8]{1,0:T(4,128)S(1)}, s32[4,8]{1,0:T(4,128)S(1)}, u32[]{:S(2)}, u32[]{:S(2)}) collective-permute-start(s32[4,8]{1,0:T(4,128)S(1)} %get-tuple-element.41), channel_id=1, source_target_pairs={{0,8},{8,0},{16,24},{24,16},{1,9},{9,1},{17,25},{25,17},{2,10},{10... | collective-permute-start | bytes 392 | tf_op jit(solution)/shard_map/ppermute | solution.py:73
  10.9 2.0 %collective-permute-done.2 = s32[4,8]{1,0:T(4,128)S(1)} collective-permute-done((s32[4,8]{1,0:T(4,128)S(1)}, s32[4,8]{1,0:T(4,128)S(1)}, u32[]{:S(2)}, u32[]{:S(2)}) %collective-permute-start.2) | collective-permute-done | bytes 160 | tf_op jit(solution)/shard_map/ppermute | solution.py:73
  13.0 0.7 collective-permute-start.4
  13.7 4.4 %collective-permute-start.3 = (bf16[2,8,32,256]{3,2,1,0:T(8,128)(2,1)S(1)}, bf16[2,8,32,256]{3,2,1,0:T(8,128)(2,1)S(1)}, u32[]{:S(2)}, u32[]{:S(2)}) collective-permute-start(bf16[2,8,32,256]{3,2,1,0:T(8,128)(2,1)S(1)} %get-tuple-element.44), channel_id=1, source_target_pairs={{0,8},{16,24},{8,0},{24,16},{1,9},{17,25},{9,1},{25,17},{2,10},{18... | collective-permute-start | bytes 786440 | tf_op jit(solution)/shard_map/ppermute | solution.py:66
  18.5 4.5 %shard_map.76 = (bf16[128,2048]{1,0:T(8,128)(2,1)S(1)}, bf16[128,2048]{1,0:T(8,128)(2,1)}, bf16[1152,128]{1,0:T(8,128)(2,1)}) custom-call(s32[1,8]{1,0:T(1,128)S(1)} %copy-done.7, bf16[1,1920,128]{2,1,0:T(8,128)(2,1)} %basis_kept), custom_call_target="tpu_custom_call" | custom-call | flops 402653184 | bytes 1474560 | tf_op jit(solution)/shard_map/pallas_call | solution.py:512
  23.0 1.9 %collective-permute-done.5 = s32[4,8]{1,0:T(4,128)S(1)} collective-permute-done((s32[4,8]{1,0:T(4,128)S(1)}, s32[4,8]{1,0:T(4,128)S(1)}, u32[]{:S(2)}, u32[]{:S(2)}) %collective-permute-start.5) | collective-permute-done | bytes 160 | tf_op jit(solution)/shard_map/ppermute | solution.py:73
  25.1 1.4 %shard_map.77 = (bf16[8,128,128]{2,1,0:T(8,128)(2,1)}, bf16[64,32,256]{2,1,0:T(8,128)(2,1)}) custom-call(f32[36,32,256]{2,1,0:T(8,128)S(1)} %get-tuple-element.37.sol.sol_kept, f32[36,32,256]{2,1,0:T(8,128)S(1)} %get-tuple-element.38.base.refs_0_, bf16[2,6,32,256]{3,2,1,0:T(8,128)(2,1)S(1)} %collective-permute-done.first_in.first_q, ...), custom_call_target="tpu_custom_call" | custom-call | flops 134217728 | bytes 5111808 | tf_op jit(solution)/shard_map/pallas_call | solution.py:27
  26.5 3.8 %all-to-all-start = ((bf16[8,128,128]{2,1,0:T(8,128)(2,1)}), bf16[8,128,128]{2,1,0:T(8,128)(2,1)S(1)}, u32[]{:S(2)}, u32[]{:S(2)}) async-start(bf16[8,128,128]{2,1,0:T(8,128)(2,1)} %get-tuple-element.52), calls=%async_computation | async-start | bytes 524288 | tf_op jit(solution)/shard_map/all_to_all | solution.py:714
  30.9 4.5 %shard_map.78.spread = bf16[1024,1024]{1,0:T(8,128)(2,1)} custom-call(s32[4,8]{1,0:T(4,128)S(1)} %add.7.every, bf16[4,64,512]{2,1,0:T(8,128)(2,1)} %inverse_kept.3, bf16[4,64,512]{2,1,0:T(8,128)(2,1)} %copy-done.9), custom_call_target="tpu_custom_call" | custom-call | flops 1073741824 | bytes 2097152 | tf_op jit(solution)/shard_map/pallas_call | solution.py:592
  35.5 0.8 all-to-all-done
  36.3 1.6 %copy-done.3 = bf16[1024,1024]{1,0:T(8,128)(2,1)S(1)} copy-done((bf16[1024,1024]{1,0:T(8,128)(2,1)S(1)}, bf16[1024,1024]{1,0:T(8,128)(2,1)}, u32[]{:S(2)}) %copy-start.3) | copy-done | bytes 2097176
  37.9 1.4 %shard_map.79 = bf16[1024,128]{1,0:T(8,128)(2,1)} custom-call(bf16[1024,1024]{1,0:T(8,128)(2,1)S(1)} %copy-done.3, bf16[1024,128]{1,0:T(8,128)(2,1)S(1)} %bitcast.12), custom_call_target="tpu_custom_call" | custom-call | flops 268435456 | bytes 2621440 | tf_op jit(solution)/shard_map/pallas_call | solution.py:27
  39.3 4.6 %all-to-all-start.1 = ((bf16[32,32,128]{2,1,0:T(8,128)(2,1)}), bf16[32,32,128]{2,1,0:T(8,128)(2,1)S(1)}, u32[]{:S(2)}, u32[]{:S(2)}) async-start(bf16[32,32,128]{2,1,0:T(8,128)(2,1)} %bitcast.21), calls=%async_computation.1 | async-start | bytes 524288 | tf_op jit(solution)/shard_map/all_to_all | solution.py:723
  43.9 7.1 %shard_map.80 = (f32[36,32,256]{2,1,0:T(8,128)}, f32[36,32,256]{2,1,0:T(8,128)}) custom-call(bf16[64,32,256]{2,1,0:T(8,128)(2,1)} %get-tuple-element.56.local_kept, bf16[1,1920,1920]{2,1,0:T(8,128)(2,1)} %inverse_kept.5, f32[36,32,256]{2,1,0:T(8,128)} %copy-done, f32[36,32,256]{2,1,0:T(8,128)} %copy-done.1, f32[6,6,3,10]{3,2,1,0:T(4,128)S(1)} %copy-done.5), custom_call_target="tpu_custom_call" | custom-call | flops 1415577600 | bytes 13144288 | tf_op jit(solution)/shard_map/pallas_call | solution.py:27
  51.0 3.6 %all-to-all-done.1 = bf16[32,32,128]{2,1,0:T(8,128)(2,1)S(1)} async-done(((bf16[32,32,128]{2,1,0:T(8,128)(2,1)}), bf16[32,32,128]{2,1,0:T(8,128)(2,1)S(1)}, u32[]{:S(2)}, u32[]{:S(2)}) %all-to-all-start.1) | async-done | bytes 262176 | tf_op jit(solution)/shard_map/all_to_all | solution.py:723
  54.6 1.7 %shard_map.81 = (bf16[2,6,32,256]{3,2,1,0:T(8,128)(2,1)S(1)}, bf16[2,6,32,256]{3,2,1,0:T(8,128)(2,1)S(1)}, f32[36,32,256]{2,1,0:T(8,128)S(1)}) custom-call(bf16[4,8,32,128]{3,2,1,0:T(8,128)(2,1)S(1)} %bitcast.11, bf16[1152,128]{1,0:T(8,128)(2,1)} %get-tuple-element.55.basis_kept, f32[6,6,32,256]{3,2,1,0:T(8,128)} %bitcast.19, f32[6,6,32,256]{3,2,1,0:T(8,128)} %bitcast.20, ...), custom_call_target="tpu_custom_call" | custom-call | bytes 4493536 | tf_op jit(solution)/shard_map/pallas_call | solution.py:27
  56.3 0.9 collective-permute-start.7
  57.8 2.5 %shard_map.82 = (f32[36,32,256]{2,1,0:T(8,128)S(1)}, f32[36,32,256]{2,1,0:T(8,128)S(1)}) custom-call(f32[36,32,256]{2,1,0:T(8,128)S(1)} %get-tuple-element.59.coarse, f32[36,32,256]{2,1,0:T(8,128)} %get-tuple-element.57.sol_kept, f32[36,32,256]{2,1,0:T(8,128)} %get-tuple-element.58.base_kept, f32[6,6,3,10]{3,2,1,0:T(4,128)} %stiffness.7), custom_call_target="tpu_custom_call" | custom-call | bytes 5902560 | tf_op jit(solution)/shard_map/pallas_call | solution.py:27
  60.3 2.9 %collective-permute-done.7.first_in.first_q = bf16[2,6,32,256]{3,2,1,0:T(8,128)(2,1)S(1)} collective-permute-done((bf16[2,6,32,256]{3,2,1,0:T(8,128)(2,1)S(1)}, bf16[2,6,32,256]{3,2,1,0:T(8,128)(2,1)S(1)}, u32[]{:S(2)}, u32[]{:S(2)}) %collective-permute-start.7) | collective-permute-done | bytes 196640 | tf_op jit(solution)/shard_map/ppermute | solution.py:66
  63.3 1.7 %collective-permute-start.9 = (bf16[2,8,32,256]{3,2,1,0:T(8,128)(2,1)S(1)}, bf16[2,8,32,256]{3,2,1,0:T(8,128)(2,1)S(1)}, u32[]{:S(2)}, u32[]{:S(2)}) collective-permute-start(bf16[2,8,32,256]{3,2,1,0:T(8,128)(2,1)S(1)} %get-tuple-element.64), channel_id=1, source_target_pairs={{0,8},{16,24},{8,0},{24,16},{1,9},{17,25},{9,1},{25,17},{2,10},{18... | collective-permute-start | bytes 786440 | tf_op jit(solution)/shard_map/ppermute | solution.py:66
  65.0 0.8 collective-permute-start.10
  65.8 5.6 %collective-permute-done.9.first_s = bf16[2,8,32,256]{3,2,1,0:T(8,128)(2,1)S(1)} collective-permute-done((bf16[2,8,32,256]{3,2,1,0:T(8,128)(2,1)S(1)}, bf16[2,8,32,256]{3,2,1,0:T(8,128)(2,1)S(1)}, u32[]{:S(2)}, u32[]{:S(2)}) %collective-permute-start.9) | collective-permute-done | bytes 262176 | tf_op jit(solution)/shard_map/ppermute | solution.py:66
  71.4 1.4 %shard_map.84 = (bf16[8,128,128]{2,1,0:T(8,128)(2,1)}, bf16[64,32,256]{2,1,0:T(8,128)(2,1)}) custom-call(f32[36,32,256]{2,1,0:T(8,128)S(1)} %get-tuple-element.60.sol.sol_kept, f32[36,32,256]{2,1,0:T(8,128)S(1)} %get-tuple-element.61.base, bf16[2,6,32,256]{3,2,1,0:T(8,128)(2,1)S(1)} %collective-permute-done.7.first_in.first_q, ...), custom_call_target="tpu_custom_call" | custom-call | flops 134217728 | bytes 5111808 | tf_op jit(solution)/shard_map/pallas_call | solution.py:27
  72.8 11.0 %all_to_all.20 = bf16[8,128,128]{2,1,0:T(8,128)(2,1)S(1)} all-to-all(bf16[8,128,128]{2,1,0:T(8,128)(2,1)} %get-tuple-element.67), channel_id=1, replica_groups=mesh['sub'=4,'crow'=4,'ccol'=2] {'crow','ccol'}, dimensions={0} | all-to-all | bytes 524288 | tf_op jit(solution)/shard_map/all_to_all | solution.py:714
  83.8 1.4 %shard_map.85 = bf16[1024,128]{1,0:T(8,128)(2,1)} custom-call(bf16[1024,1024]{1,0:T(8,128)(2,1)S(1)} %copy-done.4, bf16[1024,128]{1,0:T(8,128)(2,1)S(1)} %bitcast.14), custom_call_target="tpu_custom_call" | custom-call | flops 268435456 | bytes 2621440 | tf_op jit(solution)/shard_map/pallas_call | solution.py:27
  85.2 4.9 %all-to-all-start.3 = ((bf16[32,32,128]{2,1,0:T(8,128)(2,1)}), bf16[32,32,128]{2,1,0:T(8,128)(2,1)S(1)}, u32[]{:S(2)}, u32[]{:S(2)}) async-start(bf16[32,32,128]{2,1,0:T(8,128)(2,1)} %bitcast.22), calls=%async_computation.3 | async-start | bytes 524288 | tf_op jit(solution)/shard_map/all_to_all | solution.py:723
  90.2 6.1 %shard_map.86.sol_kept = f32[36,32,256]{2,1,0:T(8,128)} custom-call(bf16[64,32,256]{2,1,0:T(8,128)(2,1)} %get-tuple-element.68.local_kept, bf16[1,1920,1920]{2,1,0:T(8,128)(2,1)} %inverse_kept.5, f32[36,32,256]{2,1,0:T(8,128)} %copy-done.2), custom_call_target="tpu_custom_call" | custom-call | flops 1415577600 | bytes 10780672 | tf_op jit(solution)/shard_map/pallas_call | solution.py:27
  96.2 4.6 %all-to-all-done.3 = bf16[32,32,128]{2,1,0:T(8,128)(2,1)S(1)} async-done(((bf16[32,32,128]{2,1,0:T(8,128)(2,1)}), bf16[32,32,128]{2,1,0:T(8,128)(2,1)S(1)}, u32[]{:S(2)}, u32[]{:S(2)}) %all-to-all-start.3) | async-done | bytes 262176 | tf_op jit(solution)/shard_map/all_to_all | solution.py:723
  100.8 2.9 %shard_map.87 = f32[6,6,10,3,256]{4,3,2,1,0:T(4,128)} custom-call(bf16[4,8,32,128]{3,2,1,0:T(8,128)(2,1)S(1)} %bitcast.13, bf16[1152,128]{1,0:T(8,128)(2,1)} %get-tuple-element.55.basis_kept, f32[36,32,256]{2,1,0:T(8,128)} %shard_map.86.sol_kept), custom_call_target="tpu_custom_call" | custom-call | bytes 2842624 | tf_op jit(solution)/shard_map/pallas_call | solution.py:27
  (34 shorter events, 2.7 us)
Async XLA Ops:
  2.0 10.8 %collective-permute-start = (bf16[2,6,32,256]{3,2,1,0:T(8,128)(2,1)S(1)}, bf16[2,6,32,256]{3,2,1,0:T(8,128)(2,1)S(1)}, u32[]{:S(2)}, u32[]{:S(2)}) collective-permute-start(bf16[2,6,32,256]{3,2,1,0:T(8,128)(2,1)S(1)} %get-tuple-element.39), channel_id=1, source_target_pairs={{0,1},{2,3},{4,5},{6,7},{1,0},{3,2},{5,4},{7,6},{8,9},{10,11},{12,... | collective-permute-start | bytes 589832 | tf_op jit(solution)/shard_map/ppermute | solution.py:66
  5.1 7.8 %collective-permute-start.1 = (bf16[2,6,32,256]{3,2,1,0:T(8,128)(2,1)S(1)}, bf16[2,6,32,256]{3,2,1,0:T(8,128)(2,1)S(1)}, u32[]{:S(2)}, u32[]{:S(2)}) collective-permute-start(bf16[2,6,32,256]{3,2,1,0:T(8,128)(2,1)S(1)} %get-tuple-element.40), channel_id=1, source_target_pairs={{1,2},{3,4},{5,6},{2,1},{4,3},{6,5},{9,10},{11,12},{13,14},{10,9},... | collective-permute-start | bytes 589832 | tf_op jit(solution)/shard_map/ppermute | solution.py:67
  9.2 15.9 %copy-start = (f32[36,32,256]{2,1,0:T(8,128)}, f32[36,32,256]{2,1,0:T(8,128)S(1)}, u32[]{:S(2)}) copy-start(f32[36,32,256]{2,1,0:T(8,128)S(1)} %get-tuple-element.37.sol.sol_kept) | copy-start | bytes 3538948
  9.2 15.9 %copy-start.1 = (f32[36,32,256]{2,1,0:T(8,128)}, f32[36,32,256]{2,1,0:T(8,128)S(1)}, u32[]{:S(2)}) copy-start(f32[36,32,256]{2,1,0:T(8,128)S(1)} %get-tuple-element.38.base.refs_0_) | copy-start | bytes 3538948
  9.2 3.7 %collective-permute-start.2 = (s32[4,8]{1,0:T(4,128)S(1)}, s32[4,8]{1,0:T(4,128)S(1)}, u32[]{:S(2)}, u32[]{:S(2)}) collective-permute-start(s32[4,8]{1,0:T(4,128)S(1)} %get-tuple-element.41), channel_id=1, source_target_pairs={{0,8},{8,0},{16,24},{24,16},{1,9},{9,1},{17,25},{25,17},{2,10},{10... | collective-permute-start | bytes 392 | tf_op jit(solution)/shard_map/ppermute | solution.py:73
  12.9 5.3 %copy-start.8 = (bf16[4,64,512]{2,1,0:T(8,128)(2,1)S(1)}, bf16[4,64,512]{2,1,0:T(8,128)(2,1)}, u32[]{:S(2)}) copy-start(bf16[4,64,512]{2,1,0:T(8,128)(2,1)} %inverse_kept.3) | copy-start | bytes 786436
  12.9 5.6 %copy-start.7 = (s32[1,8]{1,0:T(1,128)S(1)}, s32[1,8]{1,0:T(1,128)}, u32[]{:S(2)}) copy-start(s32[1,8]{1,0:T(1,128)} %offsets.3) | copy-start | bytes 100
  13.0 12.0 %collective-permute-start.4 = (bf16[2,8,32,256]{3,2,1,0:T(8,128)(2,1)S(1)}, bf16[2,8,32,256]{3,2,1,0:T(8,128)(2,1)S(1)}, u32[]{:S(2)}, u32[]{:S(2)}) collective-permute-start(bf16[2,8,32,256]{3,2,1,0:T(8,128)(2,1)S(1)} %get-tuple-element.45), channel_id=1, source_target_pairs={{8,16},{16,8},{9,17},{17,9},{10,18},{18,10},{11,19},{19,11},{12,20... | collective-permute-start | bytes 786440 | tf_op jit(solution)/shard_map/ppermute | solution.py:67
  13.7 11.4 %collective-permute-start.3 = (bf16[2,8,32,256]{3,2,1,0:T(8,128)(2,1)S(1)}, bf16[2,8,32,256]{3,2,1,0:T(8,128)(2,1)S(1)}, u32[]{:S(2)}, u32[]{:S(2)}) collective-permute-start(bf16[2,8,32,256]{3,2,1,0:T(8,128)(2,1)S(1)} %get-tuple-element.44), channel_id=1, source_target_pairs={{0,8},{16,24},{8,0},{24,16},{1,9},{17,25},{9,1},{25,17},{2,10},{18... | collective-permute-start | bytes 786440 | tf_op jit(solution)/shard_map/ppermute | solution.py:66
  18.1 12.1 %collective-permute-start.6 = (bf16[4,64,512]{2,1,0:T(8,128)(2,1)S(1)}, bf16[4,64,512]{2,1,0:T(8,128)(2,1)S(1)}, u32[]{:S(2)}, u32[]{:S(2)}) collective-permute-start(bf16[4,64,512]{2,1,0:T(8,128)(2,1)S(1)} %copy-done.8), channel_id=1, source_target_pairs={{0,2},{1,3},{2,0},{3,1},{4,6},{5,7},{6,4},{7,5},{8,10},{9,11},{10,... | collective-permute-start | bytes 786440 | tf_op jit(solution)/shard_map/ppermute | solution.py:694
  18.3 6.7 %collective-permute-start.5 = (s32[4,8]{1,0:T(4,128)S(1)}, s32[4,8]{1,0:T(4,128)S(1)}, u32[]{:S(2)}, u32[]{:S(2)}) collective-permute-start(s32[4,8]{1,0:T(4,128)S(1)} %add.6), channel_id=1, source_target_pairs={{0,16},{8,24},{16,0},{24,8},{1,17},{9,25},{17,1},{25,9},{2,18},{10... | collective-permute-start | bytes 392 | tf_op jit(solution)/shard_map/ppermute | solution.py:73
  26.5 9.8 %all-to-all-start = ((bf16[8,128,128]{2,1,0:T(8,128)(2,1)}), bf16[8,128,128]{2,1,0:T(8,128)(2,1)S(1)}, u32[]{:S(2)}, u32[]{:S(2)}) async-start(bf16[8,128,128]{2,1,0:T(8,128)(2,1)} %get-tuple-element.52), calls=%async_computation | async-start | bytes 524288 | tf_op jit(solution)/shard_map/all_to_all | solution.py:714
  30.3 0.7 copy-start.9
  36.3 1.6 %copy-start.3 = (bf16[1024,1024]{1,0:T(8,128)(2,1)S(1)}, bf16[1024,1024]{1,0:T(8,128)(2,1)}, u32[]{:S(2)}) copy-start(bf16[1024,1024]{1,0:T(8,128)(2,1)} %shard_map.78.spread) | copy-start | bytes 6291460
  37.9 6.0 %copy-start.5 = (f32[6,6,3,10]{3,2,1,0:T(4,128)S(1)}, f32[6,6,3,10]{3,2,1,0:T(4,128)}, u32[]{:S(2)}) copy-start(f32[6,6,3,10]{3,2,1,0:T(4,128)} %stiffness.7) | copy-start | bytes 12964
  39.3 15.3 %all-to-all-start.1 = ((bf16[32,32,128]{2,1,0:T(8,128)(2,1)}), bf16[32,32,128]{2,1,0:T(8,128)(2,1)S(1)}, u32[]{:S(2)}, u32[]{:S(2)}) async-start(bf16[32,32,128]{2,1,0:T(8,128)(2,1)} %bitcast.21), calls=%async_computation.1 | async-start | bytes 524288 | tf_op jit(solution)/shard_map/all_to_all | solution.py:723
  56.3 7.0 %collective-permute-start.7 = (bf16[2,6,32,256]{3,2,1,0:T(8,128)(2,1)S(1)}, bf16[2,6,32,256]{3,2,1,0:T(8,128)(2,1)S(1)}, u32[]{:S(2)}, u32[]{:S(2)}) collective-permute-start(bf16[2,6,32,256]{3,2,1,0:T(8,128)(2,1)S(1)} %get-tuple-element.62), channel_id=1, source_target_pairs={{0,1},{2,3},{4,5},{6,7},{1,0},{3,2},{5,4},{7,6},{8,9},{10,11},{12,... | collective-permute-start | bytes 589832 | tf_op jit(solution)/shard_map/ppermute | solution.py:66
  57.1 6.1 %collective-permute-start.8 = (bf16[2,6,32,256]{3,2,1,0:T(8,128)(2,1)S(1)}, bf16[2,6,32,256]{3,2,1,0:T(8,128)(2,1)S(1)}, u32[]{:S(2)}, u32[]{:S(2)}) collective-permute-start(bf16[2,6,32,256]{3,2,1,0:T(8,128)(2,1)S(1)} %get-tuple-element.63), channel_id=1, source_target_pairs={{1,2},{3,4},{5,6},{2,1},{4,3},{6,5},{9,10},{11,12},{13,14},{10,9},... | collective-permute-start | bytes 589832 | tf_op jit(solution)/shard_map/ppermute | solution.py:67
  60.3 11.1 %copy-start.2 = (f32[36,32,256]{2,1,0:T(8,128)}, f32[36,32,256]{2,1,0:T(8,128)S(1)}, u32[]{:S(2)}) copy-start(f32[36,32,256]{2,1,0:T(8,128)S(1)} %get-tuple-element.60.sol.sol_kept) | copy-start | bytes 3538948
  63.2 8.2 %copy-start.6 = (bf16[128,2048]{1,0:T(8,128)(2,1)S(1)}, bf16[128,2048]{1,0:T(8,128)(2,1)}, u32[]{:S(2)}) copy-start(bf16[128,2048]{1,0:T(8,128)(2,1)} %get-tuple-element.66.basis_t) | copy-start | bytes 1572868
  63.3 8.1 %collective-permute-start.9 = (bf16[2,8,32,256]{3,2,1,0:T(8,128)(2,1)S(1)}, bf16[2,8,32,256]{3,2,1,0:T(8,128)(2,1)S(1)}, u32[]{:S(2)}, u32[]{:S(2)}) collective-permute-start(bf16[2,8,32,256]{3,2,1,0:T(8,128)(2,1)S(1)} %get-tuple-element.64), channel_id=1, source_target_pairs={{0,8},{16,24},{8,0},{24,16},{1,9},{17,25},{9,1},{25,17},{2,10},{18... | collective-permute-start | bytes 786440 | tf_op jit(solution)/shard_map/ppermute | solution.py:66
  65.0 6.4 %collective-permute-start.10 = (bf16[2,8,32,256]{3,2,1,0:T(8,128)(2,1)S(1)}, bf16[2,8,32,256]{3,2,1,0:T(8,128)(2,1)S(1)}, u32[]{:S(2)}, u32[]{:S(2)}) collective-permute-start(bf16[2,8,32,256]{3,2,1,0:T(8,128)(2,1)S(1)} %get-tuple-element.65), channel_id=1, source_target_pairs={{8,16},{16,8},{9,17},{17,9},{10,18},{18,10},{11,19},{19,11},{12,20... | collective-permute-start | bytes 786440 | tf_op jit(solution)/shard_map/ppermute | solution.py:67
  71.4 12.4 %copy-start.4 = (bf16[1024,1024]{1,0:T(8,128)(2,1)S(1)}, bf16[1024,1024]{1,0:T(8,128)(2,1)}, u32[]{:S(2)}) copy-start(bf16[1024,1024]{1,0:T(8,128)(2,1)} %shard_map.78.spread) | copy-start | bytes 6291460
  85.2 15.6 %all-to-all-start.3 = ((bf16[32,32,128]{2,1,0:T(8,128)(2,1)}), bf16[32,32,128]{2,1,0:T(8,128)(2,1)S(1)}, u32[]{:S(2)}, u32[]{:S(2)}) async-start(bf16[32,32,128]{2,1,0:T(8,128)(2,1)} %bitcast.22), calls=%async_computation.3 | async-start | bytes 524288 | tf_op jit(solution)/shard_map/all_to_all | solution.py:723

commit v7 on v6

--- a/solution.py
+++ b/solution.py
@@ -576,8 +576,16 @@
                 for j in range(groups):
                     at = t * span + (2 * j + b) * depth
                     picked[at : at + depth, :] = part[j * depth : (j + 1) * depth]
-        out[...] = jnp.dot(picked[...], columns[...], preferred_element_type=f32).astype(bf16)
-        begun(out, out_kept.at[pl.ds(k * size * span, size * span)], sems.at[2]).wait()
+        results = []
+        for t in range(size):
+            part = pl.ds(t * span, span)
+            out[part, :] = jnp.dot(
+                picked[part, :], columns[...], preferred_element_type=f32
+            ).astype(bf16)
+            there = pl.ds((k * size + t) * span, span)
+            results.append(begun(out.at[part], out_kept.at[there], sems.at[2 + t]))
+        for copy in results:
+            copy.wait()
         return 0
 
     lax.fori_loop(0, steps, some, 0)
@@ -599,7 +607,7 @@
             pltpu.VMEM((kgroup, groups * coarse), bf16),
             pltpu.VMEM((part, kgroup), bf16),
             pltpu.VMEM((part, groups * coarse), bf16),
-            pltpu.SemaphoreType.DMA((3,)),
+            pltpu.SemaphoreType.DMA((2 + part // (2 * coarse),)),
         ],
         compiler_params=pltpu.CompilerParams(
             vmem_limit_bytes=(16 << 20) + 4 * coarse_inverse.size + 8 * part * groups * coarse

time: 105 us -> 104 us (level)
  no operation moved by 1% of the time
where the time goes in v7:
time: 104 us; the launch traced here: 103 us
  Pallas kernels  40 us (38%)
  starting transfers between devices  27.6 us (27%)
  waiting for transfers between devices  22.2 us (21%)
  blocking collectives  11 us (11%)
  local copies, waits for them, and re-layouts  2.31 us (2%)
    pallas_call x13, Pallas kernels, call(): pl.pallas_call(body, out_shape=tuple(outs), in_specs=[HBM if i in held el...  31.5 us
    all_to_all x1, blocking collectives, shards(): gathered = lax.all_to_all(message, GROUP_AXES, 0, 0, tiled=True)  11 us
    ppermute x4, starting transfers between devices, swap(): lax.ppermute(first, axis, even + [(b, a) for a, b in even])  10 us
    all_to_all x2, starting transfers between devices, shards(): lax.all_to_all(terms.reshape(n_sub * groups, 2 * depth, columns // 2), AL...  8.94 us
    ppermute x4, waiting for transfers between devices, swap(): lax.ppermute(first, axis, even + [(b, a) for a, b in even])  8.63 us
    all_to_all x2, waiting for transfers between devices, shards(): lax.all_to_all(terms.reshape(n_sub * groups, 2 * depth, columns // 2), AL...  8.22 us
    pallas_call x1, Pallas kernels, ordered_basis(): pl.pallas_call(functools.partial(basis_kernel, cell, dims), out_shape=(ja...  4.48 us
    pallas_call x1, Pallas kernels, spread_inverse(): pl.pallas_call(functools.partial(spread_kernel, (groups, depth, kgroup)),...  3.98 us
  transfers between devices with their start and end apart: 14, of which 8 were waited for; matrix products, arithmetic and copies ran while one was open for 0% of the time, Pallas kernels for 28%

profile of v7, /device:TPU:0, one launch (start us, length us, event | category | flops | bytes accessed | tf_op | source)
XLA Modules:
  0.0 103.4 jit_solution(10845138648901156452)
XLA Ops:
  0.0 2.0 %shard_map.74 = (bf16[2,6,32,256]{3,2,1,0:T(8,128)(2,1)S(1)}, bf16[2,6,32,256]{3,2,1,0:T(8,128)(2,1)S(1)}) custom-call(f32[6,6,10,3,256]{4,3,2,1,0:T(4,128)} %bitcast.15, f32[6,6,10,3,256]{4,3,2,1,0:T(4,128)} %bitcast.17, f32[6,6,3,10]{3,2,1,0:T(4,128)} %stiffness.7), custom_call_target="tpu_custom_call" | custom-call | bytes 2609376 | tf_op jit(solution)/shard_map/pallas_call | solution.py:27
  2.0 3.0 %collective-permute-start = (bf16[2,6,32,256]{3,2,1,0:T(8,128)(2,1)S(1)}, bf16[2,6,32,256]{3,2,1,0:T(8,128)(2,1)S(1)}, u32[]{:S(2)}, u32[]{:S(2)}) collective-permute-start(bf16[2,6,32,256]{3,2,1,0:T(8,128)(2,1)S(1)} %get-tuple-element.39), channel_id=1, source_target_pairs={{0,1},{2,3},{4,5},{6,7},{1,0},{3,2},{5,4},{7,6},{8,9},{10,11},{12,... | collective-permute-start | bytes 589832 | tf_op jit(solution)/shard_map/ppermute | solution.py:66
  5.7 3.5 %shard_map.73 = (f32[36,32,256]{2,1,0:T(8,128)S(1)}, f32[36,32,256]{2,1,0:T(8,128)S(1)}, s32[4,8]{1,0:T(4,128)S(1)}) custom-call(f32[6,6,10,3,256]{4,3,2,1,0:T(4,128)} %bitcast.16, f32[6,6,10,3,256]{4,3,2,1,0:T(4,128)} %bitcast.18, f32[6,6,3,10]{3,2,1,0:T(4,128)} %stiffness.7, s32[1,8]{1,0:T(1,128)} %offsets.3), custom_call_target="tpu_custom_call" | custom-call | bytes 4575616 | tf_op jit(solution)/shard_map/pallas_call | solution.py:27
  9.2 1.6 %collective-permute-start.2 = (s32[4,8]{1,0:T(4,128)S(1)}, s32[4,8]{1,0:T(4,128)S(1)}, u32[]{:S(2)}, u32[]{:S(2)}) collective-permute-start(s32[4,8]{1,0:T(4,128)S(1)} %get-tuple-element.41), channel_id=1, source_target_pairs={{0,8},{8,0},{16,24},{24,16},{1,9},{9,1},{17,25},{25,17},{2,10},{10... | collective-permute-start | bytes 392 | tf_op jit(solution)/shard_map/ppermute | solution.py:73
  10.9 2.0 %collective-permute-done.2 = s32[4,8]{1,0:T(4,128)S(1)} collective-permute-done((s32[4,8]{1,0:T(4,128)S(1)}, s32[4,8]{1,0:T(4,128)S(1)}, u32[]{:S(2)}, u32[]{:S(2)}) %collective-permute-start.2) | collective-permute-done | bytes 160 | tf_op jit(solution)/shard_map/ppermute | solution.py:73
  13.0 0.7 collective-permute-start.4
  13.7 4.4 %collective-permute-start.3 = (bf16[2,8,32,256]{3,2,1,0:T(8,128)(2,1)S(1)}, bf16[2,8,32,256]{3,2,1,0:T(8,128)(2,1)S(1)}, u32[]{:S(2)}, u32[]{:S(2)}) collective-permute-start(bf16[2,8,32,256]{3,2,1,0:T(8,128)(2,1)S(1)} %get-tuple-element.44), channel_id=1, source_target_pairs={{0,8},{16,24},{8,0},{24,16},{1,9},{17,25},{9,1},{25,17},{2,10},{18... | collective-permute-start | bytes 786440 | tf_op jit(solution)/shard_map/ppermute | solution.py:66
  18.5 4.5 %shard_map.76 = (bf16[128,2048]{1,0:T(8,128)(2,1)S(1)}, bf16[128,2048]{1,0:T(8,128)(2,1)}, bf16[1152,128]{1,0:T(8,128)(2,1)}) custom-call(s32[1,8]{1,0:T(1,128)S(1)} %copy-done.7, bf16[1,1920,128]{2,1,0:T(8,128)(2,1)} %basis_kept), custom_call_target="tpu_custom_call" | custom-call | flops 402653184 | bytes 1474560 | tf_op jit(solution)/shard_map/pallas_call | solution.py:512
  23.0 1.9 %collective-permute-done.5 = s32[4,8]{1,0:T(4,128)S(1)} collective-permute-done((s32[4,8]{1,0:T(4,128)S(1)}, s32[4,8]{1,0:T(4,128)S(1)}, u32[]{:S(2)}, u32[]{:S(2)}) %collective-permute-start.5) | collective-permute-done | bytes 160 | tf_op jit(solution)/shard_map/ppermute | solution.py:73
  25.1 1.4 %shard_map.77 = (bf16[8,128,128]{2,1,0:T(8,128)(2,1)}, bf16[64,32,256]{2,1,0:T(8,128)(2,1)}) custom-call(f32[36,32,256]{2,1,0:T(8,128)S(1)} %get-tuple-element.37.sol.sol_kept, f32[36,32,256]{2,1,0:T(8,128)S(1)} %get-tuple-element.38.base.refs_0_, bf16[2,6,32,256]{3,2,1,0:T(8,128)(2,1)S(1)} %collective-permute-done.first_in.first_q, ...), custom_call_target="tpu_custom_call" | custom-call | flops 134217728 | bytes 5111808 | tf_op jit(solution)/shard_map/pallas_call | solution.py:27
  26.5 3.8 %all-to-all-start = ((bf16[8,128,128]{2,1,0:T(8,128)(2,1)}), bf16[8,128,128]{2,1,0:T(8,128)(2,1)S(1)}, u32[]{:S(2)}, u32[]{:S(2)}) async-start(bf16[8,128,128]{2,1,0:T(8,128)(2,1)} %get-tuple-element.52), calls=%async_computation | async-start | bytes 524288 | tf_op jit(solution)/shard_map/all_to_all | solution.py:722
  30.9 4.0 %shard_map.78.spread = bf16[1024,1024]{1,0:T(8,128)(2,1)} custom-call(s32[4,8]{1,0:T(4,128)S(1)} %add.7.every, bf16[4,64,512]{2,1,0:T(8,128)(2,1)} %inverse_kept.3, bf16[4,64,512]{2,1,0:T(8,128)(2,1)} %copy-done.9), custom_call_target="tpu_custom_call" | custom-call | flops 1073741824 | bytes 2097152 | tf_op jit(solution)/shard_map/pallas_call | solution.py:600
  34.9 1.4 %all-to-all-done = bf16[8,128,128]{2,1,0:T(8,128)(2,1)S(1)} async-done(((bf16[8,128,128]{2,1,0:T(8,128)(2,1)}), bf16[8,128,128]{2,1,0:T(8,128)(2,1)S(1)}, u32[]{:S(2)}, u32[]{:S(2)}) %all-to-all-start) | async-done | bytes 262176 | tf_op jit(solution)/shard_map/all_to_all | solution.py:722
  36.3 1.6 %copy-done.3 = bf16[1024,1024]{1,0:T(8,128)(2,1)S(1)} copy-done((bf16[1024,1024]{1,0:T(8,128)(2,1)S(1)}, bf16[1024,1024]{1,0:T(8,128)(2,1)}, u32[]{:S(2)}) %copy-start.3) | copy-done | bytes 2097176
  37.9 1.4 %shard_map.79 = bf16[1024,128]{1,0:T(8,128)(2,1)} custom-call(bf16[1024,1024]{1,0:T(8,128)(2,1)S(1)} %copy-done.3, bf16[1024,128]{1,0:T(8,128)(2,1)S(1)} %bitcast.12), custom_call_target="tpu_custom_call" | custom-call | flops 268435456 | bytes 2621440 | tf_op jit(solution)/shard_map/pallas_call | solution.py:27
  39.3 4.0 %all-to-all-start.1 = ((bf16[32,32,128]{2,1,0:T(8,128)(2,1)}), bf16[32,32,128]{2,1,0:T(8,128)(2,1)S(1)}, u32[]{:S(2)}, u32[]{:S(2)}) async-start(bf16[32,32,128]{2,1,0:T(8,128)(2,1)} %bitcast.21), calls=%async_computation.1 | async-start | bytes 524288 | tf_op jit(solution)/shard_map/all_to_all | solution.py:731
  43.4 7.1 %shard_map.80 = (f32[36,32,256]{2,1,0:T(8,128)}, f32[36,32,256]{2,1,0:T(8,128)}) custom-call(bf16[64,32,256]{2,1,0:T(8,128)(2,1)} %get-tuple-element.56.local_kept, bf16[1,1920,1920]{2,1,0:T(8,128)(2,1)} %inverse_kept.5, f32[36,32,256]{2,1,0:T(8,128)} %copy-done, f32[36,32,256]{2,1,0:T(8,128)} %copy-done.1, f32[6,6,3,10]{3,2,1,0:T(4,128)S(1)} %copy-done.5), custom_call_target="tpu_custom_call" | custom-call | flops 1415577600 | bytes 13144288 | tf_op jit(solution)/shard_map/pallas_call | solution.py:27
  50.5 3.6 %all-to-all-done.1 = bf16[32,32,128]{2,1,0:T(8,128)(2,1)S(1)} async-done(((bf16[32,32,128]{2,1,0:T(8,128)(2,1)}), bf16[32,32,128]{2,1,0:T(8,128)(2,1)S(1)}, u32[]{:S(2)}, u32[]{:S(2)}) %all-to-all-start.1) | async-done | bytes 262176 | tf_op jit(solution)/shard_map/all_to_all | solution.py:731
  54.1 1.7 %shard_map.81 = (bf16[2,6,32,256]{3,2,1,0:T(8,128)(2,1)S(1)}, bf16[2,6,32,256]{3,2,1,0:T(8,128)(2,1)S(1)}, f32[36,32,256]{2,1,0:T(8,128)S(1)}) custom-call(bf16[4,8,32,128]{3,2,1,0:T(8,128)(2,1)S(1)} %bitcast.11, bf16[1152,128]{1,0:T(8,128)(2,1)} %get-tuple-element.55.basis_kept, f32[6,6,32,256]{3,2,1,0:T(8,128)} %bitcast.19, f32[6,6,32,256]{3,2,1,0:T(8,128)} %bitcast.20, ...), custom_call_target="tpu_custom_call" | custom-call | bytes 4493536 | tf_op jit(solution)/shard_map/pallas_call | solution.py:27
  55.7 0.9 collective-permute-start.7
  57.3 2.5 %shard_map.82 = (f32[36,32,256]{2,1,0:T(8,128)S(1)}, f32[36,32,256]{2,1,0:T(8,128)S(1)}) custom-call(f32[36,32,256]{2,1,0:T(8,128)S(1)} %get-tuple-element.59.coarse, f32[36,32,256]{2,1,0:T(8,128)} %get-tuple-element.57.sol_kept, f32[36,32,256]{2,1,0:T(8,128)} %get-tuple-element.58.base_kept, f32[6,6,3,10]{3,2,1,0:T(4,128)} %stiffness.7), custom_call_target="tpu_custom_call" | custom-call | bytes 5902560 | tf_op jit(solution)/shard_map/pallas_call | solution.py:27
  59.8 3.0 %collective-permute-done.7.first_in.first_q = bf16[2,6,32,256]{3,2,1,0:T(8,128)(2,1)S(1)} collective-permute-done((bf16[2,6,32,256]{3,2,1,0:T(8,128)(2,1)S(1)}, bf16[2,6,32,256]{3,2,1,0:T(8,128)(2,1)S(1)}, u32[]{:S(2)}, u32[]{:S(2)}) %collective-permute-start.7) | collective-permute-done | bytes 196640 | tf_op jit(solution)/shard_map/ppermute | solution.py:66
  62.8 1.7 %collective-permute-start.9 = (bf16[2,8,32,256]{3,2,1,0:T(8,128)(2,1)S(1)}, bf16[2,8,32,256]{3,2,1,0:T(8,128)(2,1)S(1)}, u32[]{:S(2)}, u32[]{:S(2)}) collective-permute-start(bf16[2,8,32,256]{3,2,1,0:T(8,128)(2,1)S(1)} %get-tuple-element.64), channel_id=1, source_target_pairs={{0,8},{16,24},{8,0},{24,16},{1,9},{17,25},{9,1},{25,17},{2,10},{18... | collective-permute-start | bytes 786440 | tf_op jit(solution)/shard_map/ppermute | solution.py:66
  64.5 0.8 collective-permute-start.10
  65.3 5.6 %collective-permute-done.9.first_s = bf16[2,8,32,256]{3,2,1,0:T(8,128)(2,1)S(1)} collective-permute-done((bf16[2,8,32,256]{3,2,1,0:T(8,128)(2,1)S(1)}, bf16[2,8,32,256]{3,2,1,0:T(8,128)(2,1)S(1)}, u32[]{:S(2)}, u32[]{:S(2)}) %collective-permute-start.9) | collective-permute-done | bytes 262176 | tf_op jit(solution)/shard_map/ppermute | solution.py:66
  70.9 1.4 %shard_map.84 = (bf16[8,128,128]{2,1,0:T(8,128)(2,1)}, bf16[64,32,256]{2,1,0:T(8,128)(2,1)}) custom-call(f32[36,32,256]{2,1,0:T(8,128)S(1)} %get-tuple-element.60.sol.sol_kept, f32[36,32,256]{2,1,0:T(8,128)S(1)} %get-tuple-element.61.base, bf16[2,6,32,256]{3,2,1,0:T(8,128)(2,1)S(1)} %collective-permute-done.7.first_in.first_q, ...), custom_call_target="tpu_custom_call" | custom-call | flops 134217728 | bytes 5111808 | tf_op jit(solution)/shard_map/pallas_call | solution.py:27
  72.3 11.0 %all_to_all.20 = bf16[8,128,128]{2,1,0:T(8,128)(2,1)S(1)} all-to-all(bf16[8,128,128]{2,1,0:T(8,128)(2,1)} %get-tuple-element.67), channel_id=1, replica_groups=mesh['sub'=4,'crow'=4,'ccol'=2] {'crow','ccol'}, dimensions={0} | all-to-all | bytes 524288 | tf_op jit(solution)/shard_map/all_to_all | solution.py:722
  83.3 1.4 %shard_map.85 = bf16[1024,128]{1,0:T(8,128)(2,1)} custom-call(bf16[1024,1024]{1,0:T(8,128)(2,1)S(1)} %copy-done.4, bf16[1024,128]{1,0:T(8,128)(2,1)S(1)} %bitcast.14), custom_call_target="tpu_custom_call" | custom-call | flops 268435456 | bytes 2621440 | tf_op jit(solution)/shard_map/pallas_call | solution.py:27
  84.7 4.9 %all-to-all-start.3 = ((bf16[32,32,128]{2,1,0:T(8,128)(2,1)}), bf16[32,32,128]{2,1,0:T(8,128)(2,1)S(1)}, u32[]{:S(2)}, u32[]{:S(2)}) async-start(bf16[32,32,128]{2,1,0:T(8,128)(2,1)} %bitcast.22), calls=%async_computation.3 | async-start | bytes 524288 | tf_op jit(solution)/shard_map/all_to_all | solution.py:731
  89.6 6.1 %shard_map.86.sol_kept = f32[36,32,256]{2,1,0:T(8,128)} custom-call(bf16[64,32,256]{2,1,0:T(8,128)(2,1)} %get-tuple-element.68.local_kept, bf16[1,1920,1920]{2,1,0:T(8,128)(2,1)} %inverse_kept.5, f32[36,32,256]{2,1,0:T(8,128)} %copy-done.2), custom_call_target="tpu_custom_call" | custom-call | flops 1415577600 | bytes 10780672 | tf_op jit(solution)/shard_map/pallas_call | solution.py:27
  95.7 4.6 %all-to-all-done.3 = bf16[32,32,128]{2,1,0:T(8,128)(2,1)S(1)} async-done(((bf16[32,32,128]{2,1,0:T(8,128)(2,1)}), bf16[32,32,128]{2,1,0:T(8,128)(2,1)S(1)}, u32[]{:S(2)}, u32[]{:S(2)}) %all-to-all-start.3) | async-done | bytes 262176 | tf_op jit(solution)/shard_map/all_to_all | solution.py:731
  100.3 2.9 %shard_map.87 = f32[6,6,10,3,256]{4,3,2,1,0:T(4,128)} custom-call(bf16[4,8,32,128]{3,2,1,0:T(8,128)(2,1)S(1)} %bitcast.13, bf16[1152,128]{1,0:T(8,128)(2,1)} %get-tuple-element.55.basis_kept, f32[36,32,256]{2,1,0:T(8,128)} %shard_map.86.sol_kept), custom_call_target="tpu_custom_call" | custom-call | bytes 2842624 | tf_op jit(solution)/shard_map/pallas_call | solution.py:27
  (34 shorter events, 2.7 us)
Async XLA Ops:
  2.0 10.8 %collective-permute-start = (bf16[2,6,32,256]{3,2,1,0:T(8,128)(2,1)S(1)}, bf16[2,6,32,256]{3,2,1,0:T(8,128)(2,1)S(1)}, u32[]{:S(2)}, u32[]{:S(2)}) collective-permute-start(bf16[2,6,32,256]{3,2,1,0:T(8,128)(2,1)S(1)} %get-tuple-element.39), channel_id=1, source_target_pairs={{0,1},{2,3},{4,5},{6,7},{1,0},{3,2},{5,4},{7,6},{8,9},{10,11},{12,... | collective-permute-start | bytes 589832 | tf_op jit(solution)/shard_map/ppermute | solution.py:66
  5.1 7.8 %collective-permute-start.1 = (bf16[2,6,32,256]{3,2,1,0:T(8,128)(2,1)S(1)}, bf16[2,6,32,256]{3,2,1,0:T(8,128)(2,1)S(1)}, u32[]{:S(2)}, u32[]{:S(2)}) collective-permute-start(bf16[2,6,32,256]{3,2,1,0:T(8,128)(2,1)S(1)} %get-tuple-element.40), channel_id=1, source_target_pairs={{1,2},{3,4},{5,6},{2,1},{4,3},{6,5},{9,10},{11,12},{13,14},{10,9},... | collective-permute-start | bytes 589832 | tf_op jit(solution)/shard_map/ppermute | solution.py:67
  9.2 15.9 %copy-start = (f32[36,32,256]{2,1,0:T(8,128)}, f32[36,32,256]{2,1,0:T(8,128)S(1)}, u32[]{:S(2)}) copy-start(f32[36,32,256]{2,1,0:T(8,128)S(1)} %get-tuple-element.37.sol.sol_kept) | copy-start | bytes 3538948
  9.2 15.9 %copy-start.1 = (f32[36,32,256]{2,1,0:T(8,128)}, f32[36,32,256]{2,1,0:T(8,128)S(1)}, u32[]{:S(2)}) copy-start(f32[36,32,256]{2,1,0:T(8,128)S(1)} %get-tuple-element.38.base.refs_0_) | copy-start | bytes 3538948
  9.2 3.7 %collective-permute-start.2 = (s32[4,8]{1,0:T(4,128)S(1)}, s32[4,8]{1,0:T(4,128)S(1)}, u32[]{:S(2)}, u32[]{:S(2)}) collective-permute-start(s32[4,8]{1,0:T(4,128)S(1)} %get-tuple-element.41), channel_id=1, source_target_pairs={{0,8},{8,0},{16,24},{24,16},{1,9},{9,1},{17,25},{25,17},{2,10},{10... | collective-permute-start | bytes 392 | tf_op jit(solution)/shard_map/ppermute | solution.py:73
  12.9 5.3 %copy-start.8 = (bf16[4,64,512]{2,1,0:T(8,128)(2,1)S(1)}, bf16[4,64,512]{2,1,0:T(8,128)(2,1)}, u32[]{:S(2)}) copy-start(bf16[4,64,512]{2,1,0:T(8,128)(2,1)} %inverse_kept.3) | copy-start | bytes 786436
  12.9 5.6 %copy-start.7 = (s32[1,8]{1,0:T(1,128)S(1)}, s32[1,8]{1,0:T(1,128)}, u32[]{:S(2)}) copy-start(s32[1,8]{1,0:T(1,128)} %offsets.3) | copy-start | bytes 100
  13.0 12.0 %collective-permute-start.4 = (bf16[2,8,32,256]{3,2,1,0:T(8,128)(2,1)S(1)}, bf16[2,8,32,256]{3,2,1,0:T(8,128)(2,1)S(1)}, u32[]{:S(2)}, u32[]{:S(2)}) collective-permute-start(bf16[2,8,32,256]{3,2,1,0:T(8,128)(2,1)S(1)} %get-tuple-element.45), channel_id=1, source_target_pairs={{8,16},{16,8},{9,17},{17,9},{10,18},{18,10},{11,19},{19,11},{12,20... | collective-permute-start | bytes 786440 | tf_op jit(solution)/shard_map/ppermute | solution.py:67
  13.7 11.4 %collective-permute-start.3 = (bf16[2,8,32,256]{3,2,1,0:T(8,128)(2,1)S(1)}, bf16[2,8,32,256]{3,2,1,0:T(8,128)(2,1)S(1)}, u32[]{:S(2)}, u32[]{:S(2)}) collective-permute-start(bf16[2,8,32,256]{3,2,1,0:T(8,128)(2,1)S(1)} %get-tuple-element.44), channel_id=1, source_target_pairs={{0,8},{16,24},{8,0},{24,16},{1,9},{17,25},{9,1},{25,17},{2,10},{18... | collective-permute-start | bytes 786440 | tf_op jit(solution)/shard_map/ppermute | solution.py:66
  18.1 12.1 %collective-permute-start.6 = (bf16[4,64,512]{2,1,0:T(8,128)(2,1)S(1)}, bf16[4,64,512]{2,1,0:T(8,128)(2,1)S(1)}, u32[]{:S(2)}, u32[]{:S(2)}) collective-permute-start(bf16[4,64,512]{2,1,0:T(8,128)(2,1)S(1)} %copy-done.8), channel_id=1, source_target_pairs={{0,2},{1,3},{2,0},{3,1},{4,6},{5,7},{6,4},{7,5},{8,10},{9,11},{10,... | collective-permute-start | bytes 786440 | tf_op jit(solution)/shard_map/ppermute | solution.py:702
  18.3 6.7 %collective-permute-start.5 = (s32[4,8]{1,0:T(4,128)S(1)}, s32[4,8]{1,0:T(4,128)S(1)}, u32[]{:S(2)}, u32[]{:S(2)}) collective-permute-start(s32[4,8]{1,0:T(4,128)S(1)} %add.6), channel_id=1, source_target_pairs={{0,16},{8,24},{16,0},{24,8},{1,17},{9,25},{17,1},{25,9},{2,18},{10... | collective-permute-start | bytes 392 | tf_op jit(solution)/shard_map/ppermute | solution.py:73
  26.5 9.8 %all-to-all-start = ((bf16[8,128,128]{2,1,0:T(8,128)(2,1)}), bf16[8,128,128]{2,1,0:T(8,128)(2,1)S(1)}, u32[]{:S(2)}, u32[]{:S(2)}) async-start(bf16[8,128,128]{2,1,0:T(8,128)(2,1)} %get-tuple-element.52), calls=%async_computation | async-start | bytes 524288 | tf_op jit(solution)/shard_map/all_to_all | solution.py:722
  30.3 0.7 copy-start.9
  36.3 1.6 %copy-start.3 = (bf16[1024,1024]{1,0:T(8,128)(2,1)S(1)}, bf16[1024,1024]{1,0:T(8,128)(2,1)}, u32[]{:S(2)}) copy-start(bf16[1024,1024]{1,0:T(8,128)(2,1)} %shard_map.78.spread) | copy-start | bytes 6291460
  37.9 5.5 %copy-start.5 = (f32[6,6,3,10]{3,2,1,0:T(4,128)S(1)}, f32[6,6,3,10]{3,2,1,0:T(4,128)}, u32[]{:S(2)}) copy-start(f32[6,6,3,10]{3,2,1,0:T(4,128)} %stiffness.7) | copy-start | bytes 12964
  39.3 14.7 %all-to-all-start.1 = ((bf16[32,32,128]{2,1,0:T(8,128)(2,1)}), bf16[32,32,128]{2,1,0:T(8,128)(2,1)S(1)}, u32[]{:S(2)}, u32[]{:S(2)}) async-start(bf16[32,32,128]{2,1,0:T(8,128)(2,1)} %bitcast.21), calls=%async_computation.1 | async-start | bytes 524288 | tf_op jit(solution)/shard_map/all_to_all | solution.py:731
  55.7 7.0 %collective-permute-start.7 = (bf16[2,6,32,256]{3,2,1,0:T(8,128)(2,1)S(1)}, bf16[2,6,32,256]{3,2,1,0:T(8,128)(2,1)S(1)}, u32[]{:S(2)}, u32[]{:S(2)}) collective-permute-start(bf16[2,6,32,256]{3,2,1,0:T(8,128)(2,1)S(1)} %get-tuple-element.62), channel_id=1, source_target_pairs={{0,1},{2,3},{4,5},{6,7},{1,0},{3,2},{5,4},{7,6},{8,9},{10,11},{12,... | collective-permute-start | bytes 589832 | tf_op jit(solution)/shard_map/ppermute | solution.py:66
  56.6 6.1 %collective-permute-start.8 = (bf16[2,6,32,256]{3,2,1,0:T(8,128)(2,1)S(1)}, bf16[2,6,32,256]{3,2,1,0:T(8,128)(2,1)S(1)}, u32[]{:S(2)}, u32[]{:S(2)}) collective-permute-start(bf16[2,6,32,256]{3,2,1,0:T(8,128)(2,1)S(1)} %get-tuple-element.63), channel_id=1, source_target_pairs={{1,2},{3,4},{5,6},{2,1},{4,3},{6,5},{9,10},{11,12},{13,14},{10,9},... | collective-permute-start | bytes 589832 | tf_op jit(solution)/shard_map/ppermute | solution.py:67
  59.8 11.1 %copy-start.2 = (f32[36,32,256]{2,1,0:T(8,128)}, f32[36,32,256]{2,1,0:T(8,128)S(1)}, u32[]{:S(2)}) copy-start(f32[36,32,256]{2,1,0:T(8,128)S(1)} %get-tuple-element.60.sol.sol_kept) | copy-start | bytes 3538948
  62.7 8.2 %copy-start.6 = (bf16[128,2048]{1,0:T(8,128)(2,1)S(1)}, bf16[128,2048]{1,0:T(8,128)(2,1)}, u32[]{:S(2)}) copy-start(bf16[128,2048]{1,0:T(8,128)(2,1)} %get-tuple-element.66.basis_t) | copy-start | bytes 1572868
  62.8 8.1 %collective-permute-start.9 = (bf16[2,8,32,256]{3,2,1,0:T(8,128)(2,1)S(1)}, bf16[2,8,32,256]{3,2,1,0:T(8,128)(2,1)S(1)}, u32[]{:S(2)}, u32[]{:S(2)}) collective-permute-start(bf16[2,8,32,256]{3,2,1,0:T(8,128)(2,1)S(1)} %get-tuple-element.64), channel_id=1, source_target_pairs={{0,8},{16,24},{8,0},{24,16},{1,9},{17,25},{9,1},{25,17},{2,10},{18... | collective-permute-start | bytes 786440 | tf_op jit(solution)/shard_map/ppermute | solution.py:66
  64.5 6.4 %collective-permute-start.10 = (bf16[2,8,32,256]{3,2,1,0:T(8,128)(2,1)S(1)}, bf16[2,8,32,256]{3,2,1,0:T(8,128)(2,1)S(1)}, u32[]{:S(2)}, u32[]{:S(2)}) collective-permute-start(bf16[2,8,32,256]{3,2,1,0:T(8,128)(2,1)S(1)} %get-tuple-element.65), channel_id=1, source_target_pairs={{8,16},{16,8},{9,17},{17,9},{10,18},{18,10},{11,19},{19,11},{12,20... | collective-permute-start | bytes 786440 | tf_op jit(solution)/shard_map/ppermute | solution.py:67
  70.9 12.4 %copy-start.4 = (bf16[1024,1024]{1,0:T(8,128)(2,1)S(1)}, bf16[1024,1024]{1,0:T(8,128)(2,1)}, u32[]{:S(2)}) copy-start(bf16[1024,1024]{1,0:T(8,128)(2,1)} %shard_map.78.spread) | copy-start | bytes 6291460
  84.7 15.6 %all-to-all-start.3 = ((bf16[32,32,128]{2,1,0:T(8,128)(2,1)}), bf16[32,32,128]{2,1,0:T(8,128)(2,1)S(1)}, u32[]{:S(2)}, u32[]{:S(2)}) async-start(bf16[32,32,128]{2,1,0:T(8,128)(2,1)} %bitcast.22), calls=%async_computation.3 | async-start | bytes 524288 | tf_op jit(solution)/shard_map/all_to_all | solution.py:731

commit v8 on v7

--- a/solution.py
+++ b/solution.py
@@ -21,7 +21,7 @@
     return math.prod(x.shape) * jnp.dtype(x.dtype).itemsize
 
 
-def call(body, ins, outs, scratch=(), flops=0, held=()):
+def call(body, ins, outs, scratch=(), flops=0, held=(), aliases=None):
     size = sum(sized(x) for x in (*ins, *outs))
     room = size + sum(sized(x) for x in scratch if getattr(x, "dtype", None) in (bf16, f32))
     return pl.pallas_call(
@@ -32,6 +32,7 @@
             HBM if getattr(x, "memory_space", None) == pltpu.HBM else VMEM for x in outs
         ),
         scratch_shapes=list(scratch),
+        input_output_aliases=aliases or {},
         compiler_params=pltpu.CompilerParams(vmem_limit_bytes=room + (4 << 20)),
         cost_estimate=pl.CostEstimate(flops=flops, bytes_accessed=size, transcendentals=0),
     )(
@@ -214,6 +215,32 @@
 
 def side_of(member):
     return (member // PARTNER) % 2
+
+
+def middle_window_kernel(
+    shape, sol, base, first_q, second_q, basis_t, local_kept, product, local, sems
+):
+    cells_s, cells_q, _, pad, columns = shape
+    wide = cells_q + 2
+    low, high = column_sides(first_q, second_q)
+    copies = []
+    for s in range(1, cells_s - 1):
+        left, right = edge_cells(low, high, sol, s, cells_q)
+        values = [left] + [base[s * cells_q + q] for q in range(cells_q)] + [right]
+        values[1] = values[1] + low(1, s)
+        values[cells_q] = values[cells_q] + high(1, s)
+        for w in range(wide):
+            local[(s - 1) * wide + w] = values[w].astype(bf16)
+        part, there = pl.ds((s - 1) * wide, wide), pl.ds((s + 1) * wide, wide)
+        copies.append(begun(local.at[part], local_kept.at[there], sems.at[len(copies)]))
+    chunk = wide * pad
+    product[...] = jnp.dot(
+        basis_t[:, 2 * chunk : cells_s * chunk],
+        local[...].reshape(-1, columns),
+        preferred_element_type=f32,
+    )
+    for copy in copies:
+        copy.wait()
 
 
 def window_kernel(
@@ -270,6 +297,77 @@
     product = jnp.dot(
         basis_t[...], local[...].reshape(-1, columns), preferred_element_type=f32
     ).astype(bf16)
+    half = columns // 2
+    for k in range(2):
+        restricted[k] = product[:, k * half : (k + 1) * half]
+    for j in range(message.shape[0]):
+        copies.append(begun(restricted.at[side_of(j)], message.at[j], sems.at[len(copies)]))
+    for copy in copies:
+        copy.wait()
+
+
+def outer_window_kernel(
+    shape,
+    sol,
+    base,
+    first_q,
+    second_q,
+    first_s,
+    second_s,
+    basis_t,
+    middle,
+    begun_kept,
+    message,
+    local_kept,
+    local,
+    restricted,
+    sems,
+):
+    cells_s, cells_q, _, pad, columns = shape
+    wide = cells_q + 2
+    low, high = column_sides(first_q, second_q)
+    row, rows = lax.axis_index("sub"), lax.axis_size("sub")
+    even = row % 2 == 0
+
+    def above(kind, w):
+        return jnp.where(even, second_s[kind, w].astype(f32), first_s[kind, w].astype(f32))
+
+    def below(kind, w):
+        return jnp.where(even, first_s[kind, w].astype(f32), second_s[kind, w].astype(f32))
+
+    copies = []
+    for s in (0, cells_s - 1):
+        left, right = edge_cells(low, high, sol, s, cells_q)
+        values = [left] + [base[s * cells_q + q] for q in range(cells_q)] + [right]
+        values[1] = values[1] + low(1, s)
+        values[cells_q] = values[cells_q] + high(1, s)
+        for w in range(wide):
+            value = values[w]
+            if s == 0:
+                value = value + above(1, w)
+            if s == cells_s - 1:
+                value = value + below(1, w)
+            local[(s + 1) * wide + w] = value.astype(bf16)
+        part = pl.ds((s + 1) * wide, wide)
+        copies.append(begun(local.at[part], local_kept.at[part], sems.at[len(copies)]))
+    for s, side, place, there in (
+        (0, above, 0, row > 0),
+        (cells_s - 1, below, (cells_s + 1) * wide, row < rows - 1),
+    ):
+        near = [low(1, s)] + [sol[s * cells_q + q] for q in range(cells_q)] + [high(1, s)]
+        for w in range(wide):
+            local[place + w] = jnp.where(there, side(0, w) + near[w], 0.0).astype(bf16)
+        part = pl.ds(place, wide)
+        copies.append(begun(local.at[part], local_kept.at[part], sems.at[len(copies)]))
+    chunk = wide * pad
+    product = middle[...]
+    for r in (0, cells_s):
+        product = product + jnp.dot(
+            basis_t[:, r * chunk : (r + 2) * chunk],
+            local[r * wide : (r + 2) * wide].reshape(-1, columns),
+            preferred_element_type=f32,
+        )
+    product = product.astype(bf16)
     half = columns // 2
     for k in range(2):
         restricted[k] = product[:, k * half : (k + 1) * half]
@@ -702,20 +800,51 @@
             partner = lax.ppermute(shared, GROUP_AXES, pairs)
             every = doubled(every, 1 << (rounds - 1))
             first_s, second_s, every = lax.optimization_barrier((first_s, second_s, every))
-        message, local = call(
-            functools.partial(window_kernel, shape),
-            (solution, base, first_q, second_q, first_s, second_s, basis_t if sweep == 0 else basis_kept),
-            (
-                pltpu.HBM((groups, coarse, columns // 2), bf16),
-                pltpu.HBM(((cells_s + 2) * wide, pad, columns), bf16),
-            ),
-            scratch=(
-                pltpu.VMEM(((cells_s + 2) * wide, pad, columns), bf16),
-                pltpu.VMEM((2, coarse, columns // 2), bf16),
-                pltpu.SemaphoreType.DMA((groups + cells_s + 2,)),
-            ),
-            flops=2 * rows * coarse * columns,
-        )
+        if last:
+            begun_kept, middle = call(
+                functools.partial(middle_window_kernel, shape),
+                (solution, base, first_q, second_q, basis_kept),
+                (
+                    pltpu.HBM(((cells_s + 2) * wide, pad, columns), bf16),
+                    jax.ShapeDtypeStruct((coarse, columns), f32),
+                ),
+                scratch=(
+                    pltpu.VMEM(((cells_s - 2) * wide, pad, columns), bf16),
+                    pltpu.SemaphoreType.DMA((cells_s - 2,)),
+                ),
+                flops=rows * coarse * columns,
+            )
+            message, local = call(
+                functools.partial(outer_window_kernel, shape),
+                (solution, base, first_q, second_q, first_s, second_s, basis_kept, middle, begun_kept),
+                (
+                    pltpu.HBM((groups, coarse, columns // 2), bf16),
+                    pltpu.HBM(((cells_s + 2) * wide, pad, columns), bf16),
+                ),
+                scratch=(
+                    pltpu.VMEM(((cells_s + 2) * wide, pad, columns), bf16),
+                    pltpu.VMEM((2, coarse, columns // 2), bf16),
+                    pltpu.SemaphoreType.DMA((groups + cells_s + 2,)),
+                ),
+                flops=rows * coarse * columns,
+                held=(8,),
+                aliases={8: 1},
+            )
+        else:
+            message, local = call(
+                functools.partial(window_kernel, shape),
+                (solution, base, first_q, second_q, first_s, second_s, basis_t if sweep == 0 else basis_kept),
+                (
+                    pltpu.HBM((groups, coarse, columns // 2), bf16),
+                    pltpu.HBM(((cells_s + 2) * wide, pad, columns), bf16),
+                ),
+                scratch=(
+                    pltpu.VMEM(((cells_s + 2) * wide, pad, columns), bf16),
+                    pltpu.VMEM((2, coarse, columns // 2), bf16),
+                    pltpu.SemaphoreType.DMA((groups + cells_s + 2,)),
+                ),
+                flops=2 * rows * coarse * columns,
+            )
         if sweep == 0:
             waited, _ = lax.optimization_barrier((every, message))
             spread = spread_inverse(waited, coarse_inverse, partner, depth)

time: 104 us -> 104 us (level)
    pallas_call x13 -> x14, Pallas kernels: 31.5 us -> 32.1 us  [call(): pl.pallas_call(body, out_shape=tuple(outs), in_specs=[HBM if i in held el...]
  transfers between devices with their start and end apart: 14 -> 14, of which waited for: 8 -> 8; matrix products, arithmetic and copies ran while one was open for 0% -> 0% of each run, Pallas kernels for 28% -> 29%
where the time goes in v8:
time: 104 us; the launch traced here: 103 us
  Pallas kernels  40.6 us (39%)
  starting transfers between devices  27.6 us (27%)
  waiting for transfers between devices  21.3 us (20%)
  blocking collectives  11 us (11%)
  local copies, waits for them, and re-layouts  2.31 us (2%)
    pallas_call x14, Pallas kernels, call(): pl.pallas_call(body, out_shape=tuple(outs), in_specs=[HBM if i in held el...  32.1 us
    all_to_all x1, blocking collectives, shards(): gathered = lax.all_to_all(message, GROUP_AXES, 0, 0, tiled=True)  11 us
    ppermute x4, starting transfers between devices, swap(): lax.ppermute(first, axis, even + [(b, a) for a, b in even])  10 us
    all_to_all x2, starting transfers between devices, shards(): lax.all_to_all(terms.reshape(n_sub * groups, 2 * depth, columns // 2), AL...  8.94 us
    all_to_all x2, waiting for transfers between devices, shards(): lax.all_to_all(terms.reshape(n_sub * groups, 2 * depth, columns // 2), AL...  8.21 us
    ppermute x4, waiting for transfers between devices, swap(): lax.ppermute(first, axis, even + [(b, a) for a, b in even])  7.77 us
    pallas_call x1, Pallas kernels, ordered_basis(): pl.pallas_call(functools.partial(basis_kernel, cell, dims), out_shape=(ja...  4.47 us
    pallas_call x1, Pallas kernels, spread_inverse(): pl.pallas_call(functools.partial(spread_kernel, (groups, depth, kgroup)),...  3.98 us
  transfers between devices with their start and end apart: 14, of which 8 were waited for; matrix products, arithmetic and copies ran while one was open for 0% of the time, Pallas kernels for 29%

profile of v8, /device:TPU:0, one launch (start us, length us, event | category | flops | bytes accessed | tf_op | source)
XLA Modules:
  0.0 103.2 jit_solution(3385099087631819628)
XLA Ops:
  0.0 2.0 %shard_map.74 = (bf16[2,6,32,256]{3,2,1,0:T(8,128)(2,1)S(1)}, bf16[2,6,32,256]{3,2,1,0:T(8,128)(2,1)S(1)}) custom-call(f32[6,6,10,3,256]{4,3,2,1,0:T(4,128)} %bitcast.15, f32[6,6,10,3,256]{4,3,2,1,0:T(4,128)} %bitcast.17, f32[6,6,3,10]{3,2,1,0:T(4,128)} %stiffness.7), custom_call_target="tpu_custom_call" | custom-call | bytes 2609376 | tf_op jit(solution)/shard_map/pallas_call | solution.py:27
  2.0 3.0 %collective-permute-start = (bf16[2,6,32,256]{3,2,1,0:T(8,128)(2,1)S(1)}, bf16[2,6,32,256]{3,2,1,0:T(8,128)(2,1)S(1)}, u32[]{:S(2)}, u32[]{:S(2)}) collective-permute-start(bf16[2,6,32,256]{3,2,1,0:T(8,128)(2,1)S(1)} %get-tuple-element.41), channel_id=1, source_target_pairs={{0,1},{2,3},{4,5},{6,7},{1,0},{3,2},{5,4},{7,6},{8,9},{10,11},{12,... | collective-permute-start | bytes 589832 | tf_op jit(solution)/shard_map/ppermute | solution.py:67
  5.7 3.5 %shard_map.73 = (f32[36,32,256]{2,1,0:T(8,128)S(1)}, f32[36,32,256]{2,1,0:T(8,128)S(1)}, s32[4,8]{1,0:T(4,128)S(1)}) custom-call(f32[6,6,10,3,256]{4,3,2,1,0:T(4,128)} %bitcast.16, f32[6,6,10,3,256]{4,3,2,1,0:T(4,128)} %bitcast.18, f32[6,6,3,10]{3,2,1,0:T(4,128)} %stiffness.7, s32[1,8]{1,0:T(1,128)} %offsets.3), custom_call_target="tpu_custom_call" | custom-call | bytes 4575616 | tf_op jit(solution)/shard_map/pallas_call | solution.py:27
  9.2 1.6 %collective-permute-start.2 = (s32[4,8]{1,0:T(4,128)S(1)}, s32[4,8]{1,0:T(4,128)S(1)}, u32[]{:S(2)}, u32[]{:S(2)}) collective-permute-start(s32[4,8]{1,0:T(4,128)S(1)} %get-tuple-element.43), channel_id=1, source_target_pairs={{0,8},{8,0},{16,24},{24,16},{1,9},{9,1},{17,25},{25,17},{2,10},{10... | collective-permute-start | bytes 392 | tf_op jit(solution)/shard_map/ppermute | solution.py:74
  10.9 2.0 %collective-permute-done.2 = s32[4,8]{1,0:T(4,128)S(1)} collective-permute-done((s32[4,8]{1,0:T(4,128)S(1)}, s32[4,8]{1,0:T(4,128)S(1)}, u32[]{:S(2)}, u32[]{:S(2)}) %collective-permute-start.2) | collective-permute-done | bytes 160 | tf_op jit(solution)/shard_map/ppermute | solution.py:74
  13.7 4.4 %collective-permute-start.3 = (bf16[2,8,32,256]{3,2,1,0:T(8,128)(2,1)S(1)}, bf16[2,8,32,256]{3,2,1,0:T(8,128)(2,1)S(1)}, u32[]{:S(2)}, u32[]{:S(2)}) collective-permute-start(bf16[2,8,32,256]{3,2,1,0:T(8,128)(2,1)S(1)} %get-tuple-element.46), channel_id=1, source_target_pairs={{0,8},{16,24},{8,0},{24,16},{1,9},{17,25},{9,1},{25,17},{2,10},{18... | collective-permute-start | bytes 786440 | tf_op jit(solution)/shard_map/ppermute | solution.py:67
  18.5 4.5 %shard_map.76 = (bf16[128,2048]{1,0:T(8,128)(2,1)S(1)}, bf16[128,2048]{1,0:T(8,128)(2,1)}, bf16[1152,128]{1,0:T(8,128)(2,1)}) custom-call(s32[1,8]{1,0:T(1,128)S(1)} %copy-done.7, bf16[1,1920,128]{2,1,0:T(8,128)(2,1)} %basis_kept), custom_call_target="tpu_custom_call" | custom-call | flops 402653184 | bytes 1474560 | tf_op jit(solution)/shard_map/pallas_call | solution.py:610
  23.0 2.0 %collective-permute-done.5 = s32[4,8]{1,0:T(4,128)S(1)} collective-permute-done((s32[4,8]{1,0:T(4,128)S(1)}, s32[4,8]{1,0:T(4,128)S(1)}, u32[]{:S(2)}, u32[]{:S(2)}) %collective-permute-start.5) | collective-permute-done | bytes 160 | tf_op jit(solution)/shard_map/ppermute | solution.py:74
  25.1 1.4 %shard_map.77 = (bf16[8,128,128]{2,1,0:T(8,128)(2,1)}, bf16[64,32,256]{2,1,0:T(8,128)(2,1)}) custom-call(f32[36,32,256]{2,1,0:T(8,128)S(1)} %get-tuple-element.39.sol.sol_kept, f32[36,32,256]{2,1,0:T(8,128)S(1)} %get-tuple-element.40.base.refs_0_, bf16[2,6,32,256]{3,2,1,0:T(8,128)(2,1)S(1)} %collective-permute-done.first_in.first_q, ...), custom_call_target="tpu_custom_call" | custom-call | flops 134217728 | bytes 5111808 | tf_op jit(solution)/shard_map/pallas_call | solution.py:27
  26.5 3.8 %all-to-all-start = ((bf16[8,128,128]{2,1,0:T(8,128)(2,1)}), bf16[8,128,128]{2,1,0:T(8,128)(2,1)S(1)}, u32[]{:S(2)}, u32[]{:S(2)}) async-start(bf16[8,128,128]{2,1,0:T(8,128)(2,1)} %get-tuple-element.54), calls=%async_computation | async-start | bytes 524288 | tf_op jit(solution)/shard_map/all_to_all | solution.py:851
  30.9 4.0 %shard_map.78.spread = bf16[1024,1024]{1,0:T(8,128)(2,1)} custom-call(s32[4,8]{1,0:T(4,128)S(1)} %add.7.every, bf16[4,64,512]{2,1,0:T(8,128)(2,1)} %inverse_kept.3, bf16[4,64,512]{2,1,0:T(8,128)(2,1)} %copy-done.9), custom_call_target="tpu_custom_call" | custom-call | flops 1073741824 | bytes 2097152 | tf_op jit(solution)/shard_map/pallas_call | solution.py:698
  34.9 1.4 %all-to-all-done = bf16[8,128,128]{2,1,0:T(8,128)(2,1)S(1)} async-done(((bf16[8,128,128]{2,1,0:T(8,128)(2,1)}), bf16[8,128,128]{2,1,0:T(8,128)(2,1)S(1)}, u32[]{:S(2)}, u32[]{:S(2)}) %all-to-all-start) | async-done | bytes 262176 | tf_op jit(solution)/shard_map/all_to_all | solution.py:851
  36.3 1.6 %copy-done.3 = bf16[1024,1024]{1,0:T(8,128)(2,1)S(1)} copy-done((bf16[1024,1024]{1,0:T(8,128)(2,1)S(1)}, bf16[1024,1024]{1,0:T(8,128)(2,1)}, u32[]{:S(2)}) %copy-start.3) | copy-done | bytes 2097176
  37.9 1.4 %shard_map.79 = bf16[1024,128]{1,0:T(8,128)(2,1)} custom-call(bf16[1024,1024]{1,0:T(8,128)(2,1)S(1)} %copy-done.3, bf16[1024,128]{1,0:T(8,128)(2,1)S(1)} %bitcast.12), custom_call_target="tpu_custom_call" | custom-call | flops 268435456 | bytes 2621440 | tf_op jit(solution)/shard_map/pallas_call | solution.py:27
  39.3 4.0 %all-to-all-start.1 = ((bf16[32,32,128]{2,1,0:T(8,128)(2,1)}), bf16[32,32,128]{2,1,0:T(8,128)(2,1)S(1)}, u32[]{:S(2)}, u32[]{:S(2)}) async-start(bf16[32,32,128]{2,1,0:T(8,128)(2,1)} %bitcast.21), calls=%async_computation.1 | async-start | bytes 524288 | tf_op jit(solution)/shard_map/all_to_all | solution.py:860
  43.4 7.1 %shard_map.80 = (f32[36,32,256]{2,1,0:T(8,128)}, f32[36,32,256]{2,1,0:T(8,128)}) custom-call(bf16[64,32,256]{2,1,0:T(8,128)(2,1)} %get-tuple-element.58.local_kept, bf16[1,1920,1920]{2,1,0:T(8,128)(2,1)} %inverse_kept.5, f32[36,32,256]{2,1,0:T(8,128)} %copy-done.1, f32[36,32,256]{2,1,0:T(8,128)} %copy-done.2, f32[6,6,3,10]{3,2,1,0:T(4,128)S(1)} %copy-done.6), custom_call_target="tpu_custom_call" | custom-call | flops 1415577600 | bytes 13144288 | tf_op jit(solution)/shard_map/pallas_call | solution.py:27
  50.5 3.6 %all-to-all-done.1 = bf16[32,32,128]{2,1,0:T(8,128)(2,1)S(1)} async-done(((bf16[32,32,128]{2,1,0:T(8,128)(2,1)}), bf16[32,32,128]{2,1,0:T(8,128)(2,1)S(1)}, u32[]{:S(2)}, u32[]{:S(2)}) %all-to-all-start.1) | async-done | bytes 262176 | tf_op jit(solution)/shard_map/all_to_all | solution.py:860
  54.1 1.6 %shard_map.81 = (bf16[2,6,32,256]{3,2,1,0:T(8,128)(2,1)S(1)}, bf16[2,6,32,256]{3,2,1,0:T(8,128)(2,1)S(1)}, f32[36,32,256]{2,1,0:T(8,128)S(1)}) custom-call(bf16[4,8,32,128]{3,2,1,0:T(8,128)(2,1)S(1)} %bitcast.11, bf16[1152,128]{1,0:T(8,128)(2,1)} %get-tuple-element.57.basis_kept, f32[6,6,32,256]{3,2,1,0:T(8,128)} %bitcast.19, f32[6,6,32,256]{3,2,1,0:T(8,128)} %bitcast.20, ...), custom_call_target="tpu_custom_call" | custom-call | bytes 4493536 | tf_op jit(solution)/shard_map/pallas_call | solution.py:27
  55.7 0.9 collective-permute-start.7
  57.2 2.5 %shard_map.82 = (f32[36,32,256]{2,1,0:T(8,128)S(1)}, f32[36,32,256]{2,1,0:T(8,128)S(1)}) custom-call(f32[36,32,256]{2,1,0:T(8,128)S(1)} %get-tuple-element.61.coarse, f32[36,32,256]{2,1,0:T(8,128)} %get-tuple-element.59.sol_kept, f32[36,32,256]{2,1,0:T(8,128)} %get-tuple-element.60.base_kept, f32[6,6,3,10]{3,2,1,0:T(4,128)} %stiffness.7), custom_call_target="tpu_custom_call" | custom-call | bytes 5902560 | tf_op jit(solution)/shard_map/pallas_call | solution.py:27
  59.7 3.0 %collective-permute-done.7.first_in.first_q = bf16[2,6,32,256]{3,2,1,0:T(8,128)(2,1)S(1)} collective-permute-done((bf16[2,6,32,256]{3,2,1,0:T(8,128)(2,1)S(1)}, bf16[2,6,32,256]{3,2,1,0:T(8,128)(2,1)S(1)}, u32[]{:S(2)}, u32[]{:S(2)}) %collective-permute-start.7) | collective-permute-done | bytes 196640 | tf_op jit(solution)/shard_map/ppermute | solution.py:67
  62.8 1.7 %collective-permute-start.9 = (bf16[2,8,32,256]{3,2,1,0:T(8,128)(2,1)S(1)}, bf16[2,8,32,256]{3,2,1,0:T(8,128)(2,1)S(1)}, u32[]{:S(2)}, u32[]{:S(2)}) collective-permute-start(bf16[2,8,32,256]{3,2,1,0:T(8,128)(2,1)S(1)} %get-tuple-element.66), channel_id=1, source_target_pairs={{0,8},{16,24},{8,0},{24,16},{1,9},{17,25},{9,1},{25,17},{2,10},{18... | collective-permute-start | bytes 786440 | tf_op jit(solution)/shard_map/ppermute | solution.py:67
  64.4 0.8 collective-permute-start.10
  65.3 0.9 shard_map.84
  66.2 4.7 %collective-permute-done.9.first_s = bf16[2,8,32,256]{3,2,1,0:T(8,128)(2,1)S(1)} collective-permute-done((bf16[2,8,32,256]{3,2,1,0:T(8,128)(2,1)S(1)}, bf16[2,8,32,256]{3,2,1,0:T(8,128)(2,1)S(1)}, u32[]{:S(2)}, u32[]{:S(2)}) %collective-permute-start.9) | collective-permute-done | bytes 262176 | tf_op jit(solution)/shard_map/ppermute | solution.py:67
  70.9 1.2 %shard_map.85 = (bf16[8,128,128]{2,1,0:T(8,128)(2,1)}, bf16[64,32,256]{2,1,0:T(8,128)(2,1)}) custom-call(f32[36,32,256]{2,1,0:T(8,128)S(1)} %get-tuple-element.62.sol.sol_kept, f32[36,32,256]{2,1,0:T(8,128)S(1)} %get-tuple-element.63.base, bf16[2,6,32,256]{3,2,1,0:T(8,128)(2,1)S(1)} %collective-permute-done.7.first_in.first_q, ...), custom_call_target="tpu_custom_call", output_to_operand_aliasing={{1}: (8, {})} | custom-call | flops 67108864 | bytes 6291456 | tf_op jit(solution)/shard_map/pallas_call | solution.py:27
  72.1 11.0 %all_to_all.20 = bf16[8,128,128]{2,1,0:T(8,128)(2,1)S(1)} all-to-all(bf16[8,128,128]{2,1,0:T(8,128)(2,1)} %get-tuple-element.71), channel_id=1, replica_groups=mesh['sub'=4,'crow'=4,'ccol'=2] {'crow','ccol'}, dimensions={0} | all-to-all | bytes 524288 | tf_op jit(solution)/shard_map/all_to_all | solution.py:851
  83.1 1.4 %shard_map.86 = bf16[1024,128]{1,0:T(8,128)(2,1)} custom-call(bf16[1024,1024]{1,0:T(8,128)(2,1)S(1)} %copy-done.4, bf16[1024,128]{1,0:T(8,128)(2,1)S(1)} %bitcast.14), custom_call_target="tpu_custom_call" | custom-call | flops 268435456 | bytes 2621440 | tf_op jit(solution)/shard_map/pallas_call | solution.py:27
  84.5 4.9 %all-to-all-start.3 = ((bf16[32,32,128]{2,1,0:T(8,128)(2,1)}), bf16[32,32,128]{2,1,0:T(8,128)(2,1)S(1)}, u32[]{:S(2)}, u32[]{:S(2)}) async-start(bf16[32,32,128]{2,1,0:T(8,128)(2,1)} %bitcast.22), calls=%async_computation.3 | async-start | bytes 524288 | tf_op jit(solution)/shard_map/all_to_all | solution.py:860
  89.4 6.1 %shard_map.87.sol_kept = f32[36,32,256]{2,1,0:T(8,128)} custom-call(bf16[64,32,256]{2,1,0:T(8,128)(2,1)} %get-tuple-element.72.local_kept, bf16[1,1920,1920]{2,1,0:T(8,128)(2,1)} %inverse_kept.5, f32[36,32,256]{2,1,0:T(8,128)} %copy-done), custom_call_target="tpu_custom_call" | custom-call | flops 1415577600 | bytes 10780672 | tf_op jit(solution)/shard_map/pallas_call | solution.py:27
  95.5 4.6 %all-to-all-done.3 = bf16[32,32,128]{2,1,0:T(8,128)(2,1)S(1)} async-done(((bf16[32,32,128]{2,1,0:T(8,128)(2,1)}), bf16[32,32,128]{2,1,0:T(8,128)(2,1)S(1)}, u32[]{:S(2)}, u32[]{:S(2)}) %all-to-all-start.3) | async-done | bytes 262176 | tf_op jit(solution)/shard_map/all_to_all | solution.py:860
  100.1 2.9 %shard_map.88 = f32[6,6,10,3,256]{4,3,2,1,0:T(4,128)} custom-call(bf16[4,8,32,128]{3,2,1,0:T(8,128)(2,1)S(1)} %bitcast.13, bf16[1152,128]{1,0:T(8,128)(2,1)} %get-tuple-element.57.basis_kept, f32[36,32,256]{2,1,0:T(8,128)} %shard_map.87.sol_kept), custom_call_target="tpu_custom_call" | custom-call | bytes 2842624 | tf_op jit(solution)/shard_map/pallas_call | solution.py:27
  (35 shorter events, 3.4 us)
Async XLA Ops:
  2.0 10.8 %collective-permute-start = (bf16[2,6,32,256]{3,2,1,0:T(8,128)(2,1)S(1)}, bf16[2,6,32,256]{3,2,1,0:T(8,128)(2,1)S(1)}, u32[]{:S(2)}, u32[]{:S(2)}) collective-permute-start(bf16[2,6,32,256]{3,2,1,0:T(8,128)(2,1)S(1)} %get-tuple-element.41), channel_id=1, source_target_pairs={{0,1},{2,3},{4,5},{6,7},{1,0},{3,2},{5,4},{7,6},{8,9},{10,11},{12,... | collective-permute-start | bytes 589832 | tf_op jit(solution)/shard_map/ppermute | solution.py:67
  5.1 7.8 %collective-permute-start.1 = (bf16[2,6,32,256]{3,2,1,0:T(8,128)(2,1)S(1)}, bf16[2,6,32,256]{3,2,1,0:T(8,128)(2,1)S(1)}, u32[]{:S(2)}, u32[]{:S(2)}) collective-permute-start(bf16[2,6,32,256]{3,2,1,0:T(8,128)(2,1)S(1)} %get-tuple-element.42), channel_id=1, source_target_pairs={{1,2},{3,4},{5,6},{2,1},{4,3},{6,5},{9,10},{11,12},{13,14},{10,9},... | collective-permute-start | bytes 589832 | tf_op jit(solution)/shard_map/ppermute | solution.py:68
  9.2 15.9 %copy-start.1 = (f32[36,32,256]{2,1,0:T(8,128)}, f32[36,32,256]{2,1,0:T(8,128)S(1)}, u32[]{:S(2)}) copy-start(f32[36,32,256]{2,1,0:T(8,128)S(1)} %get-tuple-element.39.sol.sol_kept) | copy-start | bytes 3538948
  9.2 15.9 %copy-start.2 = (f32[36,32,256]{2,1,0:T(8,128)}, f32[36,32,256]{2,1,0:T(8,128)S(1)}, u32[]{:S(2)}) copy-start(f32[36,32,256]{2,1,0:T(8,128)S(1)} %get-tuple-element.40.base.refs_0_) | copy-start | bytes 3538948
  9.2 3.7 %collective-permute-start.2 = (s32[4,8]{1,0:T(4,128)S(1)}, s32[4,8]{1,0:T(4,128)S(1)}, u32[]{:S(2)}, u32[]{:S(2)}) collective-permute-start(s32[4,8]{1,0:T(4,128)S(1)} %get-tuple-element.43), channel_id=1, source_target_pairs={{0,8},{8,0},{16,24},{24,16},{1,9},{9,1},{17,25},{25,17},{2,10},{10... | collective-permute-start | bytes 392 | tf_op jit(solution)/shard_map/ppermute | solution.py:74
  12.9 5.3 %copy-start.8 = (bf16[4,64,512]{2,1,0:T(8,128)(2,1)S(1)}, bf16[4,64,512]{2,1,0:T(8,128)(2,1)}, u32[]{:S(2)}) copy-start(bf16[4,64,512]{2,1,0:T(8,128)(2,1)} %inverse_kept.3) | copy-start | bytes 786436
  12.9 5.6 %copy-start.7 = (s32[1,8]{1,0:T(1,128)S(1)}, s32[1,8]{1,0:T(1,128)}, u32[]{:S(2)}) copy-start(s32[1,8]{1,0:T(1,128)} %offsets.3) | copy-start | bytes 100
  13.0 12.0 %collective-permute-start.4 = (bf16[2,8,32,256]{3,2,1,0:T(8,128)(2,1)S(1)}, bf16[2,8,32,256]{3,2,1,0:T(8,128)(2,1)S(1)}, u32[]{:S(2)}, u32[]{:S(2)}) collective-permute-start(bf16[2,8,32,256]{3,2,1,0:T(8,128)(2,1)S(1)} %get-tuple-element.47), channel_id=1, source_target_pairs={{8,16},{16,8},{9,17},{17,9},{10,18},{18,10},{11,19},{19,11},{12,20... | collective-permute-start | bytes 786440 | tf_op jit(solution)/shard_map/ppermute | solution.py:68
  13.7 11.4 %collective-permute-start.3 = (bf16[2,8,32,256]{3,2,1,0:T(8,128)(2,1)S(1)}, bf16[2,8,32,256]{3,2,1,0:T(8,128)(2,1)S(1)}, u32[]{:S(2)}, u32[]{:S(2)}) collective-permute-start(bf16[2,8,32,256]{3,2,1,0:T(8,128)(2,1)S(1)} %get-tuple-element.46), channel_id=1, source_target_pairs={{0,8},{16,24},{8,0},{24,16},{1,9},{17,25},{9,1},{25,17},{2,10},{18... | collective-permute-start | bytes 786440 | tf_op jit(solution)/shard_map/ppermute | solution.py:67
  18.1 12.1 %collective-permute-start.6 = (bf16[4,64,512]{2,1,0:T(8,128)(2,1)S(1)}, bf16[4,64,512]{2,1,0:T(8,128)(2,1)S(1)}, u32[]{:S(2)}, u32[]{:S(2)}) collective-permute-start(bf16[4,64,512]{2,1,0:T(8,128)(2,1)S(1)} %copy-done.8), channel_id=1, source_target_pairs={{0,2},{1,3},{2,0},{3,1},{4,6},{5,7},{6,4},{7,5},{8,10},{9,11},{10,... | collective-permute-start | bytes 786440 | tf_op jit(solution)/shard_map/ppermute | solution.py:800
  18.3 6.7 %collective-permute-start.5 = (s32[4,8]{1,0:T(4,128)S(1)}, s32[4,8]{1,0:T(4,128)S(1)}, u32[]{:S(2)}, u32[]{:S(2)}) collective-permute-start(s32[4,8]{1,0:T(4,128)S(1)} %add.6), channel_id=1, source_target_pairs={{0,16},{8,24},{16,0},{24,8},{1,17},{9,25},{17,1},{25,9},{2,18},{10... | collective-permute-start | bytes 392 | tf_op jit(solution)/shard_map/ppermute | solution.py:74
  26.5 9.8 %all-to-all-start = ((bf16[8,128,128]{2,1,0:T(8,128)(2,1)}), bf16[8,128,128]{2,1,0:T(8,128)(2,1)S(1)}, u32[]{:S(2)}, u32[]{:S(2)}) async-start(bf16[8,128,128]{2,1,0:T(8,128)(2,1)} %get-tuple-element.54), calls=%async_computation | async-start | bytes 524288 | tf_op jit(solution)/shard_map/all_to_all | solution.py:851
  30.3 0.7 copy-start.9
  36.3 1.6 %copy-start.3 = (bf16[1024,1024]{1,0:T(8,128)(2,1)S(1)}, bf16[1024,1024]{1,0:T(8,128)(2,1)}, u32[]{:S(2)}) copy-start(bf16[1024,1024]{1,0:T(8,128)(2,1)} %shard_map.78.spread) | copy-start | bytes 6291460
  37.9 5.5 %copy-start.6 = (f32[6,6,3,10]{3,2,1,0:T(4,128)S(1)}, f32[6,6,3,10]{3,2,1,0:T(4,128)}, u32[]{:S(2)}) copy-start(f32[6,6,3,10]{3,2,1,0:T(4,128)} %stiffness.7) | copy-start | bytes 12964
  39.3 14.7 %all-to-all-start.1 = ((bf16[32,32,128]{2,1,0:T(8,128)(2,1)}), bf16[32,32,128]{2,1,0:T(8,128)(2,1)S(1)}, u32[]{:S(2)}, u32[]{:S(2)}) async-start(bf16[32,32,128]{2,1,0:T(8,128)(2,1)} %bitcast.21), calls=%async_computation.1 | async-start | bytes 524288 | tf_op jit(solution)/shard_map/all_to_all | solution.py:860
  55.7 7.0 %collective-permute-start.7 = (bf16[2,6,32,256]{3,2,1,0:T(8,128)(2,1)S(1)}, bf16[2,6,32,256]{3,2,1,0:T(8,128)(2,1)S(1)}, u32[]{:S(2)}, u32[]{:S(2)}) collective-permute-start(bf16[2,6,32,256]{3,2,1,0:T(8,128)(2,1)S(1)} %get-tuple-element.64), channel_id=1, source_target_pairs={{0,1},{2,3},{4,5},{6,7},{1,0},{3,2},{5,4},{7,6},{8,9},{10,11},{12,... | collective-permute-start | bytes 589832 | tf_op jit(solution)/shard_map/ppermute | solution.py:67
  56.6 6.1 %collective-permute-start.8 = (bf16[2,6,32,256]{3,2,1,0:T(8,128)(2,1)S(1)}, bf16[2,6,32,256]{3,2,1,0:T(8,128)(2,1)S(1)}, u32[]{:S(2)}, u32[]{:S(2)}) collective-permute-start(bf16[2,6,32,256]{3,2,1,0:T(8,128)(2,1)S(1)} %get-tuple-element.65), channel_id=1, source_target_pairs={{1,2},{3,4},{5,6},{2,1},{4,3},{6,5},{9,10},{11,12},{13,14},{10,9},... | collective-permute-start | bytes 589832 | tf_op jit(solution)/shard_map/ppermute | solution.py:68
  59.7 11.2 %copy-start = (f32[36,32,256]{2,1,0:T(8,128)}, f32[36,32,256]{2,1,0:T(8,128)S(1)}, u32[]{:S(2)}) copy-start(f32[36,32,256]{2,1,0:T(8,128)S(1)} %get-tuple-element.62.sol.sol_kept) | copy-start | bytes 3538948
  62.7 2.6 %copy-start.5 = (bf16[128,2048]{1,0:T(8,128)(2,1)S(1)}, bf16[128,2048]{1,0:T(8,128)(2,1)}, u32[]{:S(2)}) copy-start(bf16[128,2048]{1,0:T(8,128)(2,1)} %get-tuple-element.68.basis_t) | copy-start | bytes 1572868
  62.8 8.1 %collective-permute-start.9 = (bf16[2,8,32,256]{3,2,1,0:T(8,128)(2,1)S(1)}, bf16[2,8,32,256]{3,2,1,0:T(8,128)(2,1)S(1)}, u32[]{:S(2)}, u32[]{:S(2)}) collective-permute-start(bf16[2,8,32,256]{3,2,1,0:T(8,128)(2,1)S(1)} %get-tuple-element.66), channel_id=1, source_target_pairs={{0,8},{16,24},{8,0},{24,16},{1,9},{17,25},{9,1},{25,17},{2,10},{18... | collective-permute-start | bytes 786440 | tf_op jit(solution)/shard_map/ppermute | solution.py:67
  64.4 6.4 %collective-permute-start.10 = (bf16[2,8,32,256]{3,2,1,0:T(8,128)(2,1)S(1)}, bf16[2,8,32,256]{3,2,1,0:T(8,128)(2,1)S(1)}, u32[]{:S(2)}, u32[]{:S(2)}) collective-permute-start(bf16[2,8,32,256]{3,2,1,0:T(8,128)(2,1)S(1)} %get-tuple-element.67), channel_id=1, source_target_pairs={{8,16},{16,8},{9,17},{17,9},{10,18},{18,10},{11,19},{19,11},{12,20... | collective-permute-start | bytes 786440 | tf_op jit(solution)/shard_map/ppermute | solution.py:68
  70.9 12.2 %copy-start.4 = (bf16[1024,1024]{1,0:T(8,128)(2,1)S(1)}, bf16[1024,1024]{1,0:T(8,128)(2,1)}, u32[]{:S(2)}) copy-start(bf16[1024,1024]{1,0:T(8,128)(2,1)} %shard_map.78.spread) | copy-start | bytes 6291460
  84.5 15.6 %all-to-all-start.3 = ((bf16[32,32,128]{2,1,0:T(8,128)(2,1)}), bf16[32,32,128]{2,1,0:T(8,128)(2,1)S(1)}, u32[]{:S(2)}, u32[]{:S(2)}) async-start(bf16[32,32,128]{2,1,0:T(8,128)(2,1)} %bitcast.22), calls=%async_computation.3 | async-start | bytes 524288 | tf_op jit(solution)/shard_map/all_to_all | solution.py:860

commit v9 on v7

--- a/solution.py
+++ b/solution.py
@@ -21,7 +21,7 @@
     return math.prod(x.shape) * jnp.dtype(x.dtype).itemsize
 
 
-def call(body, ins, outs, scratch=(), flops=0, held=()):
+def call(body, ins, outs, scratch=(), flops=0, held=(), aliases=None):
     size = sum(sized(x) for x in (*ins, *outs))
     room = size + sum(sized(x) for x in scratch if getattr(x, "dtype", None) in (bf16, f32))
     return pl.pallas_call(
@@ -32,6 +32,7 @@
             HBM if getattr(x, "memory_space", None) == pltpu.HBM else VMEM for x in outs
         ),
         scratch_shapes=list(scratch),
+        input_output_aliases=aliases or {},
         compiler_params=pltpu.CompilerParams(vmem_limit_bytes=room + (4 << 20)),
         cost_estimate=pl.CostEstimate(flops=flops, bytes_accessed=size, transcendentals=0),
     )(
@@ -216,7 +217,33 @@
     return (member // PARTNER) % 2
 
 
-def window_kernel(
+def middle_window_kernel(
+    shape, sol, base, first_q, second_q, basis_t, local_kept, product, local, sems
+):
+    cells_s, cells_q, _, pad, columns = shape
+    wide = cells_q + 2
+    low, high = column_sides(first_q, second_q)
+    copies = []
+    for s in range(1, cells_s - 1):
+        left, right = edge_cells(low, high, sol, s, cells_q)
+        values = [left] + [base[s * cells_q + q] for q in range(cells_q)] + [right]
+        values[1] = values[1] + low(1, s)
+        values[cells_q] = values[cells_q] + high(1, s)
+        for w in range(wide):
+            local[(s - 1) * wide + w] = values[w].astype(bf16)
+        part, there = pl.ds((s - 1) * wide, wide), pl.ds((s + 1) * wide, wide)
+        copies.append(begun(local.at[part], local_kept.at[there], sems.at[len(copies)]))
+    chunk = wide * pad
+    product[...] = jnp.dot(
+        basis_t[:, 2 * chunk : cells_s * chunk],
+        local[...].reshape(-1, columns),
+        preferred_element_type=f32,
+    )
+    for copy in copies:
+        copy.wait()
+
+
+def outer_window_kernel(
     shape,
     sol,
     base,
@@ -225,6 +252,8 @@
     first_s,
     second_s,
     basis_t,
+    middle,
+    begun_kept,
     message,
     local_kept,
     local,
@@ -244,7 +273,7 @@
         return jnp.where(even, first_s[kind, w].astype(f32), second_s[kind, w].astype(f32))
 
     copies = []
-    for s in range(cells_s):
+    for s in (0, cells_s - 1):
         left, right = edge_cells(low, high, sol, s, cells_q)
         values = [left] + [base[s * cells_q + q] for q in range(cells_q)] + [right]
         values[1] = values[1] + low(1, s)
@@ -267,9 +296,15 @@
             local[place + w] = jnp.where(there, side(0, w) + near[w], 0.0).astype(bf16)
         part = pl.ds(place, wide)
         copies.append(begun(local.at[part], local_kept.at[part], sems.at[len(copies)]))
-    product = jnp.dot(
-        basis_t[...], local[...].reshape(-1, columns), preferred_element_type=f32
-    ).astype(bf16)
+    chunk = wide * pad
+    product = middle[...]
+    for r in (0, cells_s):
+        product = product + jnp.dot(
+            basis_t[:, r * chunk : (r + 2) * chunk],
+            local[r * wide : (r + 2) * wide].reshape(-1, columns),
+            preferred_element_type=f32,
+        )
+    product = product.astype(bf16)
     half = columns // 2
     for k in range(2):
         restricted[k] = product[:, k * half : (k + 1) * half]
@@ -702,9 +737,23 @@
             partner = lax.ppermute(shared, GROUP_AXES, pairs)
             every = doubled(every, 1 << (rounds - 1))
             first_s, second_s, every = lax.optimization_barrier((first_s, second_s, every))
+        turned = basis_t if sweep == 0 else basis_kept
+        begun_kept, middle = call(
+            functools.partial(middle_window_kernel, shape),
+            (solution, base, first_q, second_q, turned),
+            (
+                pltpu.HBM(((cells_s + 2) * wide, pad, columns), bf16),
+                jax.ShapeDtypeStruct((coarse, columns), f32),
+            ),
+            scratch=(
+                pltpu.VMEM(((cells_s - 2) * wide, pad, columns), bf16),
+                pltpu.SemaphoreType.DMA((cells_s - 2,)),
+            ),
+            flops=rows * coarse * columns,
+        )
         message, local = call(
-            functools.partial(window_kernel, shape),
-            (solution, base, first_q, second_q, first_s, second_s, basis_t if sweep == 0 else basis_kept),
+            functools.partial(outer_window_kernel, shape),
+            (solution, base, first_q, second_q, first_s, second_s, turned, middle, begun_kept),
             (
                 pltpu.HBM((groups, coarse, columns // 2), bf16),
                 pltpu.HBM(((cells_s + 2) * wide, pad, columns), bf16),
@@ -714,7 +763,9 @@
                 pltpu.VMEM((2, coarse, columns // 2), bf16),
                 pltpu.SemaphoreType.DMA((groups + cells_s + 2,)),
             ),
-            flops=2 * rows * coarse * columns,
+            flops=rows * coarse * columns,
+            held=(8,),
+            aliases={8: 1},
         )
         if sweep == 0:
             waited, _ = lax.optimization_barrier((every, message))

time: 104 us -> 104 us (level)
  waiting for transfers between devices: 22.2 us -> 20.4 us
  Pallas kernels: 40 us -> 41.4 us
    pallas_call x13 -> x15, Pallas kernels: 31.5 us -> 32.9 us  [call(): pl.pallas_call(body, out_shape=tuple(outs), in_specs=[HBM if i in held el...]
  transfers between devices with their start and end apart: 14 -> 14, of which waited for: 8 -> 8; matrix products, arithmetic and copies ran while one was open for 0% -> 0% of each run, Pallas kernels for 28% -> 30%
where the time goes in v9:
time: 104 us; the launch traced here: 103 us
  Pallas kernels  41.4 us (40%)
  starting transfers between devices  27.6 us (27%)
  waiting for transfers between devices  20.4 us (20%)
  blocking collectives  11 us (11%)
  local copies, waits for them, and re-layouts  2.32 us (2%)
    pallas_call x15, Pallas kernels, call(): pl.pallas_call(body, out_shape=tuple(outs), in_specs=[HBM if i in held el...  32.9 us
    all_to_all x1, blocking collectives, shards(): gathered = lax.all_to_all(message, GROUP_AXES, 0, 0, tiled=True)  11 us
    ppermute x4, starting transfers between devices, swap(): lax.ppermute(first, axis, even + [(b, a) for a, b in even])  10 us
    all_to_all x2, starting transfers between devices, shards(): lax.all_to_all(terms.reshape(n_sub * groups, 2 * depth, columns // 2), AL...  8.96 us
    all_to_all x2, waiting for transfers between devices, shards(): lax.all_to_all(terms.reshape(n_sub * groups, 2 * depth, columns // 2), AL...  8.21 us
    ppermute x4, waiting for transfers between devices, swap(): lax.ppermute(first, axis, even + [(b, a) for a, b in even])  7.77 us
    pallas_call x1, Pallas kernels, ordered_basis(): pl.pallas_call(functools.partial(basis_kernel, cell, dims), out_shape=(ja...  4.48 us
    pallas_call x1, Pallas kernels, spread_inverse(): pl.pallas_call(functools.partial(spread_kernel, (groups, depth, kgroup)),...  3.99 us
  transfers between devices with their start and end apart: 14, of which 8 were waited for; matrix products, arithmetic and copies ran while one was open for 0% of the time, Pallas kernels for 30%

profile of v9, /device:TPU:0, one launch (start us, length us, event | category | flops | bytes accessed | tf_op | source)
XLA Modules:
  0.0 103.1 jit_solution(6000509868304253000)
XLA Ops:
  0.0 2.0 %shard_map.74 = (bf16[2,6,32,256]{3,2,1,0:T(8,128)(2,1)S(1)}, bf16[2,6,32,256]{3,2,1,0:T(8,128)(2,1)S(1)}) custom-call(f32[6,6,10,3,256]{4,3,2,1,0:T(4,128)} %bitcast.15, f32[6,6,10,3,256]{4,3,2,1,0:T(4,128)} %bitcast.17, f32[6,6,3,10]{3,2,1,0:T(4,128)} %stiffness.7), custom_call_target="tpu_custom_call" | custom-call | bytes 2609376 | tf_op jit(solution)/shard_map/pallas_call | solution.py:27
  2.0 3.0 %collective-permute-start = (bf16[2,6,32,256]{3,2,1,0:T(8,128)(2,1)S(1)}, bf16[2,6,32,256]{3,2,1,0:T(8,128)(2,1)S(1)}, u32[]{:S(2)}, u32[]{:S(2)}) collective-permute-start(bf16[2,6,32,256]{3,2,1,0:T(8,128)(2,1)S(1)} %get-tuple-element.43), channel_id=1, source_target_pairs={{0,1},{2,3},{4,5},{6,7},{1,0},{3,2},{5,4},{7,6},{8,9},{10,11},{12,... | collective-permute-start | bytes 589832 | tf_op jit(solution)/shard_map/ppermute | solution.py:67
  5.7 3.5 %shard_map.73 = (f32[36,32,256]{2,1,0:T(8,128)S(1)}, f32[36,32,256]{2,1,0:T(8,128)S(1)}, s32[4,8]{1,0:T(4,128)S(1)}) custom-call(f32[6,6,10,3,256]{4,3,2,1,0:T(4,128)} %bitcast.16, f32[6,6,10,3,256]{4,3,2,1,0:T(4,128)} %bitcast.18, f32[6,6,3,10]{3,2,1,0:T(4,128)} %stiffness.7, s32[1,8]{1,0:T(1,128)} %offsets.3), custom_call_target="tpu_custom_call" | custom-call | bytes 4575616 | tf_op jit(solution)/shard_map/pallas_call | solution.py:27
  9.2 1.6 %collective-permute-start.2 = (s32[4,8]{1,0:T(4,128)S(1)}, s32[4,8]{1,0:T(4,128)S(1)}, u32[]{:S(2)}, u32[]{:S(2)}) collective-permute-start(s32[4,8]{1,0:T(4,128)S(1)} %get-tuple-element.45), channel_id=1, source_target_pairs={{0,8},{8,0},{16,24},{24,16},{1,9},{9,1},{17,25},{25,17},{2,10},{10... | collective-permute-start | bytes 392 | tf_op jit(solution)/shard_map/ppermute | solution.py:74
  10.9 2.0 %collective-permute-done.2 = s32[4,8]{1,0:T(4,128)S(1)} collective-permute-done((s32[4,8]{1,0:T(4,128)S(1)}, s32[4,8]{1,0:T(4,128)S(1)}, u32[]{:S(2)}, u32[]{:S(2)}) %collective-permute-start.2) | collective-permute-done | bytes 160 | tf_op jit(solution)/shard_map/ppermute | solution.py:74
  13.7 4.4 %collective-permute-start.3 = (bf16[2,8,32,256]{3,2,1,0:T(8,128)(2,1)S(1)}, bf16[2,8,32,256]{3,2,1,0:T(8,128)(2,1)S(1)}, u32[]{:S(2)}, u32[]{:S(2)}) collective-permute-start(bf16[2,8,32,256]{3,2,1,0:T(8,128)(2,1)S(1)} %get-tuple-element.48), channel_id=1, source_target_pairs={{0,8},{16,24},{8,0},{24,16},{1,9},{17,25},{9,1},{25,17},{2,10},{18... | collective-permute-start | bytes 786440 | tf_op jit(solution)/shard_map/ppermute | solution.py:67
  18.5 4.5 %shard_map.76 = (bf16[128,2048]{1,0:T(8,128)(2,1)S(1)}, bf16[128,2048]{1,0:T(8,128)(2,1)}, bf16[1152,128]{1,0:T(8,128)(2,1)}) custom-call(s32[1,8]{1,0:T(1,128)S(1)} %copy-done.7, bf16[1,1920,128]{2,1,0:T(8,128)(2,1)} %basis_kept), custom_call_target="tpu_custom_call" | custom-call | flops 402653184 | bytes 1474560 | tf_op jit(solution)/shard_map/pallas_call | solution.py:547
  23.0 0.9 shard_map.77
  23.9 1.1 %collective-permute-done.5 = s32[4,8]{1,0:T(4,128)S(1)} collective-permute-done((s32[4,8]{1,0:T(4,128)S(1)}, s32[4,8]{1,0:T(4,128)S(1)}, u32[]{:S(2)}, u32[]{:S(2)}) %collective-permute-start.5) | collective-permute-done | bytes 160 | tf_op jit(solution)/shard_map/ppermute | solution.py:74
  25.1 1.3 %shard_map.78 = (bf16[8,128,128]{2,1,0:T(8,128)(2,1)}, bf16[64,32,256]{2,1,0:T(8,128)(2,1)}) custom-call(f32[36,32,256]{2,1,0:T(8,128)S(1)} %get-tuple-element.41.sol.sol_kept, f32[36,32,256]{2,1,0:T(8,128)S(1)} %get-tuple-element.42.base.refs_0_, bf16[2,6,32,256]{3,2,1,0:T(8,128)(2,1)S(1)} %collective-permute-done.first_in.first_q, ...), custom_call_target="tpu_custom_call", output_to_operand_aliasing={{1}: (8, {})} | custom-call | flops 67108864 | bytes 6291456 | tf_op jit(solution)/shard_map/pallas_call | solution.py:27
  26.4 3.7 %all-to-all-start = ((bf16[8,128,128]{2,1,0:T(8,128)(2,1)}), bf16[8,128,128]{2,1,0:T(8,128)(2,1)S(1)}, u32[]{:S(2)}, u32[]{:S(2)}) async-start(bf16[8,128,128]{2,1,0:T(8,128)(2,1)} %get-tuple-element.58), calls=%async_computation | async-start | bytes 524288 | tf_op jit(solution)/shard_map/all_to_all | solution.py:773
  30.8 4.0 %shard_map.79.spread = bf16[1024,1024]{1,0:T(8,128)(2,1)} custom-call(s32[4,8]{1,0:T(4,128)S(1)} %add.7.every, bf16[4,64,512]{2,1,0:T(8,128)(2,1)} %inverse_kept.3, bf16[4,64,512]{2,1,0:T(8,128)(2,1)} %copy-done.9), custom_call_target="tpu_custom_call" | custom-call | flops 1073741824 | bytes 2097152 | tf_op jit(solution)/shard_map/pallas_call | solution.py:635
  34.8 1.3 %all-to-all-done = bf16[8,128,128]{2,1,0:T(8,128)(2,1)S(1)} async-done(((bf16[8,128,128]{2,1,0:T(8,128)(2,1)}), bf16[8,128,128]{2,1,0:T(8,128)(2,1)S(1)}, u32[]{:S(2)}, u32[]{:S(2)}) %all-to-all-start) | async-done | bytes 262176 | tf_op jit(solution)/shard_map/all_to_all | solution.py:773
  36.2 1.6 %copy-done.3 = bf16[1024,1024]{1,0:T(8,128)(2,1)S(1)} copy-done((bf16[1024,1024]{1,0:T(8,128)(2,1)S(1)}, bf16[1024,1024]{1,0:T(8,128)(2,1)}, u32[]{:S(2)}) %copy-start.3) | copy-done | bytes 2097176
  37.8 1.4 %shard_map.80 = bf16[1024,128]{1,0:T(8,128)(2,1)} custom-call(bf16[1024,1024]{1,0:T(8,128)(2,1)S(1)} %copy-done.3, bf16[1024,128]{1,0:T(8,128)(2,1)S(1)} %bitcast.12), custom_call_target="tpu_custom_call" | custom-call | flops 268435456 | bytes 2621440 | tf_op jit(solution)/shard_map/pallas_call | solution.py:27
  39.2 4.1 %all-to-all-start.1 = ((bf16[32,32,128]{2,1,0:T(8,128)(2,1)}), bf16[32,32,128]{2,1,0:T(8,128)(2,1)S(1)}, u32[]{:S(2)}, u32[]{:S(2)}) async-start(bf16[32,32,128]{2,1,0:T(8,128)(2,1)} %bitcast.21), calls=%async_computation.1 | async-start | bytes 524288 | tf_op jit(solution)/shard_map/all_to_all | solution.py:782
  43.3 7.1 %shard_map.81 = (f32[36,32,256]{2,1,0:T(8,128)}, f32[36,32,256]{2,1,0:T(8,128)}) custom-call(bf16[64,32,256]{2,1,0:T(8,128)(2,1)} %get-tuple-element.62.local_kept, bf16[1,1920,1920]{2,1,0:T(8,128)(2,1)} %inverse_kept.5, f32[36,32,256]{2,1,0:T(8,128)} %copy-done, f32[36,32,256]{2,1,0:T(8,128)} %copy-done.1, f32[6,6,3,10]{3,2,1,0:T(4,128)S(1)} %copy-done.6), custom_call_target="tpu_custom_call" | custom-call | flops 1415577600 | bytes 13144288 | tf_op jit(solution)/shard_map/pallas_call | solution.py:27
  50.4 3.6 %all-to-all-done.1 = bf16[32,32,128]{2,1,0:T(8,128)(2,1)S(1)} async-done(((bf16[32,32,128]{2,1,0:T(8,128)(2,1)}), bf16[32,32,128]{2,1,0:T(8,128)(2,1)S(1)}, u32[]{:S(2)}, u32[]{:S(2)}) %all-to-all-start.1) | async-done | bytes 262176 | tf_op jit(solution)/shard_map/all_to_all | solution.py:782
  54.0 1.6 %shard_map.82 = (bf16[2,6,32,256]{3,2,1,0:T(8,128)(2,1)S(1)}, bf16[2,6,32,256]{3,2,1,0:T(8,128)(2,1)S(1)}, f32[36,32,256]{2,1,0:T(8,128)S(1)}) custom-call(bf16[4,8,32,128]{3,2,1,0:T(8,128)(2,1)S(1)} %bitcast.11, bf16[1152,128]{1,0:T(8,128)(2,1)} %get-tuple-element.61.basis_kept, f32[6,6,32,256]{3,2,1,0:T(8,128)} %bitcast.19, f32[6,6,32,256]{3,2,1,0:T(8,128)} %bitcast.20, ...), custom_call_target="tpu_custom_call" | custom-call | bytes 4493536 | tf_op jit(solution)/shard_map/pallas_call | solution.py:27
  55.6 0.9 collective-permute-start.7
  57.1 2.5 %shard_map.83 = (f32[36,32,256]{2,1,0:T(8,128)S(1)}, f32[36,32,256]{2,1,0:T(8,128)S(1)}) custom-call(f32[36,32,256]{2,1,0:T(8,128)S(1)} %get-tuple-element.65.coarse, f32[36,32,256]{2,1,0:T(8,128)} %get-tuple-element.63.sol_kept, f32[36,32,256]{2,1,0:T(8,128)} %get-tuple-element.64.base_kept, f32[6,6,3,10]{3,2,1,0:T(4,128)} %stiffness.7), custom_call_target="tpu_custom_call" | custom-call | bytes 5902560 | tf_op jit(solution)/shard_map/pallas_call | solution.py:27
  59.6 3.0 %collective-permute-done.7.first_in.first_q = bf16[2,6,32,256]{3,2,1,0:T(8,128)(2,1)S(1)} collective-permute-done((bf16[2,6,32,256]{3,2,1,0:T(8,128)(2,1)S(1)}, bf16[2,6,32,256]{3,2,1,0:T(8,128)(2,1)S(1)}, u32[]{:S(2)}, u32[]{:S(2)}) %collective-permute-start.7) | collective-permute-done | bytes 196640 | tf_op jit(solution)/shard_map/ppermute | solution.py:67
  62.7 1.7 %collective-permute-start.9 = (bf16[2,8,32,256]{3,2,1,0:T(8,128)(2,1)S(1)}, bf16[2,8,32,256]{3,2,1,0:T(8,128)(2,1)S(1)}, u32[]{:S(2)}, u32[]{:S(2)}) collective-permute-start(bf16[2,8,32,256]{3,2,1,0:T(8,128)(2,1)S(1)} %get-tuple-element.70), channel_id=1, source_target_pairs={{0,8},{16,24},{8,0},{24,16},{1,9},{17,25},{9,1},{25,17},{2,10},{18... | collective-permute-start | bytes 786440 | tf_op jit(solution)/shard_map/ppermute | solution.py:67
  65.2 0.9 shard_map.85
  66.1 4.7 %collective-permute-done.9.first_s = bf16[2,8,32,256]{3,2,1,0:T(8,128)(2,1)S(1)} collective-permute-done((bf16[2,8,32,256]{3,2,1,0:T(8,128)(2,1)S(1)}, bf16[2,8,32,256]{3,2,1,0:T(8,128)(2,1)S(1)}, u32[]{:S(2)}, u32[]{:S(2)}) %collective-permute-start.9) | collective-permute-done | bytes 262176 | tf_op jit(solution)/shard_map/ppermute | solution.py:67
  70.8 1.3 %shard_map.86 = (bf16[8,128,128]{2,1,0:T(8,128)(2,1)}, bf16[64,32,256]{2,1,0:T(8,128)(2,1)}) custom-call(f32[36,32,256]{2,1,0:T(8,128)S(1)} %get-tuple-element.66.sol.sol_kept, f32[36,32,256]{2,1,0:T(8,128)S(1)} %get-tuple-element.67.base, bf16[2,6,32,256]{3,2,1,0:T(8,128)(2,1)S(1)} %collective-permute-done.7.first_in.first_q, ...), custom_call_target="tpu_custom_call", output_to_operand_aliasing={{1}: (8, {})} | custom-call | flops 67108864 | bytes 6291456 | tf_op jit(solution)/shard_map/pallas_call | solution.py:27
  72.0 11.0 %all_to_all.20 = bf16[8,128,128]{2,1,0:T(8,128)(2,1)S(1)} all-to-all(bf16[8,128,128]{2,1,0:T(8,128)(2,1)} %get-tuple-element.75), channel_id=1, replica_groups=mesh['sub'=4,'crow'=4,'ccol'=2] {'crow','ccol'}, dimensions={0} | all-to-all | bytes 524288 | tf_op jit(solution)/shard_map/all_to_all | solution.py:773
  83.0 1.4 %shard_map.87 = bf16[1024,128]{1,0:T(8,128)(2,1)} custom-call(bf16[1024,1024]{1,0:T(8,128)(2,1)S(1)} %copy-done.4, bf16[1024,128]{1,0:T(8,128)(2,1)S(1)} %bitcast.14), custom_call_target="tpu_custom_call" | custom-call | flops 268435456 | bytes 2621440 | tf_op jit(solution)/shard_map/pallas_call | solution.py:27
  84.4 4.9 %all-to-all-start.3 = ((bf16[32,32,128]{2,1,0:T(8,128)(2,1)}), bf16[32,32,128]{2,1,0:T(8,128)(2,1)S(1)}, u32[]{:S(2)}, u32[]{:S(2)}) async-start(bf16[32,32,128]{2,1,0:T(8,128)(2,1)} %bitcast.22), calls=%async_computation.3 | async-start | bytes 524288 | tf_op jit(solution)/shard_map/all_to_all | solution.py:782
  89.3 6.1 %shard_map.88.sol_kept = f32[36,32,256]{2,1,0:T(8,128)} custom-call(bf16[64,32,256]{2,1,0:T(8,128)(2,1)} %get-tuple-element.76.local_kept, bf16[1,1920,1920]{2,1,0:T(8,128)(2,1)} %inverse_kept.5, f32[36,32,256]{2,1,0:T(8,128)} %copy-done.2), custom_call_target="tpu_custom_call" | custom-call | flops 1415577600 | bytes 10780672 | tf_op jit(solution)/shard_map/pallas_call | solution.py:27
  95.4 4.6 %all-to-all-done.3 = bf16[32,32,128]{2,1,0:T(8,128)(2,1)S(1)} async-done(((bf16[32,32,128]{2,1,0:T(8,128)(2,1)}), bf16[32,32,128]{2,1,0:T(8,128)(2,1)S(1)}, u32[]{:S(2)}, u32[]{:S(2)}) %all-to-all-start.3) | async-done | bytes 262176 | tf_op jit(solution)/shard_map/all_to_all | solution.py:782
  100.0 2.9 %shard_map.89 = f32[6,6,10,3,256]{4,3,2,1,0:T(4,128)} custom-call(bf16[4,8,32,128]{3,2,1,0:T(8,128)(2,1)S(1)} %bitcast.13, bf16[1152,128]{1,0:T(8,128)(2,1)} %get-tuple-element.61.basis_kept, f32[36,32,256]{2,1,0:T(8,128)} %shard_map.88.sol_kept), custom_call_target="tpu_custom_call" | custom-call | bytes 2842624 | tf_op jit(solution)/shard_map/pallas_call | solution.py:27
  (36 shorter events, 4.2 us)
Async XLA Ops:
  2.0 10.8 %collective-permute-start = (bf16[2,6,32,256]{3,2,1,0:T(8,128)(2,1)S(1)}, bf16[2,6,32,256]{3,2,1,0:T(8,128)(2,1)S(1)}, u32[]{:S(2)}, u32[]{:S(2)}) collective-permute-start(bf16[2,6,32,256]{3,2,1,0:T(8,128)(2,1)S(1)} %get-tuple-element.43), channel_id=1, source_target_pairs={{0,1},{2,3},{4,5},{6,7},{1,0},{3,2},{5,4},{7,6},{8,9},{10,11},{12,... | collective-permute-start | bytes 589832 | tf_op jit(solution)/shard_map/ppermute | solution.py:67
  5.1 7.8 %collective-permute-start.1 = (bf16[2,6,32,256]{3,2,1,0:T(8,128)(2,1)S(1)}, bf16[2,6,32,256]{3,2,1,0:T(8,128)(2,1)S(1)}, u32[]{:S(2)}, u32[]{:S(2)}) collective-permute-start(bf16[2,6,32,256]{3,2,1,0:T(8,128)(2,1)S(1)} %get-tuple-element.44), channel_id=1, source_target_pairs={{1,2},{3,4},{5,6},{2,1},{4,3},{6,5},{9,10},{11,12},{13,14},{10,9},... | collective-permute-start | bytes 589832 | tf_op jit(solution)/shard_map/ppermute | solution.py:68
  9.2 15.9 %copy-start = (f32[36,32,256]{2,1,0:T(8,128)}, f32[36,32,256]{2,1,0:T(8,128)S(1)}, u32[]{:S(2)}) copy-start(f32[36,32,256]{2,1,0:T(8,128)S(1)} %get-tuple-element.41.sol.sol_kept) | copy-start | bytes 3538948
  9.2 15.9 %copy-start.1 = (f32[36,32,256]{2,1,0:T(8,128)}, f32[36,32,256]{2,1,0:T(8,128)S(1)}, u32[]{:S(2)}) copy-start(f32[36,32,256]{2,1,0:T(8,128)S(1)} %get-tuple-element.42.base.refs_0_) | copy-start | bytes 3538948
  9.2 3.7 %collective-permute-start.2 = (s32[4,8]{1,0:T(4,128)S(1)}, s32[4,8]{1,0:T(4,128)S(1)}, u32[]{:S(2)}, u32[]{:S(2)}) collective-permute-start(s32[4,8]{1,0:T(4,128)S(1)} %get-tuple-element.45), channel_id=1, source_target_pairs={{0,8},{8,0},{16,24},{24,16},{1,9},{9,1},{17,25},{25,17},{2,10},{10... | collective-permute-start | bytes 392 | tf_op jit(solution)/shard_map/ppermute | solution.py:74
  12.9 5.3 %copy-start.8 = (bf16[4,64,512]{2,1,0:T(8,128)(2,1)S(1)}, bf16[4,64,512]{2,1,0:T(8,128)(2,1)}, u32[]{:S(2)}) copy-start(bf16[4,64,512]{2,1,0:T(8,128)(2,1)} %inverse_kept.3) | copy-start | bytes 786436
  12.9 5.6 %copy-start.7 = (s32[1,8]{1,0:T(1,128)S(1)}, s32[1,8]{1,0:T(1,128)}, u32[]{:S(2)}) copy-start(s32[1,8]{1,0:T(1,128)} %offsets.3) | copy-start | bytes 100
  13.0 12.0 %collective-permute-start.4 = (bf16[2,8,32,256]{3,2,1,0:T(8,128)(2,1)S(1)}, bf16[2,8,32,256]{3,2,1,0:T(8,128)(2,1)S(1)}, u32[]{:S(2)}, u32[]{:S(2)}) collective-permute-start(bf16[2,8,32,256]{3,2,1,0:T(8,128)(2,1)S(1)} %get-tuple-element.49), channel_id=1, source_target_pairs={{8,16},{16,8},{9,17},{17,9},{10,18},{18,10},{11,19},{19,11},{12,20... | collective-permute-start | bytes 786440 | tf_op jit(solution)/shard_map/ppermute | solution.py:68
  13.7 11.4 %collective-permute-start.3 = (bf16[2,8,32,256]{3,2,1,0:T(8,128)(2,1)S(1)}, bf16[2,8,32,256]{3,2,1,0:T(8,128)(2,1)S(1)}, u32[]{:S(2)}, u32[]{:S(2)}) collective-permute-start(bf16[2,8,32,256]{3,2,1,0:T(8,128)(2,1)S(1)} %get-tuple-element.48), channel_id=1, source_target_pairs={{0,8},{16,24},{8,0},{24,16},{1,9},{17,25},{9,1},{25,17},{2,10},{18... | collective-permute-start | bytes 786440 | tf_op jit(solution)/shard_map/ppermute | solution.py:67
  18.1 12.0 %collective-permute-start.6 = (bf16[4,64,512]{2,1,0:T(8,128)(2,1)S(1)}, bf16[4,64,512]{2,1,0:T(8,128)(2,1)S(1)}, u32[]{:S(2)}, u32[]{:S(2)}) collective-permute-start(bf16[4,64,512]{2,1,0:T(8,128)(2,1)S(1)} %copy-done.8), channel_id=1, source_target_pairs={{0,2},{1,3},{2,0},{3,1},{4,6},{5,7},{6,4},{7,5},{8,10},{9,11},{10,... | collective-permute-start | bytes 786440 | tf_op jit(solution)/shard_map/ppermute | solution.py:737
  18.3 6.7 %collective-permute-start.5 = (s32[4,8]{1,0:T(4,128)S(1)}, s32[4,8]{1,0:T(4,128)S(1)}, u32[]{:S(2)}, u32[]{:S(2)}) collective-permute-start(s32[4,8]{1,0:T(4,128)S(1)} %add.6), channel_id=1, source_target_pairs={{0,16},{8,24},{16,0},{24,8},{1,17},{9,25},{17,1},{25,9},{2,18},{10... | collective-permute-start | bytes 392 | tf_op jit(solution)/shard_map/ppermute | solution.py:74
  26.4 9.8 %all-to-all-start = ((bf16[8,128,128]{2,1,0:T(8,128)(2,1)}), bf16[8,128,128]{2,1,0:T(8,128)(2,1)S(1)}, u32[]{:S(2)}, u32[]{:S(2)}) async-start(bf16[8,128,128]{2,1,0:T(8,128)(2,1)} %get-tuple-element.58), calls=%async_computation | async-start | bytes 524288 | tf_op jit(solution)/shard_map/all_to_all | solution.py:773
  30.1 0.7 copy-start.9
  36.2 1.6 %copy-start.3 = (bf16[1024,1024]{1,0:T(8,128)(2,1)S(1)}, bf16[1024,1024]{1,0:T(8,128)(2,1)}, u32[]{:S(2)}) copy-start(bf16[1024,1024]{1,0:T(8,128)(2,1)} %shard_map.79.spread) | copy-start | bytes 6291460
  37.8 5.5 %copy-start.6 = (f32[6,6,3,10]{3,2,1,0:T(4,128)S(1)}, f32[6,6,3,10]{3,2,1,0:T(4,128)}, u32[]{:S(2)}) copy-start(f32[6,6,3,10]{3,2,1,0:T(4,128)} %stiffness.7) | copy-start | bytes 12964
  39.2 14.8 %all-to-all-start.1 = ((bf16[32,32,128]{2,1,0:T(8,128)(2,1)}), bf16[32,32,128]{2,1,0:T(8,128)(2,1)S(1)}, u32[]{:S(2)}, u32[]{:S(2)}) async-start(bf16[32,32,128]{2,1,0:T(8,128)(2,1)} %bitcast.21), calls=%async_computation.1 | async-start | bytes 524288 | tf_op jit(solution)/shard_map/all_to_all | solution.py:782
  55.6 7.0 %collective-permute-start.7 = (bf16[2,6,32,256]{3,2,1,0:T(8,128)(2,1)S(1)}, bf16[2,6,32,256]{3,2,1,0:T(8,128)(2,1)S(1)}, u32[]{:S(2)}, u32[]{:S(2)}) collective-permute-start(bf16[2,6,32,256]{3,2,1,0:T(8,128)(2,1)S(1)} %get-tuple-element.68), channel_id=1, source_target_pairs={{0,1},{2,3},{4,5},{6,7},{1,0},{3,2},{5,4},{7,6},{8,9},{10,11},{12,... | collective-permute-start | bytes 589832 | tf_op jit(solution)/shard_map/ppermute | solution.py:67
  56.5 6.1 %collective-permute-start.8 = (bf16[2,6,32,256]{3,2,1,0:T(8,128)(2,1)S(1)}, bf16[2,6,32,256]{3,2,1,0:T(8,128)(2,1)S(1)}, u32[]{:S(2)}, u32[]{:S(2)}) collective-permute-start(bf16[2,6,32,256]{3,2,1,0:T(8,128)(2,1)S(1)} %get-tuple-element.69), channel_id=1, source_target_pairs={{1,2},{3,4},{5,6},{2,1},{4,3},{6,5},{9,10},{11,12},{13,14},{10,9},... | collective-permute-start | bytes 589832 | tf_op jit(solution)/shard_map/ppermute | solution.py:68
  59.6 11.2 %copy-start.2 = (f32[36,32,256]{2,1,0:T(8,128)}, f32[36,32,256]{2,1,0:T(8,128)S(1)}, u32[]{:S(2)}) copy-start(f32[36,32,256]{2,1,0:T(8,128)S(1)} %get-tuple-element.66.sol.sol_kept) | copy-start | bytes 3538948
  62.6 2.6 %copy-start.5 = (bf16[128,2048]{1,0:T(8,128)(2,1)S(1)}, bf16[128,2048]{1,0:T(8,128)(2,1)}, u32[]{:S(2)}) copy-start(bf16[128,2048]{1,0:T(8,128)(2,1)} %get-tuple-element.72.basis_t) | copy-start | bytes 1572868
  62.7 8.1 %collective-permute-start.9 = (bf16[2,8,32,256]{3,2,1,0:T(8,128)(2,1)S(1)}, bf16[2,8,32,256]{3,2,1,0:T(8,128)(2,1)S(1)}, u32[]{:S(2)}, u32[]{:S(2)}) collective-permute-start(bf16[2,8,32,256]{3,2,1,0:T(8,128)(2,1)S(1)} %get-tuple-element.70), channel_id=1, source_target_pairs={{0,8},{16,24},{8,0},{24,16},{1,9},{17,25},{9,1},{25,17},{2,10},{18... | collective-permute-start | bytes 786440 | tf_op jit(solution)/shard_map/ppermute | solution.py:67
  64.3 6.4 %collective-permute-start.10 = (bf16[2,8,32,256]{3,2,1,0:T(8,128)(2,1)S(1)}, bf16[2,8,32,256]{3,2,1,0:T(8,128)(2,1)S(1)}, u32[]{:S(2)}, u32[]{:S(2)}) collective-permute-start(bf16[2,8,32,256]{3,2,1,0:T(8,128)(2,1)S(1)} %get-tuple-element.71), channel_id=1, source_target_pairs={{8,16},{16,8},{9,17},{17,9},{10,18},{18,10},{11,19},{19,11},{12,20... | collective-permute-start | bytes 786440 | tf_op jit(solution)/shard_map/ppermute | solution.py:68
  70.8 12.2 %copy-start.4 = (bf16[1024,1024]{1,0:T(8,128)(2,1)S(1)}, bf16[1024,1024]{1,0:T(8,128)(2,1)}, u32[]{:S(2)}) copy-start(bf16[1024,1024]{1,0:T(8,128)(2,1)} %shard_map.79.spread) | copy-start | bytes 6291460
  84.4 15.6 %all-to-all-start.3 = ((bf16[32,32,128]{2,1,0:T(8,128)(2,1)}), bf16[32,32,128]{2,1,0:T(8,128)(2,1)S(1)}, u32[]{:S(2)}, u32[]{:S(2)}) async-start(bf16[32,32,128]{2,1,0:T(8,128)(2,1)} %bitcast.22), calls=%async_computation.3 | async-start | bytes 524288 | tf_op jit(solution)/shard_map/all_to_all | solution.py:782
